TPU v7x, 256 devices: a whole 4x4x8 slice. The times are simulated.
256 devices in a mesh: prow: 8 (over y, core), pcol: 32 (over x, z).
Axes of the slice: x: 4, y: 4, z: 8, core: 2. Of those that a mesh axis runs over, the one named last changes fastest.
Arguments:
- state: float32 [3, 176, 4096], P(None, 'prow', 'pcol'), may hold values from -6 to 6
- adjoint: float32 [3, 176, 4096], P(None, 'prow', 'pcol'), may hold values from -6 to 6
- thickness: float32 [32768], P(('prow', 'pcol')), may hold values from 0.5 to 1.5
- direction: float32 [32768], P(('prow', 'pcol')), may hold values from -4 to 4
- design_map: int32 [176, 4096], P('prow', 'pcol'), may hold values from 0 to 32767, as said below
- levels: int32 [8, 32], P('prow', 'pcol'), may hold values from 1 to 4, as said below
- blocks: float32 [576, 72, 4096], P('prow', None, 'pcol'), may hold values from -1 to 1.5, as said below
Outputs:
- tangent: float32 [3, 176, 4096], P(None, 'prow', 'pcol')
- second_adjoint: float32 [3, 176, 4096], P(None, 'prow', 'pcol')
- hess: float32 [32768], P(('prow', 'pcol'))
Inputs may be any that keep to these rules, and one draw needn't show every extreme that they name: `design_map`: each design thickness covers a contiguous region of the shell of about 22 rows by 1 column, with ragged edges; every thickness is taken by some cell; the numbering of the regions is unrelated to their place on the grid. `levels`: each patch's refinement level; some patch has level 4 and some has level 1. `blocks`: each column's block is symmetric with a diagonal that exceeds the sum of the magnitudes of the rest of its row.
All inputs are finite; a program needn't handle non-finite values.
Results may differ from a plain program's by a relative error of at most 0.0003.
Values sent between devices are 32-bit elements; how exact they have to be, the bound alone decides.
No kernel may reach another device: no remote copies, remote signals or barrier semaphores. Data moves between devices by JAX's collectives and lax.ppermute only.
A program may use at most 64 MiB of HBM per device.

v0:
```python
import jax
import jax.numpy as jnp
from jax import lax
from jax.sharding import PartitionSpec as P

CR = 22
CC = 128
DV_DEV = 128
ITERS = 2
BLK = 72


HIGH = lax.Precision.HIGHEST


def with_halo(block, sides, width, periodic):
    for axis, dim in sides:
        count = lax.axis_size(axis)
        forward = [(i, i + 1) for i in range(count - 1)]
        if periodic:
            forward.append((count - 1, 0))
        backward = [(target, source) for source, target in forward]
        low = lax.ppermute(
            lax.slice_in_dim(block, block.shape[dim] - width, None, axis=dim), axis, forward
        )
        high = lax.ppermute(lax.slice_in_dim(block, 0, width, axis=dim), axis, backward)
        block = jnp.concatenate([low, block, high], axis=dim)
    return block


def borders(field):
    rows = with_halo(field, (("prow", 2),), 1, False)
    cols = with_halo(field, (("pcol", 3),), 1, True)
    return (rows[:, :, :-2, :], rows[:, :, 2:, :], cols[:, :, :, :-2], cols[:, :, :, 2:])


def stiffness_with(weights, field, around, shift):
    total = shift * field
    for weight, other in zip(weights, around):
        total = total + weight * (field - other)
    return total


def precondition(resid, matrices, level):
    extended = with_halo(resid, (("prow", 2),), 1, False)
    flat = extended.reshape(2, BLK, CC)
    term = jnp.einsum("abj,nbj->naj", matrices, flat, precision=HIGH)

    def further(order, carry):
        current, total = carry
        current = 0.5 * jnp.einsum("abj,nbj->naj", matrices, current, precision=HIGH)
        return (current, total + current)

    term, total = lax.fori_loop(1, level, further, (term, term))
    total = total.reshape(2, 3, CR + 2, CC)
    edges = jnp.concatenate([total[:, :, :1, :], total[:, :, -1:, :]], axis=2)
    returned = with_halo(edges, (("prow", 2),), 1, False)
    inner = total[:, :, 1:-1, :]
    inner = inner.at[:, :, 0, :].add(returned[:, :, 0, :])
    inner = inner.at[:, :, -1, :].add(returned[:, :, 3, :])
    return inner


def spread(values):
    return values[:, None, None, None]


def local_sums(first, second):
    return jnp.sum(first * second, axis=(1, 2, 3))


def classic_sum(first, second):
    return lax.psum(local_sums(first, second), ("prow", "pcol"))


def per_device(state, adjoint, thickness, direction, design_map, levels, blocks):
    designs = lax.all_gather(
        jnp.stack([thickness, direction]), ("prow", "pcol"), axis=1, tiled=True
    )
    t_cell = jnp.take(designs[0], design_map)
    d_cell = jnp.take(designs[1], design_map)
    stiff = t_cell * t_cell * t_cell
    slope = 3.0 * t_cell * t_cell * d_cell
    curve = 6.0 * t_cell * d_cell
    coeff_n = borders(jnp.stack([stiff, slope])[:, None, :, :])
    weights = tuple((0.5 * (stiff + other[0, 0]) for other in coeff_n))
    dweights = tuple((0.5 * (slope + other[1, 0]) for other in coeff_n))
    level = levels[0, 0]
    known = jnp.stack([state, adjoint])
    known_n = borders(known)
    rhs = -stiffness_with(dweights, known, known_n, 0.0)
    solved = jnp.zeros_like(rhs)
    resid = rhs
    pre = precondition(resid, blocks, level)
    search = pre
    gamma = classic_sum(resid, pre)
    for step in range(ITERS):
        image = stiffness_with(weights, search, borders(search), 1.0)
        alpha = gamma / classic_sum(search, image)
        solved = solved + spread(alpha) * search
        if step + 1 < ITERS:
            resid = resid - spread(alpha) * image
            pre = precondition(resid, blocks, level)
            gamma_new = classic_sum(resid, pre)
            search = pre + spread(gamma_new / gamma) * search
            gamma = gamma_new
    solved_n = borders(solved)
    first_acc = jnp.zeros_like(stiff)
    second_acc = jnp.zeros_like(stiff)
    for known_o, solved_o in zip(known_n, solved_n):
        known_d = known - known_o
        solved_d = solved - solved_o
        first_acc = first_acc + jnp.sum(solved_d[1] * known_d[0] + known_d[1] * solved_d[0], axis=0)
        second_acc = second_acc + jnp.sum(known_d[1] * known_d[0], axis=0)
    cellterm = -(0.5 * 3.0 * t_cell * t_cell * first_acc + 0.5 * curve * second_acc)
    contrib = jax.ops.segment_sum(
        cellterm.reshape(-1), design_map.reshape(-1), num_segments=designs.shape[1]
    )
    summed = lax.psum(contrib, ("prow", "pcol"))
    owned = lax.dynamic_slice_in_dim(summed, lax.axis_index(("prow", "pcol")) * DV_DEV, DV_DEV, 0)
    return (solved[0], solved[1], owned)


def solution(mesh):
    placed = (
        P(None, "prow", "pcol"),
        P(None, "prow", "pcol"),
        P(("prow", "pcol")),
        P(("prow", "pcol")),
        P("prow", "pcol"),
        P("prow", "pcol"),
        P("prow", None, "pcol"),
    )
    return jax.shard_map(
        per_device,
        mesh=mesh,
        in_specs=placed,
        out_specs=(P(None, "prow", "pcol"), P(None, "prow", "pcol"), P(("prow", "pcol"))),
        check_vma=False,
    )
```

profile of v0, /device:TPU:1, one launch (start us, length us, event | category | flops | bytes accessed | tf_op | source)
XLA Modules:
  0.0 761.0 jit_solution(17763169965979234398)
XLA Ops:
  7.9 66.5 %all_gather.3 = f32[2,32768]{1,0:T(2,128)S(1)} all-gather(f32[2,128]{1,0:T(2,128)S(1)} %pad_maximum_fusion.27), channel_id=1, replica_groups=mesh['prow'=8,'pcol'=32] {'prow','pcol'}, dimensions={1}, use_global_device_ids=true | all-gather | bytes 263168 | tf_op jit(solution)/shard_map/all_gather | solution.py:77
  75.3 14.9 %gather_fusion = f32[2816]{0:T(1024)S(1)} fusion(f32[32768]{0:T(1024)S(1)} %bitcast.132, s32[3072]{0:T(1024)S(1)} %pad_clamp_fusion), kind=kCustom, calls=%fused_computation.clone | custom fusion | bytes 33792 | tf_op jit(solution)/shard_map/jit(_take)/gather | solution.py:80
  90.3 14.9 %gather_fusion.1 = f32[2816]{0:T(1024)S(1)} fusion(f32[32768]{0:T(1024)S(1)} %bitcast.131, s32[3072]{0:T(1024)S(1)} %pad_clamp_fusion), kind=kCustom, calls=%fused_computation.1.clone | custom fusion | bytes 33792 | tf_op jit(solution)/shard_map/jit(_take)/gather | solution.py:81
  105.4 4.8 collective-permute-start.6
  110.2 3.7 collective-permute-start
  113.9 2.8 collective-permute-start.2
  116.9 4.8 collective-permute-start.7
  121.7 3.3 collective-permute-start.1
  125.1 1.9 collective-permute-start.3
  127.1 2.8 collective-permute-done.3
  130.1 2.0 collective-permute-start.8
  132.1 2.4 collective-permute-start.9
  134.5 3.5 copy.19
  138.1 9.2 %convolution_bitcast_fusion.1 = f32[2,72,128]{1,0,2:T(2,128)S(1)} fusion(f32[2,72,128]{1,0,2:T(2,128)S(1)} %copy.18, f32[72,72,128]{1,0,2:T(8,128)} %copy.19), kind=kOutput, calls=%fused_computation.8 | convolution fusion | flops 15925248 | bytes 2801664 | tf_op jit(solution)/shard_map/abj,nbj->naj/dot_general | solution.py:47
  147.3 30.6 %while.28 = (s32[]{:T(128)}, f32[2,72,128]{1,0,2:T(2,128)S(1)}, f32[2,72,128]{1,0,2:T(2,128)S(1)}, s32[]{:T(128)}, f32[72,72,128]{1,0,2:T(8,128)}, /*index=5*/s32[]{:T(128)}) while((s32[]{:T(128)}, f32[2,72,128]{1,0,2:T(2,128)S(1)}, f32[2,72,128]{1,0,2:T(2,128)S(1)}, s32[]{:T(128)}, f32[72,72,128]{1,0,2:T(8,128)}, /*index=5*/s32[]{:T(128)}) %tuple.104), condition=%wide.region_1.3_spmd, body=%wide.region_0.0_spmd.sunk | while | flops 15962114 | bytes 3096645 | solution.py:54
  148.0 9.3 %fusion.113 = (f32[2,72,128]{1,0,2:T(2,128)S(1)}, f32[2,72,128]{1,0,2:T(2,128)S(1)}) fusion(f32[2,72,128]{1,0,2:T(2,128)S(1)} %get-tuple-element.304, f32[2,72,128]{1,0,2:T(2,128)S(1)} %copy.51, f32[72,72,128]{1,0,2:T(8,128)} %get-tuple-element.312), kind=kOutput, calls=%fused_computation.164.clone.1 | convolution fusion | flops 15962112 | bytes 2949120 | tf_op jit(solution)/shard_map/while/body/abj,nbj->naj/dot_general | solution.py:51
  158.0 9.3 %fusion.113 = (f32[2,72,128]{1,0,2:T(2,128)S(1)}, f32[2,72,128]{1,0,2:T(2,128)S(1)}) fusion(f32[2,72,128]{1,0,2:T(2,128)S(1)} %get-tuple-element.304, f32[2,72,128]{1,0,2:T(2,128)S(1)} %copy.51, f32[72,72,128]{1,0,2:T(8,128)} %get-tuple-element.312), kind=kOutput, calls=%fused_computation.164.clone.1 | convolution fusion | flops 15962112 | bytes 2949120 | tf_op jit(solution)/shard_map/while/body/abj,nbj->naj/dot_general | solution.py:51
  168.0 9.3 %fusion.113 = (f32[2,72,128]{1,0,2:T(2,128)S(1)}, f32[2,72,128]{1,0,2:T(2,128)S(1)}) fusion(f32[2,72,128]{1,0,2:T(2,128)S(1)} %get-tuple-element.304, f32[2,72,128]{1,0,2:T(2,128)S(1)} %copy.51, f32[72,72,128]{1,0,2:T(8,128)} %get-tuple-element.312), kind=kOutput, calls=%fused_computation.164.clone.1 | convolution fusion | flops 15962112 | bytes 2949120 | tf_op jit(solution)/shard_map/while/body/abj,nbj->naj/dot_general | solution.py:51
  178.1 1.9 collective-permute-start.10
  180.0 2.4 collective-permute-start.11
  182.5 2.4 collective-permute-done.11
  184.9 1.9 collective-permute-start.12
  186.9 2.4 collective-permute-start.13
  189.7 4.8 collective-permute-start.15
  194.5 2.5 collective-permute-done.14
  197.3 75.3 %all-reduce = (f32[2]{0:T(128)S(1)}, f32[2]{0:T(128)S(1)}) all-reduce(f32[2]{0:T(128)S(1)} %get-tuple-element.139, f32[2]{0:T(128)S(1)} %get-tuple-element.138), channel_id=1, replica_groups=mesh['prow'=8,'pcol'=32] {'prow','pcol'}, use_global_device_ids=true, to_apply=%region_3.5 | all-reduce | flops 4 | bytes 32 | tf_op jit(solution)/shard_map/psum | solution.py:73
  272.7 3.6 collective-permute-start.16
  276.3 1.9 collective-permute-start.17
  278.2 3.0 collective-permute-done.17
  281.4 9.2 %convolution_bitcast_fusion = f32[2,72,128]{1,0,2:T(2,128)S(1)} fusion(f32[2,72,128]{1,0,2:T(2,128)S(1)} %copy.22, f32[72,72,128]{1,0,2:T(8,128)} %get-tuple-element.333), kind=kOutput, calls=%fused_computation.7 | convolution fusion | flops 15925248 | bytes 2801664 | tf_op jit(solution)/shard_map/abj,nbj->naj/dot_general | solution.py:47
  290.6 30.6 %while.29 = (s32[]{:T(128)}, f32[2,72,128]{1,0,2:T(2,128)S(1)}, f32[2,72,128]{1,0,2:T(2,128)S(1)}, s32[]{:T(128)}, f32[72,72,128]{1,0,2:T(8,128)}, /*index=5*/s32[]{:T(128)}) while((s32[]{:T(128)}, f32[2,72,128]{1,0,2:T(2,128)S(1)}, f32[2,72,128]{1,0,2:T(2,128)S(1)}, s32[]{:T(128)}, f32[72,72,128]{1,0,2:T(8,128)}, /*index=5*/s32[]{:T(128)}) %tuple.112), condition=%wide.region_7.9_spmd, body=%wide.region_6.8_spmd.sunk | while | flops 15962114 | bytes 3096645 | solution.py:54
  291.3 9.3 %fusion.116 = (f32[2,72,128]{1,0,2:T(2,128)S(1)}, f32[2,72,128]{1,0,2:T(2,128)S(1)}) fusion(f32[2,72,128]{1,0,2:T(2,128)S(1)} %get-tuple-element.322, f32[2,72,128]{1,0,2:T(2,128)S(1)} %copy.52, f32[72,72,128]{1,0,2:T(8,128)} %get-tuple-element.330), kind=kOutput, calls=%fused_computation.165.clone.1 | convolution fusion | flops 15962112 | bytes 2949120 | tf_op jit(solution)/shard_map/while/body/abj,nbj->naj/dot_general | solution.py:51
  301.3 9.3 %fusion.116 = (f32[2,72,128]{1,0,2:T(2,128)S(1)}, f32[2,72,128]{1,0,2:T(2,128)S(1)}) fusion(f32[2,72,128]{1,0,2:T(2,128)S(1)} %get-tuple-element.322, f32[2,72,128]{1,0,2:T(2,128)S(1)} %copy.52, f32[72,72,128]{1,0,2:T(8,128)} %get-tuple-element.330), kind=kOutput, calls=%fused_computation.165.clone.1 | convolution fusion | flops 15962112 | bytes 2949120 | tf_op jit(solution)/shard_map/while/body/abj,nbj->naj/dot_general | solution.py:51
  311.3 9.3 %fusion.116 = (f32[2,72,128]{1,0,2:T(2,128)S(1)}, f32[2,72,128]{1,0,2:T(2,128)S(1)}) fusion(f32[2,72,128]{1,0,2:T(2,128)S(1)} %get-tuple-element.322, f32[2,72,128]{1,0,2:T(2,128)S(1)} %copy.52, f32[72,72,128]{1,0,2:T(8,128)} %get-tuple-element.330), kind=kOutput, calls=%fused_computation.165.clone.1 | convolution fusion | flops 15962112 | bytes 2949120 | tf_op jit(solution)/shard_map/while/body/abj,nbj->naj/dot_general | solution.py:51
  321.3 1.9 collective-permute-start.18
  323.3 2.4 collective-permute-start.19
  325.8 2.4 collective-permute-done.19
  328.4 72.2 %psum.37 = f32[2]{0:T(128)S(1)} all-reduce(f32[2]{0:T(128)S(1)} %multiply_reduce_fusion), channel_id=1, replica_groups=mesh['prow'=8,'pcol'=32] {'prow','pcol'}, use_global_device_ids=true, to_apply=%region_9.11 | all-reduce | flops 2 | bytes 16 | tf_op jit(solution)/shard_map/psum | solution.py:73
  400.7 2.4 collective-permute-start.20
  407.0 3.0 collective-permute-start.23
  410.0 2.5 collective-permute-done.22
  412.8 76.0 %psum.38 = f32[2]{0:T(128)S(1)} all-reduce(f32[2]{0:T(128)S(1)} %fusion.12), channel_id=1, replica_groups=mesh['prow'=8,'pcol'=32] {'prow','pcol'}, use_global_device_ids=true, to_apply=%region_11.13 | all-reduce | flops 2 | bytes 16 | tf_op jit(solution)/shard_map/psum | solution.py:73
  489.2 4.7 collective-permute-start.27
  493.9 4.3 collective-permute-start.24
  498.1 1.9 collective-permute-start.25
  500.1 2.9 collective-permute-done.25
  503.3 15.9 %scatter_custom_fusion = f32[32768]{0:T(1024)} fusion(s32[2816]{0:T(1024)S(1)} %bitcast.155, f32[2816]{0:T(1024)S(1)} %fusion.52, f32[]{:T(128)} %constant.129.clone.1), kind=kCustom, calls=%fused_computation.83 | custom fusion | flops 2816 | bytes 131076 | tf_op jit(solution)/shard_map/scatter-add | solution.py:116
  519.8 233.1 %all-reduce.3.cloned.1.call-done = f32[32768]{0:T(1024)} async-done(((f32[32768]{0:T(1024)}), f32[32768]{0:T(1024)}) %all-reduce.3.cloned.1.call-update) | async-done | bytes 131088 | tf_op jit(solution)/shard_map/psum | solution.py:119
  (101 shorter events, 10.7 us)
Async XLA Ops:
  7.2 745.7 %all-reduce.3.cloned.1.call-start = ((), (), s32[]{:S(2)}) async-start(), calls=%async_computation | async-start | bytes 262144 | tf_op jit(solution)/shard_map/psum | solution.py:119
  75.3 14.9 %copy-start.3 = (s32[22,128]{1,0:T(8,128)S(1)}, s32[22,128]{1,0:T(8,128)}, u32[]{:S(2)}) copy-start(s32[22,128]{1,0:T(8,128)} %param.25) | copy-start | bytes 33796
  90.3 26.4 %copy-start.1 = (f32[3,22,128]{2,1,0:T(8,128)S(1)}, f32[3,22,128]{2,1,0:T(8,128)}, u32[]{:S(2)}) copy-start(f32[3,22,128]{2,1,0:T(8,128)} %param.22) | copy-start | bytes 101380
  90.3 26.4 %copy-start.2 = (f32[3,22,128]{2,1,0:T(8,128)S(1)}, f32[3,22,128]{2,1,0:T(8,128)}, u32[]{:S(2)}) copy-start(f32[3,22,128]{2,1,0:T(8,128)} %param.21) | copy-start | bytes 101380
  90.3 44.1 %copy-start = (f32[72,72,128]{2,1,0:T(8,128)S(1)}, f32[72,72,128]{2,1,0:T(8,128)}, u32[]{:S(2)}) copy-start(f32[72,72,128]{2,1,0:T(8,128)} %param.27) | copy-start | bytes 7962628
  105.4 11.5 %collective-permute-start.4 = (f32[2,1,22,1]{3,2,1,0:T(8,128)S(1)}, f32[2,1,22,1]{3,2,1,0:T(8,128)S(1)}, u32[]{:S(2)}, u32[]{:S(2)}) collective-permute-start(f32[2,1,22,1]{3,2,1,0:T(8,128)S(1)} %get-tuple-element.218), channel_id=1, source_target_pairs={{0,1},{1,2},{2,3},{3,4},{4,5},{5,6},{6,7},{7,8},{8,9},{9,10},{10,1... | collective-permute-start | bytes 536 | tf_op jit(solution)/shard_map/ppermute | solution.py:23
  105.4 16.3 %collective-permute-start.6 = (f32[2,1,22,1]{3,2,1,0:T(8,128)S(1)}, f32[2,1,22,1]{3,2,1,0:T(8,128)S(1)}, u32[]{:S(2)}, u32[]{:S(2)}) collective-permute-start(f32[2,1,22,1]{3,2,1,0:T(8,128)S(1)} %get-tuple-element.219), channel_id=1, source_target_pairs={{1,0},{2,1},{3,2},{4,3},{5,4},{6,5},{7,6},{8,7},{9,8},{10,9},{11,1... | collective-permute-start | bytes 536 | tf_op jit(solution)/shard_map/ppermute | solution.py:26
  110.2 14.9 %collective-permute-start = (f32[2,1,1,128]{3,2,1,0:T(1,128)S(1)}, f32[2,1,1,128]{3,2,1,0:T(1,128)S(1)}, u32[]{:S(2)}, u32[]{:S(2)}) collective-permute-start(f32[2,1,1,128]{3,2,1,0:T(1,128)S(1)} %get-tuple-element.216), channel_id=1, source_target_pairs={{0,32},{32,64},{64,96},{96,128},{128,160},{160,192},{192,224},{1,3... | collective-permute-start | bytes 3080 | tf_op jit(solution)/shard_map/ppermute | solution.py:23
  113.9 13.1 %collective-permute-start.2 = (f32[2,1,1,128]{3,2,1,0:T(1,128)S(1)}, f32[2,1,1,128]{3,2,1,0:T(1,128)S(1)}, u32[]{:S(2)}, u32[]{:S(2)}) collective-permute-start(f32[2,1,1,128]{3,2,1,0:T(1,128)S(1)} %get-tuple-element.217), channel_id=1, source_target_pairs={{32,0},{64,32},{96,64},{128,96},{160,128},{192,160},{224,192},{33,... | collective-permute-start | bytes 3080 | tf_op jit(solution)/shard_map/ppermute | solution.py:26
  116.8 10.3 %collective-permute-start.5 = (f32[2,3,22,1]{3,2,1,0:T(8,128)S(1)}, f32[2,3,22,1]{3,2,1,0:T(8,128)S(1)}, u32[]{:S(2)}, u32[]{:S(2)}) collective-permute-start(f32[2,3,22,1]{3,2,1,0:T(8,128)S(1)} %get-tuple-element.199), channel_id=1, source_target_pairs={{0,1},{1,2},{2,3},{3,4},{4,5},{5,6},{6,7},{7,8},{8,9},{9,10},{10,1... | collective-permute-start | bytes 1592 | tf_op jit(solution)/shard_map/ppermute | solution.py:23
  116.9 10.2 %collective-permute-start.7 = (f32[2,3,22,1]{3,2,1,0:T(8,128)S(1)}, f32[2,3,22,1]{3,2,1,0:T(8,128)S(1)}, u32[]{:S(2)}, u32[]{:S(2)}) collective-permute-start(f32[2,3,22,1]{3,2,1,0:T(8,128)S(1)} %get-tuple-element.198), channel_id=1, source_target_pairs={{1,0},{2,1},{3,2},{4,3},{5,4},{6,5},{7,6},{8,7},{9,8},{10,9},{11,1... | collective-permute-start | bytes 1592 | tf_op jit(solution)/shard_map/ppermute | solution.py:26
  121.7 5.4 collective-permute-start.1
  125.1 4.9 collective-permute-start.3
  130.1 7.8 %collective-permute-start.8 = (f32[2,3,1,128]{3,2,1,0:T(1,128)S(1)}, f32[2,3,1,128]{3,2,1,0:T(1,128)S(1)}, u32[]{:S(2)}, u32[]{:S(2)}) collective-permute-start(f32[2,3,1,128]{3,2,1,0:T(1,128)S(1)} %get-tuple-element.196), channel_id=1, source_target_pairs={{0,32},{32,64},{64,96},{96,128},{128,160},{160,192},{192,224},{1,3... | collective-permute-start | bytes 9224 | tf_op jit(solution)/shard_map/ppermute | solution.py:23
  132.1 5.9 collective-permute-start.9
  178.1 4.4 collective-permute-start.10
  180.0 4.9 collective-permute-start.11
  184.9 12.0 %collective-permute-start.12 = (f32[2,3,1,128]{3,2,1,0:T(1,128)S(1)}, f32[2,3,1,128]{3,2,1,0:T(1,128)S(1)}, u32[]{:S(2)}, u32[]{:S(2)}) collective-permute-start(f32[2,3,1,128]{3,2,1,0:T(1,128)S(1)} %slice_add_fusion.2), channel_id=1, source_target_pairs={{0,32},{32,64},{64,96},{96,128},{128,160},{160,192},{192,224},{1,3... | collective-permute-start | bytes 9224 | tf_op jit(solution)/shard_map/ppermute | solution.py:23
  186.9 10.0 %collective-permute-start.13 = (f32[2,3,1,128]{3,2,1,0:T(1,128)S(1)}, f32[2,3,1,128]{3,2,1,0:T(1,128)S(1)}, u32[]{:S(2)}, u32[]{:S(2)}) collective-permute-start(f32[2,3,1,128]{3,2,1,0:T(1,128)S(1)} %slice.476), channel_id=1, source_target_pairs={{32,0},{64,32},{96,64},{128,96},{160,128},{192,160},{224,192},{33,... | collective-permute-start | bytes 9224 | tf_op jit(solution)/shard_map/ppermute | solution.py:26
  189.4 7.5 collective-permute-start.14
  189.7 7.3 collective-permute-start.15
  272.7 5.5 collective-permute-start.16
  276.3 4.9 collective-permute-start.17
  321.3 4.4 collective-permute-start.18
  323.3 4.9 collective-permute-start.19
  400.7 11.8 %collective-permute-start.20 = (f32[2,3,1,128]{3,2,1,0:T(1,128)S(1)}, f32[2,3,1,128]{3,2,1,0:T(1,128)S(1)}, u32[]{:S(2)}, u32[]{:S(2)}) collective-permute-start(f32[2,3,1,128]{3,2,1,0:T(1,128)S(1)} %get-tuple-element.184), channel_id=1, source_target_pairs={{0,32},{32,64},{64,96},{96,128},{128,160},{160,192},{192,224},{1,3... | collective-permute-start | bytes 9224 | tf_op jit(solution)/shard_map/ppermute | solution.py:23
  403.1 9.3 %collective-permute-start.21 = (f32[2,3,1,128]{3,2,1,0:T(1,128)S(1)}, f32[2,3,1,128]{3,2,1,0:T(1,128)S(1)}, u32[]{:S(2)}, u32[]{:S(2)}) collective-permute-start(f32[2,3,1,128]{3,2,1,0:T(1,128)S(1)} %get-tuple-element.185), channel_id=1, source_target_pairs={{32,0},{64,32},{96,64},{128,96},{160,128},{192,160},{224,192},{33,... | collective-permute-start | bytes 9224 | tf_op jit(solution)/shard_map/ppermute | solution.py:26
  405.1 7.3 collective-permute-start.22
  407.0 5.5 collective-permute-start.23
  489.0 11.1 %collective-permute-start.26 = (f32[2,3,22,1]{3,2,1,0:T(8,128)S(1)}, f32[2,3,22,1]{3,2,1,0:T(8,128)S(1)}, u32[]{:S(2)}, u32[]{:S(2)}) collective-permute-start(f32[2,3,22,1]{3,2,1,0:T(8,128)S(1)} %get-tuple-element.180), channel_id=1, source_target_pairs={{0,1},{1,2},{2,3},{3,4},{4,5},{5,6},{6,7},{7,8},{8,9},{9,10},{10,1... | collective-permute-start | bytes 1592 | tf_op jit(solution)/shard_map/ppermute | solution.py:23
  489.2 10.9 %collective-permute-start.27 = (f32[2,3,22,1]{3,2,1,0:T(8,128)S(1)}, f32[2,3,22,1]{3,2,1,0:T(8,128)S(1)}, u32[]{:S(2)}, u32[]{:S(2)}) collective-permute-start(f32[2,3,22,1]{3,2,1,0:T(8,128)S(1)} %get-tuple-element.181), channel_id=1, source_target_pairs={{1,0},{2,1},{3,2},{4,3},{5,4},{6,5},{7,6},{8,7},{9,8},{10,9},{11,1... | collective-permute-start | bytes 1592 | tf_op jit(solution)/shard_map/ppermute | solution.py:26
  493.9 6.3 collective-permute-start.24
  498.1 4.9 collective-permute-start.25
Sparse Core Ops, SparseCore 0:
  519.3 233.5 all-reduce.2
where the time goes:
time: 762 us; the launch traced here: 761 us
  blocking collectives  290 us (38%)
  waiting for transfers between devices  252 us (33%)
  matrix products  74.2 us (10%)
  starting transfers between devices  69.5 us (9%)
  local copies, waits for them, and re-layouts  36.5 us (5%)
  other arithmetic  18.9 us (2%)
  between operations  14.7 us (2%)
    psum x1, waiting for transfers between devices, per_device(): summed = lax.psum(contrib, ('prow', 'pcol'))  233 us
    psum x3, blocking collectives, classic_sum(): return lax.psum(local_sums(first, second), ('prow', 'pcol'))  223 us
    all_gather x1, blocking collectives, per_device(): lax.all_gather(jnp.stack([thickness, direction]), ('prow', 'pcol'), axis=...  66.5 us
    dot_general x6, matrix products, further(): jnp.einsum('abj,nbj->naj', matrices, current, precision=HIGH)  55.8 us
    ppermute x14, starting transfers between devices, with_halo(): lax.ppermute(lax.slice_in_dim(block, 0, width, axis=dim), axis, backward)  42.1 us
    ppermute x14, starting transfers between devices, with_halo(): lax.ppermute(lax.slice_in_dim(block, block.shape[dim] - width, None, axis...  27.4 us
    dot_general x2, matrix products, precondition(): term = jnp.einsum('abj,nbj->naj', matrices, flat, precision=HIGH)  18.4 us
    scatter-add x1, other arithmetic, per_device(): jax.ops.segment_sum(cellterm.reshape(-1), design_map.reshape(-1), num_seg...  15.9 us
  transfers between devices with their start and end apart: 29, of which 8 were waited for; matrix products, arithmetic and copies ran while one was open for 1% of the time, Pallas kernels for 0%

commit v1 on v0

v1 whole, which is shorter than its diff:
```python
import functools

import jax
import jax.numpy as jnp
from jax import lax
from jax.experimental import pallas as pl
from jax.experimental.pallas import tpu as pltpu
from jax.sharding import PartitionSpec as P

CR = 22
CC = 128
DV = 128
BLK = 72
EXT = CR + 2
FR = 32
BOTH = ("prow", "pcol")
F32 = jnp.float32
BF16 = jnp.bfloat16

VMEM = pl.BlockSpec(memory_space=pltpu.VMEM)
SMEM = pl.BlockSpec(memory_space=pltpu.SMEM)
ANY = pl.BlockSpec(memory_space=pl.ANY)


def call(kernel, out_shapes, in_specs, scratch=(), out_specs=None):
    return pl.pallas_call(
        kernel,
        out_shape=[jax.ShapeDtypeStruct(s, F32) for s in out_shapes],
        in_specs=list(in_specs),
        out_specs=[VMEM] * len(out_shapes) if out_specs is None else out_specs,
        scratch_shapes=list(scratch),
        compiler_params=pltpu.CompilerParams(vmem_limit_bytes=48 * 1024 * 1024),
    )


def iota(shape, dim):
    return lax.broadcasted_iota(jnp.int32, shape, dim)


def pack_edges(tiles, width):
    lane = iota((8, CC), 1)
    first = jnp.zeros((8, CC), F32)
    last = jnp.zeros((8, CC), F32)
    for k, tile in enumerate(tiles):
        at = k * width
        here = (lane >= at) & (lane < at + width)
        first = jnp.where(here, pltpu.roll(tile, at, 1) if at else tile, first)
        last = jnp.where(here, pltpu.roll(tile, at + width, 1), last)
    return first, last


def unpack_edges(from_left, from_right, count, width):
    lane = iota((8, CC), 1)
    tiles = []
    for k in range(count):
        at = k * width
        right = pltpu.roll(from_right, CC - at, 1) if at else from_right
        shift = (CC - width - at) % CC
        left = pltpu.roll(from_left, shift, 1) if shift else from_left
        tiles.append(jnp.where(lane < width, right, jnp.where(lane >= CC - width, left, 0.0)))
    return tiles


def lanes_of(x):
    return iota(x.shape, x.ndim - 1)


def left_of(main, side):
    dim = main.ndim - 1
    return jnp.where(lanes_of(main) == 0, pltpu.roll(side, 1, dim), pltpu.roll(main, 1, dim))


def right_of(main, side):
    dim = main.ndim - 1
    return jnp.where(
        lanes_of(main) == CC - 1, pltpu.roll(side, CC - 1, dim), pltpu.roll(main, CC - 1, dim)
    )


def grid_mask(prow, last, start, rows):
    row = iota((rows, CC), 0) + (start - 8)
    outside = ((row < 0) & (prow == 0)) | ((row >= CR) & (prow == last))
    return jnp.where(outside, 0.0, 1.0).astype(F32)


def start_kernel(state, adjoint, dmap, first_out, last_out, scr):
    scr[...] = jnp.zeros_like(scr)
    scr[0:3, 0:CR, :] = state[...]
    scr[3:6, 0:CR, :] = adjoint[...]
    scr[6, 0:CR, :] = dmap[...].astype(F32)
    tiles = [scr[f, 8 * g:8 * g + 8, :] for f in range(7) for g in range(3)]
    first, last = pack_edges(tiles, 1)
    first_out[...] = first
    last_out[...] = last


def rows_kernel(state, adjoint, dmap, from_left, from_right, side_out, up_out, down_out, scr):
    scr[...] = jnp.zeros_like(scr)
    scr[0:3, 0:CR, :] = state[...]
    scr[3:6, 0:CR, :] = adjoint[...]
    scr[6, 0:CR, :] = dmap[...].astype(F32)
    tiles = unpack_edges(from_left[...], from_right[...], 21, 1)
    for f in range(7):
        for g in range(3):
            side_out[f, 8 * g:8 * g + 8, :] = tiles[3 * f + g]
    up_out[...] = jnp.zeros_like(up_out)
    down_out[...] = jnp.zeros_like(down_out)
    for f in range(7):
        up_out[0, 2 * f:2 * f + 2, :] = scr[f, 0:2, :]
        up_out[1, 2 * f:2 * f + 2, :] = side_out[f, 0:2, :]
        down_out[0, 2 * f:2 * f + 2, :] = scr[f, CR - 2:CR, :]
        down_out[1, 2 * f:2 * f + 2, :] = side_out[f, CR - 2:CR, :]


def apply_blocks(mats, vec):
    def rows(step, carry):
        one, two = carry
        for u in range(8):
            at = step * 8 + u
            mat = mats[at]
            one = one + mat * vec[0, pl.ds(at, 1), :]
            two = two + mat * vec[1, pl.ds(at, 1), :]
        return one, two

    zero = jnp.zeros((BLK, CC), F32)
    return lax.fori_loop(0, BLK // 8, rows, (zero, zero))


def local_solve(mats, vec, total, level):
    one, two = apply_blocks(mats, vec)
    total[0] = one
    total[1] = two
    vec[0] = one
    vec[1] = two

    def further(_, carry):
        one, two = apply_blocks(mats, vec)
        one = 0.5 * one
        two = 0.5 * two
        vec[0] = one
        vec[1] = two
        total[0] += one
        total[1] += two
        return carry

    lax.fori_loop(1, level, further, 0)


def look_up(table, index, tcell, dcell):
    flipped = table[...].T
    part0 = flipped.astype(BF16)
    part1 = (flipped - part0.astype(F32)).astype(BF16)
    lhs = jnp.concatenate([part0, part1], axis=0)
    high = [ix // DV for ix in index]
    low = [ix % DV for ix in index]
    lane1 = iota((1, CC), 1)

    def both(vh, vl):
        hot = jnp.where(iota((256, 2 * CC), 0) == vh, 1.0, 0.0).astype(BF16)
        got = jnp.dot(lhs, hot, preferred_element_type=F32)
        mine = iota((DV, 2 * CC), 0) == vl
        tv = jnp.sum(jnp.where(mine, got[0:DV] + got[2 * DV:3 * DV], 0.0), axis=0, keepdims=True)
        dv = jnp.sum(jnp.where(mine, got[DV:2 * DV] + got[3 * DV:4 * DV], 0.0), axis=0, keepdims=True)
        return tv, dv

    for r in range(6, FR, 2):
        vh = jnp.concatenate([high[0][r:r + 1], high[0][r + 1:r + 2]], axis=1)
        vl = jnp.concatenate([low[0][r:r + 1], low[0][r + 1:r + 2]], axis=1)
        tv, dv = both(vh, vl)
        for h in range(2):
            tcell[0, r + h:r + h + 1, :] = tv[:, h * CC:(h + 1) * CC]
            dcell[0, r + h:r + h + 1, :] = dv[:, h * CC:(h + 1) * CC]
    packs = []
    for half in range(2):
        vec = jnp.zeros((1, CC), jnp.int32)
        for i in range(16):
            r = 16 * half + i
            vec = jnp.where(lane1 // 8 == i, pltpu.roll(index[1][r:r + 1], (8 * i + 4) % CC, 1), vec)
        packs.append(vec)
    vec = jnp.concatenate(packs, axis=1)
    tv, dv = both(vec // DV, vec % DV)
    for half in range(2):
        for i in range(16):
            r = 16 * half + i
            shift = (CC - 8 * i - 4) % CC
            keep = (lane1 < 4) | (lane1 >= CC - 4)
            cut = slice(half * CC, (half + 1) * CC)
            tcell[1, r:r + 1, :] = jnp.where(keep, pltpu.roll(tv[:, cut], shift, 1), 0.0)
            dcell[1, r:r + 1, :] = jnp.where(keep, pltpu.roll(dv[:, cut], shift, 1), 0.0)


def weights_of(main, side, lo, hi):
    here = main[lo:hi]
    return [
        0.5 * (here + main[lo - 1:hi - 1]),
        0.5 * (here + main[lo + 1:hi + 1]),
        0.5 * (here + left_of(here, side[lo:hi])),
        0.5 * (here + right_of(here, side[lo:hi])),
    ]


def differences(main, side, lo, hi):
    here = main[:, lo:hi, :]
    beside = side[:, lo:hi, :]
    return [
        here - main[:, lo - 1:hi - 1, :],
        here - main[:, lo + 1:hi + 1, :],
        here - left_of(here, beside),
        here - right_of(here, beside),
    ]


def first_kernel(
    last, info, table, state, adjoint, dmap, side, from_up, from_down, blocks,
    resid_out, local_out, up_out, down_out, main_f, side_f, tcell, dcell,
    mats, vec, total, index_scr, sem,
):
    copy = pltpu.make_async_copy(blocks, mats, sem)
    copy.start()
    level, prow = info[0], info[1]
    main_f[...] = jnp.zeros_like(main_f)
    side_f[...] = jnp.zeros_like(side_f)
    index_scr[...] = jnp.zeros_like(index_scr)
    main_f[0:3, 8:8 + CR, :] = state[...]
    main_f[3:6, 8:8 + CR, :] = adjoint[...]
    for f in range(6):
        side_f[f, 8:8 + CR, :] = side[f, 0:CR, :]
        for tile, ref in ((0, main_f), (1, side_f)):
            ref[f, 6:8, :] = from_up[tile, 2 * f:2 * f + 2, :]
            ref[f, 8 + CR:10 + CR, :] = from_down[tile, 2 * f:2 * f + 2, :]
    index_scr[0, 8:8 + CR, :] = dmap[...].astype(F32)
    index_scr[1, 8:8 + CR, :] = side[6, 0:CR, :]
    for tile in range(2):
        index_scr[tile, 6:8, :] = from_up[tile, 12:14, :]
        index_scr[tile, 8 + CR:10 + CR, :] = from_down[tile, 12:14, :]
    index = [index_scr[tile].astype(jnp.int32) for tile in range(2)]
    tcell[...] = jnp.zeros_like(tcell)
    dcell[...] = jnp.zeros_like(dcell)
    look_up(table, index, tcell, dcell)
    inside = grid_mask(prow, last, 0, FR)
    for tile in range(2):
        tcell[tile] = tcell[tile] * inside
    slope = [3.0 * tcell[tile] * tcell[tile] * dcell[tile] for tile in range(2)]
    lo, hi = 7, 7 + EXT
    parts = differences(main_f, side_f, lo, hi)
    rhs = jnp.zeros((6, EXT, CC), F32)
    for weight, diff in zip(weights_of(slope[0], slope[1], lo, hi), parts):
        rhs = rhs - weight[None] * diff
    rhs = rhs * inside[lo:hi][None]
    resid_out[...] = rhs
    vec[...] = rhs.reshape(2, BLK, CC)
    copy.wait()
    local_solve(mats, vec, total, level)
    local = total[...].reshape(6, EXT, CC)
    local_out[...] = local
    up_out[...] = local[:, 0:8, :]
    down_out[...] = local[:, EXT - 8:EXT, :]


def join_kernel(last, info, local, from_up, from_down, frame_out, first_out, last_out):
    prow = info[1]
    frame_out[...] = jnp.zeros_like(frame_out)
    frame_out[:, 7:7 + EXT, :] = local[...]
    frame_out[:, 6:9, :] += from_up[:, 5:8, :]
    frame_out[:, 7 + CR:10 + CR, :] += from_down[:, 0:3, :]
    inside = grid_mask(prow, last, 0, FR)
    frame_out[...] = frame_out[...] * inside[None]
    tiles = []
    for f in range(6):
        field = frame_out[f, 7:7 + EXT, :]
        tiles += [field[8 * g:8 * g + 8] for g in range(3)]
    first, last_lanes = pack_edges(tiles, 1)
    first_out[...] = first
    last_out[...] = last_lanes


def fill_side(side_f, from_left, from_right):
    tiles = unpack_edges(from_left[...], from_right[...], 18, 1)
    side_f[...] = jnp.zeros_like(side_f)
    for f in range(6):
        for g in range(3):
            side_f[f, 7 + 8 * g:15 + 8 * g, :] = tiles[3 * f + g]


def stiffness(main_f, side_f, tcell, lo, hi):
    stiff = [tcell[tile] * tcell[tile] * tcell[tile] for tile in range(2)]
    out = main_f[:, lo:hi, :]
    parts = differences(main_f, side_f, lo, hi)
    for weight, diff in zip(weights_of(stiff[0], stiff[1], lo, hi), parts):
        out = out + weight[None] * diff
    return out


def second_kernel(
    last, info, frame, from_left, from_right, tcell, blocks,
    image_out, side_out, local_out, up_out, down_out, mats, vec, total, sem,
):
    copy = pltpu.make_async_copy(blocks, mats, sem)
    copy.start()
    level, prow = info[0], info[1]
    fill_side(side_out, from_left, from_right)
    lo, hi = 7, 7 + EXT
    image = stiffness(frame, side_out, tcell, lo, hi)
    image = image * grid_mask(prow, last, lo, EXT)[None]
    image_out[...] = image
    vec[...] = image.reshape(2, BLK, CC)
    copy.wait()
    local_solve(mats, vec, total, level)
    local = total[...].reshape(6, EXT, CC)
    local_out[...] = local
    up_out[...] = local[:, 0:8, :]
    down_out[...] = local[:, EXT - 8:EXT, :]


def third_kernel(
    dmap, resid, image, zframe, zside, wframe, from_left, from_right, tcell, dcell, main_f, side_f,
    sums_out, wside, left_op, right_op,
):
    fill_side(wside, from_left, from_right)
    lo, hi = 8, 8 + CR
    v = stiffness(wframe, wside, tcell, lo, hi)
    r = resid[:, 1:1 + CR, :]
    q = image[:, 1:1 + CR, :]
    z = zframe[:, lo:hi, :]
    w = wframe[:, lo:hi, :]
    lane = iota((1, CC), 1)
    dots = jnp.zeros((1, CC), F32)
    pairs = ((r, z), (z, q), (r, w), (q, w), (z, v), (w, v))
    for k, (a, b) in enumerate(pairs):
        ab = a * b
        for s in range(2):
            part = ab[3 * s] + ab[3 * s + 1] + ab[3 * s + 2]
            value = jnp.sum(jnp.sum(part, axis=0, keepdims=True), axis=1, keepdims=True)
            dots = jnp.where(lane == 2 * k + s, value, dots)
    t = tcell[0, lo:hi, :]
    d = dcell[0, lo:hi, :]
    known_d = differences(main_f, side_f, lo, hi)
    z_d = differences(zframe, zside, lo, hi)
    w_d = differences(wframe, wside, lo, hi)

    def dot3(a, b, i, j):
        out = jnp.zeros((CR, CC), F32)
        for an, bn in zip(a, b):
            for c in range(3):
                out = out + an[i + c] * bn[j + c]
        return out

    slope2 = -1.5 * t * t
    values = [
        (-3.0 * t * d) * dot3(known_d, known_d, 3, 0),
        slope2 * dot3(z_d, known_d, 3, 0),
        slope2 * dot3(w_d, known_d, 3, 0),
        slope2 * dot3(known_d, z_d, 3, 0),
        slope2 * dot3(known_d, w_d, 3, 0),
    ]
    high = dmap[...] // DV
    low = dmap[...] % DV
    for row in range(CR):
        hot = jnp.where(iota((256, CC), 0) == high[row:row + 1], 1.0, 0.0).astype(BF16)
        at = 2 * CC * row
        left_op[:, at:at + CC] = hot
        left_op[:, at + CC:at + 2 * CC] = hot
        mine = iota((DV, CC), 0) == low[row:row + 1]
        for k, value in enumerate(values):
            one = value[row:row + 1]
            top = one.astype(BF16).astype(F32)
            right_op[k * DV:(k + 1) * DV, at:at + CC] = jnp.where(mine, top, 0.0).astype(BF16)
            right_op[k * DV:(k + 1) * DV, at + CC:at + 2 * CC] = jnp.where(mine, one - top, 0.0).astype(BF16)
    sums = lax.dot_general(
        left_op[...], right_op[...], (((1,), (1,)), ((), ())), preferred_element_type=F32
    )
    sums_out[:, 0:CC] = jnp.broadcast_to(dots, (256, CC))
    sums_out[:, CC:] = sums


def last_kernel(got, zframe, wframe, tangent, second, owned):
    sums = jnp.sum(got[...], axis=0, keepdims=True)
    dots = sums[:, 0:CC]
    lane = iota((1, CC), 1)

    def pick(k):
        return jnp.sum(jnp.where(lane == k, dots, 0.0), axis=1, keepdims=True)

    coeffs = []
    for s in range(2):
        rz, zq, rw, qw, zv, wv = (pick(2 * k + s) for k in range(6))
        alpha = rz / zq
        rz1 = rz - alpha * (zq + rw) + alpha * alpha * qw
        grow = 1.0 + rz1 / rz
        pq = grow * grow * zq - grow * alpha * (zv + qw) + alpha * alpha * wv
        alpha1 = rz1 / pq
        coeffs.append((alpha + alpha1 * grow, -alpha1 * alpha))
    for s, out in ((0, tangent), (1, second)):
        c0, c1 = coeffs[s]
        for f in range(3):
            out[f] = c0 * zframe[3 * s + f, 8:8 + CR, :] + c1 * wframe[3 * s + f, 8:8 + CR, :]
    h = [sums[:, (k + 1) * CC:(k + 2) * CC] for k in range(5)]
    owned[...] = (
        h[0] + coeffs[1][0] * h[1] + coeffs[1][1] * h[2] + coeffs[0][0] * h[3] + coeffs[0][1] * h[4]
    )


def shift_pair(axis, count, periodic, to_next, to_previous):
    forward = [(i, i + 1) for i in range(count - 1)]
    if periodic:
        forward.append((count - 1, 0))
    backward = [(b, a) for a, b in forward]
    return lax.ppermute(to_next, axis, forward), lax.ppermute(to_previous, axis, backward)


def per_device(state, adjoint, thickness, direction, design_map, levels, blocks):
    n_row, n_col = lax.axis_size("prow"), lax.axis_size("pcol")
    n_dev = n_row * n_col
    last = n_row - 1
    info = jnp.stack([levels[0, 0], lax.axis_index("prow").astype(jnp.int32)])
    rows = functools.partial(shift_pair, "prow", n_row, False)
    cols = functools.partial(shift_pair, "pcol", n_col, True)

    first, end = call(start_kernel, [(8, CC)] * 2, [VMEM] * 3, [pltpu.VMEM((7, EXT, CC), F32)])(
        state, adjoint, design_map
    )
    from_left, from_right = cols(end, first)
    own = jnp.concatenate([thickness, direction])
    table = lax.all_to_all(
        jnp.broadcast_to(own[None], (n_col, 2 * DV)), "pcol", 0, 0, tiled=True
    )
    side, up, down = call(
        rows_kernel, [(7, EXT, CC), (2, 16, CC), (2, 16, CC)], [VMEM] * 5,
        [pltpu.VMEM((7, EXT, CC), F32)],
    )(state, adjoint, design_map, from_left, from_right)
    from_up, from_down = rows(down, up)
    table = lax.all_to_all(
        jnp.broadcast_to(table[None], (n_row, n_col, 2 * DV)), "prow", 0, 0, tiled=True
    ).reshape(n_dev, 2 * DV)
    if n_dev < 256:
        table = jnp.concatenate([table, jnp.zeros((256 - n_dev, 2 * DV), F32)], axis=0)

    solve_scratch = [
        pltpu.VMEM((BLK, BLK, CC), F32), pltpu.VMEM((2, BLK, CC), F32), pltpu.VMEM((2, BLK, CC), F32)
    ]
    resid, local, up, down, main_f, side_f, tcell, dcell = call(
        functools.partial(first_kernel, last),
        [(6, EXT, CC), (6, EXT, CC), (6, 8, CC), (6, 8, CC), (6, FR, CC), (6, FR, CC), (2, FR, CC), (2, FR, CC)],
        [SMEM] + [VMEM] * 7 + [ANY],
        solve_scratch + [pltpu.VMEM((2, FR, CC), F32), pltpu.SemaphoreType.DMA(())],
    )(info, table, state, adjoint, design_map, side, from_up, from_down, blocks)

    join = call(
        functools.partial(join_kernel, last), [(6, FR, CC), (8, CC), (8, CC)], [SMEM] + [VMEM] * 3
    )
    zframe, first, end = join(info, local, *rows(down, up))
    image, zside, local, up, down = call(
        functools.partial(second_kernel, last),
        [(6, EXT, CC), (6, FR, CC), (6, EXT, CC), (6, 8, CC), (6, 8, CC)],
        [SMEM] + [VMEM] * 4 + [ANY],
        solve_scratch + [pltpu.SemaphoreType.DMA(())],
    )(info, zframe, *cols(end, first), tcell, blocks)
    wframe, first, end = join(info, local, *rows(down, up))
    (sums,) = call(
        third_kernel, [(256, 6 * CC)], [VMEM] * 12,
        [
            pltpu.VMEM((6, FR, CC), F32), pltpu.VMEM((256, CR * 2 * CC), BF16),
            pltpu.VMEM((5 * DV, CR * 2 * CC), BF16),
        ],
    )(design_map, resid, image, zframe, zside, wframe, *cols(end, first), tcell, dcell, main_f, side_f)
    got = lax.all_to_all(sums[:n_dev], BOTH, 0, 0, tiled=True)
    tangent, second, owned = call(
        last_kernel, [(3, CR, CC), (3, CR, CC), (1, CC)], [VMEM] * 3
    )(got, zframe, wframe)
    return tangent, second, owned.reshape(DV)


def solution(mesh):
    placed = (
        P(None, "prow", "pcol"),
        P(None, "prow", "pcol"),
        P(("prow", "pcol")),
        P(("prow", "pcol")),
        P("prow", "pcol"),
        P("prow", "pcol"),
        P("prow", None, "pcol"),
    )
    return jax.shard_map(
        per_device,
        mesh=mesh,
        in_specs=placed,
        out_specs=(P(None, "prow", "pcol"), P(None, "prow", "pcol"), P(("prow", "pcol"))),
        check_vma=False,
    )
```

time: 762 us -> 130 us (0.17)
  waiting for transfers between devices: 252 us -> 11.2 us
  blocking collectives: 290 us -> 56.9 us
  matrix products: 74.2 us -> 0 us
  starting transfers between devices: 69.5 us -> 38.4 us
  local copies, waits for them, and re-layouts: 36.5 us -> 10.1 us
  other arithmetic: 18.9 us -> 0.76 us
  between operations: 14.7 us -> 1.45 us
  Pallas kernels: 0 us -> 10.9 us
    psum x1 -> x0, waiting for transfers between devices: 233 us -> none  [per_device(): summed = lax.psum(contrib, ('prow', 'pcol'))]
    psum x3 -> x0, blocking collectives: 223 us -> none  [classic_sum(): return lax.psum(local_sums(first, second), ('prow', 'pcol'))]
    dot_general x8 -> x0, matrix products: 74.2 us -> none  [the longest x6 55.8 us: further(): jnp.einsum('abj,nbj->naj', matrices, current, precision=HIGH)]
    all_gather x1 -> x0, blocking collectives: 66.5 us -> none  [per_device(): lax.all_gather(jnp.stack([thickness, direction]), ('prow', 'pcol'), axis=...]
    all_to_all x0 -> x2, blocking collectives: none -> 56.9 us  [the longest x1 36.5 us: per_device(): got = lax.all_to_all(sums[:n_dev], BOTH, 0, 0, tiled=True)]
    ppermute x28 -> x12, starting transfers between devices: 69.5 us -> 31.9 us  [the longest x6 21.8 us: shift_pair(): lax.ppermute(to_previous, axis, backward)]
    gather x2 -> x0, local copies, waits for them, and re-layouts: 29.9 us -> none  [the longest x1 14.9 us: per_device(): d_cell = jnp.take(designs[1], design_map)]
    scatter-add x1 -> x0, other arithmetic: 15.9 us -> none  [per_device(): jax.ops.segment_sum(cellterm.reshape(-1), design_map.reshape(-1), num_seg...]
  transfers between devices with their start and end apart: 29 -> 13, of which waited for: 8 -> 6; matrix products, arithmetic and copies ran while one was open for 1% -> 0% of each run, Pallas kernels for 0% -> 0%
where the time goes in v1:
time: 130 us
  blocking collectives  56.9 us (44%)
  starting transfers between devices  38.4 us (30%)
  waiting for transfers between devices  11.2 us (9%)
  Pallas kernels  10.9 us (8%)
  local copies, waits for them, and re-layouts  10.1 us (8%)
  between operations  1.45 us (1%)
    all_to_all x1, blocking collectives, per_device(): got = lax.all_to_all(sums[:n_dev], BOTH, 0, 0, tiled=True)  36.5 us
    ppermute x6, starting transfers between devices, shift_pair(): lax.ppermute(to_previous, axis, backward)  21.8 us
    all_to_all x1, blocking collectives, per_device(): lax.all_to_all(jnp.broadcast_to(own[None], (n_col, 2 * DV)), 'pcol', 0, 0...  20.4 us
    ppermute x6, starting transfers between devices, shift_pair(): lax.ppermute(to_next, axis, forward)  10.1 us
    ppermute x6, waiting for transfers between devices, shift_pair(): lax.ppermute(to_previous, axis, backward)  8.99 us
    unnamed x26, local copies, waits for them, and re-layouts  8.54 us
    all_to_all x1, starting transfers between devices, per_device(): lax.all_to_all(jnp.broadcast_to(table[None], (n_row, n_col, 2 * DV)), 'pr...  6.57 us
    pallas_call x1, Pallas kernels, per_device(): call(third_kernel, [(256, 6 * CC)], [VMEM] * 12, [pltpu.VMEM((6, FR, CC),...  3.43 us
  transfers between devices with their start and end apart: 13, of which 6 were waited for; matrix products, arithmetic and copies ran while one was open for 0% of the time, Pallas kernels for 0%

profile of v1, /device:TPU:1, one launch (start us, length us, event | category | flops | bytes accessed | tf_op | source)
XLA Modules:
  0.0 129.7 jit_solution(10543770212416429779)
XLA Ops:
  0.6 0.7 pad_maximum_fusion
  1.3 20.4 %all_to_all.22 = f32[32,1,256]{2,1,0:T(1,128)S(1)} all-to-all(f32[32,1,256]{2,1,0:T(1,128)S(1)} %broadcast_in_dim.6), channel_id=1, replica_groups=mesh['prow'=8,'pcol'=32] {'pcol'}, dimensions={0} | all-to-all | bytes 65536 | tf_op jit(solution)/shard_map/all_to_all | solution.py:424
  21.8 0.7 broadcast_in_dim.16
  22.5 6.6 %all-to-all-start.1 = ((f32[8,32,256]{2,1,0:T(8,128)}), f32[8,32,256]{2,1,0:T(8,128)S(1)}, u32[]{:S(2)}, u32[]{:S(2)}) async-start(f32[8,32,256]{2,1,0:T(8,128)} %broadcast_in_dim.16), calls=%async_computation.1 | async-start | bytes 524288 | tf_op jit(solution)/shard_map/all_to_all | solution.py:432
  29.1 0.8 copy-done.2
  29.8 0.8 copy-done.5
  30.6 0.7 copy-done.8
  31.3 0.1 shard_map.94
  31.4 0.5 collective-permute-start
  31.9 4.4 %collective-permute-start.1 = (f32[8,128]{1,0:T(8,128)S(1)}, f32[8,128]{1,0:T(8,128)S(1)}, u32[]{:S(2)}, u32[]{:S(2)}) collective-permute-start(f32[8,128]{1,0:T(8,128)S(1)} %get-tuple-element.31), channel_id=1, source_target_pairs={{1,0},{2,1},{3,2},{4,3},{5,4},{6,5},{7,6},{8,7},{9,8},{10,9},{11,1... | collective-permute-start | bytes 12296 | tf_op jit(solution)/shard_map/ppermute | solution.py:408
  36.9 0.3 collective-permute-done.from_left
  37.3 0.0 collective-permute-done.1.from_right
  37.3 0.8 copy-done.3
  38.0 0.8 copy-done.6
  38.8 0.7 copy-done.9
  39.5 0.1 shard_map.95
  39.6 4.7 %collective-permute-start.2 = (f32[2,16,128]{2,1,0:T(8,128)S(1)}, f32[2,16,128]{2,1,0:T(8,128)S(1)}, u32[]{:S(2)}, u32[]{:S(2)}) collective-permute-start(f32[2,16,128]{2,1,0:T(8,128)S(1)} %get-tuple-element.33), channel_id=1, source_target_pairs={{0,32},{32,64},{64,96},{96,128},{128,160},{160,192},{192,224},{1,3... | collective-permute-start | bytes 49160 | tf_op jit(solution)/shard_map/ppermute | solution.py:408
  44.3 1.9 %collective-permute-start.3 = (f32[2,16,128]{2,1,0:T(8,128)S(1)}, f32[2,16,128]{2,1,0:T(8,128)S(1)}, u32[]{:S(2)}, u32[]{:S(2)}) collective-permute-start(f32[2,16,128]{2,1,0:T(8,128)S(1)} %get-tuple-element.34), channel_id=1, source_target_pairs={{32,0},{64,32},{96,64},{128,96},{160,128},{192,160},{224,192},{33,... | collective-permute-start | bytes 49160 | tf_op jit(solution)/shard_map/ppermute | solution.py:408
  46.3 0.1 pad_add_fusion.info
  46.3 3.0 %collective-permute-done.3.from_down = f32[2,16,128]{2,1,0:T(8,128)S(1)} collective-permute-done((f32[2,16,128]{2,1,0:T(8,128)S(1)}, f32[2,16,128]{2,1,0:T(8,128)S(1)}, u32[]{:S(2)}, u32[]{:S(2)}) %collective-permute-start.3) | collective-permute-done | bytes 16416 | tf_op jit(solution)/shard_map/ppermute | solution.py:408
  49.4 0.0 all-to-all-done.1
  49.4 1.7 %copy-done = f32[72,72,128]{2,1,0:T(8,128)S(1)} copy-done((f32[72,72,128]{2,1,0:T(8,128)S(1)}, f32[72,72,128]{2,1,0:T(8,128)}, u32[]{:S(2)}) %copy-start) | copy-done | bytes 2654232
  51.2 0.8 copy-done.4
  51.9 0.8 copy-done.7
  52.7 0.7 copy-done.10
  53.4 3.3 %shard_map.96 = (f32[6,24,128]{2,1,0:T(8,128)S(1)}, f32[6,24,128]{2,1,0:T(8,128)S(1)}, f32[6,8,128]{2,1,0:T(8,128)S(1)}, f32[6,8,128]{2,1,0:T(8,128)S(1)}, f32[6...) custom-call(s32[2]{0:T(128)S(1)} %pad_add_fusion.info, ...), custom_call_target="tpu_custom_call" | custom-call | tf_op jit(solution)/shard_map/pallas_call | solution.py:441
  56.7 1.9 %collective-permute-start.4 = (f32[6,8,128]{2,1,0:T(8,128)S(1)}, f32[6,8,128]{2,1,0:T(8,128)S(1)}, u32[]{:S(2)}, u32[]{:S(2)}) collective-permute-start(f32[6,8,128]{2,1,0:T(8,128)S(1)} %get-tuple-element.37), channel_id=1, source_target_pairs={{0,32},{32,64},{64,96},{96,128},{128,160},{160,192},{192,224},{1,3... | collective-permute-start | bytes 73736 | tf_op jit(solution)/shard_map/ppermute | solution.py:408
  58.6 2.4 %collective-permute-start.5 = (f32[6,8,128]{2,1,0:T(8,128)S(1)}, f32[6,8,128]{2,1,0:T(8,128)S(1)}, u32[]{:S(2)}, u32[]{:S(2)}) collective-permute-start(f32[6,8,128]{2,1,0:T(8,128)S(1)} %get-tuple-element.38), channel_id=1, source_target_pairs={{32,0},{64,32},{96,64},{128,96},{160,128},{192,160},{224,192},{33,... | collective-permute-start | bytes 73736 | tf_op jit(solution)/shard_map/ppermute | solution.py:408
  61.0 0.0 collective-permute-done.4.from_up
  61.0 2.7 %collective-permute-done.5.from_down = f32[6,8,128]{2,1,0:T(8,128)S(1)} collective-permute-done((f32[6,8,128]{2,1,0:T(8,128)S(1)}, f32[6,8,128]{2,1,0:T(8,128)S(1)}, u32[]{:S(2)}, u32[]{:S(2)}) %collective-permute-start.5) | collective-permute-done | bytes 24608 | tf_op jit(solution)/shard_map/ppermute | solution.py:408
  63.8 0.7 shard_map.97
  64.4 0.1 collective-permute-start.6
  64.5 6.0 %collective-permute-start.7 = (f32[8,128]{1,0:T(8,128)S(1)}, f32[8,128]{1,0:T(8,128)S(1)}, u32[]{:S(2)}, u32[]{:S(2)}) collective-permute-start(f32[8,128]{1,0:T(8,128)S(1)} %get-tuple-element.41), channel_id=1, source_target_pairs={{1,0},{2,1},{3,2},{4,3},{5,4},{6,5},{7,6},{8,7},{9,8},{10,9},{11,1... | collective-permute-start | bytes 12296 | tf_op jit(solution)/shard_map/ppermute | solution.py:408
  70.5 0.9 collective-permute-done.6.from_left
  71.4 1.9 %shard_map.98 = (f32[6,24,128]{2,1,0:T(8,128)S(1)}, f32[6,32,128]{2,1,0:T(8,128)S(1)}, f32[6,24,128]{2,1,0:T(8,128)S(1)}, f32[6,8,128]{2,1,0:T(8,128)S(1)}, f32[6,8,128]{2,1,0:T(8,128)S(1)}) custom-call(s32[2]{0:T(128)S(1)} %pad_add_fusion.info, f32[6,32,128]{2,1,0:T(8,128)S(1)} %get-tuple-element.39.frame.zframe, ...), custom_call_target="tpu_custom_call" | custom-call | tf_op jit(solution)/shard_map/pallas_call | solution.py:452
  73.3 2.8 %collective-permute-start.8 = (f32[6,8,128]{2,1,0:T(8,128)S(1)}, f32[6,8,128]{2,1,0:T(8,128)S(1)}, u32[]{:S(2)}, u32[]{:S(2)}) collective-permute-start(f32[6,8,128]{2,1,0:T(8,128)S(1)} %get-tuple-element.46), channel_id=1, source_target_pairs={{0,32},{32,64},{64,96},{96,128},{128,160},{160,192},{192,224},{1,3... | collective-permute-start | bytes 73736 | tf_op jit(solution)/shard_map/ppermute | solution.py:408
  76.1 1.9 %collective-permute-start.9 = (f32[6,8,128]{2,1,0:T(8,128)S(1)}, f32[6,8,128]{2,1,0:T(8,128)S(1)}, u32[]{:S(2)}, u32[]{:S(2)}) collective-permute-start(f32[6,8,128]{2,1,0:T(8,128)S(1)} %get-tuple-element.47), channel_id=1, source_target_pairs={{32,0},{64,32},{96,64},{128,96},{160,128},{192,160},{224,192},{33,... | collective-permute-start | bytes 73736 | tf_op jit(solution)/shard_map/ppermute | solution.py:408
  78.0 3.2 %collective-permute-done.9.from_down = f32[6,8,128]{2,1,0:T(8,128)S(1)} collective-permute-done((f32[6,8,128]{2,1,0:T(8,128)S(1)}, f32[6,8,128]{2,1,0:T(8,128)S(1)}, u32[]{:S(2)}, u32[]{:S(2)}) %collective-permute-start.9) | collective-permute-done | bytes 24608 | tf_op jit(solution)/shard_map/ppermute | solution.py:408
  81.2 0.7 shard_map.99
  81.9 0.1 collective-permute-start.10
  82.0 5.2 %collective-permute-start.11 = (f32[8,128]{1,0:T(8,128)S(1)}, f32[8,128]{1,0:T(8,128)S(1)}, u32[]{:S(2)}, u32[]{:S(2)}) collective-permute-start(f32[8,128]{1,0:T(8,128)S(1)} %get-tuple-element.50), channel_id=1, source_target_pairs={{1,0},{2,1},{3,2},{4,3},{5,4},{6,5},{7,6},{8,7},{9,8},{10,9},{11,1... | collective-permute-start | bytes 12296 | tf_op jit(solution)/shard_map/ppermute | solution.py:408
  87.2 0.9 collective-permute-done.10.from_left
  88.1 0.0 collective-permute-done.11.from_right
  88.1 3.4 %shard_map.100 = f32[256,768]{1,0:T(8,128)S(1)} custom-call(s32[22,128]{1,0:T(8,128)S(1)} %copy-done.11, f32[6,24,128]{2,1,0:T(8,128)S(1)} %get-tuple-element.35.resid, f32[6,24,128]{2,1,0:T(8,128)S(1)} %get-tuple-element.43.image, f32[6,32,128]{2,1,0:T(8,128)S(1)} %get-tuple-element.39.frame.zframe, f32[6,32,128]{2,1,0:T(8,128)S(1)} %get-tuple-element.44.zside, ...), custom_call_target="tpu_custom_call" | custom-call | tf_op jit(solution)/shard_map/pallas_call | solution.py:459
  91.5 0.8 copy.10
  92.4 36.5 %all_to_all.23 = f32[256,1,768]{2,1,0:T(1,128)S(1)} all-to-all(f32[256,1,768]{2,1,0:T(1,128)S(1)} %copy.10), channel_id=1, replica_groups=mesh['prow'=8,'pcol'=32] {'prow','pcol'}, dimensions={0} | all-to-all | bytes 1572864 | tf_op jit(solution)/shard_map/all_to_all | solution.py:466
  128.9 0.1 copy.15
  128.9 0.8 shard_map.101
  (19 shorter events, 0.1 us)
Async XLA Ops:
  22.5 26.9 %all-to-all-start.1 = ((f32[8,32,256]{2,1,0:T(8,128)}), f32[8,32,256]{2,1,0:T(8,128)S(1)}, u32[]{:S(2)}, u32[]{:S(2)}) async-start(f32[8,32,256]{2,1,0:T(8,128)} %broadcast_in_dim.16), calls=%async_computation.1 | async-start | bytes 524288 | tf_op jit(solution)/shard_map/all_to_all | solution.py:432
  29.1 0.8 copy-start.2
  29.8 0.8 copy-start.5
  30.6 0.7 copy-start.8
  31.4 5.9 %collective-permute-start = (f32[8,128]{1,0:T(8,128)S(1)}, f32[8,128]{1,0:T(8,128)S(1)}, u32[]{:S(2)}, u32[]{:S(2)}) collective-permute-start(f32[8,128]{1,0:T(8,128)S(1)} %get-tuple-element.30), channel_id=1, source_target_pairs={{0,1},{1,2},{2,3},{3,4},{4,5},{5,6},{6,7},{7,8},{8,9},{9,10},{10,1... | collective-permute-start | bytes 12296 | tf_op jit(solution)/shard_map/ppermute | solution.py:408
  31.9 5.4 %collective-permute-start.1 = (f32[8,128]{1,0:T(8,128)S(1)}, f32[8,128]{1,0:T(8,128)S(1)}, u32[]{:S(2)}, u32[]{:S(2)}) collective-permute-start(f32[8,128]{1,0:T(8,128)S(1)} %get-tuple-element.31), channel_id=1, source_target_pairs={{1,0},{2,1},{3,2},{4,3},{5,4},{6,5},{7,6},{8,7},{9,8},{10,9},{11,1... | collective-permute-start | bytes 12296 | tf_op jit(solution)/shard_map/ppermute | solution.py:408
  37.3 0.8 copy-start.3
  38.0 0.8 copy-start.6
  38.8 0.7 copy-start.9
  39.6 6.7 %collective-permute-start.2 = (f32[2,16,128]{2,1,0:T(8,128)S(1)}, f32[2,16,128]{2,1,0:T(8,128)S(1)}, u32[]{:S(2)}, u32[]{:S(2)}) collective-permute-start(f32[2,16,128]{2,1,0:T(8,128)S(1)} %get-tuple-element.33), channel_id=1, source_target_pairs={{0,32},{32,64},{64,96},{96,128},{128,160},{160,192},{192,224},{1,3... | collective-permute-start | bytes 49160 | tf_op jit(solution)/shard_map/ppermute | solution.py:408
  44.3 5.1 %collective-permute-start.3 = (f32[2,16,128]{2,1,0:T(8,128)S(1)}, f32[2,16,128]{2,1,0:T(8,128)S(1)}, u32[]{:S(2)}, u32[]{:S(2)}) collective-permute-start(f32[2,16,128]{2,1,0:T(8,128)S(1)} %get-tuple-element.34), channel_id=1, source_target_pairs={{32,0},{64,32},{96,64},{128,96},{160,128},{192,160},{224,192},{33,... | collective-permute-start | bytes 49160 | tf_op jit(solution)/shard_map/ppermute | solution.py:408
  49.4 1.8 %copy-start = (f32[72,72,128]{2,1,0:T(8,128)S(1)}, f32[72,72,128]{2,1,0:T(8,128)}, u32[]{:S(2)}) copy-start(f32[72,72,128]{2,1,0:T(8,128)} %blocks.3) | copy-start | bytes 7962628
  51.2 0.8 copy-start.4
  51.9 0.8 copy-start.7
  52.7 0.7 copy-start.10
  53.4 18.0 %copy-start.1 = (f32[72,72,128]{2,1,0:T(8,128)S(1)}, f32[72,72,128]{2,1,0:T(8,128)}, u32[]{:S(2)}) copy-start(f32[72,72,128]{2,1,0:T(8,128)} %blocks.3) | copy-start | bytes 7962628
  53.4 34.7 %copy-start.11 = (s32[22,128]{1,0:T(8,128)S(1)}, s32[22,128]{1,0:T(8,128)}, u32[]{:S(2)}) copy-start(s32[22,128]{1,0:T(8,128)} %dmap.7) | copy-start | bytes 33796
  56.7 4.3 %collective-permute-start.4 = (f32[6,8,128]{2,1,0:T(8,128)S(1)}, f32[6,8,128]{2,1,0:T(8,128)S(1)}, u32[]{:S(2)}, u32[]{:S(2)}) collective-permute-start(f32[6,8,128]{2,1,0:T(8,128)S(1)} %get-tuple-element.37), channel_id=1, source_target_pairs={{0,32},{32,64},{64,96},{96,128},{128,160},{160,192},{192,224},{1,3... | collective-permute-start | bytes 73736 | tf_op jit(solution)/shard_map/ppermute | solution.py:408
  58.6 5.1 %collective-permute-start.5 = (f32[6,8,128]{2,1,0:T(8,128)S(1)}, f32[6,8,128]{2,1,0:T(8,128)S(1)}, u32[]{:S(2)}, u32[]{:S(2)}) collective-permute-start(f32[6,8,128]{2,1,0:T(8,128)S(1)} %get-tuple-element.38), channel_id=1, source_target_pairs={{32,0},{64,32},{96,64},{128,96},{160,128},{192,160},{224,192},{33,... | collective-permute-start | bytes 73736 | tf_op jit(solution)/shard_map/ppermute | solution.py:408
  64.4 7.0 %collective-permute-start.6 = (f32[8,128]{1,0:T(8,128)S(1)}, f32[8,128]{1,0:T(8,128)S(1)}, u32[]{:S(2)}, u32[]{:S(2)}) collective-permute-start(f32[8,128]{1,0:T(8,128)S(1)} %get-tuple-element.40), channel_id=1, source_target_pairs={{0,1},{1,2},{2,3},{3,4},{4,5},{5,6},{6,7},{7,8},{8,9},{9,10},{10,1... | collective-permute-start | bytes 12296 | tf_op jit(solution)/shard_map/ppermute | solution.py:408
  64.5 6.9 %collective-permute-start.7 = (f32[8,128]{1,0:T(8,128)S(1)}, f32[8,128]{1,0:T(8,128)S(1)}, u32[]{:S(2)}, u32[]{:S(2)}) collective-permute-start(f32[8,128]{1,0:T(8,128)S(1)} %get-tuple-element.41), channel_id=1, source_target_pairs={{1,0},{2,1},{3,2},{4,3},{5,4},{6,5},{7,6},{8,7},{9,8},{10,9},{11,1... | collective-permute-start | bytes 12296 | tf_op jit(solution)/shard_map/ppermute | solution.py:408
  73.3 4.7 %collective-permute-start.8 = (f32[6,8,128]{2,1,0:T(8,128)S(1)}, f32[6,8,128]{2,1,0:T(8,128)S(1)}, u32[]{:S(2)}, u32[]{:S(2)}) collective-permute-start(f32[6,8,128]{2,1,0:T(8,128)S(1)} %get-tuple-element.46), channel_id=1, source_target_pairs={{0,32},{32,64},{64,96},{96,128},{128,160},{160,192},{192,224},{1,3... | collective-permute-start | bytes 73736 | tf_op jit(solution)/shard_map/ppermute | solution.py:408
  76.1 5.1 %collective-permute-start.9 = (f32[6,8,128]{2,1,0:T(8,128)S(1)}, f32[6,8,128]{2,1,0:T(8,128)S(1)}, u32[]{:S(2)}, u32[]{:S(2)}) collective-permute-start(f32[6,8,128]{2,1,0:T(8,128)S(1)} %get-tuple-element.47), channel_id=1, source_target_pairs={{32,0},{64,32},{96,64},{128,96},{160,128},{192,160},{224,192},{33,... | collective-permute-start | bytes 73736 | tf_op jit(solution)/shard_map/ppermute | solution.py:408
  81.9 6.2 %collective-permute-start.10 = (f32[8,128]{1,0:T(8,128)S(1)}, f32[8,128]{1,0:T(8,128)S(1)}, u32[]{:S(2)}, u32[]{:S(2)}) collective-permute-start(f32[8,128]{1,0:T(8,128)S(1)} %get-tuple-element.49), channel_id=1, source_target_pairs={{0,1},{1,2},{2,3},{3,4},{4,5},{5,6},{6,7},{7,8},{8,9},{9,10},{10,1... | collective-permute-start | bytes 12296 | tf_op jit(solution)/shard_map/ppermute | solution.py:408
  82.0 6.1 %collective-permute-start.11 = (f32[8,128]{1,0:T(8,128)S(1)}, f32[8,128]{1,0:T(8,128)S(1)}, u32[]{:S(2)}, u32[]{:S(2)}) collective-permute-start(f32[8,128]{1,0:T(8,128)S(1)} %get-tuple-element.50), channel_id=1, source_target_pairs={{1,0},{2,1},{3,2},{4,3},{5,4},{6,5},{7,6},{8,7},{9,8},{10,9},{11,1... | collective-permute-start | bytes 12296 | tf_op jit(solution)/shard_map/ppermute | solution.py:408

commit v2 on v1

--- a/solution.py
+++ b/solution.py
@@ -13,13 +13,13 @@
 BLK = 72
 EXT = CR + 2
 FR = 32
-BOTH = ("prow", "pcol")
+ROW = ("y", "core")
 F32 = jnp.float32
 BF16 = jnp.bfloat16
 
 VMEM = pl.BlockSpec(memory_space=pltpu.VMEM)
 SMEM = pl.BlockSpec(memory_space=pltpu.SMEM)
-ANY = pl.BlockSpec(memory_space=pl.ANY)
+HBM = pl.BlockSpec(memory_space=pltpu.HBM)
 
 
 def call(kernel, out_shapes, in_specs, scratch=(), out_specs=None):
@@ -29,7 +29,7 @@
         in_specs=list(in_specs),
         out_specs=[VMEM] * len(out_shapes) if out_specs is None else out_specs,
         scratch_shapes=list(scratch),
-        compiler_params=pltpu.CompilerParams(vmem_limit_bytes=48 * 1024 * 1024),
+        compiler_params=pltpu.CompilerParams(vmem_limit_bytes=20 * 1024 * 1024),
     )
 
 
@@ -83,33 +83,45 @@
     return jnp.where(outside, 0.0, 1.0).astype(F32)
 
 
-def start_kernel(state, adjoint, dmap, first_out, last_out, scr):
-    scr[...] = jnp.zeros_like(scr)
-    scr[0:3, 0:CR, :] = state[...]
-    scr[3:6, 0:CR, :] = adjoint[...]
-    scr[6, 0:CR, :] = dmap[...].astype(F32)
-    tiles = [scr[f, 8 * g:8 * g + 8, :] for f in range(7) for g in range(3)]
+def start_kernel(
+    state, adjoint, dmap, thickness, direction, frame_out, own_out, first_out, last_out,
+    known, cells, own, sem,
+):
+    copies = [
+        pltpu.make_async_copy(thickness, own.at[0], sem.at[0]),
+        pltpu.make_async_copy(direction, own.at[1], sem.at[1]),
+        pltpu.make_async_copy(state, known.at[0:3], sem.at[2]),
+        pltpu.make_async_copy(adjoint, known.at[3:6], sem.at[3]),
+        pltpu.make_async_copy(dmap, cells, sem.at[4]),
+    ]
+    for copy in copies:
+        copy.start()
+    frame_out[...] = jnp.zeros_like(frame_out)
+    for copy in copies:
+        copy.wait()
+    for k in range(2):
+        own_out[:, k * DV:(k + 1) * DV] = jnp.broadcast_to(own[k], (own_out.shape[0], DV))
+    frame_out[0:6, 8:8 + CR, :] = known[...]
+    frame_out[6, 8:8 + CR, :] = cells[...].astype(F32)
+    tiles = [frame_out[f, 8 + 8 * g:16 + 8 * g, :] for f in range(7) for g in range(3)]
     first, last = pack_edges(tiles, 1)
     first_out[...] = first
     last_out[...] = last
 
 
-def rows_kernel(state, adjoint, dmap, from_left, from_right, side_out, up_out, down_out, scr):
-    scr[...] = jnp.zeros_like(scr)
-    scr[0:3, 0:CR, :] = state[...]
-    scr[3:6, 0:CR, :] = adjoint[...]
-    scr[6, 0:CR, :] = dmap[...].astype(F32)
+def rows_kernel(frame, from_left, from_right, table, side_out, up_out, down_out, table_out):
     tiles = unpack_edges(from_left[...], from_right[...], 21, 1)
+    side_out[...] = jnp.zeros_like(side_out)
     for f in range(7):
         for g in range(3):
-            side_out[f, 8 * g:8 * g + 8, :] = tiles[3 * f + g]
+            side_out[f, 8 + 8 * g:16 + 8 * g, :] = tiles[3 * f + g]
     up_out[...] = jnp.zeros_like(up_out)
     down_out[...] = jnp.zeros_like(down_out)
-    for f in range(7):
-        up_out[0, 2 * f:2 * f + 2, :] = scr[f, 0:2, :]
-        up_out[1, 2 * f:2 * f + 2, :] = side_out[f, 0:2, :]
-        down_out[0, 2 * f:2 * f + 2, :] = scr[f, CR - 2:CR, :]
-        down_out[1, 2 * f:2 * f + 2, :] = side_out[f, CR - 2:CR, :]
+    for tile, ref in ((0, frame), (1, side_out)):
+        for f in range(7):
+            up_out[tile, 2 * f:2 * f + 2, :] = ref[f, 8:10, :]
+            down_out[tile, 2 * f:2 * f + 2, :] = ref[f, 6 + CR:8 + CR, :]
+    table_out[...] = jnp.broadcast_to(table[...][None], table_out.shape)
 
 
 def apply_blocks(mats, vec):
@@ -211,33 +223,24 @@
 
 
 def first_kernel(
-    last, info, table, state, adjoint, dmap, side, from_up, from_down, blocks,
-    resid_out, local_out, up_out, down_out, main_f, side_f, tcell, dcell,
-    mats, vec, total, index_scr, sem,
+    last, info, table, frame, side, from_up, from_down, blocks,
+    resid_out, local_out, up_out, down_out, main_f, side_f, tcell, dcell, mats,
+    vec, total, index_scr, sem,
 ):
     copy = pltpu.make_async_copy(blocks, mats, sem)
     copy.start()
     level, prow = info[0], info[1]
-    main_f[...] = jnp.zeros_like(main_f)
-    side_f[...] = jnp.zeros_like(side_f)
-    index_scr[...] = jnp.zeros_like(index_scr)
-    main_f[0:3, 8:8 + CR, :] = state[...]
-    main_f[3:6, 8:8 + CR, :] = adjoint[...]
-    for f in range(6):
-        side_f[f, 8:8 + CR, :] = side[f, 0:CR, :]
-        for tile, ref in ((0, main_f), (1, side_f)):
-            ref[f, 6:8, :] = from_up[tile, 2 * f:2 * f + 2, :]
-            ref[f, 8 + CR:10 + CR, :] = from_down[tile, 2 * f:2 * f + 2, :]
-    index_scr[0, 8:8 + CR, :] = dmap[...].astype(F32)
-    index_scr[1, 8:8 + CR, :] = side[6, 0:CR, :]
-    for tile in range(2):
-        index_scr[tile, 6:8, :] = from_up[tile, 12:14, :]
-        index_scr[tile, 8 + CR:10 + CR, :] = from_down[tile, 12:14, :]
+    inside = grid_mask(prow, last, 0, FR)
+    for tile, ref, source in ((0, main_f, frame), (1, side_f, side)):
+        for f in range(7):
+            out = ref.at[f] if f < 6 else index_scr.at[tile]
+            out[...] = source[f]
+            out[6:8, :] = from_up[tile, 2 * f:2 * f + 2, :] * inside[6:8]
+            out[8 + CR:10 + CR, :] = from_down[tile, 2 * f:2 * f + 2, :] * inside[8 + CR:10 + CR]
     index = [index_scr[tile].astype(jnp.int32) for tile in range(2)]
     tcell[...] = jnp.zeros_like(tcell)
     dcell[...] = jnp.zeros_like(dcell)
     look_up(table, index, tcell, dcell)
-    inside = grid_mask(prow, last, 0, FR)
     for tile in range(2):
         tcell[tile] = tcell[tile] * inside
     slope = [3.0 * tcell[tile] * tcell[tile] * dcell[tile] for tile in range(2)]
@@ -261,8 +264,8 @@
     prow = info[1]
     frame_out[...] = jnp.zeros_like(frame_out)
     frame_out[:, 7:7 + EXT, :] = local[...]
-    frame_out[:, 6:9, :] += from_up[:, 5:8, :]
-    frame_out[:, 7 + CR:10 + CR, :] += from_down[:, 0:3, :]
+    frame_out[:, 6:9, :] += jnp.where(prow == 0, 0.0, from_up[:, 5:8, :])
+    frame_out[:, 7 + CR:10 + CR, :] += jnp.where(prow == last, 0.0, from_down[:, 0:3, :])
     inside = grid_mask(prow, last, 0, FR)
     frame_out[...] = frame_out[...] * inside[None]
     tiles = []
@@ -292,11 +295,9 @@
 
 
 def second_kernel(
-    last, info, frame, from_left, from_right, tcell, blocks,
-    image_out, side_out, local_out, up_out, down_out, mats, vec, total, sem,
+    last, info, frame, from_left, from_right, tcell, mats,
+    image_out, side_out, local_out, up_out, down_out, vec, total,
 ):
-    copy = pltpu.make_async_copy(blocks, mats, sem)
-    copy.start()
     level, prow = info[0], info[1]
     fill_side(side_out, from_left, from_right)
     lo, hi = 7, 7 + EXT
@@ -304,7 +305,6 @@
     image = image * grid_mask(prow, last, lo, EXT)[None]
     image_out[...] = image
     vec[...] = image.reshape(2, BLK, CC)
-    copy.wait()
     local_solve(mats, vec, total, level)
     local = total[...].reshape(6, EXT, CC)
     local_out[...] = local
@@ -313,8 +313,8 @@
 
 
 def third_kernel(
-    dmap, resid, image, zframe, zside, wframe, from_left, from_right, tcell, dcell, main_f, side_f,
-    sums_out, wside, left_op, right_op,
+    n_col, info, frame, resid, image, zframe, zside, wframe, from_left, from_right, tcell, dcell, main_f, side_f,
+    keep_out, send_out, wside, left_op, right_op,
 ):
     fill_side(wside, from_left, from_right)
     lo, hi = 8, 8 + CR
@@ -353,8 +353,11 @@
         slope2 * dot3(known_d, z_d, 3, 0),
         slope2 * dot3(known_d, w_d, 3, 0),
     ]
-    high = dmap[...] // DV
-    low = dmap[...] % DV
+    cells = frame[6, lo:hi, :].astype(jnp.int32)
+    owner = cells // DV
+    low = cells % DV
+    other = jnp.where((owner // n_col) % 2 == info[1] % 2, 0, 128)
+    high = other + (owner // (2 * n_col)) * n_col + owner % n_col
     for row in range(CR):
         hot = jnp.where(iota((256, CC), 0) == high[row:row + 1], 1.0, 0.0).astype(BF16)
         at = 2 * CC * row
@@ -369,8 +372,10 @@
     sums = lax.dot_general(
         left_op[...], right_op[...], (((1,), (1,)), ((), ())), preferred_element_type=F32
     )
-    sums_out[:, 0:CC] = jnp.broadcast_to(dots, (256, CC))
-    sums_out[:, CC:] = sums
+    for half, out in ((0, keep_out), (1, send_out)):
+        count = out.shape[0]
+        out[:, 0:CC] = jnp.broadcast_to(dots, (count, CC))
+        out[:, CC:] = sums[128 * half:128 * half + count]
 
 
 def last_kernel(got, zframe, wframe, tangent, second, owned):
@@ -400,50 +405,47 @@
     )
 
 
-def shift_pair(axis, count, periodic, to_next, to_previous):
-    forward = [(i, i + 1) for i in range(count - 1)]
-    if periodic:
-        forward.append((count - 1, 0))
+def ring(axis, count, to_next, to_previous):
+    forward = [(i, (i + 1) % count) for i in range(count)]
     backward = [(b, a) for a, b in forward]
     return lax.ppermute(to_next, axis, forward), lax.ppermute(to_previous, axis, backward)
 
 
 def per_device(state, adjoint, thickness, direction, design_map, levels, blocks):
-    n_row, n_col = lax.axis_size("prow"), lax.axis_size("pcol")
+    n_row, n_col = lax.axis_size(ROW), lax.axis_size("pcol")
     n_dev = n_row * n_col
     last = n_row - 1
-    info = jnp.stack([levels[0, 0], lax.axis_index("prow").astype(jnp.int32)])
-    rows = functools.partial(shift_pair, "prow", n_row, False)
-    cols = functools.partial(shift_pair, "pcol", n_col, True)
-
-    first, end = call(start_kernel, [(8, CC)] * 2, [VMEM] * 3, [pltpu.VMEM((7, EXT, CC), F32)])(
-        state, adjoint, design_map
-    )
+    info = jnp.stack([levels[0, 0], lax.axis_index(ROW).astype(jnp.int32)])
+    rows = functools.partial(ring, ROW, n_row)
+    cols = functools.partial(ring, "pcol", n_col)
+
+    frame, own, first, end = call(
+        start_kernel, [(7, FR, CC), (n_col, 2 * DV), (8, CC), (8, CC)], [HBM] * 5,
+        [
+            pltpu.VMEM((6, CR, CC), F32), pltpu.VMEM((CR, CC), jnp.int32),
+            pltpu.VMEM((2, 1, DV), F32), pltpu.SemaphoreType.DMA((5,)),
+        ],
+    )(state, adjoint, design_map, thickness.reshape(1, DV), direction.reshape(1, DV))
     from_left, from_right = cols(end, first)
-    own = jnp.concatenate([thickness, direction])
-    table = lax.all_to_all(
-        jnp.broadcast_to(own[None], (n_col, 2 * DV)), "pcol", 0, 0, tiled=True
-    )
-    side, up, down = call(
-        rows_kernel, [(7, EXT, CC), (2, 16, CC), (2, 16, CC)], [VMEM] * 5,
-        [pltpu.VMEM((7, EXT, CC), F32)],
-    )(state, adjoint, design_map, from_left, from_right)
+    table = lax.all_to_all(own, "pcol", 0, 0, tiled=True)
+    side, up, down, table = call(
+        rows_kernel, [(7, FR, CC), (2, 16, CC), (2, 16, CC), (n_row, n_col, 2 * DV)], [VMEM] * 4,
+    )(frame, from_left, from_right, table)
     from_up, from_down = rows(down, up)
-    table = lax.all_to_all(
-        jnp.broadcast_to(table[None], (n_row, n_col, 2 * DV)), "prow", 0, 0, tiled=True
-    ).reshape(n_dev, 2 * DV)
+    table = lax.all_to_all(table, ROW, 0, 0, tiled=True).reshape(n_dev, 2 * DV)
     if n_dev < 256:
         table = jnp.concatenate([table, jnp.zeros((256 - n_dev, 2 * DV), F32)], axis=0)
 
-    solve_scratch = [
-        pltpu.VMEM((BLK, BLK, CC), F32), pltpu.VMEM((2, BLK, CC), F32), pltpu.VMEM((2, BLK, CC), F32)
-    ]
-    resid, local, up, down, main_f, side_f, tcell, dcell = call(
+    solve_scratch = [pltpu.VMEM((2, BLK, CC), F32), pltpu.VMEM((2, BLK, CC), F32)]
+    resid, local, up, down, main_f, side_f, tcell, dcell, mats = call(
         functools.partial(first_kernel, last),
-        [(6, EXT, CC), (6, EXT, CC), (6, 8, CC), (6, 8, CC), (6, FR, CC), (6, FR, CC), (2, FR, CC), (2, FR, CC)],
-        [SMEM] + [VMEM] * 7 + [ANY],
+        [
+            (6, EXT, CC), (6, EXT, CC), (6, 8, CC), (6, 8, CC), (6, FR, CC), (6, FR, CC),
+            (2, FR, CC), (2, FR, CC), (BLK, BLK, CC),
+        ],
+        [SMEM] + [VMEM] * 5 + [HBM],
         solve_scratch + [pltpu.VMEM((2, FR, CC), F32), pltpu.SemaphoreType.DMA(())],
-    )(info, table, state, adjoint, design_map, side, from_up, from_down, blocks)
+    )(info, table, frame, side, from_up, from_down, blocks)
 
     join = call(
         functools.partial(join_kernel, last), [(6, FR, CC), (8, CC), (8, CC)], [SMEM] + [VMEM] * 3
@@ -452,18 +454,19 @@
     image, zside, local, up, down = call(
         functools.partial(second_kernel, last),
         [(6, EXT, CC), (6, FR, CC), (6, EXT, CC), (6, 8, CC), (6, 8, CC)],
-        [SMEM] + [VMEM] * 4 + [ANY],
-        solve_scratch + [pltpu.SemaphoreType.DMA(())],
-    )(info, zframe, *cols(end, first), tcell, blocks)
+        [SMEM] + [VMEM] * 5,
+        solve_scratch,
+    )(info, zframe, *cols(end, first), tcell, mats)
     wframe, first, end = join(info, local, *rows(down, up))
-    (sums,) = call(
-        third_kernel, [(256, 6 * CC)], [VMEM] * 12,
+    keep, send = call(
+        functools.partial(third_kernel, n_col), [(n_dev // 2, 6 * CC)] * 2, [SMEM] + [VMEM] * 12,
         [
             pltpu.VMEM((6, FR, CC), F32), pltpu.VMEM((256, CR * 2 * CC), BF16),
             pltpu.VMEM((5 * DV, CR * 2 * CC), BF16),
         ],
-    )(design_map, resid, image, zframe, zside, wframe, *cols(end, first), tcell, dcell, main_f, side_f)
-    got = lax.all_to_all(sums[:n_dev], BOTH, 0, 0, tiled=True)
+    )(info, frame, resid, image, zframe, zside, wframe, *cols(end, first), tcell, dcell, main_f, side_f)
+    sums = keep + lax.ppermute(send, "core", [(0, 1), (1, 0)])
+    got = lax.all_to_all(sums, ("y", "pcol"), 0, 0, tiled=True)
     tangent, second, owned = call(
         last_kernel, [(3, CR, CC), (3, CR, CC), (1, CC)], [VMEM] * 3
     )(got, zframe, wframe)
@@ -471,19 +474,14 @@
 
 
 def solution(mesh):
-    placed = (
-        P(None, "prow", "pcol"),
-        P(None, "prow", "pcol"),
-        P(("prow", "pcol")),
-        P(("prow", "pcol")),
-        P("prow", "pcol"),
-        P("prow", "pcol"),
-        P("prow", None, "pcol"),
-    )
+    n_row, n_col = mesh.devices.shape
+    fine = jax.sharding.Mesh(mesh.devices.reshape(n_row // 2, 2, n_col), ("y", "core", "pcol"))
+    field = P(None, ROW, "pcol")
+    design = P(("y", "core", "pcol"))
     return jax.shard_map(
         per_device,
-        mesh=mesh,
-        in_specs=placed,
-        out_specs=(P(None, "prow", "pcol"), P(None, "prow", "pcol"), P(("prow", "pcol"))),
+        mesh=fine,
+        in_specs=(field, field, design, design, P(ROW, "pcol"), P(ROW, "pcol"), P(ROW, None, "pcol")),
+        out_specs=(field, field, design),
         check_vma=False,
     )

time: 130 us -> 106 us (0.82)
  blocking collectives: 56.9 us -> 26.5 us
  starting transfers between devices: 38.4 us -> 45.6 us
  local copies, waits for them, and re-layouts: 10.1 us -> 6.38 us
  waiting for transfers between devices: 11.2 us -> 14.7 us
    all_to_all x2 -> x1, blocking collectives: 56.9 us -> 26.5 us  [per_device(): got = lax.all_to_all(sums, ('y', 'pcol'), 0, 0, tiled=True)]
    all_to_all x1 -> x2, starting transfers between devices: 6.57 us -> 18.4 us  [the longest x1 11.9 us: per_device(): table = lax.all_to_all(own, 'pcol', 0, 0, tiled=True)]
    all_to_all x1 -> x2, waiting for transfers between devices: 0.01 us -> 4.71 us  [the longest x1 3.9 us: per_device(): table = lax.all_to_all(own, 'pcol', 0, 0, tiled=True)]
    ppermute x12 -> x13, starting transfers between devices: 31.9 us -> 27.2 us  [the longest x6 15.2 us: ring(): lax.ppermute(to_previous, axis, backward)]
    unnamed x26 -> x14, local copies, waits for them, and re-layouts: 8.54 us -> 5.32 us
    ppermute x12 -> x13, waiting for transfers between devices: 11.1 us -> 10 us  [the longest x6 4.55 us: ring(): lax.ppermute(to_next, axis, forward)]
  transfers between devices with their start and end apart: 13 -> 15, of which waited for: 6 -> 11; matrix products, arithmetic and copies ran while one was open for 0% -> 0% of each run, Pallas kernels for 0% -> 0%
where the time goes in v2:
time: 106 us
  starting transfers between devices  45.6 us (43%)
  blocking collectives  26.5 us (25%)
  waiting for transfers between devices  14.7 us (14%)
  Pallas kernels  11 us (10%)
  local copies, waits for them, and re-layouts  6.38 us (6%)
  between operations  1.39 us (1%)
    all_to_all x1, blocking collectives, per_device(): got = lax.all_to_all(sums, ('y', 'pcol'), 0, 0, tiled=True)  26.5 us
    ppermute x6, starting transfers between devices, ring(): lax.ppermute(to_previous, axis, backward)  15.2 us
    all_to_all x1, starting transfers between devices, per_device(): table = lax.all_to_all(own, 'pcol', 0, 0, tiled=True)  11.9 us
    ppermute x6, starting transfers between devices, ring(): lax.ppermute(to_next, axis, forward)  7.34 us
    all_to_all x1, starting transfers between devices, per_device(): table = lax.all_to_all(table, ROW, 0, 0, tiled=True).reshape(n_dev, 2 * DV)  6.57 us
    unnamed x14, local copies, waits for them, and re-layouts  5.32 us
    ppermute x1, starting transfers between devices, per_device(): sums = keep + lax.ppermute(send, 'core', [(0, 1), (1, 0)])  4.59 us
    ppermute x6, waiting for transfers between devices, ring(): lax.ppermute(to_next, axis, forward)  4.55 us
  transfers between devices with their start and end apart: 15, of which 11 were waited for; matrix products, arithmetic and copies ran while one was open for 0% of the time, Pallas kernels for 0%

profile of v2, /device:TPU:1, one launch (start us, length us, event | category | flops | bytes accessed | tf_op | source)
XLA Modules:
  0.0 105.7 jit_solution(2030600557976903650)
XLA Ops:
  0.6 0.8 copy-done.1
  1.4 0.8 copy-done.2
  2.2 0.7 copy-done.3
  2.9 0.7 copy-done.4
  3.5 0.7 copy-done.5
  4.2 0.2 shard_map.94
  4.4 0.6 copy.10
  5.0 11.9 %all-to-all-start = ((f32[32,1,256]{2,1,0:T(1,128)}), f32[32,1,256]{2,1,0:T(1,128)S(1)}, u32[]{:S(2)}, u32[]{:S(2)}) async-start(f32[32,1,256]{2,1,0:T(1,128)} %copy.10), calls=%async_computation | async-start | bytes 65536 | tf_op jit(solution)/shard_map/all_to_all | solution.py:430
  16.9 1.3 %collective-permute-start = (f32[8,128]{1,0:T(8,128)S(1)}, f32[8,128]{1,0:T(8,128)S(1)}, u32[]{:S(2)}, u32[]{:S(2)}) collective-permute-start(f32[8,128]{1,0:T(8,128)S(1)} %get-tuple-element.37), channel_id=1, source_target_pairs={{0,1},{1,2},{2,3},{3,4},{4,5},{5,6},{6,7},{7,8},{8,9},{9,10},{10,1... | collective-permute-start | bytes 12296 | tf_op jit(solution)/shard_map/ppermute | solution.py:411
  18.2 3.6 %collective-permute-start.1 = (f32[8,128]{1,0:T(8,128)S(1)}, f32[8,128]{1,0:T(8,128)S(1)}, u32[]{:S(2)}, u32[]{:S(2)}) collective-permute-start(f32[8,128]{1,0:T(8,128)S(1)} %get-tuple-element.38), channel_id=1, source_target_pairs={{1,0},{2,1},{3,2},{4,3},{5,4},{6,5},{7,6},{8,7},{9,8},{10,9},{11,1... | collective-permute-start | bytes 12296 | tf_op jit(solution)/shard_map/ppermute | solution.py:411
  21.8 3.9 %all-to-all-done = f32[32,1,256]{2,1,0:T(1,128)S(1)} async-done(((f32[32,1,256]{2,1,0:T(1,128)}), f32[32,1,256]{2,1,0:T(1,128)S(1)}, u32[]{:S(2)}, u32[]{:S(2)}) %all-to-all-start) | async-done | bytes 32800 | tf_op jit(solution)/shard_map/all_to_all | solution.py:430
  25.7 0.0 collective-permute-done.from_left
  25.7 0.0 collective-permute-done.1.from_right
  25.7 0.7 shard_map.95
  26.4 6.6 %all-to-all-start.1 = ((f32[8,32,256]{2,1,0:T(8,128)}), f32[8,32,256]{2,1,0:T(8,128)S(1)}, u32[]{:S(2)}, u32[]{:S(2)}) async-start(f32[8,32,256]{2,1,0:T(8,128)} %get-tuple-element.40), calls=%async_computation.1 | async-start | bytes 524288 | tf_op jit(solution)/shard_map/all_to_all | solution.py:435
  33.7 1.6 %collective-permute-start.2 = (f32[2,16,128]{2,1,0:T(8,128)S(1)}, f32[2,16,128]{2,1,0:T(8,128)S(1)}, u32[]{:S(2)}, u32[]{:S(2)}) collective-permute-start(f32[2,16,128]{2,1,0:T(8,128)S(1)} %get-tuple-element.42), channel_id=1, source_target_pairs={{0,32},{32,64},{64,96},{96,128},{128,160},{160,192},{192,224},{224... | collective-permute-start | bytes 49160 | tf_op jit(solution)/shard_map/ppermute | solution.py:411
  35.3 0.0 collective-permute-start.3
  35.3 0.1 pad_add_fusion.info
  35.4 1.3 %collective-permute-done.2.from_up = f32[2,16,128]{2,1,0:T(8,128)S(1)} collective-permute-done((f32[2,16,128]{2,1,0:T(8,128)S(1)}, f32[2,16,128]{2,1,0:T(8,128)S(1)}, u32[]{:S(2)}, u32[]{:S(2)}) %collective-permute-start.2) | collective-permute-done | bytes 16416 | tf_op jit(solution)/shard_map/ppermute | solution.py:411
  36.7 2.1 %collective-permute-done.3.from_down = f32[2,16,128]{2,1,0:T(8,128)S(1)} collective-permute-done((f32[2,16,128]{2,1,0:T(8,128)S(1)}, f32[2,16,128]{2,1,0:T(8,128)S(1)}, u32[]{:S(2)}, u32[]{:S(2)}) %collective-permute-start.3) | collective-permute-done | bytes 16416 | tf_op jit(solution)/shard_map/ppermute | solution.py:411
  38.8 0.8 all-to-all-done.1
  39.6 1.7 %copy-done = f32[72,72,128]{2,1,0:T(8,128)S(1)} copy-done((f32[72,72,128]{2,1,0:T(8,128)S(1)}, f32[72,72,128]{2,1,0:T(8,128)}, u32[]{:S(2)}) %copy-start) | copy-done | bytes 2654232
  41.4 2.8 %shard_map.96 = (f32[6,24,128]{2,1,0:T(8,128)S(1)}, f32[6,24,128]{2,1,0:T(8,128)S(1)}, f32[6,8,128]{2,1,0:T(8,128)S(1)}, f32[6,8,128]{2,1,0:T(8,128)S(1)}, f32[6...) custom-call(s32[2]{0:T(128)S(1)} %pad_add_fusion.info, ...), custom_call_target="tpu_custom_call" | custom-call | tf_op jit(solution)/shard_map/pallas_call | solution.py:440
  44.2 1.2 %collective-permute-start.4 = (f32[6,8,128]{2,1,0:T(8,128)S(1)}, f32[6,8,128]{2,1,0:T(8,128)S(1)}, u32[]{:S(2)}, u32[]{:S(2)}) collective-permute-start(f32[6,8,128]{2,1,0:T(8,128)S(1)} %get-tuple-element.46), channel_id=1, source_target_pairs={{0,32},{32,64},{64,96},{96,128},{128,160},{160,192},{192,224},{224... | collective-permute-start | bytes 73736 | tf_op jit(solution)/shard_map/ppermute | solution.py:411
  45.4 0.8 collective-permute-start.5
  46.2 0.7 collective-permute-done.4.from_up
  46.9 1.8 %collective-permute-done.5.from_down = f32[6,8,128]{2,1,0:T(8,128)S(1)} collective-permute-done((f32[6,8,128]{2,1,0:T(8,128)S(1)}, f32[6,8,128]{2,1,0:T(8,128)S(1)}, u32[]{:S(2)}, u32[]{:S(2)}) %collective-permute-start.5) | collective-permute-done | bytes 24608 | tf_op jit(solution)/shard_map/ppermute | solution.py:411
  48.7 0.7 shard_map.97
  49.3 2.0 %collective-permute-start.6 = (f32[8,128]{1,0:T(8,128)S(1)}, f32[8,128]{1,0:T(8,128)S(1)}, u32[]{:S(2)}, u32[]{:S(2)}) collective-permute-start(f32[8,128]{1,0:T(8,128)S(1)} %get-tuple-element.49), channel_id=1, source_target_pairs={{0,1},{1,2},{2,3},{3,4},{4,5},{5,6},{6,7},{7,8},{8,9},{9,10},{10,1... | collective-permute-start | bytes 12296 | tf_op jit(solution)/shard_map/ppermute | solution.py:411
  51.3 2.9 %collective-permute-start.7 = (f32[8,128]{1,0:T(8,128)S(1)}, f32[8,128]{1,0:T(8,128)S(1)}, u32[]{:S(2)}, u32[]{:S(2)}) collective-permute-start(f32[8,128]{1,0:T(8,128)S(1)} %get-tuple-element.50), channel_id=1, source_target_pairs={{1,0},{2,1},{3,2},{4,3},{5,4},{6,5},{7,6},{8,7},{9,8},{10,9},{11,1... | collective-permute-start | bytes 12296 | tf_op jit(solution)/shard_map/ppermute | solution.py:411
  54.2 1.0 collective-permute-done.6.from_left
  55.2 0.0 collective-permute-done.7.from_right
  55.2 1.2 %shard_map.98 = (f32[6,24,128]{2,1,0:T(8,128)S(1)}, f32[6,32,128]{2,1,0:T(8,128)S(1)}, f32[6,24,128]{2,1,0:T(8,128)S(1)}, f32[6,8,128]{2,1,0:T(8,128)S(1)}, f32[6,8,128]{2,1,0:T(8,128)S(1)}) custom-call(s32[2]{0:T(128)S(1)} %pad_add_fusion.info, f32[6,32,128]{2,1,0:T(8,128)S(1)} %get-tuple-element.48.frame.zframe, ...), custom_call_target="tpu_custom_call" | custom-call | tf_op jit(solution)/shard_map/pallas_call | solution.py:454
  56.4 1.2 %collective-permute-start.8 = (f32[6,8,128]{2,1,0:T(8,128)S(1)}, f32[6,8,128]{2,1,0:T(8,128)S(1)}, u32[]{:S(2)}, u32[]{:S(2)}) collective-permute-start(f32[6,8,128]{2,1,0:T(8,128)S(1)} %get-tuple-element.56), channel_id=1, source_target_pairs={{0,32},{32,64},{64,96},{96,128},{128,160},{160,192},{192,224},{224... | collective-permute-start | bytes 73736 | tf_op jit(solution)/shard_map/ppermute | solution.py:411
  57.6 2.9 %collective-permute-start.9 = (f32[6,8,128]{2,1,0:T(8,128)S(1)}, f32[6,8,128]{2,1,0:T(8,128)S(1)}, u32[]{:S(2)}, u32[]{:S(2)}) collective-permute-start(f32[6,8,128]{2,1,0:T(8,128)S(1)} %get-tuple-element.57), channel_id=1, source_target_pairs={{32,0},{64,32},{96,64},{128,96},{160,128},{192,160},{224,192},{0,2... | collective-permute-start | bytes 73736 | tf_op jit(solution)/shard_map/ppermute | solution.py:411
  60.4 0.7 collective-permute-done.8.from_up
  61.1 0.2 collective-permute-done.9.from_down
  61.3 0.7 shard_map.99
  62.0 0.1 collective-permute-start.10
  62.0 5.1 %collective-permute-start.11 = (f32[8,128]{1,0:T(8,128)S(1)}, f32[8,128]{1,0:T(8,128)S(1)}, u32[]{:S(2)}, u32[]{:S(2)}) collective-permute-start(f32[8,128]{1,0:T(8,128)S(1)} %get-tuple-element.60), channel_id=1, source_target_pairs={{1,0},{2,1},{3,2},{4,3},{5,4},{6,5},{7,6},{8,7},{9,8},{10,9},{11,1... | collective-permute-start | bytes 12296 | tf_op jit(solution)/shard_map/ppermute | solution.py:411
  67.2 0.9 collective-permute-done.10.from_left
  68.1 0.0 collective-permute-done.11.from_right
  68.1 4.0 %shard_map.100 = (f32[128,768]{1,0:T(8,128)S(1)}, f32[128,768]{1,0:T(8,128)S(1)}) custom-call(s32[2]{0:T(128)S(1)} %pad_add_fusion.info, f32[7,32,128]{2,1,0:T(8,128)S(1)} %get-tuple-element.36.frame, f32[6,24,128]{2,1,0:T(8,128)S(1)} %get-tuple-element.44.resid, f32[6,24,128]{2,1,0:T(8,128)S(1)} %get-tuple-element.53.image, ...), custom_call_target="tpu_custom_call" | custom-call | tf_op jit(solution)/shard_map/pallas_call | solution.py:461
  72.0 4.6 %collective-permute-start.12 = (f32[128,768]{1,0:T(8,128)S(1)}, f32[128,768]{1,0:T(8,128)S(1)}, u32[]{:S(2)}, u32[]{:S(2)}) collective-permute-start(f32[128,768]{1,0:T(8,128)S(1)} %get-tuple-element.65), channel_id=1, source_target_pairs={{0,32},{32,0},{1,33},{33,1},{2,34},{34,2},{3,35},{35,3},{4,36},{36... | collective-permute-start | bytes 1179656 | tf_op jit(solution)/shard_map/ppermute | solution.py:468
  76.6 1.3 %collective-permute-done.12 = f32[128,768]{1,0:T(8,128)S(1)} collective-permute-done((f32[128,768]{1,0:T(8,128)S(1)}, f32[128,768]{1,0:T(8,128)S(1)}, u32[]{:S(2)}, u32[]{:S(2)}) %collective-permute-start.12) | collective-permute-done | bytes 393248 | tf_op jit(solution)/shard_map/ppermute | solution.py:468
  78.0 0.4 copy.11
  78.4 26.5 %all_to_all.27 = f32[128,1,768]{2,1,0:T(1,128)S(1)} all-to-all(f32[128,1,768]{2,1,0:T(1,128)S(1)} %copy.11), channel_id=1, replica_groups=mesh['y'=4,'core'=2,'pcol'=32] {'y','pcol'}, dimensions={0} | all-to-all | bytes 786432 | tf_op jit(solution)/shard_map/all_to_all | solution.py:469
  105.0 0.8 shard_map.101
  (9 shorter events, 0.1 us)
Async XLA Ops:
  0.6 0.8 copy-start.1
  1.4 0.8 copy-start.2
  2.2 0.7 copy-start.3
  2.9 0.7 copy-start.4
  3.5 0.7 copy-start.5
  5.0 20.6 %all-to-all-start = ((f32[32,1,256]{2,1,0:T(1,128)}), f32[32,1,256]{2,1,0:T(1,128)S(1)}, u32[]{:S(2)}, u32[]{:S(2)}) async-start(f32[32,1,256]{2,1,0:T(1,128)} %copy.10), calls=%async_computation | async-start | bytes 65536 | tf_op jit(solution)/shard_map/all_to_all | solution.py:430
  16.9 8.8 %collective-permute-start = (f32[8,128]{1,0:T(8,128)S(1)}, f32[8,128]{1,0:T(8,128)S(1)}, u32[]{:S(2)}, u32[]{:S(2)}) collective-permute-start(f32[8,128]{1,0:T(8,128)S(1)} %get-tuple-element.37), channel_id=1, source_target_pairs={{0,1},{1,2},{2,3},{3,4},{4,5},{5,6},{6,7},{7,8},{8,9},{9,10},{10,1... | collective-permute-start | bytes 12296 | tf_op jit(solution)/shard_map/ppermute | solution.py:411
  18.2 7.5 %collective-permute-start.1 = (f32[8,128]{1,0:T(8,128)S(1)}, f32[8,128]{1,0:T(8,128)S(1)}, u32[]{:S(2)}, u32[]{:S(2)}) collective-permute-start(f32[8,128]{1,0:T(8,128)S(1)} %get-tuple-element.38), channel_id=1, source_target_pairs={{1,0},{2,1},{3,2},{4,3},{5,4},{6,5},{7,6},{8,7},{9,8},{10,9},{11,1... | collective-permute-start | bytes 12296 | tf_op jit(solution)/shard_map/ppermute | solution.py:411
  26.4 13.2 %all-to-all-start.1 = ((f32[8,32,256]{2,1,0:T(8,128)}), f32[8,32,256]{2,1,0:T(8,128)S(1)}, u32[]{:S(2)}, u32[]{:S(2)}) async-start(f32[8,32,256]{2,1,0:T(8,128)} %get-tuple-element.40), calls=%async_computation.1 | async-start | bytes 524288 | tf_op jit(solution)/shard_map/all_to_all | solution.py:435
  33.7 3.0 %collective-permute-start.2 = (f32[2,16,128]{2,1,0:T(8,128)S(1)}, f32[2,16,128]{2,1,0:T(8,128)S(1)}, u32[]{:S(2)}, u32[]{:S(2)}) collective-permute-start(f32[2,16,128]{2,1,0:T(8,128)S(1)} %get-tuple-element.42), channel_id=1, source_target_pairs={{0,32},{32,64},{64,96},{96,128},{128,160},{160,192},{192,224},{224... | collective-permute-start | bytes 49160 | tf_op jit(solution)/shard_map/ppermute | solution.py:411
  35.3 3.5 %collective-permute-start.3 = (f32[2,16,128]{2,1,0:T(8,128)S(1)}, f32[2,16,128]{2,1,0:T(8,128)S(1)}, u32[]{:S(2)}, u32[]{:S(2)}) collective-permute-start(f32[2,16,128]{2,1,0:T(8,128)S(1)} %get-tuple-element.43), channel_id=1, source_target_pairs={{32,0},{64,32},{96,64},{128,96},{160,128},{192,160},{224,192},{0,2... | collective-permute-start | bytes 49160 | tf_op jit(solution)/shard_map/ppermute | solution.py:411
  39.6 1.8 %copy-start = (f32[72,72,128]{2,1,0:T(8,128)S(1)}, f32[72,72,128]{2,1,0:T(8,128)}, u32[]{:S(2)}) copy-start(f32[72,72,128]{2,1,0:T(8,128)} %blocks.1) | copy-start | bytes 7962628
  44.2 2.6 %collective-permute-start.4 = (f32[6,8,128]{2,1,0:T(8,128)S(1)}, f32[6,8,128]{2,1,0:T(8,128)S(1)}, u32[]{:S(2)}, u32[]{:S(2)}) collective-permute-start(f32[6,8,128]{2,1,0:T(8,128)S(1)} %get-tuple-element.46), channel_id=1, source_target_pairs={{0,32},{32,64},{64,96},{96,128},{128,160},{160,192},{192,224},{224... | collective-permute-start | bytes 73736 | tf_op jit(solution)/shard_map/ppermute | solution.py:411
  45.4 3.3 %collective-permute-start.5 = (f32[6,8,128]{2,1,0:T(8,128)S(1)}, f32[6,8,128]{2,1,0:T(8,128)S(1)}, u32[]{:S(2)}, u32[]{:S(2)}) collective-permute-start(f32[6,8,128]{2,1,0:T(8,128)S(1)} %get-tuple-element.47), channel_id=1, source_target_pairs={{32,0},{64,32},{96,64},{128,96},{160,128},{192,160},{224,192},{0,2... | collective-permute-start | bytes 73736 | tf_op jit(solution)/shard_map/ppermute | solution.py:411
  49.3 5.9 %collective-permute-start.6 = (f32[8,128]{1,0:T(8,128)S(1)}, f32[8,128]{1,0:T(8,128)S(1)}, u32[]{:S(2)}, u32[]{:S(2)}) collective-permute-start(f32[8,128]{1,0:T(8,128)S(1)} %get-tuple-element.49), channel_id=1, source_target_pairs={{0,1},{1,2},{2,3},{3,4},{4,5},{5,6},{6,7},{7,8},{8,9},{9,10},{10,1... | collective-permute-start | bytes 12296 | tf_op jit(solution)/shard_map/ppermute | solution.py:411
  51.3 3.9 %collective-permute-start.7 = (f32[8,128]{1,0:T(8,128)S(1)}, f32[8,128]{1,0:T(8,128)S(1)}, u32[]{:S(2)}, u32[]{:S(2)}) collective-permute-start(f32[8,128]{1,0:T(8,128)S(1)} %get-tuple-element.50), channel_id=1, source_target_pairs={{1,0},{2,1},{3,2},{4,3},{5,4},{6,5},{7,6},{8,7},{9,8},{10,9},{11,1... | collective-permute-start | bytes 12296 | tf_op jit(solution)/shard_map/ppermute | solution.py:411
  56.4 4.7 %collective-permute-start.8 = (f32[6,8,128]{2,1,0:T(8,128)S(1)}, f32[6,8,128]{2,1,0:T(8,128)S(1)}, u32[]{:S(2)}, u32[]{:S(2)}) collective-permute-start(f32[6,8,128]{2,1,0:T(8,128)S(1)} %get-tuple-element.56), channel_id=1, source_target_pairs={{0,32},{32,64},{64,96},{96,128},{128,160},{160,192},{192,224},{224... | collective-permute-start | bytes 73736 | tf_op jit(solution)/shard_map/ppermute | solution.py:411
  57.6 3.7 %collective-permute-start.9 = (f32[6,8,128]{2,1,0:T(8,128)S(1)}, f32[6,8,128]{2,1,0:T(8,128)S(1)}, u32[]{:S(2)}, u32[]{:S(2)}) collective-permute-start(f32[6,8,128]{2,1,0:T(8,128)S(1)} %get-tuple-element.57), channel_id=1, source_target_pairs={{32,0},{64,32},{96,64},{128,96},{160,128},{192,160},{224,192},{0,2... | collective-permute-start | bytes 73736 | tf_op jit(solution)/shard_map/ppermute | solution.py:411
  62.0 6.1 %collective-permute-start.10 = (f32[8,128]{1,0:T(8,128)S(1)}, f32[8,128]{1,0:T(8,128)S(1)}, u32[]{:S(2)}, u32[]{:S(2)}) collective-permute-start(f32[8,128]{1,0:T(8,128)S(1)} %get-tuple-element.59), channel_id=1, source_target_pairs={{0,1},{1,2},{2,3},{3,4},{4,5},{5,6},{6,7},{7,8},{8,9},{9,10},{10,1... | collective-permute-start | bytes 12296 | tf_op jit(solution)/shard_map/ppermute | solution.py:411
  62.0 6.0 %collective-permute-start.11 = (f32[8,128]{1,0:T(8,128)S(1)}, f32[8,128]{1,0:T(8,128)S(1)}, u32[]{:S(2)}, u32[]{:S(2)}) collective-permute-start(f32[8,128]{1,0:T(8,128)S(1)} %get-tuple-element.60), channel_id=1, source_target_pairs={{1,0},{2,1},{3,2},{4,3},{5,4},{6,5},{7,6},{8,7},{9,8},{10,9},{11,1... | collective-permute-start | bytes 12296 | tf_op jit(solution)/shard_map/ppermute | solution.py:411
  72.0 5.9 %collective-permute-start.12 = (f32[128,768]{1,0:T(8,128)S(1)}, f32[128,768]{1,0:T(8,128)S(1)}, u32[]{:S(2)}, u32[]{:S(2)}) collective-permute-start(f32[128,768]{1,0:T(8,128)S(1)} %get-tuple-element.65), channel_id=1, source_target_pairs={{0,32},{32,0},{1,33},{33,1},{2,34},{34,2},{3,35},{35,3},{4,36},{36... | collective-permute-start | bytes 1179656 | tf_op jit(solution)/shard_map/ppermute | solution.py:468

commit v3 on v2

--- a/solution.py
+++ b/solution.py
@@ -14,12 +14,13 @@
 EXT = CR + 2
 FR = 32
 ROW = ("y", "core")
+WIDE = 3
+HALVES = (4, 8, 16, 32, 64)
 F32 = jnp.float32
 BF16 = jnp.bfloat16
 
 VMEM = pl.BlockSpec(memory_space=pltpu.VMEM)
 SMEM = pl.BlockSpec(memory_space=pltpu.SMEM)
-HBM = pl.BlockSpec(memory_space=pltpu.HBM)
 
 
 def call(kernel, out_shapes, in_specs, scratch=(), out_specs=None):
@@ -83,34 +84,32 @@
     return jnp.where(outside, 0.0, 1.0).astype(F32)
 
 
-def start_kernel(
-    state, adjoint, dmap, thickness, direction, frame_out, own_out, first_out, last_out,
-    known, cells, own, sem,
+def start_kernel(info, state, adjoint, dmap, mats, frame_out, first_out, last_out, edge_out):
+    frame_out[...] = jnp.zeros_like(frame_out)
+    frame_out[0:3, 8:8 + CR, :] = state[...]
+    frame_out[3:6, 8:8 + CR, :] = adjoint[...]
+    frame_out[6, 8:8 + CR, :] = dmap[...].astype(F32)
+    tiles = [frame_out[f, 8 + 8 * g:16 + 8 * g, :] for f in range(7) for g in range(3)]
+    first, last = pack_edges(tiles, WIDE)
+    upper = iota((8, CC), 1) >= 64
+    level = info[0].astype(F32)
+    first_out[...] = jnp.where(upper, level, first)
+    last_out[...] = jnp.where(upper, level, last)
+    lane = iota((BLK, CC), 1)
+    for c in range(3):
+        packed = jnp.zeros((BLK, CC), F32)
+        for i in range(min(32, BLK - 32 * c)):
+            mat = mats[32 * c + i]
+            here = ((lane - 4 * i + 2) & (CC - 1)) < 4
+            packed = jnp.where(here, pltpu.roll(mat, 4 * i, 1) if i else mat, packed)
+        edge_out[c] = packed
+
+
+def rows_kernel(
+    frame, from_left, from_right, left_edge, right_edge,
+    side_out, up_out, down_out, edge_out, levels_out,
 ):
-    copies = [
-        pltpu.make_async_copy(thickness, own.at[0], sem.at[0]),
-        pltpu.make_async_copy(direction, own.at[1], sem.at[1]),
-        pltpu.make_async_copy(state, known.at[0:3], sem.at[2]),
-        pltpu.make_async_copy(adjoint, known.at[3:6], sem.at[3]),
-        pltpu.make_async_copy(dmap, cells, sem.at[4]),
-    ]
-    for copy in copies:
-        copy.start()
-    frame_out[...] = jnp.zeros_like(frame_out)
-    for copy in copies:
-        copy.wait()
-    for k in range(2):
-        own_out[:, k * DV:(k + 1) * DV] = jnp.broadcast_to(own[k], (own_out.shape[0], DV))
-    frame_out[0:6, 8:8 + CR, :] = known[...]
-    frame_out[6, 8:8 + CR, :] = cells[...].astype(F32)
-    tiles = [frame_out[f, 8 + 8 * g:16 + 8 * g, :] for f in range(7) for g in range(3)]
-    first, last = pack_edges(tiles, 1)
-    first_out[...] = first
-    last_out[...] = last
-
-
-def rows_kernel(frame, from_left, from_right, table, side_out, up_out, down_out, table_out):
-    tiles = unpack_edges(from_left[...], from_right[...], 21, 1)
+    tiles = unpack_edges(from_left[...], from_right[...], 21, WIDE)
     side_out[...] = jnp.zeros_like(side_out)
     for f in range(7):
         for g in range(3):
@@ -121,7 +120,11 @@
         for f in range(7):
             up_out[tile, 2 * f:2 * f + 2, :] = ref[f, 8:10, :]
             down_out[tile, 2 * f:2 * f + 2, :] = ref[f, 6 + CR:8 + CR, :]
-    table_out[...] = jnp.broadcast_to(table[...][None], table_out.shape)
+    upper = iota((8, CC), 1) >= 64
+    levels_out[...] = jnp.where(upper, from_left[...], pltpu.roll(from_right[...], 64, 1))
+    lane = iota((BLK, CC), 1)
+    for c in range(3):
+        edge_out[c] = jnp.where(lane % 4 < 2, right_edge[c], pltpu.roll(left_edge[c], 4, 1))
 
 
 def apply_blocks(mats, vec):
@@ -138,24 +141,69 @@
     return lax.fori_loop(0, BLK // 8, rows, (zero, zero))
 
 
-def local_solve(mats, vec, total, level):
-    one, two = apply_blocks(mats, vec)
-    total[0] = one
-    total[1] = two
-    vec[0] = one
-    vec[1] = two
-
-    def further(_, carry):
-        one, two = apply_blocks(mats, vec)
-        one = 0.5 * one
-        two = 0.5 * two
-        vec[0] = one
-        vec[1] = two
-        total[0] += one
-        total[1] += two
+def over_columns(x):
+    for shift in HALVES:
+        x = x + pltpu.roll(x, shift, 1)
+    return x
+
+
+def apply_edge(edge, vec):
+    row = iota((BLK, CC), 0)
+    place = iota((BLK, CC), 1) // 4
+    out = jnp.zeros((BLK, CC), F32)
+    for c in range(3):
+        low, high = 32 * c, min(32 * c + 32, BLK)
+        mine = row[low:high] == place[low:high] + 32 * c
+        flat = jnp.sum(jnp.where(mine, vec[low:high], 0.0), axis=0, keepdims=True)
+        out = out + edge[c] * flat
+    return over_columns(out)
+
+
+def local_solve(mats, edge, vec, total, side_vec, side_total, level, levels):
+    lane = iota((BLK, CC), 1)
+    ours = (lane < 2) | (lane >= CC - 2)
+    for n in range(2):
+        side_vec[n] = over_columns(jnp.where(ours, side_vec[n], 0.0))
+    total[...] = jnp.zeros_like(total)
+    side_total[...] = jnp.zeros_like(side_total)
+    top = jnp.maximum(level, jnp.max(levels[...]).astype(jnp.int32))
+
+    def term(order, carry):
+        scale = jnp.where(order == 0, 1.0, 0.5).astype(F32)
+        keep = jnp.where(order < level, 1.0, 0.0).astype(F32)
+        side_keep = levels[0:1, :] > order.astype(F32)
+        for n in range(2):
+            out = scale * apply_edge(edge, side_vec[n])
+            side_vec[n] = out
+            side_total[n] += jnp.where(side_keep, out, 0.0)
+        for n, out in enumerate(apply_blocks(mats, vec)):
+            out = scale * out
+            vec[n] = out
+            total[n] += keep * out
         return carry
 
-    lax.fori_loop(1, level, further, 0)
+    lax.fori_loop(0, top, term, 0)
+
+
+def put_results(total, side_total, local_out, up_out, down_out):
+    up_out[...] = jnp.zeros_like(up_out)
+    down_out[...] = jnp.zeros_like(down_out)
+    for tile, ref in ((0, total), (1, side_total)):
+        local_out[tile] = ref[...].reshape(6, EXT, CC)
+        for f in range(6):
+            up_out[tile, 3 * f:3 * f + 3, :] = local_out[tile, f, 0:3, :]
+            down_out[tile, 3 * f:3 * f + 3, :] = local_out[tile, f, EXT - 3:EXT, :]
+
+
+def join(prow, last, local, from_up, from_down, frames):
+    inside = grid_mask(prow, last, 0, FR)
+    for tile, frame in enumerate(frames):
+        frame[...] = jnp.zeros_like(frame)
+        frame[:, 7:7 + EXT, :] = local[tile]
+        for f in range(6):
+            frame[f, 6:9, :] += jnp.where(prow == 0, 0.0, from_up[tile, 3 * f:3 * f + 3, :])
+            frame[f, 7 + CR:10 + CR, :] += jnp.where(prow == last, 0.0, from_down[tile, 3 * f:3 * f + 3, :])
+        frame[...] = frame[...] * inside[None]
 
 
 def look_up(table, index, tcell, dcell):
@@ -223,12 +271,10 @@
 
 
 def first_kernel(
-    last, info, table, frame, side, from_up, from_down, blocks,
-    resid_out, local_out, up_out, down_out, main_f, side_f, tcell, dcell, mats,
-    vec, total, index_scr, sem,
+    last, info, table, frame, side, from_up, from_down, mats, edge, levels,
+    resid_out, local_out, up_out, down_out, main_f, side_f, tcell, dcell,
+    vec, total, side_vec, side_total, index_scr,
 ):
-    copy = pltpu.make_async_copy(blocks, mats, sem)
-    copy.start()
     level, prow = info[0], info[1]
     inside = grid_mask(prow, last, 0, FR)
     for tile, ref, source in ((0, main_f, frame), (1, side_f, side)):
@@ -245,48 +291,24 @@
         tcell[tile] = tcell[tile] * inside
     slope = [3.0 * tcell[tile] * tcell[tile] * dcell[tile] for tile in range(2)]
     lo, hi = 7, 7 + EXT
-    parts = differences(main_f, side_f, lo, hi)
-    rhs = jnp.zeros((6, EXT, CC), F32)
-    for weight, diff in zip(weights_of(slope[0], slope[1], lo, hi), parts):
-        rhs = rhs - weight[None] * diff
-    rhs = rhs * inside[lo:hi][None]
-    resid_out[...] = rhs
-    vec[...] = rhs.reshape(2, BLK, CC)
-    copy.wait()
-    local_solve(mats, vec, total, level)
-    local = total[...].reshape(6, EXT, CC)
-    local_out[...] = local
-    up_out[...] = local[:, 0:8, :]
-    down_out[...] = local[:, EXT - 8:EXT, :]
-
-
-def join_kernel(last, info, local, from_up, from_down, frame_out, first_out, last_out):
-    prow = info[1]
-    frame_out[...] = jnp.zeros_like(frame_out)
-    frame_out[:, 7:7 + EXT, :] = local[...]
-    frame_out[:, 6:9, :] += jnp.where(prow == 0, 0.0, from_up[:, 5:8, :])
-    frame_out[:, 7 + CR:10 + CR, :] += jnp.where(prow == last, 0.0, from_down[:, 0:3, :])
-    inside = grid_mask(prow, last, 0, FR)
-    frame_out[...] = frame_out[...] * inside[None]
-    tiles = []
-    for f in range(6):
-        field = frame_out[f, 7:7 + EXT, :]
-        tiles += [field[8 * g:8 * g + 8] for g in range(3)]
-    first, last_lanes = pack_edges(tiles, 1)
-    first_out[...] = first
-    last_out[...] = last_lanes
-
-
-def fill_side(side_f, from_left, from_right):
-    tiles = unpack_edges(from_left[...], from_right[...], 18, 1)
-    side_f[...] = jnp.zeros_like(side_f)
-    for f in range(6):
-        for g in range(3):
-            side_f[f, 7 + 8 * g:15 + 8 * g, :] = tiles[3 * f + g]
-
-
-def stiffness(main_f, side_f, tcell, lo, hi):
-    stiff = [tcell[tile] * tcell[tile] * tcell[tile] for tile in range(2)]
+    frames = (main_f, side_f)
+    for tile, out in ((0, vec), (1, side_vec)):
+        here, beside = frames[tile], frames[1 - tile]
+        rhs = jnp.zeros((6, EXT, CC), F32)
+        for weight, diff in zip(
+            weights_of(slope[tile], slope[1 - tile], lo, hi), differences(here, beside, lo, hi)
+        ):
+            rhs = rhs - weight[None] * diff
+        rhs = rhs * inside[lo:hi][None]
+        if tile == 0:
+            resid_out[...] = rhs
+        out[...] = rhs.reshape(2, BLK, CC)
+    local_solve(mats, edge, vec, total, side_vec, side_total, level, levels)
+    put_results(total, side_total, local_out, up_out, down_out)
+
+
+def stiffness(main_f, side_f, main_t, side_t, lo, hi):
+    stiff = [t * t * t for t in (main_t[...], side_t[...])]
     out = main_f[:, lo:hi, :]
     parts = differences(main_f, side_f, lo, hi)
     for weight, diff in zip(weights_of(stiff[0], stiff[1], lo, hi), parts):
@@ -295,30 +317,33 @@
 
 
 def second_kernel(
-    last, info, frame, from_left, from_right, tcell, mats,
-    image_out, side_out, local_out, up_out, down_out, vec, total,
+    last, info, local, from_up, from_down, tcell, mats, edge, levels,
+    main_f, side_f, image_out, local_out, up_out, down_out, vec, total, side_vec, side_total,
 ):
     level, prow = info[0], info[1]
-    fill_side(side_out, from_left, from_right)
+    frames = (main_f, side_f)
+    join(prow, last, local, from_up, from_down, frames)
     lo, hi = 7, 7 + EXT
-    image = stiffness(frame, side_out, tcell, lo, hi)
-    image = image * grid_mask(prow, last, lo, EXT)[None]
-    image_out[...] = image
-    vec[...] = image.reshape(2, BLK, CC)
-    local_solve(mats, vec, total, level)
-    local = total[...].reshape(6, EXT, CC)
-    local_out[...] = local
-    up_out[...] = local[:, 0:8, :]
-    down_out[...] = local[:, EXT - 8:EXT, :]
+    inside = grid_mask(prow, last, lo, EXT)
+    for tile, out in ((0, vec), (1, side_vec)):
+        image = stiffness(
+            frames[tile], frames[1 - tile], tcell.at[tile], tcell.at[1 - tile], lo, hi
+        ) * inside[None]
+        if tile == 0:
+            image_out[...] = image
+        out[...] = image.reshape(2, BLK, CC)
+    local_solve(mats, edge, vec, total, side_vec, side_total, level, levels)
+    put_results(total, side_total, local_out, up_out, down_out)
 
 
 def third_kernel(
-    n_col, info, frame, resid, image, zframe, zside, wframe, from_left, from_right, tcell, dcell, main_f, side_f,
-    keep_out, send_out, wside, left_op, right_op,
+    last, n_col, info, frame, resid, image, zframe, zside, local, from_up, from_down,
+    tcell, dcell, main_f, side_f,
+    wframe, keep_out, send_out, wside, left_op, right_op,
 ):
-    fill_side(wside, from_left, from_right)
+    join(info[1], last, local, from_up, from_down, (wframe, wside))
     lo, hi = 8, 8 + CR
-    v = stiffness(wframe, wside, tcell, lo, hi)
+    v = stiffness(wframe, wside, tcell.at[0], tcell.at[1], lo, hi)
     r = resid[:, 1:1 + CR, :]
     q = image[:, 1:1 + CR, :]
     z = zframe[:, lo:hi, :]
@@ -419,52 +444,43 @@
     rows = functools.partial(ring, ROW, n_row)
     cols = functools.partial(ring, "pcol", n_col)
 
-    frame, own, first, end = call(
-        start_kernel, [(7, FR, CC), (n_col, 2 * DV), (8, CC), (8, CC)], [HBM] * 5,
-        [
-            pltpu.VMEM((6, CR, CC), F32), pltpu.VMEM((CR, CC), jnp.int32),
-            pltpu.VMEM((2, 1, DV), F32), pltpu.SemaphoreType.DMA((5,)),
-        ],
-    )(state, adjoint, design_map, thickness.reshape(1, DV), direction.reshape(1, DV))
-    from_left, from_right = cols(end, first)
-    table = lax.all_to_all(own, "pcol", 0, 0, tiled=True)
-    side, up, down, table = call(
-        rows_kernel, [(7, FR, CC), (2, 16, CC), (2, 16, CC), (n_row, n_col, 2 * DV)], [VMEM] * 4,
-    )(frame, from_left, from_right, table)
-    from_up, from_down = rows(down, up)
-    table = lax.all_to_all(table, ROW, 0, 0, tiled=True).reshape(n_dev, 2 * DV)
+    own = jnp.concatenate([thickness, direction])
+    table = lax.all_to_all(
+        jnp.broadcast_to(own[None], (n_dev, 2 * DV)), ROW + ("pcol",), 0, 0, tiled=True
+    )
     if n_dev < 256:
         table = jnp.concatenate([table, jnp.zeros((256 - n_dev, 2 * DV), F32)], axis=0)
-
-    solve_scratch = [pltpu.VMEM((2, BLK, CC), F32), pltpu.VMEM((2, BLK, CC), F32)]
-    resid, local, up, down, main_f, side_f, tcell, dcell, mats = call(
+    frame, first, end, edge = call(
+        start_kernel, [(7, FR, CC), (8, CC), (8, CC), (3, BLK, CC)], [SMEM] + [VMEM] * 4
+    )(info, state, adjoint, design_map, blocks)
+    side, up, down, edge, around = call(
+        rows_kernel, [(7, FR, CC), (2, 16, CC), (2, 16, CC), (3, BLK, CC), (8, CC)], [VMEM] * 5
+    )(frame, *cols(end, first), *cols(edge, edge))
+
+    solve_scratch = [pltpu.VMEM((2, BLK, CC), F32)] * 4
+    resid, local, up, down, main_f, side_f, tcell, dcell = call(
         functools.partial(first_kernel, last),
         [
-            (6, EXT, CC), (6, EXT, CC), (6, 8, CC), (6, 8, CC), (6, FR, CC), (6, FR, CC),
-            (2, FR, CC), (2, FR, CC), (BLK, BLK, CC),
+            (6, EXT, CC), (2, 6, EXT, CC), (2, 24, CC), (2, 24, CC), (6, FR, CC), (6, FR, CC),
+            (2, FR, CC), (2, FR, CC),
         ],
-        [SMEM] + [VMEM] * 5 + [HBM],
-        solve_scratch + [pltpu.VMEM((2, FR, CC), F32), pltpu.SemaphoreType.DMA(())],
-    )(info, table, frame, side, from_up, from_down, blocks)
-
-    join = call(
-        functools.partial(join_kernel, last), [(6, FR, CC), (8, CC), (8, CC)], [SMEM] + [VMEM] * 3
-    )
-    zframe, first, end = join(info, local, *rows(down, up))
-    image, zside, local, up, down = call(
+        [SMEM] + [VMEM] * 8,
+        solve_scratch + [pltpu.VMEM((2, FR, CC), F32)],
+    )(info, table, frame, side, *rows(down, up), blocks, edge, around)
+    zframe, zside, image, local, up, down = call(
         functools.partial(second_kernel, last),
-        [(6, EXT, CC), (6, FR, CC), (6, EXT, CC), (6, 8, CC), (6, 8, CC)],
-        [SMEM] + [VMEM] * 5,
+        [(6, FR, CC), (6, FR, CC), (6, EXT, CC), (2, 6, EXT, CC), (2, 24, CC), (2, 24, CC)],
+        [SMEM] + [VMEM] * 7,
         solve_scratch,
-    )(info, zframe, *cols(end, first), tcell, mats)
-    wframe, first, end = join(info, local, *rows(down, up))
-    keep, send = call(
-        functools.partial(third_kernel, n_col), [(n_dev // 2, 6 * CC)] * 2, [SMEM] + [VMEM] * 12,
+    )(info, local, *rows(down, up), tcell, blocks, edge, around)
+    wframe, keep, send = call(
+        functools.partial(third_kernel, last, n_col),
+        [(6, FR, CC)] + [(n_dev // 2, 6 * CC)] * 2, [SMEM] + [VMEM] * 12,
         [
             pltpu.VMEM((6, FR, CC), F32), pltpu.VMEM((256, CR * 2 * CC), BF16),
             pltpu.VMEM((5 * DV, CR * 2 * CC), BF16),
         ],
-    )(info, frame, resid, image, zframe, zside, wframe, *cols(end, first), tcell, dcell, main_f, side_f)
+    )(info, frame, resid, image, zframe, zside, local, *rows(down, up), tcell, dcell, main_f, side_f)
     sums = keep + lax.ppermute(send, "core", [(0, 1), (1, 0)])
     got = lax.all_to_all(sums, ("y", "pcol"), 0, 0, tiled=True)
     tangent, second, owned = call(

time: 106 us -> 96.9 us (0.914)
  starting transfers between devices: 45.6 us -> 35.6 us
  Pallas kernels: 11 us -> 14.9 us
  waiting for transfers between devices: 14.7 us -> 11.9 us
  local copies, waits for them, and re-layouts: 6.38 us -> 5.28 us
    all_to_all x2 -> x1, waiting for transfers between devices: 4.71 us -> 0.01 us  [per_device(): lax.all_to_all(jnp.broadcast_to(own[None], (n_dev, 2 * DV)), ROW + ('pcol...]
    ppermute x6 -> x5, starting transfers between devices: 7.34 us -> 2.7 us  [ring(): lax.ppermute(to_next, axis, forward)]
    pallas_call x7 -> x5, Pallas kernels: 10.3 us -> 14.1 us  [the longest x1 5.03 us: per_device(): call(functools.partial(first_kernel, last), [(6, EXT, CC), (2, 6, EXT, CC...]
    all_to_all x2 -> x1, starting transfers between devices: 18.4 us -> 15.7 us  [per_device(): lax.all_to_all(jnp.broadcast_to(own[None], (n_dev, 2 * DV)), ROW + ('pcol...]
    ppermute x1, starting transfers between devices: 4.59 us -> 2.74 us  [per_device(): sums = keep + lax.ppermute(send, 'core', [(0, 1), (1, 0)])]
    ppermute x6 -> x5, waiting for transfers between devices: 4.11 us -> 5.79 us  [ring(): lax.ppermute(to_previous, axis, backward)]
    unnamed x14 -> x12, local copies, waits for them, and re-layouts: 5.32 us -> 4.04 us
    ppermute x6 -> x5, starting transfers between devices: 15.2 us -> 14.5 us  [ring(): lax.ppermute(to_previous, axis, backward)]
  transfers between devices with their start and end apart: 15 -> 12, of which waited for: 11 -> 8; matrix products, arithmetic and copies ran while one was open for 0% -> 0% of each run, Pallas kernels for 0% -> 2%
where the time goes in v3:
time: 96.9 us; the launch traced here: 96.5 us
  starting transfers between devices  35.6 us (37%)
  blocking collectives  26.6 us (27%)
  Pallas kernels  14.9 us (15%)
  waiting for transfers between devices  11.9 us (12%)
  local copies, waits for them, and re-layouts  5.28 us (5%)
  between operations  1.37 us (1%)
    all_to_all x1, blocking collectives, per_device(): got = lax.all_to_all(sums, ('y', 'pcol'), 0, 0, tiled=True)  26.6 us
    all_to_all x1, starting transfers between devices, per_device(): lax.all_to_all(jnp.broadcast_to(own[None], (n_dev, 2 * DV)), ROW + ('pcol...  15.7 us
    ppermute x5, starting transfers between devices, ring(): lax.ppermute(to_previous, axis, backward)  14.5 us
    ppermute x5, waiting for transfers between devices, ring(): lax.ppermute(to_previous, axis, backward)  5.79 us
    pallas_call x1, Pallas kernels, per_device(): call(functools.partial(first_kernel, last), [(6, EXT, CC), (2, 6, EXT, CC...  5.03 us
    ppermute x5, waiting for transfers between devices, ring(): lax.ppermute(to_next, axis, forward)  4.73 us
    unnamed x12, local copies, waits for them, and re-layouts  4.04 us
    pallas_call x1, Pallas kernels, per_device(): call(functools.partial(third_kernel, last, n_col), [(6, FR, CC)] + [(n_de...  3.97 us
  transfers between devices with their start and end apart: 12, of which 8 were waited for; matrix products, arithmetic and copies ran while one was open for 0% of the time, Pallas kernels for 2%

profile of v3, /device:TPU:1, one launch (start us, length us, event | category | flops | bytes accessed | tf_op | source)
XLA Modules:
  0.0 96.5 jit_solution(9713825826410749333)
XLA Ops:
  0.6 0.7 pad_maximum_fusion
  1.3 0.8 broadcast_in_dim.2
  2.1 15.7 %all-to-all-start = ((f32[256,1,256]{2,1,0:T(1,128)}), f32[256,1,256]{2,1,0:T(1,128)S(1)}, u32[]{:S(2)}, u32[]{:S(2)}) async-start(f32[256,1,256]{2,1,0:T(1,128)} %broadcast_in_dim.2), calls=%async_computation | async-start | bytes 524288 | tf_op jit(solution)/shard_map/all_to_all | solution.py:448
  18.5 0.1 pad_add_fusion.info
  18.5 0.0 copy-start
  18.5 1.7 %copy-done = f32[72,72,128]{2,1,0:T(8,128)S(1)} copy-done((f32[72,72,128]{2,1,0:T(8,128)S(1)}, f32[72,72,128]{2,1,0:T(8,128)}, u32[]{:S(2)}) %copy-start) | copy-done | bytes 2654232
  20.3 0.0 copy-start.2
  20.3 0.8 copy-done.2
  21.1 0.0 copy-start.3
  21.1 0.8 copy-done.3
  21.8 0.0 copy-start.4
  21.8 0.7 copy-done.4
  22.5 0.0 copy-start.1
  22.5 1.3 %shard_map.94 = (f32[7,32,128]{2,1,0:T(8,128)S(1)}, f32[8,128]{1,0:T(8,128)S(1)}, f32[8,128]{1,0:T(8,128)S(1)}, f32[3,72,128]{2,1,0:T(8,128)S(1)}) custom-call(s32[2]{0:T(128)S(1)} %pad_add_fusion.info, f32[3,22,128]{2,1,0:T(8,128)S(1)} %copy-done.2, f32[3,22,128]{2,1,0:T(8,128)S(1)} %copy-done.3, s32[22,128]{1,0:T(8,128)S(1)} %copy-done.4, ...), custom_call_target="tpu_custom_call" | custom-call | tf_op jit(solution)/shard_map/pallas_call | solution.py:453
  23.9 6.6 %collective-permute-start.3 = (f32[3,72,128]{2,1,0:T(8,128)S(1)}, f32[3,72,128]{2,1,0:T(8,128)S(1)}, u32[]{:S(2)}, u32[]{:S(2)}) collective-permute-start(f32[3,72,128]{2,1,0:T(8,128)S(1)} %get-tuple-element.35), channel_id=1, source_target_pairs={{1,0},{2,1},{3,2},{4,3},{5,4},{6,5},{7,6},{8,7},{9,8},{10,9},{11,1... | collective-permute-start | bytes 331784 | tf_op jit(solution)/shard_map/ppermute | solution.py:436
  30.5 0.0 collective-permute-start.2
  30.5 0.0 collective-permute-start
  30.5 4.8 %collective-permute-start.1 = (f32[8,128]{1,0:T(8,128)S(1)}, f32[8,128]{1,0:T(8,128)S(1)}, u32[]{:S(2)}, u32[]{:S(2)}) collective-permute-start(f32[8,128]{1,0:T(8,128)S(1)} %get-tuple-element.34), channel_id=1, source_target_pairs={{1,0},{2,1},{3,2},{4,3},{5,4},{6,5},{7,6},{8,7},{9,8},{10,9},{11,1... | collective-permute-start | bytes 12296 | tf_op jit(solution)/shard_map/ppermute | solution.py:436
  35.3 2.6 %collective-permute-done.from_left = f32[8,128]{1,0:T(8,128)S(1)} collective-permute-done((f32[8,128]{1,0:T(8,128)S(1)}, f32[8,128]{1,0:T(8,128)S(1)}, u32[]{:S(2)}, u32[]{:S(2)}) %collective-permute-start) | collective-permute-done | bytes 4128 | tf_op jit(solution)/shard_map/ppermute | solution.py:436
  37.8 0.0 collective-permute-done.1.from_right
  37.8 0.0 collective-permute-done.3.right_edge
  37.8 0.0 collective-permute-done.2.left_edge
  37.8 0.2 shard_map.95
  38.0 2.7 %collective-permute-start.4 = (f32[2,16,128]{2,1,0:T(8,128)S(1)}, f32[2,16,128]{2,1,0:T(8,128)S(1)}, u32[]{:S(2)}, u32[]{:S(2)}) collective-permute-start(f32[2,16,128]{2,1,0:T(8,128)S(1)} %get-tuple-element.37), channel_id=1, source_target_pairs={{0,32},{32,64},{64,96},{96,128},{128,160},{160,192},{192,224},{224... | collective-permute-start | bytes 49160 | tf_op jit(solution)/shard_map/ppermute | solution.py:436
  40.7 0.0 collective-permute-start.5
  40.7 0.0 all-to-all-done
  40.7 0.8 collective-permute-done.4.from_up
  41.5 2.3 %collective-permute-done.5.from_down = f32[2,16,128]{2,1,0:T(8,128)S(1)} collective-permute-done((f32[2,16,128]{2,1,0:T(8,128)S(1)}, f32[2,16,128]{2,1,0:T(8,128)S(1)}, u32[]{:S(2)}, u32[]{:S(2)}) %collective-permute-start.5) | collective-permute-done | bytes 16416 | tf_op jit(solution)/shard_map/ppermute | solution.py:436
  43.8 0.0 copy-done.1
  43.8 5.0 %shard_map.96 = (f32[6,24,128]{2,1,0:T(8,128)S(1)}, f32[2,6,24,128]{3,2,1,0:T(8,128)S(1)}, f32[2,24,128]{2,1,0:T(8,128)S(1)}, f32[2,24,128]{2,1,0:T(8,128)S(1)},...) custom-call(s32[2]{0:T(128)S(1)} %pad_add_fusion.info, ...), custom_call_target="tpu_custom_call" | custom-call | tf_op jit(solution)/shard_map/pallas_call | solution.py:461
  48.9 0.0 collective-permute-start.6
  48.9 0.9 collective-permute-start.7
  49.8 0.7 collective-permute-done.6.from_up
  50.5 2.4 %collective-permute-done.7.from_down = f32[2,24,128]{2,1,0:T(8,128)S(1)} collective-permute-done((f32[2,24,128]{2,1,0:T(8,128)S(1)}, f32[2,24,128]{2,1,0:T(8,128)S(1)}, u32[]{:S(2)}, u32[]{:S(2)}) %collective-permute-start.7) | collective-permute-done | bytes 24608 | tf_op jit(solution)/shard_map/ppermute | solution.py:436
  52.8 3.6 %shard_map.97 = (f32[6,32,128]{2,1,0:T(8,128)S(1)}, f32[6,32,128]{2,1,0:T(8,128)S(1)}, f32[6,24,128]{2,1,0:T(8,128)S(1)}, f32[2,6,24,128]{3,2,1,0:T(8,128)S(1)},...) custom-call(s32[2]{0:T(128)S(1)} %pad_add_fusion.info, f32[2,6,24,128]{3,2,1,0:T(8,128)S(1)} %get-tuple-element.42.local, ...), custom_call_target="tpu_custom_call" | custom-call | tf_op jit(solution)/shard_map/pallas_call | solution.py:470
  56.4 0.0 collective-permute-start.8
  56.5 2.3 %collective-permute-start.9 = (f32[2,24,128]{2,1,0:T(8,128)S(1)}, f32[2,24,128]{2,1,0:T(8,128)S(1)}, u32[]{:S(2)}, u32[]{:S(2)}) collective-permute-start(f32[2,24,128]{2,1,0:T(8,128)S(1)} %get-tuple-element.51), channel_id=1, source_target_pairs={{32,0},{64,32},{96,64},{128,96},{160,128},{192,160},{224,192},{0,2... | collective-permute-start | bytes 73736 | tf_op jit(solution)/shard_map/ppermute | solution.py:436
  58.7 0.7 collective-permute-done.8.from_up
  59.4 1.1 %collective-permute-done.9.from_down = f32[2,24,128]{2,1,0:T(8,128)S(1)} collective-permute-done((f32[2,24,128]{2,1,0:T(8,128)S(1)}, f32[2,24,128]{2,1,0:T(8,128)S(1)}, u32[]{:S(2)}, u32[]{:S(2)}) %collective-permute-start.9) | collective-permute-done | bytes 24608 | tf_op jit(solution)/shard_map/ppermute | solution.py:436
  60.5 4.0 %shard_map.98 = (f32[6,32,128]{2,1,0:T(8,128)S(1)}, f32[128,768]{1,0:T(8,128)S(1)}, f32[128,768]{1,0:T(8,128)S(1)}) custom-call(s32[2]{0:T(128)S(1)} %pad_add_fusion.info, f32[7,32,128]{2,1,0:T(8,128)S(1)} %get-tuple-element.32.frame, f32[6,24,128]{2,1,0:T(8,128)S(1)} %get-tuple-element.41.resid, f32[6,24,128]{2,1,0:T(8,128)S(1)} %get-tuple-element.46.image, ...), custom_call_target="tpu_custom_call" | custom-call | tf_op jit(solution)/shard_map/pallas_call | solution.py:476
  64.5 2.7 %collective-permute-start.10 = (f32[128,768]{1,0:T(8,128)S(1)}, f32[128,768]{1,0:T(8,128)S(1)}, u32[]{:S(2)}, u32[]{:S(2)}) collective-permute-start(f32[128,768]{1,0:T(8,128)S(1)} %get-tuple-element.56), channel_id=1, source_target_pairs={{0,32},{32,0},{1,33},{33,1},{2,34},{34,2},{3,35},{35,3},{4,36},{36... | collective-permute-start | bytes 1179656 | tf_op jit(solution)/shard_map/ppermute | solution.py:484
  67.2 1.3 %collective-permute-done.10 = f32[128,768]{1,0:T(8,128)S(1)} collective-permute-done((f32[128,768]{1,0:T(8,128)S(1)}, f32[128,768]{1,0:T(8,128)S(1)}, u32[]{:S(2)}, u32[]{:S(2)}) %collective-permute-start.10) | collective-permute-done | bytes 393248 | tf_op jit(solution)/shard_map/ppermute | solution.py:484
  68.6 0.4 copy.10
  69.1 26.6 %all_to_all.19 = f32[128,1,768]{2,1,0:T(1,128)S(1)} all-to-all(f32[128,1,768]{2,1,0:T(1,128)S(1)} %copy.10), channel_id=1, replica_groups=mesh['y'=4,'core'=2,'pcol'=32] {'y','pcol'}, dimensions={0} | all-to-all | bytes 786432 | tf_op jit(solution)/shard_map/all_to_all | solution.py:485
  95.7 0.8 shard_map.99
  (3 shorter events, 0.1 us)
Async XLA Ops:
  2.1 38.5 %all-to-all-start = ((f32[256,1,256]{2,1,0:T(1,128)}), f32[256,1,256]{2,1,0:T(1,128)S(1)}, u32[]{:S(2)}, u32[]{:S(2)}) async-start(f32[256,1,256]{2,1,0:T(1,128)} %broadcast_in_dim.2), calls=%async_computation | async-start | bytes 524288 | tf_op jit(solution)/shard_map/all_to_all | solution.py:448
  18.5 1.8 %copy-start = (f32[72,72,128]{2,1,0:T(8,128)S(1)}, f32[72,72,128]{2,1,0:T(8,128)}, u32[]{:S(2)}) copy-start(f32[72,72,128]{2,1,0:T(8,128)} %mats.5) | copy-start | bytes 7962628
  20.3 0.8 copy-start.2
  21.1 0.8 copy-start.3
  21.8 0.7 copy-start.4
  22.5 21.3 %copy-start.1 = (f32[72,72,128]{2,1,0:T(8,128)S(1)}, f32[72,72,128]{2,1,0:T(8,128)}, u32[]{:S(2)}) copy-start(f32[72,72,128]{2,1,0:T(8,128)} %mats.5) | copy-start | bytes 7962628
  23.9 13.9 %collective-permute-start.3 = (f32[3,72,128]{2,1,0:T(8,128)S(1)}, f32[3,72,128]{2,1,0:T(8,128)S(1)}, u32[]{:S(2)}, u32[]{:S(2)}) collective-permute-start(f32[3,72,128]{2,1,0:T(8,128)S(1)} %get-tuple-element.35), channel_id=1, source_target_pairs={{1,0},{2,1},{3,2},{4,3},{5,4},{6,5},{7,6},{8,7},{9,8},{10,9},{11,1... | collective-permute-start | bytes 331784 | tf_op jit(solution)/shard_map/ppermute | solution.py:436
  30.5 7.4 %collective-permute-start.2 = (f32[3,72,128]{2,1,0:T(8,128)S(1)}, f32[3,72,128]{2,1,0:T(8,128)S(1)}, u32[]{:S(2)}, u32[]{:S(2)}) collective-permute-start(f32[3,72,128]{2,1,0:T(8,128)S(1)} %get-tuple-element.35), channel_id=1, source_target_pairs={{0,1},{1,2},{2,3},{3,4},{4,5},{5,6},{6,7},{7,8},{8,9},{9,10},{10,1... | collective-permute-start | bytes 331784 | tf_op jit(solution)/shard_map/ppermute | solution.py:436
  30.5 7.4 %collective-permute-start = (f32[8,128]{1,0:T(8,128)S(1)}, f32[8,128]{1,0:T(8,128)S(1)}, u32[]{:S(2)}, u32[]{:S(2)}) collective-permute-start(f32[8,128]{1,0:T(8,128)S(1)} %get-tuple-element.33), channel_id=1, source_target_pairs={{0,1},{1,2},{2,3},{3,4},{4,5},{5,6},{6,7},{7,8},{8,9},{9,10},{10,1... | collective-permute-start | bytes 12296 | tf_op jit(solution)/shard_map/ppermute | solution.py:436
  30.5 7.4 %collective-permute-start.1 = (f32[8,128]{1,0:T(8,128)S(1)}, f32[8,128]{1,0:T(8,128)S(1)}, u32[]{:S(2)}, u32[]{:S(2)}) collective-permute-start(f32[8,128]{1,0:T(8,128)S(1)} %get-tuple-element.34), channel_id=1, source_target_pairs={{1,0},{2,1},{3,2},{4,3},{5,4},{6,5},{7,6},{8,7},{9,8},{10,9},{11,1... | collective-permute-start | bytes 12296 | tf_op jit(solution)/shard_map/ppermute | solution.py:436
  38.0 3.5 %collective-permute-start.4 = (f32[2,16,128]{2,1,0:T(8,128)S(1)}, f32[2,16,128]{2,1,0:T(8,128)S(1)}, u32[]{:S(2)}, u32[]{:S(2)}) collective-permute-start(f32[2,16,128]{2,1,0:T(8,128)S(1)} %get-tuple-element.37), channel_id=1, source_target_pairs={{0,32},{32,64},{64,96},{96,128},{128,160},{160,192},{192,224},{224... | collective-permute-start | bytes 49160 | tf_op jit(solution)/shard_map/ppermute | solution.py:436
  40.7 3.2 %collective-permute-start.5 = (f32[2,16,128]{2,1,0:T(8,128)S(1)}, f32[2,16,128]{2,1,0:T(8,128)S(1)}, u32[]{:S(2)}, u32[]{:S(2)}) collective-permute-start(f32[2,16,128]{2,1,0:T(8,128)S(1)} %get-tuple-element.38), channel_id=1, source_target_pairs={{32,0},{64,32},{96,64},{128,96},{160,128},{192,160},{224,192},{0,2... | collective-permute-start | bytes 49160 | tf_op jit(solution)/shard_map/ppermute | solution.py:436
  48.9 1.6 %collective-permute-start.6 = (f32[2,24,128]{2,1,0:T(8,128)S(1)}, f32[2,24,128]{2,1,0:T(8,128)S(1)}, u32[]{:S(2)}, u32[]{:S(2)}) collective-permute-start(f32[2,24,128]{2,1,0:T(8,128)S(1)} %get-tuple-element.43), channel_id=1, source_target_pairs={{0,32},{32,64},{64,96},{96,128},{128,160},{160,192},{192,224},{224... | collective-permute-start | bytes 73736 | tf_op jit(solution)/shard_map/ppermute | solution.py:436
  48.9 3.9 %collective-permute-start.7 = (f32[2,24,128]{2,1,0:T(8,128)S(1)}, f32[2,24,128]{2,1,0:T(8,128)S(1)}, u32[]{:S(2)}, u32[]{:S(2)}) collective-permute-start(f32[2,24,128]{2,1,0:T(8,128)S(1)} %get-tuple-element.44), channel_id=1, source_target_pairs={{32,0},{64,32},{96,64},{128,96},{160,128},{192,160},{224,192},{0,2... | collective-permute-start | bytes 73736 | tf_op jit(solution)/shard_map/ppermute | solution.py:436
  56.4 2.9 %collective-permute-start.8 = (f32[2,24,128]{2,1,0:T(8,128)S(1)}, f32[2,24,128]{2,1,0:T(8,128)S(1)}, u32[]{:S(2)}, u32[]{:S(2)}) collective-permute-start(f32[2,24,128]{2,1,0:T(8,128)S(1)} %get-tuple-element.50), channel_id=1, source_target_pairs={{0,32},{32,64},{64,96},{96,128},{128,160},{160,192},{192,224},{224... | collective-permute-start | bytes 73736 | tf_op jit(solution)/shard_map/ppermute | solution.py:436
  56.5 4.1 %collective-permute-start.9 = (f32[2,24,128]{2,1,0:T(8,128)S(1)}, f32[2,24,128]{2,1,0:T(8,128)S(1)}, u32[]{:S(2)}, u32[]{:S(2)}) collective-permute-start(f32[2,24,128]{2,1,0:T(8,128)S(1)} %get-tuple-element.51), channel_id=1, source_target_pairs={{32,0},{64,32},{96,64},{128,96},{160,128},{192,160},{224,192},{0,2... | collective-permute-start | bytes 73736 | tf_op jit(solution)/shard_map/ppermute | solution.py:436
  64.5 4.1 %collective-permute-start.10 = (f32[128,768]{1,0:T(8,128)S(1)}, f32[128,768]{1,0:T(8,128)S(1)}, u32[]{:S(2)}, u32[]{:S(2)}) collective-permute-start(f32[128,768]{1,0:T(8,128)S(1)} %get-tuple-element.56), channel_id=1, source_target_pairs={{0,32},{32,0},{1,33},{33,1},{2,34},{34,2},{3,35},{35,3},{4,36},{36... | collective-permute-start | bytes 1179656 | tf_op jit(solution)/shard_map/ppermute | solution.py:484

commit v4 on v3

--- a/solution.py
+++ b/solution.py
@@ -23,12 +23,16 @@
 SMEM = pl.BlockSpec(memory_space=pltpu.SMEM)
 
 
-def call(kernel, out_shapes, in_specs, scratch=(), out_specs=None):
+def call(kernel, out_shapes, in_specs, scratch=(), work=None):
+    cost = None
+    if work is not None:
+        cost = pl.CostEstimate(flops=work, bytes_accessed=1 << 20, transcendentals=0)
     return pl.pallas_call(
         kernel,
         out_shape=[jax.ShapeDtypeStruct(s, F32) for s in out_shapes],
         in_specs=list(in_specs),
-        out_specs=[VMEM] * len(out_shapes) if out_specs is None else out_specs,
+        out_specs=[VMEM] * len(out_shapes),
+        cost_estimate=cost,
         scratch_shapes=list(scratch),
         compiler_params=pltpu.CompilerParams(vmem_limit_bytes=20 * 1024 * 1024),
     )
@@ -84,30 +88,29 @@
     return jnp.where(outside, 0.0, 1.0).astype(F32)
 
 
-def start_kernel(info, state, adjoint, dmap, mats, frame_out, first_out, last_out, edge_out):
-    frame_out[...] = jnp.zeros_like(frame_out)
-    frame_out[0:3, 8:8 + CR, :] = state[...]
-    frame_out[3:6, 8:8 + CR, :] = adjoint[...]
-    frame_out[6, 8:8 + CR, :] = dmap[...].astype(F32)
-    tiles = [frame_out[f, 8 + 8 * g:16 + 8 * g, :] for f in range(7) for g in range(3)]
+def start_kernel(info, frame, first_out, last_out):
+    tiles = [frame[f, 8 + 8 * g:16 + 8 * g, :] for f in range(7) for g in range(3)]
     first, last = pack_edges(tiles, WIDE)
     upper = iota((8, CC), 1) >= 64
     level = info[0].astype(F32)
     first_out[...] = jnp.where(upper, level, first)
     last_out[...] = jnp.where(upper, level, last)
+
+
+def edge_kernel(mats, after, edge_out):
     lane = iota((BLK, CC), 1)
     for c in range(3):
         packed = jnp.zeros((BLK, CC), F32)
         for i in range(min(32, BLK - 32 * c)):
-            mat = mats[32 * c + i]
+            at = 32 * c + i
+            mat = mats[at]
             here = ((lane - 4 * i + 2) & (CC - 1)) < 4
             packed = jnp.where(here, pltpu.roll(mat, 4 * i, 1) if i else mat, packed)
         edge_out[c] = packed
 
 
 def rows_kernel(
-    frame, from_left, from_right, left_edge, right_edge,
-    side_out, up_out, down_out, edge_out, levels_out,
+    frame, from_left, from_right, side_out, up_out, down_out, levels_out,
 ):
     tiles = unpack_edges(from_left[...], from_right[...], 21, WIDE)
     side_out[...] = jnp.zeros_like(side_out)
@@ -122,23 +125,16 @@
             down_out[tile, 2 * f:2 * f + 2, :] = ref[f, 6 + CR:8 + CR, :]
     upper = iota((8, CC), 1) >= 64
     levels_out[...] = jnp.where(upper, from_left[...], pltpu.roll(from_right[...], 64, 1))
-    lane = iota((BLK, CC), 1)
-    for c in range(3):
-        edge_out[c] = jnp.where(lane % 4 < 2, right_edge[c], pltpu.roll(left_edge[c], 4, 1))
 
 
 def apply_blocks(mats, vec):
-    def rows(step, carry):
-        one, two = carry
-        for u in range(8):
-            at = step * 8 + u
-            mat = mats[at]
-            one = one + mat * vec[0, pl.ds(at, 1), :]
-            two = two + mat * vec[1, pl.ds(at, 1), :]
-        return one, two
-
-    zero = jnp.zeros((BLK, CC), F32)
-    return lax.fori_loop(0, BLK // 8, rows, (zero, zero))
+    one = jnp.zeros((BLK, CC), F32)
+    two = jnp.zeros((BLK, CC), F32)
+    for at in range(BLK):
+        mat = mats[at]
+        one = one + mat * vec[0, at:at + 1, :]
+        two = two + mat * vec[1, at:at + 1, :]
+    return one, two
 
 
 def over_columns(x):
@@ -271,10 +267,13 @@
 
 
 def first_kernel(
-    last, info, table, frame, side, from_up, from_down, mats, edge, levels,
-    resid_out, local_out, up_out, down_out, main_f, side_f, tcell, dcell,
+    last, info, table, frame, side, from_up, from_down, mats, left_edge, right_edge, levels,
+    resid_out, local_out, up_out, down_out, main_f, side_f, tcell, dcell, edge,
     vec, total, side_vec, side_total, index_scr,
 ):
+    lane = iota((BLK, CC), 1)
+    for c in range(3):
+        edge[c] = jnp.where(lane % 4 < 2, right_edge[c], pltpu.roll(left_edge[c], 4, 1))
     level, prow = info[0], info[1]
     inside = grid_mask(prow, last, 0, FR)
     for tile, ref, source in ((0, main_f, frame), (1, side_f, side)):
@@ -318,7 +317,8 @@
 
 def second_kernel(
     last, info, local, from_up, from_down, tcell, mats, edge, levels,
-    main_f, side_f, image_out, local_out, up_out, down_out, vec, total, side_vec, side_total,
+    main_f, side_f, image_out, local_out, up_out, down_out,
+    vec, total, side_vec, side_total,
 ):
     level, prow = info[0], info[1]
     frames = (main_f, side_f)
@@ -336,18 +336,70 @@
     put_results(total, side_total, local_out, up_out, down_out)
 
 
+def dot3(a, b, i, j):
+    out = jnp.zeros((CR, CC), F32)
+    for an, bn in zip(a, b):
+        for c in range(3):
+            out = out + an[i + c] * bn[j + c]
+    return out
+
+
+def design_sums(n_col, info, frame, values, left_op, right_op):
+    cells = frame[6, 8:8 + CR, :].astype(jnp.int32)
+    owner = cells // DV
+    low = cells % DV
+    other = jnp.where((owner // n_col) % 2 == info[1] % 2, 0, 128)
+    high = other + (owner // (2 * n_col)) * n_col + owner % n_col
+    count = len(values)
+    tops = [value.astype(BF16) for value in values]
+    rests = [(value - top.astype(F32)).astype(BF16) for value, top in zip(values, tops)]
+    for row in range(CR):
+        cut = slice(CC * row, CC * row + CC)
+        left_op[:, cut] = jnp.where(iota((256, CC), 0) == high[row:row + 1], 1.0, 0.0).astype(BF16)
+        hot = jnp.where(iota((DV, CC), 0) == low[row:row + 1], 1.0, 0.0).astype(BF16)
+        for k, part in enumerate(tops + rests):
+            right_op[k * DV:(k + 1) * DV, cut] = hot * part[row:row + 1]
+    sums = lax.dot_general(
+        left_op[...], right_op[...], (((1,), (1,)), ((), ())), preferred_element_type=F32
+    )
+    return sums[:, :count * DV] + sums[:, count * DV:]
+
+
+LO, HI = 8, 8 + CR
+
+
+def known_sums_kernel(n_col, info, frame, tcell, dcell, main_f, side_f, out, left_op, right_op):
+    known_d = differences(main_f, side_f, LO, HI)
+    value = (-3.0 * tcell[0, LO:HI, :] * dcell[0, LO:HI, :]) * dot3(known_d, known_d, 3, 0)
+    out[...] = design_sums(n_col, info, frame, [value], left_op, right_op)
+
+
+def solved_values(tcell, known_d, solved_d):
+    t = tcell[0, LO:HI, :]
+    slope = -1.5 * t * t
+    return [slope * dot3(solved_d, known_d, 3, 0), slope * dot3(known_d, solved_d, 3, 0)]
+
+
+def solved_sums_kernel(
+    n_col, info, frame, tcell, main_f, side_f, zframe, zside, out, left_op, right_op
+):
+    values = solved_values(
+        tcell, differences(main_f, side_f, LO, HI), differences(zframe, zside, LO, HI)
+    )
+    out[...] = design_sums(n_col, info, frame, values, left_op, right_op)
+
+
 def third_kernel(
-    last, n_col, info, frame, resid, image, zframe, zside, local, from_up, from_down,
-    tcell, dcell, main_f, side_f,
+    last, n_col, info, frame, resid, image, zframe, local, from_up, from_down,
+    tcell, main_f, side_f, sums0, sums1,
     wframe, keep_out, send_out, wside, left_op, right_op,
 ):
     join(info[1], last, local, from_up, from_down, (wframe, wside))
-    lo, hi = 8, 8 + CR
-    v = stiffness(wframe, wside, tcell.at[0], tcell.at[1], lo, hi)
+    v = stiffness(wframe, wside, tcell.at[0], tcell.at[1], LO, HI)
     r = resid[:, 1:1 + CR, :]
     q = image[:, 1:1 + CR, :]
-    z = zframe[:, lo:hi, :]
-    w = wframe[:, lo:hi, :]
+    z = zframe[:, LO:HI, :]
+    w = wframe[:, LO:HI, :]
     lane = iota((1, CC), 1)
     dots = jnp.zeros((1, CC), F32)
     pairs = ((r, z), (z, q), (r, w), (q, w), (z, v), (w, v))
@@ -357,50 +409,17 @@
             part = ab[3 * s] + ab[3 * s + 1] + ab[3 * s + 2]
             value = jnp.sum(jnp.sum(part, axis=0, keepdims=True), axis=1, keepdims=True)
             dots = jnp.where(lane == 2 * k + s, value, dots)
-    t = tcell[0, lo:hi, :]
-    d = dcell[0, lo:hi, :]
-    known_d = differences(main_f, side_f, lo, hi)
-    z_d = differences(zframe, zside, lo, hi)
-    w_d = differences(wframe, wside, lo, hi)
-
-    def dot3(a, b, i, j):
-        out = jnp.zeros((CR, CC), F32)
-        for an, bn in zip(a, b):
-            for c in range(3):
-                out = out + an[i + c] * bn[j + c]
-        return out
-
-    slope2 = -1.5 * t * t
-    values = [
-        (-3.0 * t * d) * dot3(known_d, known_d, 3, 0),
-        slope2 * dot3(z_d, known_d, 3, 0),
-        slope2 * dot3(w_d, known_d, 3, 0),
-        slope2 * dot3(known_d, z_d, 3, 0),
-        slope2 * dot3(known_d, w_d, 3, 0),
-    ]
-    cells = frame[6, lo:hi, :].astype(jnp.int32)
-    owner = cells // DV
-    low = cells % DV
-    other = jnp.where((owner // n_col) % 2 == info[1] % 2, 0, 128)
-    high = other + (owner // (2 * n_col)) * n_col + owner % n_col
-    for row in range(CR):
-        hot = jnp.where(iota((256, CC), 0) == high[row:row + 1], 1.0, 0.0).astype(BF16)
-        at = 2 * CC * row
-        left_op[:, at:at + CC] = hot
-        left_op[:, at + CC:at + 2 * CC] = hot
-        mine = iota((DV, CC), 0) == low[row:row + 1]
-        for k, value in enumerate(values):
-            one = value[row:row + 1]
-            top = one.astype(BF16).astype(F32)
-            right_op[k * DV:(k + 1) * DV, at:at + CC] = jnp.where(mine, top, 0.0).astype(BF16)
-            right_op[k * DV:(k + 1) * DV, at + CC:at + 2 * CC] = jnp.where(mine, one - top, 0.0).astype(BF16)
-    sums = lax.dot_general(
-        left_op[...], right_op[...], (((1,), (1,)), ((), ())), preferred_element_type=F32
-    )
+    values = solved_values(
+        tcell, differences(main_f, side_f, LO, HI), differences(wframe, wside, LO, HI)
+    )
+    sums = design_sums(n_col, info, frame, values, left_op, right_op)
     for half, out in ((0, keep_out), (1, send_out)):
         count = out.shape[0]
+        rows = slice(128 * half, 128 * half + count)
         out[:, 0:CC] = jnp.broadcast_to(dots, (count, CC))
-        out[:, CC:] = sums[128 * half:128 * half + count]
+        out[:, CC:2 * CC] = sums0[rows, :]
+        out[:, 2 * CC:4 * CC] = sums1[rows, :]
+        out[:, 4 * CC:] = sums[rows]
 
 
 def last_kernel(got, zframe, wframe, tangent, second, owned):
@@ -426,7 +445,7 @@
             out[f] = c0 * zframe[3 * s + f, 8:8 + CR, :] + c1 * wframe[3 * s + f, 8:8 + CR, :]
     h = [sums[:, (k + 1) * CC:(k + 2) * CC] for k in range(5)]
     owned[...] = (
-        h[0] + coeffs[1][0] * h[1] + coeffs[1][1] * h[2] + coeffs[0][0] * h[3] + coeffs[0][1] * h[4]
+        h[0] + coeffs[1][0] * h[1] + coeffs[0][0] * h[2] + coeffs[1][1] * h[3] + coeffs[0][1] * h[4]
     )
 
 
@@ -450,37 +469,47 @@
     )
     if n_dev < 256:
         table = jnp.concatenate([table, jnp.zeros((256 - n_dev, 2 * DV), F32)], axis=0)
-    frame, first, end, edge = call(
-        start_kernel, [(7, FR, CC), (8, CC), (8, CC), (3, BLK, CC)], [SMEM] + [VMEM] * 4
-    )(info, state, adjoint, design_map, blocks)
-    side, up, down, edge, around = call(
-        rows_kernel, [(7, FR, CC), (2, 16, CC), (2, 16, CC), (3, BLK, CC), (8, CC)], [VMEM] * 5
-    )(frame, *cols(end, first), *cols(edge, edge))
-
+    frame = jnp.concatenate([state, adjoint, design_map.astype(F32)[None]], axis=0)
+    frame = jnp.pad(frame, ((0, 0), (8, FR - 8 - CR), (0, 0)))
+    first, end = call(start_kernel, [(8, CC)] * 2, [SMEM, VMEM])(info, frame)
+    side, up, down, around = call(
+        rows_kernel, [(7, FR, CC), (2, 16, CC), (2, 16, CC), (8, CC)], [VMEM] * 3, work=10**11
+    )(frame, *cols(end, first))
+
+    (edge,) = call(edge_kernel, [(3, BLK, CC)], [VMEM] * 2)(blocks, around)
     solve_scratch = [pltpu.VMEM((2, BLK, CC), F32)] * 4
-    resid, local, up, down, main_f, side_f, tcell, dcell = call(
+    resid, local, up, down, main_f, side_f, tcell, dcell, edge = call(
         functools.partial(first_kernel, last),
         [
             (6, EXT, CC), (2, 6, EXT, CC), (2, 24, CC), (2, 24, CC), (6, FR, CC), (6, FR, CC),
-            (2, FR, CC), (2, FR, CC),
+            (2, FR, CC), (2, FR, CC), (3, BLK, CC),
         ],
-        [SMEM] + [VMEM] * 8,
+        [SMEM] + [VMEM] * 9,
         solve_scratch + [pltpu.VMEM((2, FR, CC), F32)],
-    )(info, table, frame, side, *rows(down, up), blocks, edge, around)
+    )(info, table, frame, side, *rows(down, up), blocks, *cols(edge, edge), around)
+
+    def operands(count):
+        return [pltpu.VMEM((256, CR * CC), BF16), pltpu.VMEM((2 * count * DV, CR * CC), BF16)]
+
+    (sums0,) = call(
+        functools.partial(known_sums_kernel, n_col), [(256, DV)], [SMEM] + [VMEM] * 5, operands(1),
+        work=3 * 10**8,
+    )(info, frame, tcell, dcell, main_f, side_f)
     zframe, zside, image, local, up, down = call(
         functools.partial(second_kernel, last),
         [(6, FR, CC), (6, FR, CC), (6, EXT, CC), (2, 6, EXT, CC), (2, 24, CC), (2, 24, CC)],
         [SMEM] + [VMEM] * 7,
         solve_scratch,
     )(info, local, *rows(down, up), tcell, blocks, edge, around)
+    (sums1,) = call(
+        functools.partial(solved_sums_kernel, n_col), [(256, 2 * DV)], [SMEM] + [VMEM] * 6,
+        operands(2), work=5 * 10**8,
+    )(info, frame, tcell, main_f, side_f, zframe, zside)
     wframe, keep, send = call(
         functools.partial(third_kernel, last, n_col),
         [(6, FR, CC)] + [(n_dev // 2, 6 * CC)] * 2, [SMEM] + [VMEM] * 12,
-        [
-            pltpu.VMEM((6, FR, CC), F32), pltpu.VMEM((256, CR * 2 * CC), BF16),
-            pltpu.VMEM((5 * DV, CR * 2 * CC), BF16),
-        ],
-    )(info, frame, resid, image, zframe, zside, local, *rows(down, up), tcell, dcell, main_f, side_f)
+        [pltpu.VMEM((6, FR, CC), F32)] + operands(2),
+    )(info, frame, resid, image, zframe, local, *rows(down, up), tcell, main_f, side_f, sums0, sums1)
     sums = keep + lax.ppermute(send, "core", [(0, 1), (1, 0)])
     got = lax.all_to_all(sums, ("y", "pcol"), 0, 0, tiled=True)
     tangent, second, owned = call(

time: 96.9 us -> 88.5 us (0.913)
  starting transfers between devices: 35.6 us -> 31.2 us
  blocking collectives: 26.6 us -> 24.1 us
  local copies, waits for them, and re-layouts: 5.28 us -> 2.88 us
  waiting for transfers between devices: 11.9 us -> 9.5 us
  other arithmetic: 0.8 us -> 2.3 us
  Pallas kernels: 14.9 us -> 16.4 us
    all_to_all x1, starting transfers between devices: 15.7 us -> 10.2 us  [per_device(): lax.all_to_all(jnp.broadcast_to(own[None], (n_dev, 2 * DV)), ROW + ('pcol...]
    all_to_all x1, waiting for transfers between devices: 0.01 us -> 4.91 us  [per_device(): lax.all_to_all(jnp.broadcast_to(own[None], (n_dev, 2 * DV)), ROW + ('pcol...]
    ppermute x5, starting transfers between devices: 2.7 us -> 7.18 us  [ring(): lax.ppermute(to_next, axis, forward)]
    ppermute x5, waiting for transfers between devices: 4.73 us -> 0.55 us  [ring(): lax.ppermute(to_next, axis, forward)]
    pallas_call x2 -> x5, Pallas kernels: 1.5 us -> 4.94 us  [the longest x1 1.8 us: per_device(): call(functools.partial(solved_sums_kernel, n_col), [(256, 2 * DV)], [SMEM...]
    ppermute x5, waiting for transfers between devices: 5.79 us -> 2.69 us  [ring(): lax.ppermute(to_previous, axis, backward)]
    all_to_all x1, blocking collectives: 26.6 us -> 24.1 us  [per_device(): got = lax.all_to_all(sums, ('y', 'pcol'), 0, 0, tiled=True)]
    unnamed x12 -> x4, local copies, waits for them, and re-layouts: 4.04 us -> 1.64 us
  transfers between devices with their start and end apart: 12 -> 12, of which waited for: 8 -> 5; matrix products, arithmetic and copies ran while one was open for 0% -> 2% of each run, Pallas kernels for 2% -> 5%
where the time goes in v4:
time: 88.5 us; the launch traced here: 87.8 us
  starting transfers between devices  31.2 us (35%)
  blocking collectives  24.1 us (27%)
  Pallas kernels  16.4 us (19%)
  waiting for transfers between devices  9.5 us (11%)
  local copies, waits for them, and re-layouts  2.88 us (3%)
  other arithmetic  2.3 us (3%)
  between operations  1.44 us (2%)
    all_to_all x1, blocking collectives, per_device(): got = lax.all_to_all(sums, ('y', 'pcol'), 0, 0, tiled=True)  24.1 us
    ppermute x5, starting transfers between devices, ring(): lax.ppermute(to_previous, axis, backward)  13.1 us
    all_to_all x1, starting transfers between devices, per_device(): lax.all_to_all(jnp.broadcast_to(own[None], (n_dev, 2 * DV)), ROW + ('pcol...  10.2 us
    ppermute x5, starting transfers between devices, ring(): lax.ppermute(to_next, axis, forward)  7.18 us
    pallas_call x1, Pallas kernels, per_device(): call(functools.partial(first_kernel, last), [(6, EXT, CC), (2, 6, EXT, CC...  5.05 us
    all_to_all x1, waiting for transfers between devices, per_device(): lax.all_to_all(jnp.broadcast_to(own[None], (n_dev, 2 * DV)), ROW + ('pcol...  4.91 us
    pallas_call x1, Pallas kernels, per_device(): call(functools.partial(second_kernel, last), [(6, FR, CC), (6, FR, CC), (...  3.64 us
    ppermute x5, waiting for transfers between devices, ring(): lax.ppermute(to_previous, axis, backward)  2.69 us
  transfers between devices with their start and end apart: 12, of which 5 were waited for; matrix products, arithmetic and copies ran while one was open for 2% of the time, Pallas kernels for 5%

profile of v4, /device:TPU:1, one launch (start us, length us, event | category | flops | bytes accessed | tf_op | source)
XLA Modules:
  0.0 87.8 jit_solution(3934747646542986994)
XLA Ops:
  1.3 0.7 convert_bitcast_fusion
  2.0 0.1 pad_add_fusion.info
  2.1 0.8 select_maximum_fusion.frame
  2.9 0.6 shard_map.94
  3.5 2.5 %collective-permute-start = (f32[8,128]{1,0:T(8,128)S(1)}, f32[8,128]{1,0:T(8,128)S(1)}, u32[]{:S(2)}, u32[]{:S(2)}) collective-permute-start(f32[8,128]{1,0:T(8,128)S(1)} %get-tuple-element.30), channel_id=1, source_target_pairs={{0,1},{1,2},{2,3},{3,4},{4,5},{5,6},{6,7},{7,8},{8,9},{9,10},{10,1... | collective-permute-start | bytes 12296 | tf_op jit(solution)/shard_map/ppermute | solution.py:455
  6.1 6.2 %collective-permute-start.1 = (f32[8,128]{1,0:T(8,128)S(1)}, f32[8,128]{1,0:T(8,128)S(1)}, u32[]{:S(2)}, u32[]{:S(2)}) collective-permute-start(f32[8,128]{1,0:T(8,128)S(1)} %get-tuple-element.31), channel_id=1, source_target_pairs={{1,0},{2,1},{3,2},{4,3},{5,4},{6,5},{7,6},{8,7},{9,8},{10,9},{11,1... | collective-permute-start | bytes 12296 | tf_op jit(solution)/shard_map/ppermute | solution.py:455
  12.3 0.7 pad_maximum_fusion
  13.0 0.8 broadcast_in_dim.10
  13.8 10.2 %all-to-all-start = ((f32[256,1,256]{2,1,0:T(1,128)}), f32[256,1,256]{2,1,0:T(1,128)S(1)}, u32[]{:S(2)}, u32[]{:S(2)}) async-start(f32[256,1,256]{2,1,0:T(1,128)} %broadcast_in_dim.10), calls=%async_computation | async-start | bytes 524288 | tf_op jit(solution)/shard_map/all_to_all | solution.py:467
  24.0 0.0 copy-start
  24.0 0.0 collective-permute-done.from_left
  24.0 0.0 collective-permute-done.1.from_right
  24.0 0.1 shard_map.95
  24.2 1.6 %copy-done = f32[72,72,128]{2,1,0:T(8,128)S(1)} copy-done((f32[72,72,128]{2,1,0:T(8,128)S(1)}, f32[72,72,128]{2,1,0:T(8,128)}, u32[]{:S(2)}) %copy-start) | copy-done | bytes 2654232
  25.8 0.7 shard_map.96
  26.5 6.6 %collective-permute-start.5 = (f32[3,72,128]{2,1,0:T(8,128)S(1)}, f32[3,72,128]{2,1,0:T(8,128)S(1)}, u32[]{:S(2)}, u32[]{:S(2)}) collective-permute-start(f32[3,72,128]{2,1,0:T(8,128)S(1)} %shard_map.96), channel_id=1, source_target_pairs={{1,0},{2,1},{3,2},{4,3},{5,4},{6,5},{7,6},{8,7},{9,8},{10,9},{11,1... | collective-permute-start | bytes 331784 | tf_op jit(solution)/shard_map/ppermute | solution.py:455
  33.1 0.0 collective-permute-start.4
  33.1 1.8 %collective-permute-start.2 = (f32[2,16,128]{2,1,0:T(8,128)S(1)}, f32[2,16,128]{2,1,0:T(8,128)S(1)}, u32[]{:S(2)}, u32[]{:S(2)}) collective-permute-start(f32[2,16,128]{2,1,0:T(8,128)S(1)} %get-tuple-element.33), channel_id=1, source_target_pairs={{0,32},{32,64},{64,96},{96,128},{128,160},{160,192},{192,224},{224... | collective-permute-start | bytes 49160 | tf_op jit(solution)/shard_map/ppermute | solution.py:455
  34.8 0.0 collective-permute-start.3
  34.8 4.9 %all-to-all-done = f32[256,1,256]{2,1,0:T(1,128)S(1)} async-done(((f32[256,1,256]{2,1,0:T(1,128)}), f32[256,1,256]{2,1,0:T(1,128)S(1)}, u32[]{:S(2)}, u32[]{:S(2)}) %all-to-all-start) | async-done | bytes 262176 | tf_op jit(solution)/shard_map/all_to_all | solution.py:467
  39.8 0.0 collective-permute-done.2.from_up
  39.8 0.0 collective-permute-done.3.from_down
  39.8 0.0 collective-permute-done.5.right_edge
  39.8 0.5 collective-permute-done.4.left_edge
  40.4 5.0 %shard_map.97 = (f32[6,24,128]{2,1,0:T(8,128)S(1)}, f32[2,6,24,128]{3,2,1,0:T(8,128)S(1)}, f32[2,24,128]{2,1,0:T(8,128)S(1)}, f32[2,24,128]{2,1,0:T(8,128)S(1)},...) custom-call(s32[2]{0:T(128)S(1)} %pad_add_fusion.info, ...), custom_call_target="tpu_custom_call" | custom-call | tf_op jit(solution)/shard_map/pallas_call | solution.py:481
  45.4 2.7 %collective-permute-start.6 = (f32[2,24,128]{2,1,0:T(8,128)S(1)}, f32[2,24,128]{2,1,0:T(8,128)S(1)}, u32[]{:S(2)}, u32[]{:S(2)}) collective-permute-start(f32[2,24,128]{2,1,0:T(8,128)S(1)} %get-tuple-element.38), channel_id=1, source_target_pairs={{0,32},{32,64},{64,96},{96,128},{128,160},{160,192},{192,224},{224... | collective-permute-start | bytes 73736 | tf_op jit(solution)/shard_map/ppermute | solution.py:455
  48.1 0.0 collective-permute-start.7
  48.1 1.7 %shard_map.99.sums0 = f32[256,128]{1,0:T(8,128)S(1)} custom-call(s32[2]{0:T(128)S(1)} %pad_add_fusion.info, f32[7,32,128]{2,1,0:T(8,128)S(1)} %select_maximum_fusion.frame, f32[2,32,128]{2,1,0:T(8,128)S(1)} %get-tuple-element.40.tcell, f32[2,32,128]{2,1,0:T(8,128)S(1)} %get-tuple-element.49.dcell, f32[6,32,128]{2,1,0:T(8,128)S(1)} %get-tuple-element.47.main_f, ...), custom_call_target="tpu_custom_call" | custom-call | flops 300000000 | bytes 1048576 | tf_op jit(solution)/shard_map/pallas_call | solution.py:494
  49.7 0.0 collective-permute-done.6.from_up
  49.7 1.6 %collective-permute-done.7.from_down = f32[2,24,128]{2,1,0:T(8,128)S(1)} collective-permute-done((f32[2,24,128]{2,1,0:T(8,128)S(1)}, f32[2,24,128]{2,1,0:T(8,128)S(1)}, u32[]{:S(2)}, u32[]{:S(2)}) %collective-permute-start.7) | collective-permute-done | bytes 24608 | tf_op jit(solution)/shard_map/ppermute | solution.py:455
  51.3 3.6 %shard_map.98 = (f32[6,32,128]{2,1,0:T(8,128)S(1)}, f32[6,32,128]{2,1,0:T(8,128)S(1)}, f32[6,24,128]{2,1,0:T(8,128)S(1)}, f32[2,6,24,128]{3,2,1,0:T(8,128)S(1)},...) custom-call(s32[2]{0:T(128)S(1)} %pad_add_fusion.info, f32[2,6,24,128]{3,2,1,0:T(8,128)S(1)} %get-tuple-element.37.local, ...), custom_call_target="tpu_custom_call" | custom-call | tf_op jit(solution)/shard_map/pallas_call | solution.py:498
  55.0 0.2 collective-permute-start.8
  55.2 0.3 collective-permute-start.9
  55.5 1.8 %shard_map.100.sums1 = f32[256,256]{1,0:T(8,128)S(1)} custom-call(s32[2]{0:T(128)S(1)} %pad_add_fusion.info, f32[7,32,128]{2,1,0:T(8,128)S(1)} %select_maximum_fusion.frame, f32[2,32,128]{2,1,0:T(8,128)S(1)} %get-tuple-element.40.tcell, f32[6,32,128]{2,1,0:T(8,128)S(1)} %get-tuple-element.47.main_f, f32[6,32,128]{2,1,0:T(8,128)S(1)} %get-tuple-element.48.side_f, ...), custom_call_target="tpu_custom_call" | custom-call | flops 500000000 | bytes 1048576 | tf_op jit(solution)/shard_map/pallas_call | solution.py:504
  57.3 0.0 collective-permute-done.8.from_up
  57.3 1.1 %collective-permute-done.9.from_down = f32[2,24,128]{2,1,0:T(8,128)S(1)} collective-permute-done((f32[2,24,128]{2,1,0:T(8,128)S(1)}, f32[2,24,128]{2,1,0:T(8,128)S(1)}, u32[]{:S(2)}, u32[]{:S(2)}) %collective-permute-start.9) | collective-permute-done | bytes 24608 | tf_op jit(solution)/shard_map/ppermute | solution.py:455
  58.4 2.0 %shard_map.101 = (f32[6,32,128]{2,1,0:T(8,128)S(1)}, f32[128,768]{1,0:T(8,128)S(1)}, f32[128,768]{1,0:T(8,128)S(1)}) custom-call(s32[2]{0:T(128)S(1)} %pad_add_fusion.info, f32[7,32,128]{2,1,0:T(8,128)S(1)} %select_maximum_fusion.frame, f32[6,24,128]{2,1,0:T(8,128)S(1)} %get-tuple-element.36.resid, f32[6,24,128]{2,1,0:T(8,128)S(1)} %get-tuple-element.42.image, ...), custom_call_target="tpu_custom_call" | custom-call | tf_op jit(solution)/shard_map/pallas_call | solution.py:508
  60.4 0.7 collective-permute-start.10
  61.1 1.3 %collective-permute-done.10 = f32[128,768]{1,0:T(8,128)S(1)} collective-permute-done((f32[128,768]{1,0:T(8,128)S(1)}, f32[128,768]{1,0:T(8,128)S(1)}, u32[]{:S(2)}, u32[]{:S(2)}) %collective-permute-start.10) | collective-permute-done | bytes 393248 | tf_op jit(solution)/shard_map/ppermute | solution.py:513
  62.5 0.4 copy.10
  62.9 24.1 %all_to_all.19 = f32[128,1,768]{2,1,0:T(1,128)S(1)} all-to-all(f32[128,1,768]{2,1,0:T(1,128)S(1)} %copy.10), channel_id=1, replica_groups=mesh['y'=4,'core'=2,'pcol'=32] {'y','pcol'}, dimensions={0} | all-to-all | bytes 786432 | tf_op jit(solution)/shard_map/all_to_all | solution.py:514
  87.0 0.8 shard_map.102
  (3 shorter events, 0.1 us)
Async XLA Ops:
  3.5 20.5 %collective-permute-start = (f32[8,128]{1,0:T(8,128)S(1)}, f32[8,128]{1,0:T(8,128)S(1)}, u32[]{:S(2)}, u32[]{:S(2)}) collective-permute-start(f32[8,128]{1,0:T(8,128)S(1)} %get-tuple-element.30), channel_id=1, source_target_pairs={{0,1},{1,2},{2,3},{3,4},{4,5},{5,6},{6,7},{7,8},{8,9},{9,10},{10,1... | collective-permute-start | bytes 12296 | tf_op jit(solution)/shard_map/ppermute | solution.py:455
  6.1 18.0 %collective-permute-start.1 = (f32[8,128]{1,0:T(8,128)S(1)}, f32[8,128]{1,0:T(8,128)S(1)}, u32[]{:S(2)}, u32[]{:S(2)}) collective-permute-start(f32[8,128]{1,0:T(8,128)S(1)} %get-tuple-element.31), channel_id=1, source_target_pairs={{1,0},{2,1},{3,2},{4,3},{5,4},{6,5},{7,6},{8,7},{9,8},{10,9},{11,1... | collective-permute-start | bytes 12296 | tf_op jit(solution)/shard_map/ppermute | solution.py:455
  13.8 26.0 %all-to-all-start = ((f32[256,1,256]{2,1,0:T(1,128)}), f32[256,1,256]{2,1,0:T(1,128)S(1)}, u32[]{:S(2)}, u32[]{:S(2)}) async-start(f32[256,1,256]{2,1,0:T(1,128)} %broadcast_in_dim.10), calls=%async_computation | async-start | bytes 524288 | tf_op jit(solution)/shard_map/all_to_all | solution.py:467
  24.0 1.8 %copy-start = (f32[72,72,128]{2,1,0:T(8,128)S(1)}, f32[72,72,128]{2,1,0:T(8,128)}, u32[]{:S(2)}) copy-start(f32[72,72,128]{2,1,0:T(8,128)} %mats.5) | copy-start | bytes 7962628
  26.5 13.3 %collective-permute-start.5 = (f32[3,72,128]{2,1,0:T(8,128)S(1)}, f32[3,72,128]{2,1,0:T(8,128)S(1)}, u32[]{:S(2)}, u32[]{:S(2)}) collective-permute-start(f32[3,72,128]{2,1,0:T(8,128)S(1)} %shard_map.96), channel_id=1, source_target_pairs={{1,0},{2,1},{3,2},{4,3},{5,4},{6,5},{7,6},{8,7},{9,8},{10,9},{11,1... | collective-permute-start | bytes 331784 | tf_op jit(solution)/shard_map/ppermute | solution.py:455
  33.1 7.3 %collective-permute-start.4 = (f32[3,72,128]{2,1,0:T(8,128)S(1)}, f32[3,72,128]{2,1,0:T(8,128)S(1)}, u32[]{:S(2)}, u32[]{:S(2)}) collective-permute-start(f32[3,72,128]{2,1,0:T(8,128)S(1)} %shard_map.96), channel_id=1, source_target_pairs={{0,1},{1,2},{2,3},{3,4},{4,5},{5,6},{6,7},{7,8},{8,9},{9,10},{10,1... | collective-permute-start | bytes 331784 | tf_op jit(solution)/shard_map/ppermute | solution.py:455
  33.1 6.7 %collective-permute-start.2 = (f32[2,16,128]{2,1,0:T(8,128)S(1)}, f32[2,16,128]{2,1,0:T(8,128)S(1)}, u32[]{:S(2)}, u32[]{:S(2)}) collective-permute-start(f32[2,16,128]{2,1,0:T(8,128)S(1)} %get-tuple-element.33), channel_id=1, source_target_pairs={{0,32},{32,64},{64,96},{96,128},{128,160},{160,192},{192,224},{224... | collective-permute-start | bytes 49160 | tf_op jit(solution)/shard_map/ppermute | solution.py:455
  34.8 4.9 %collective-permute-start.3 = (f32[2,16,128]{2,1,0:T(8,128)S(1)}, f32[2,16,128]{2,1,0:T(8,128)S(1)}, u32[]{:S(2)}, u32[]{:S(2)}) collective-permute-start(f32[2,16,128]{2,1,0:T(8,128)S(1)} %get-tuple-element.34), channel_id=1, source_target_pairs={{32,0},{64,32},{96,64},{128,96},{160,128},{192,160},{224,192},{0,2... | collective-permute-start | bytes 49160 | tf_op jit(solution)/shard_map/ppermute | solution.py:455
  45.4 4.3 %collective-permute-start.6 = (f32[2,24,128]{2,1,0:T(8,128)S(1)}, f32[2,24,128]{2,1,0:T(8,128)S(1)}, u32[]{:S(2)}, u32[]{:S(2)}) collective-permute-start(f32[2,24,128]{2,1,0:T(8,128)S(1)} %get-tuple-element.38), channel_id=1, source_target_pairs={{0,32},{32,64},{64,96},{96,128},{128,160},{160,192},{192,224},{224... | collective-permute-start | bytes 73736 | tf_op jit(solution)/shard_map/ppermute | solution.py:455
  48.1 3.3 %collective-permute-start.7 = (f32[2,24,128]{2,1,0:T(8,128)S(1)}, f32[2,24,128]{2,1,0:T(8,128)S(1)}, u32[]{:S(2)}, u32[]{:S(2)}) collective-permute-start(f32[2,24,128]{2,1,0:T(8,128)S(1)} %get-tuple-element.39), channel_id=1, source_target_pairs={{32,0},{64,32},{96,64},{128,96},{160,128},{192,160},{224,192},{0,2... | collective-permute-start | bytes 73736 | tf_op jit(solution)/shard_map/ppermute | solution.py:455
  55.0 2.3 %collective-permute-start.8 = (f32[2,24,128]{2,1,0:T(8,128)S(1)}, f32[2,24,128]{2,1,0:T(8,128)S(1)}, u32[]{:S(2)}, u32[]{:S(2)}) collective-permute-start(f32[2,24,128]{2,1,0:T(8,128)S(1)} %get-tuple-element.45), channel_id=1, source_target_pairs={{0,32},{32,64},{64,96},{96,128},{128,160},{160,192},{192,224},{224... | collective-permute-start | bytes 73736 | tf_op jit(solution)/shard_map/ppermute | solution.py:455
  55.2 3.3 %collective-permute-start.9 = (f32[2,24,128]{2,1,0:T(8,128)S(1)}, f32[2,24,128]{2,1,0:T(8,128)S(1)}, u32[]{:S(2)}, u32[]{:S(2)}) collective-permute-start(f32[2,24,128]{2,1,0:T(8,128)S(1)} %get-tuple-element.46), channel_id=1, source_target_pairs={{32,0},{64,32},{96,64},{128,96},{160,128},{192,160},{224,192},{0,2... | collective-permute-start | bytes 73736 | tf_op jit(solution)/shard_map/ppermute | solution.py:455
  60.4 2.0 %collective-permute-start.10 = (f32[128,768]{1,0:T(8,128)S(1)}, f32[128,768]{1,0:T(8,128)S(1)}, u32[]{:S(2)}, u32[]{:S(2)}) collective-permute-start(f32[128,768]{1,0:T(8,128)S(1)} %get-tuple-element.52), channel_id=1, source_target_pairs={{0,32},{32,0},{1,33},{33,1},{2,34},{34,2},{3,35},{35,3},{4,36},{36... | collective-permute-start | bytes 1179656 | tf_op jit(solution)/shard_map/ppermute | solution.py:513

commit v5 on v4

--- a/solution.py
+++ b/solution.py
@@ -202,12 +202,24 @@
         frame[...] = frame[...] * inside[None]
 
 
-def look_up(table, index, tcell, dcell):
-    flipped = table[...].T
+def owner_row(cells, n_col, prow):
+    owner = cells // DV
+    other = jnp.where((owner // n_col) % 2 == prow % 2, 0, 128)
+    return other + (owner // (2 * n_col)) * n_col + owner % n_col
+
+
+def look_up(table, index, n_col, prow, tcell, dcell):
+    half = table.shape[0]
+    parts = []
+    for k in range(2):
+        parts.append(table[:, 2 * DV * k:2 * DV * k + 2 * DV])
+        if half < 128:
+            parts.append(jnp.zeros((128 - half, 2 * DV), F32))
+    flipped = jnp.concatenate(parts, axis=0).T
     part0 = flipped.astype(BF16)
     part1 = (flipped - part0.astype(F32)).astype(BF16)
     lhs = jnp.concatenate([part0, part1], axis=0)
-    high = [ix // DV for ix in index]
+    high = [owner_row(ix, n_col, prow) for ix in index]
     low = [ix % DV for ix in index]
     lane1 = iota((1, CC), 1)
 
@@ -234,7 +246,7 @@
             vec = jnp.where(lane1 // 8 == i, pltpu.roll(index[1][r:r + 1], (8 * i + 4) % CC, 1), vec)
         packs.append(vec)
     vec = jnp.concatenate(packs, axis=1)
-    tv, dv = both(vec // DV, vec % DV)
+    tv, dv = both(owner_row(vec, n_col, prow), vec % DV)
     for half in range(2):
         for i in range(16):
             r = 16 * half + i
@@ -267,7 +279,7 @@
 
 
 def first_kernel(
-    last, info, table, frame, side, from_up, from_down, mats, left_edge, right_edge, levels,
+    last, n_col, info, table, frame, side, from_up, from_down, mats, left_edge, right_edge, levels,
     resid_out, local_out, up_out, down_out, main_f, side_f, tcell, dcell, edge,
     vec, total, side_vec, side_total, index_scr,
 ):
@@ -285,7 +297,7 @@
     index = [index_scr[tile].astype(jnp.int32) for tile in range(2)]
     tcell[...] = jnp.zeros_like(tcell)
     dcell[...] = jnp.zeros_like(dcell)
-    look_up(table, index, tcell, dcell)
+    look_up(table, index, n_col, prow, tcell, dcell)
     for tile in range(2):
         tcell[tile] = tcell[tile] * inside
     slope = [3.0 * tcell[tile] * tcell[tile] * dcell[tile] for tile in range(2)]
@@ -346,10 +358,8 @@
 
 def design_sums(n_col, info, frame, values, left_op, right_op):
     cells = frame[6, 8:8 + CR, :].astype(jnp.int32)
-    owner = cells // DV
     low = cells % DV
-    other = jnp.where((owner // n_col) % 2 == info[1] % 2, 0, 128)
-    high = other + (owner // (2 * n_col)) * n_col + owner % n_col
+    high = owner_row(cells, n_col, info[1])
     count = len(values)
     tops = [value.astype(BF16) for value in values]
     rests = [(value - top.astype(F32)).astype(BF16) for value, top in zip(values, tops)]
@@ -463,23 +473,25 @@
     rows = functools.partial(ring, ROW, n_row)
     cols = functools.partial(ring, "pcol", n_col)
 
-    own = jnp.concatenate([thickness, direction])
+    half = n_dev // 2
+    own = jnp.stack([thickness, direction])
+    own = jnp.concatenate([own, lax.ppermute(own, "core", [(0, 1), (1, 0)])]).reshape(1, 4 * DV)
     table = lax.all_to_all(
-        jnp.broadcast_to(own[None], (n_dev, 2 * DV)), ROW + ("pcol",), 0, 0, tiled=True
-    )
-    if n_dev < 256:
-        table = jnp.concatenate([table, jnp.zeros((256 - n_dev, 2 * DV), F32)], axis=0)
-    frame = jnp.concatenate([state, adjoint, design_map.astype(F32)[None]], axis=0)
-    frame = jnp.pad(frame, ((0, 0), (8, FR - 8 - CR), (0, 0)))
+        jnp.broadcast_to(own, (half, 4 * DV)), ("y", "pcol"), 0, 0, tiled=True
+    )
+    frame = sum(
+        jnp.pad(x, ((at, 7 - at - x.shape[0]), (8, FR - 8 - CR), (0, 0)))
+        for at, x in ((0, state), (3, adjoint), (6, design_map[None].astype(F32)))
+    )
     first, end = call(start_kernel, [(8, CC)] * 2, [SMEM, VMEM])(info, frame)
+    (edge,) = call(edge_kernel, [(3, BLK, CC)], [VMEM] * 2)(blocks, first)
     side, up, down, around = call(
         rows_kernel, [(7, FR, CC), (2, 16, CC), (2, 16, CC), (8, CC)], [VMEM] * 3, work=10**11
     )(frame, *cols(end, first))
 
-    (edge,) = call(edge_kernel, [(3, BLK, CC)], [VMEM] * 2)(blocks, around)
     solve_scratch = [pltpu.VMEM((2, BLK, CC), F32)] * 4
     resid, local, up, down, main_f, side_f, tcell, dcell, edge = call(
-        functools.partial(first_kernel, last),
+        functools.partial(first_kernel, last, n_col),
         [
             (6, EXT, CC), (2, 6, EXT, CC), (2, 24, CC), (2, 24, CC), (6, FR, CC), (6, FR, CC),
             (2, FR, CC), (2, FR, CC), (3, BLK, CC),
@@ -507,7 +519,7 @@
     )(info, frame, tcell, main_f, side_f, zframe, zside)
     wframe, keep, send = call(
         functools.partial(third_kernel, last, n_col),
-        [(6, FR, CC)] + [(n_dev // 2, 6 * CC)] * 2, [SMEM] + [VMEM] * 12,
+        [(6, FR, CC)] + [(half, 6 * CC)] * 2, [SMEM] + [VMEM] * 12,
         [pltpu.VMEM((6, FR, CC), F32)] + operands(2),
     )(info, frame, resid, image, zframe, local, *rows(down, up), tcell, main_f, side_f, sums0, sums1)
     sums = keep + lax.ppermute(send, "core", [(0, 1), (1, 0)])

time: 88.5 us -> 93 us (1.051)
  waiting for transfers between devices: 9.5 us -> 13.4 us
  Pallas kernels: 16.4 us -> 14.1 us
  blocking collectives: 24.1 us -> 25.7 us
  starting transfers between devices: 31.2 us -> 32.6 us
    all_to_all x1, waiting for transfers between devices: 4.91 us -> 10.7 us  [per_device(): lax.all_to_all(jnp.broadcast_to(own, (half, 4 * DV)), ('y', 'pcol'), 0, 0...]
    ppermute x0 -> x1, starting transfers between devices: none -> 3.24 us  [per_device(): lax.ppermute(own, 'core', [(0, 1), (1, 0)])]
    ppermute x5, starting transfers between devices: 13.1 us -> 10.4 us  [ring(): lax.ppermute(to_previous, axis, backward)]
    ppermute x5, starting transfers between devices: 7.18 us -> 5.06 us  [ring(): lax.ppermute(to_next, axis, forward)]
    ppermute x1, starting transfers between devices: 0.66 us -> 2.55 us  [per_device(): sums = keep + lax.ppermute(send, 'core', [(0, 1), (1, 0)])]
    all_to_all x1, blocking collectives: 24.1 us -> 25.7 us  [per_device(): got = lax.all_to_all(sums, ('y', 'pcol'), 0, 0, tiled=True)]
    concatenate x2 -> x0, other arithmetic: 1.48 us -> none  [the longest x1 0.8 us: per_device(): jnp.concatenate([state, adjoint, design_map.astype(F32)[None]], axis=0)]
    ppermute x5, waiting for transfers between devices: 2.69 us -> 1.36 us  [ring(): lax.ppermute(to_previous, axis, backward)]
  transfers between devices with their start and end apart: 12 -> 13, of which waited for: 5 -> 4; matrix products, arithmetic and copies ran while one was open for 2% -> 3% of each run, Pallas kernels for 5% -> 5%
where the time goes in v5:
time: 93 us; the launch traced here: 92.7 us
  starting transfers between devices  32.6 us (35%)
  blocking collectives  25.7 us (28%)
  Pallas kernels  14.1 us (15%)
  waiting for transfers between devices  13.4 us (14%)
  local copies, waits for them, and re-layouts  3.05 us (3%)
  other arithmetic  2.36 us (3%)
  between operations  1.48 us (2%)
    all_to_all x1, blocking collectives, per_device(): got = lax.all_to_all(sums, ('y', 'pcol'), 0, 0, tiled=True)  25.7 us
    all_to_all x1, starting transfers between devices, per_device(): lax.all_to_all(jnp.broadcast_to(own, (half, 4 * DV)), ('y', 'pcol'), 0, 0...  11.3 us
    all_to_all x1, waiting for transfers between devices, per_device(): lax.all_to_all(jnp.broadcast_to(own, (half, 4 * DV)), ('y', 'pcol'), 0, 0...  10.7 us
    ppermute x5, starting transfers between devices, ring(): lax.ppermute(to_previous, axis, backward)  10.4 us
    ppermute x5, starting transfers between devices, ring(): lax.ppermute(to_next, axis, forward)  5.06 us
    pallas_call x1, Pallas kernels, per_device(): call(functools.partial(first_kernel, last, n_col), [(6, EXT, CC), (2, 6,...  3.82 us
    ppermute x1, starting transfers between devices, per_device(): lax.ppermute(own, 'core', [(0, 1), (1, 0)])  3.24 us
    pallas_call x1, Pallas kernels, per_device(): call(functools.partial(second_kernel, last), [(6, FR, CC), (6, FR, CC), (...  2.62 us
  transfers between devices with their start and end apart: 13, of which 4 were waited for; matrix products, arithmetic and copies ran while one was open for 3% of the time, Pallas kernels for 5%

profile of v5, /device:TPU:1, one launch (start us, length us, event | category | flops | bytes accessed | tf_op | source)
XLA Modules:
  0.0 92.7 jit_solution(13582900860107969079)
XLA Ops:
  0.6 0.0 copy-start.2
  0.6 0.0 copy-start.3
  0.7 0.7 pad_maximum_fusion
  1.4 3.2 %collective-permute-start = (f32[2,128]{1,0:T(2,128)S(1)}, f32[2,128]{1,0:T(2,128)S(1)}, u32[]{:S(2)}, u32[]{:S(2)}) collective-permute-start(f32[2,128]{1,0:T(2,128)S(1)} %pad_maximum_fusion), channel_id=1, source_target_pairs={{0,32},{32,0},{1,33},{33,1},{2,34},{34,2},{3,35},{35,3},{4,36},{36... | collective-permute-start | bytes 3080 | tf_op jit(solution)/shard_map/ppermute | solution.py:478
  5.3 0.7 convert_bitcast_fusion
  6.0 0.8 pad_add_fusion.frame
  6.8 0.1 pad_add_fusion.1.info
  6.9 0.6 shard_map.94
  7.5 6.1 %collective-permute-start.2 = (f32[8,128]{1,0:T(8,128)S(1)}, f32[8,128]{1,0:T(8,128)S(1)}, u32[]{:S(2)}, u32[]{:S(2)}) collective-permute-start(f32[8,128]{1,0:T(8,128)S(1)} %get-tuple-element.31.after), channel_id=1, source_target_pairs={{1,0},{2,1},{3,2},{4,3},{5,4},{6,5},{7,6},{8,7},{9,8},{10,9},{11,1... | collective-permute-start | bytes 12296 | tf_op jit(solution)/shard_map/ppermute | solution.py:465
  13.6 1.7 %copy-done = f32[72,72,128]{2,1,0:T(8,128)S(1)} copy-done((f32[72,72,128]{2,1,0:T(8,128)S(1)}, f32[72,72,128]{2,1,0:T(8,128)}, u32[]{:S(2)}) %copy-start) | copy-done | bytes 2654232
  15.4 0.8 shard_map.96
  16.1 0.8 collective-permute-start.6
  16.9 0.7 collective-permute-start.5
  17.7 0.0 collective-permute-start.1
  17.7 0.0 collective-permute-done
  17.7 0.0 copy-done.2
  17.7 0.0 copy-done.3
  17.7 0.8 broadcast_in_dim.9
  18.6 11.3 %all-to-all-start = ((f32[128,1,512]{2,1,0:T(1,128)}), f32[128,1,512]{2,1,0:T(1,128)S(1)}, u32[]{:S(2)}, u32[]{:S(2)}) async-start(f32[128,1,512]{2,1,0:T(1,128)} %broadcast_in_dim.9), calls=%async_computation | async-start | bytes 524288 | tf_op jit(solution)/shard_map/all_to_all | solution.py:479
  29.9 0.0 copy-start.1
  29.9 0.0 collective-permute-done.1.from_left
  29.9 0.0 collective-permute-done.2.from_right
  29.9 0.1 shard_map.95
  30.1 2.3 %collective-permute-start.3 = (f32[2,16,128]{2,1,0:T(8,128)S(1)}, f32[2,16,128]{2,1,0:T(8,128)S(1)}, u32[]{:S(2)}, u32[]{:S(2)}) collective-permute-start(f32[2,16,128]{2,1,0:T(8,128)S(1)} %get-tuple-element.33), channel_id=1, source_target_pairs={{0,32},{32,64},{64,96},{96,128},{128,160},{160,192},{192,224},{224... | collective-permute-start | bytes 49160 | tf_op jit(solution)/shard_map/ppermute | solution.py:465
  32.3 0.0 collective-permute-start.4
  32.3 10.7 %all-to-all-done = f32[128,1,512]{2,1,0:T(1,128)S(1)} async-done(((f32[128,1,512]{2,1,0:T(1,128)}), f32[128,1,512]{2,1,0:T(1,128)S(1)}, u32[]{:S(2)}, u32[]{:S(2)}) %all-to-all-start) | async-done | bytes 262176 | tf_op jit(solution)/shard_map/all_to_all | solution.py:479
  43.0 0.0 collective-permute-done.3.from_up
  43.0 0.0 collective-permute-done.4.from_down
  43.0 0.0 collective-permute-done.6.right_edge
  43.0 0.0 collective-permute-done.5.left_edge
  43.0 3.8 %shard_map.97 = (f32[6,24,128]{2,1,0:T(8,128)S(1)}, f32[2,6,24,128]{3,2,1,0:T(8,128)S(1)}, f32[2,24,128]{2,1,0:T(8,128)S(1)}, f32[2,24,128]{2,1,0:T(8,128)S(1)},...) custom-call(s32[2]{0:T(128)S(1)} %pad_add_fusion.1.info, ...), custom_call_target="tpu_custom_call" | custom-call | tf_op jit(solution)/shard_map/pallas_call | solution.py:493
  46.9 1.8 %collective-permute-start.7 = (f32[2,24,128]{2,1,0:T(8,128)S(1)}, f32[2,24,128]{2,1,0:T(8,128)S(1)}, u32[]{:S(2)}, u32[]{:S(2)}) collective-permute-start(f32[2,24,128]{2,1,0:T(8,128)S(1)} %get-tuple-element.38), channel_id=1, source_target_pairs={{0,32},{32,64},{64,96},{96,128},{128,160},{160,192},{192,224},{224... | collective-permute-start | bytes 73736 | tf_op jit(solution)/shard_map/ppermute | solution.py:465
  48.7 1.2 %collective-permute-start.8 = (f32[2,24,128]{2,1,0:T(8,128)S(1)}, f32[2,24,128]{2,1,0:T(8,128)S(1)}, u32[]{:S(2)}, u32[]{:S(2)}) collective-permute-start(f32[2,24,128]{2,1,0:T(8,128)S(1)} %get-tuple-element.39), channel_id=1, source_target_pairs={{32,0},{64,32},{96,64},{128,96},{160,128},{192,160},{224,192},{0,2... | collective-permute-start | bytes 73736 | tf_op jit(solution)/shard_map/ppermute | solution.py:465
  49.9 1.7 %shard_map.99.sums0 = f32[256,128]{1,0:T(8,128)S(1)} custom-call(s32[2]{0:T(128)S(1)} %pad_add_fusion.1.info, f32[7,32,128]{2,1,0:T(8,128)S(1)} %pad_add_fusion.frame, f32[2,32,128]{2,1,0:T(8,128)S(1)} %get-tuple-element.40.tcell, f32[2,32,128]{2,1,0:T(8,128)S(1)} %get-tuple-element.49.dcell, f32[6,32,128]{2,1,0:T(8,128)S(1)} %get-tuple-element.47.main_f, ...), custom_call_target="tpu_custom_call" | custom-call | flops 300000000 | bytes 1048576 | tf_op jit(solution)/shard_map/pallas_call | solution.py:506
  51.5 0.0 collective-permute-done.7.from_up
  51.5 0.4 collective-permute-done.8.from_down
  52.0 2.6 %shard_map.98 = (f32[6,32,128]{2,1,0:T(8,128)S(1)}, f32[6,32,128]{2,1,0:T(8,128)S(1)}, f32[6,24,128]{2,1,0:T(8,128)S(1)}, f32[2,6,24,128]{3,2,1,0:T(8,128)S(1)},...) custom-call(s32[2]{0:T(128)S(1)} %pad_add_fusion.1.info, f32[2,6,24,128]{3,2,1,0:T(8,128)S(1)} %get-tuple-element.37.local, ...), custom_call_target="tpu_custom_call" | custom-call | tf_op jit(solution)/shard_map/pallas_call | solution.py:510
  54.6 0.2 collective-permute-start.9
  54.8 2.4 %collective-permute-start.10 = (f32[2,24,128]{2,1,0:T(8,128)S(1)}, f32[2,24,128]{2,1,0:T(8,128)S(1)}, u32[]{:S(2)}, u32[]{:S(2)}) collective-permute-start(f32[2,24,128]{2,1,0:T(8,128)S(1)} %get-tuple-element.46), channel_id=1, source_target_pairs={{32,0},{64,32},{96,64},{128,96},{160,128},{192,160},{224,192},{0,2... | collective-permute-start | bytes 73736 | tf_op jit(solution)/shard_map/ppermute | solution.py:465
  57.1 1.8 %shard_map.100.sums1 = f32[256,256]{1,0:T(8,128)S(1)} custom-call(s32[2]{0:T(128)S(1)} %pad_add_fusion.1.info, f32[7,32,128]{2,1,0:T(8,128)S(1)} %pad_add_fusion.frame, f32[2,32,128]{2,1,0:T(8,128)S(1)} %get-tuple-element.40.tcell, f32[6,32,128]{2,1,0:T(8,128)S(1)} %get-tuple-element.47.main_f, f32[6,32,128]{2,1,0:T(8,128)S(1)} %get-tuple-element.48.side_f, ...), custom_call_target="tpu_custom_call" | custom-call | flops 500000000 | bytes 1048576 | tf_op jit(solution)/shard_map/pallas_call | solution.py:516
  58.9 0.0 collective-permute-done.9.from_up
  59.0 0.9 %collective-permute-done.10.from_down = f32[2,24,128]{2,1,0:T(8,128)S(1)} collective-permute-done((f32[2,24,128]{2,1,0:T(8,128)S(1)}, f32[2,24,128]{2,1,0:T(8,128)S(1)}, u32[]{:S(2)}, u32[]{:S(2)}) %collective-permute-start.10) | collective-permute-done | bytes 24608 | tf_op jit(solution)/shard_map/ppermute | solution.py:465
  59.9 2.0 %shard_map.101 = (f32[6,32,128]{2,1,0:T(8,128)S(1)}, f32[128,768]{1,0:T(8,128)S(1)}, f32[128,768]{1,0:T(8,128)S(1)}) custom-call(s32[2]{0:T(128)S(1)} %pad_add_fusion.1.info, f32[7,32,128]{2,1,0:T(8,128)S(1)} %pad_add_fusion.frame, f32[6,24,128]{2,1,0:T(8,128)S(1)} %get-tuple-element.36.resid, f32[6,24,128]{2,1,0:T(8,128)S(1)} %get-tuple-element.42.image, ...), custom_call_target="tpu_custom_call" | custom-call | tf_op jit(solution)/shard_map/pallas_call | solution.py:520
  61.9 2.5 %collective-permute-start.11 = (f32[128,768]{1,0:T(8,128)S(1)}, f32[128,768]{1,0:T(8,128)S(1)}, u32[]{:S(2)}, u32[]{:S(2)}) collective-permute-start(f32[128,768]{1,0:T(8,128)S(1)} %get-tuple-element.52), channel_id=1, source_target_pairs={{0,32},{32,0},{1,33},{33,1},{2,34},{34,2},{3,35},{35,3},{4,36},{36... | collective-permute-start | bytes 1179656 | tf_op jit(solution)/shard_map/ppermute | solution.py:525
  64.4 1.3 %collective-permute-done.11 = f32[128,768]{1,0:T(8,128)S(1)} collective-permute-done((f32[128,768]{1,0:T(8,128)S(1)}, f32[128,768]{1,0:T(8,128)S(1)}, u32[]{:S(2)}, u32[]{:S(2)}) %collective-permute-start.11) | collective-permute-done | bytes 393248 | tf_op jit(solution)/shard_map/ppermute | solution.py:525
  65.8 0.4 copy.10
  66.2 25.7 %all_to_all.19 = f32[128,1,768]{2,1,0:T(1,128)S(1)} all-to-all(f32[128,1,768]{2,1,0:T(1,128)S(1)} %copy.10), channel_id=1, replica_groups=mesh['y'=4,'core'=2,'pcol'=32] {'y','pcol'}, dimensions={0} | all-to-all | bytes 786432 | tf_op jit(solution)/shard_map/all_to_all | solution.py:526
  92.0 0.8 shard_map.102
  (6 shorter events, 0.1 us)
Async XLA Ops:
  0.6 17.1 %copy-start.2 = (f32[128]{0:T(128)S(1)}, f32[128]{0:T(128)}, u32[]{:S(2)}) copy-start(f32[128]{0:T(128)} %param.10) | copy-start | bytes 1540
  0.6 17.1 %copy-start.3 = (f32[128]{0:T(128)S(1)}, f32[128]{0:T(128)}, u32[]{:S(2)}) copy-start(f32[128]{0:T(128)} %param.9) | copy-start | bytes 1540
  1.4 16.3 %collective-permute-start = (f32[2,128]{1,0:T(2,128)S(1)}, f32[2,128]{1,0:T(2,128)S(1)}, u32[]{:S(2)}, u32[]{:S(2)}) collective-permute-start(f32[2,128]{1,0:T(2,128)S(1)} %pad_maximum_fusion), channel_id=1, source_target_pairs={{0,32},{32,0},{1,33},{33,1},{2,34},{34,2},{3,35},{35,3},{4,36},{36... | collective-permute-start | bytes 3080 | tf_op jit(solution)/shard_map/ppermute | solution.py:478
  7.5 22.4 %collective-permute-start.2 = (f32[8,128]{1,0:T(8,128)S(1)}, f32[8,128]{1,0:T(8,128)S(1)}, u32[]{:S(2)}, u32[]{:S(2)}) collective-permute-start(f32[8,128]{1,0:T(8,128)S(1)} %get-tuple-element.31.after), channel_id=1, source_target_pairs={{1,0},{2,1},{3,2},{4,3},{5,4},{6,5},{7,6},{8,7},{9,8},{10,9},{11,1... | collective-permute-start | bytes 12296 | tf_op jit(solution)/shard_map/ppermute | solution.py:465
  13.6 1.7 %copy-start = (f32[72,72,128]{2,1,0:T(8,128)S(1)}, f32[72,72,128]{2,1,0:T(8,128)}, u32[]{:S(2)}) copy-start(f32[72,72,128]{2,1,0:T(8,128)} %mats.5) | copy-start | bytes 7962628
  16.1 26.9 %collective-permute-start.6 = (f32[3,72,128]{2,1,0:T(8,128)S(1)}, f32[3,72,128]{2,1,0:T(8,128)S(1)}, u32[]{:S(2)}, u32[]{:S(2)}) collective-permute-start(f32[3,72,128]{2,1,0:T(8,128)S(1)} %shard_map.96), channel_id=1, source_target_pairs={{1,0},{2,1},{3,2},{4,3},{5,4},{6,5},{7,6},{8,7},{9,8},{10,9},{11,1... | collective-permute-start | bytes 331784 | tf_op jit(solution)/shard_map/ppermute | solution.py:465
  16.9 26.1 %collective-permute-start.5 = (f32[3,72,128]{2,1,0:T(8,128)S(1)}, f32[3,72,128]{2,1,0:T(8,128)S(1)}, u32[]{:S(2)}, u32[]{:S(2)}) collective-permute-start(f32[3,72,128]{2,1,0:T(8,128)S(1)} %shard_map.96), channel_id=1, source_target_pairs={{0,1},{1,2},{2,3},{3,4},{4,5},{5,6},{6,7},{7,8},{8,9},{9,10},{10,1... | collective-permute-start | bytes 331784 | tf_op jit(solution)/shard_map/ppermute | solution.py:465
  17.7 12.2 %collective-permute-start.1 = (f32[8,128]{1,0:T(8,128)S(1)}, f32[8,128]{1,0:T(8,128)S(1)}, u32[]{:S(2)}, u32[]{:S(2)}) collective-permute-start(f32[8,128]{1,0:T(8,128)S(1)} %get-tuple-element.30), channel_id=1, source_target_pairs={{0,1},{1,2},{2,3},{3,4},{4,5},{5,6},{6,7},{7,8},{8,9},{9,10},{10,1... | collective-permute-start | bytes 12296 | tf_op jit(solution)/shard_map/ppermute | solution.py:465
  18.6 24.4 %all-to-all-start = ((f32[128,1,512]{2,1,0:T(1,128)}), f32[128,1,512]{2,1,0:T(1,128)S(1)}, u32[]{:S(2)}, u32[]{:S(2)}) async-start(f32[128,1,512]{2,1,0:T(1,128)} %broadcast_in_dim.9), calls=%async_computation | async-start | bytes 524288 | tf_op jit(solution)/shard_map/all_to_all | solution.py:479
  29.9 13.1 %copy-start.1 = (f32[72,72,128]{2,1,0:T(8,128)S(1)}, f32[72,72,128]{2,1,0:T(8,128)}, u32[]{:S(2)}) copy-start(f32[72,72,128]{2,1,0:T(8,128)} %mats.5) | copy-start | bytes 7962628
  30.1 12.9 %collective-permute-start.3 = (f32[2,16,128]{2,1,0:T(8,128)S(1)}, f32[2,16,128]{2,1,0:T(8,128)S(1)}, u32[]{:S(2)}, u32[]{:S(2)}) collective-permute-start(f32[2,16,128]{2,1,0:T(8,128)S(1)} %get-tuple-element.33), channel_id=1, source_target_pairs={{0,32},{32,64},{64,96},{96,128},{128,160},{160,192},{192,224},{224... | collective-permute-start | bytes 49160 | tf_op jit(solution)/shard_map/ppermute | solution.py:465
  32.3 10.7 %collective-permute-start.4 = (f32[2,16,128]{2,1,0:T(8,128)S(1)}, f32[2,16,128]{2,1,0:T(8,128)S(1)}, u32[]{:S(2)}, u32[]{:S(2)}) collective-permute-start(f32[2,16,128]{2,1,0:T(8,128)S(1)} %get-tuple-element.34), channel_id=1, source_target_pairs={{32,0},{64,32},{96,64},{128,96},{160,128},{192,160},{224,192},{0,2... | collective-permute-start | bytes 49160 | tf_op jit(solution)/shard_map/ppermute | solution.py:465
  46.9 4.7 %collective-permute-start.7 = (f32[2,24,128]{2,1,0:T(8,128)S(1)}, f32[2,24,128]{2,1,0:T(8,128)S(1)}, u32[]{:S(2)}, u32[]{:S(2)}) collective-permute-start(f32[2,24,128]{2,1,0:T(8,128)S(1)} %get-tuple-element.38), channel_id=1, source_target_pairs={{0,32},{32,64},{64,96},{96,128},{128,160},{160,192},{192,224},{224... | collective-permute-start | bytes 73736 | tf_op jit(solution)/shard_map/ppermute | solution.py:465
  48.7 3.3 %collective-permute-start.8 = (f32[2,24,128]{2,1,0:T(8,128)S(1)}, f32[2,24,128]{2,1,0:T(8,128)S(1)}, u32[]{:S(2)}, u32[]{:S(2)}) collective-permute-start(f32[2,24,128]{2,1,0:T(8,128)S(1)} %get-tuple-element.39), channel_id=1, source_target_pairs={{32,0},{64,32},{96,64},{128,96},{160,128},{192,160},{224,192},{0,2... | collective-permute-start | bytes 73736 | tf_op jit(solution)/shard_map/ppermute | solution.py:465
  54.6 4.4 %collective-permute-start.9 = (f32[2,24,128]{2,1,0:T(8,128)S(1)}, f32[2,24,128]{2,1,0:T(8,128)S(1)}, u32[]{:S(2)}, u32[]{:S(2)}) collective-permute-start(f32[2,24,128]{2,1,0:T(8,128)S(1)} %get-tuple-element.45), channel_id=1, source_target_pairs={{0,32},{32,64},{64,96},{96,128},{128,160},{160,192},{192,224},{224... | collective-permute-start | bytes 73736 | tf_op jit(solution)/shard_map/ppermute | solution.py:465
  54.8 5.1 %collective-permute-start.10 = (f32[2,24,128]{2,1,0:T(8,128)S(1)}, f32[2,24,128]{2,1,0:T(8,128)S(1)}, u32[]{:S(2)}, u32[]{:S(2)}) collective-permute-start(f32[2,24,128]{2,1,0:T(8,128)S(1)} %get-tuple-element.46), channel_id=1, source_target_pairs={{32,0},{64,32},{96,64},{128,96},{160,128},{192,160},{224,192},{0,2... | collective-permute-start | bytes 73736 | tf_op jit(solution)/shard_map/ppermute | solution.py:465
  61.9 3.9 %collective-permute-start.11 = (f32[128,768]{1,0:T(8,128)S(1)}, f32[128,768]{1,0:T(8,128)S(1)}, u32[]{:S(2)}, u32[]{:S(2)}) collective-permute-start(f32[128,768]{1,0:T(8,128)S(1)} %get-tuple-element.52), channel_id=1, source_target_pairs={{0,32},{32,0},{1,33},{33,1},{2,34},{34,2},{3,35},{35,3},{4,36},{36... | collective-permute-start | bytes 1179656 | tf_op jit(solution)/shard_map/ppermute | solution.py:525

commit v6 on v4

--- a/solution.py
+++ b/solution.py
@@ -21,9 +21,12 @@
 
 VMEM = pl.BlockSpec(memory_space=pltpu.VMEM)
 SMEM = pl.BlockSpec(memory_space=pltpu.SMEM)
-
-
-def call(kernel, out_shapes, in_specs, scratch=(), work=None):
+HBM = pl.BlockSpec(memory_space=pltpu.HBM)
+SMALL = 20 * 1024 * 1024
+LARGE = 62 * 1024 * 1024
+
+
+def call(kernel, out_shapes, in_specs, scratch=(), work=None, limit=SMALL):
     cost = None
     if work is not None:
         cost = pl.CostEstimate(flops=work, bytes_accessed=1 << 20, transcendentals=0)
@@ -34,7 +37,7 @@
         out_specs=[VMEM] * len(out_shapes),
         cost_estimate=cost,
         scratch_shapes=list(scratch),
-        compiler_params=pltpu.CompilerParams(vmem_limit_bytes=20 * 1024 * 1024),
+        compiler_params=pltpu.CompilerParams(vmem_limit_bytes=limit),
     )
 
 
@@ -88,11 +91,30 @@
     return jnp.where(outside, 0.0, 1.0).astype(F32)
 
 
-def start_kernel(info, frame, first_out, last_out):
-    tiles = [frame[f, 8 + 8 * g:16 + 8 * g, :] for f in range(7) for g in range(3)]
-    first, last = pack_edges(tiles, WIDE)
+def start_kernel(
+    info, thickness, direction, state, adjoint, dmap, own_out, frame_out, first_out, last_out,
+    known, cells, own, sems,
+):
+    copies = [
+        pltpu.make_async_copy(thickness, own.at[0], sems.at[0]),
+        pltpu.make_async_copy(direction, own.at[1], sems.at[1]),
+        pltpu.make_async_copy(state, known.at[0:3], sems.at[2]),
+        pltpu.make_async_copy(adjoint, known.at[3:6], sems.at[3]),
+        pltpu.make_async_copy(dmap, cells, sems.at[4]),
+    ]
+    for copy in copies:
+        copy.start()
+    frame_out[...] = jnp.zeros_like(frame_out)
     upper = iota((8, CC), 1) >= 64
     level = info[0].astype(F32)
+    for copy in copies:
+        copy.wait()
+    for k in range(2):
+        own_out[:, :, k * DV:(k + 1) * DV] = jnp.broadcast_to(own[k][None], (own_out.shape[0], 1, DV))
+    frame_out[0:6, 8:8 + CR, :] = known[...]
+    frame_out[6, 8:8 + CR, :] = cells[...].astype(F32)
+    tiles = [frame_out[f, 8 + 8 * g:16 + 8 * g, :] for f in range(7) for g in range(3)]
+    first, last = pack_edges(tiles, WIDE)
     first_out[...] = jnp.where(upper, level, first)
     last_out[...] = jnp.where(upper, level, last)
 
@@ -463,20 +485,23 @@
     rows = functools.partial(ring, ROW, n_row)
     cols = functools.partial(ring, "pcol", n_col)
 
-    own = jnp.concatenate([thickness, direction])
-    table = lax.all_to_all(
-        jnp.broadcast_to(own[None], (n_dev, 2 * DV)), ROW + ("pcol",), 0, 0, tiled=True
-    )
+    own, frame, first, end = call(
+        start_kernel, [(n_dev, 1, 2 * DV), (7, FR, CC), (8, CC), (8, CC)], [SMEM] + [HBM] * 5,
+        [
+            pltpu.VMEM((6, CR, CC), F32), pltpu.VMEM((CR, CC), jnp.int32),
+            pltpu.VMEM((2, 1, DV), F32), pltpu.SemaphoreType.DMA((5,)),
+        ],
+        work=10**9, limit=LARGE,
+    )(info, thickness.reshape(1, DV), direction.reshape(1, DV), state, adjoint, design_map)
+    table = lax.all_to_all(own, ROW + ("pcol",), 0, 0, tiled=True).reshape(n_dev, 2 * DV)
     if n_dev < 256:
         table = jnp.concatenate([table, jnp.zeros((256 - n_dev, 2 * DV), F32)], axis=0)
-    frame = jnp.concatenate([state, adjoint, design_map.astype(F32)[None]], axis=0)
-    frame = jnp.pad(frame, ((0, 0), (8, FR - 8 - CR), (0, 0)))
-    first, end = call(start_kernel, [(8, CC)] * 2, [SMEM, VMEM])(info, frame)
+    from_left, from_right = cols(end, first)
+    (edge,) = call(edge_kernel, [(3, BLK, CC)], [VMEM] * 2)(blocks, from_left)
     side, up, down, around = call(
         rows_kernel, [(7, FR, CC), (2, 16, CC), (2, 16, CC), (8, CC)], [VMEM] * 3, work=10**11
-    )(frame, *cols(end, first))
-
-    (edge,) = call(edge_kernel, [(3, BLK, CC)], [VMEM] * 2)(blocks, around)
+    )(frame, from_left, from_right)
+
     solve_scratch = [pltpu.VMEM((2, BLK, CC), F32)] * 4
     resid, local, up, down, main_f, side_f, tcell, dcell, edge = call(
         functools.partial(first_kernel, last),

time: 88.5 us -> 88.6 us (level)
  starting transfers between devices: 31.2 us -> 33.4 us
  other arithmetic: 2.3 us -> 0.69 us
    pallas_call x2, Pallas kernels: 1.37 us -> 3.09 us  [the longest x1 2.36 us: per_device(): call(start_kernel, [(n_dev, 1, 2 * DV), (7, FR, CC), (8, CC), (8, CC)], [...]
    concatenate x2 -> x0, other arithmetic: 1.48 us -> none  [the longest x1 0.8 us: per_device(): jnp.concatenate([state, adjoint, design_map.astype(F32)[None]], axis=0)]
    ppermute x5, starting transfers between devices: 7.18 us -> 8.42 us  [ring(): lax.ppermute(to_next, axis, forward)]
    ppermute x1, starting transfers between devices: 0.66 us -> 1.89 us  [per_device(): sums = keep + lax.ppermute(send, 'core', [(0, 1), (1, 0)])]
    unnamed x4 -> x10, local copies, waits for them, and re-layouts: 1.64 us -> 1.8 us
  transfers between devices with their start and end apart: 12 -> 12, of which waited for: 5 -> 5; matrix products, arithmetic and copies ran while one was open for 2% -> 0% of each run, Pallas kernels for 5% -> 5%
where the time goes in v6:
time: 88.6 us; the launch traced here: 88.4 us
  starting transfers between devices  33.4 us (38%)
  blocking collectives  24 us (27%)
  Pallas kernels  17 us (19%)
  waiting for transfers between devices  9.55 us (11%)
  local copies, waits for them, and re-layouts  2.21 us (2%)
  between operations  1.46 us (2%)
    all_to_all x1, blocking collectives, per_device(): got = lax.all_to_all(sums, ('y', 'pcol'), 0, 0, tiled=True)  24 us
    ppermute x5, starting transfers between devices, ring(): lax.ppermute(to_previous, axis, backward)  12.9 us
    all_to_all x1, starting transfers between devices, per_device(): lax.all_to_all(own, ROW + ('pcol',), 0, 0, tiled=True)  10.2 us
    ppermute x5, starting transfers between devices, ring(): lax.ppermute(to_next, axis, forward)  8.42 us
    all_to_all x1, waiting for transfers between devices, per_device(): lax.all_to_all(own, ROW + ('pcol',), 0, 0, tiled=True)  4.73 us
    pallas_call x1, Pallas kernels, per_device(): call(functools.partial(first_kernel, last), [(6, EXT, CC), (2, 6, EXT, CC...  4.5 us
    pallas_call x1, Pallas kernels, per_device(): call(functools.partial(second_kernel, last), [(6, FR, CC), (6, FR, CC), (...  3.1 us
    ppermute x5, waiting for transfers between devices, ring(): lax.ppermute(to_previous, axis, backward)  2.91 us
  transfers between devices with their start and end apart: 12, of which 5 were waited for; matrix products, arithmetic and copies ran while one was open for 0% of the time, Pallas kernels for 5%

profile of v6, /device:TPU:1, one launch (start us, length us, event | category | flops | bytes accessed | tf_op | source)
XLA Modules:
  0.0 88.4 jit_solution(2781104840121800463)
XLA Ops:
  1.3 0.6 pad_add_fusion.info
  1.9 2.4 %shard_map.94 = (f32[256,1,256]{2,1,0:T(1,128)}, f32[7,32,128]{2,1,0:T(8,128)}, f32[8,128]{1,0:T(8,128)}, f32[8,128]{1,0:T(8,128)}) custom-call(s32[2]{0:T(128)} %pad_add_fusion.info, f32[1,128]{1,0:T(1,128)} %bitcast.16, f32[1,128]{1,0:T(1,128)} %bitcast.17, f32[3,22,128]{2,1,0:T(8,128)} %state.1, f32[3,22,128]{2,1,0:T(8,128)} %adjoint.1, s32[22,128]{1,0:T(8,128)} %dmap.1), custom_call_target="tpu_custom_call" | custom-call | flops 1000000000 | bytes 1048576 | tf_op jit(solution)/shard_map/pallas_call | solution.py:488
  4.3 0.0 copy-start.2
  4.3 2.5 %collective-permute-start = (f32[8,128]{1,0:T(8,128)}, f32[8,128]{1,0:T(8,128)S(1)}, u32[]{:S(2)}, u32[]{:S(2)}) collective-permute-start(f32[8,128]{1,0:T(8,128)} %get-tuple-element.34), channel_id=1, source_target_pairs={{0,1},{1,2},{2,3},{3,4},{4,5},{5,6},{6,7},{7,8},{8,9},{9,10},{10,1... | collective-permute-start | bytes 12296 | tf_op jit(solution)/shard_map/ppermute | solution.py:477
  6.9 6.2 %collective-permute-start.1 = (f32[8,128]{1,0:T(8,128)}, f32[8,128]{1,0:T(8,128)S(1)}, u32[]{:S(2)}, u32[]{:S(2)}) collective-permute-start(f32[8,128]{1,0:T(8,128)} %get-tuple-element.35), channel_id=1, source_target_pairs={{1,0},{2,1},{3,2},{4,3},{5,4},{6,5},{7,6},{8,7},{9,8},{10,9},{11,1... | collective-permute-start | bytes 12296 | tf_op jit(solution)/shard_map/ppermute | solution.py:477
  13.1 10.2 %all-to-all-start = ((f32[256,1,256]{2,1,0:T(1,128)}), f32[256,1,256]{2,1,0:T(1,128)S(1)}, u32[]{:S(2)}, u32[]{:S(2)}) async-start(f32[256,1,256]{2,1,0:T(1,128)} %get-tuple-element.33), calls=%async_computation | async-start | bytes 524288 | tf_op jit(solution)/shard_map/all_to_all | solution.py:496
  23.3 0.0 collective-permute-done.from_left.after
  23.3 0.0 copy-start
  23.3 1.7 %copy-done = f32[72,72,128]{2,1,0:T(8,128)S(1)} copy-done((f32[72,72,128]{2,1,0:T(8,128)S(1)}, f32[72,72,128]{2,1,0:T(8,128)}, u32[]{:S(2)}) %copy-start) | copy-done | bytes 2654232
  25.1 0.7 shard_map.96
  25.8 6.6 %collective-permute-start.5 = (f32[3,72,128]{2,1,0:T(8,128)S(1)}, f32[3,72,128]{2,1,0:T(8,128)S(1)}, u32[]{:S(2)}, u32[]{:S(2)}) collective-permute-start(f32[3,72,128]{2,1,0:T(8,128)S(1)} %shard_map.96), channel_id=1, source_target_pairs={{1,0},{2,1},{3,2},{4,3},{5,4},{6,5},{7,6},{8,7},{9,8},{10,9},{11,1... | collective-permute-start | bytes 331784 | tf_op jit(solution)/shard_map/ppermute | solution.py:477
  32.4 0.0 collective-permute-start.4
  32.4 0.0 collective-permute-done.1.from_right
  32.4 0.0 copy-done.2
  32.4 0.0 copy-start.1
  32.4 0.0 copy-start.3
  32.4 0.1 shard_map.95
  32.5 1.8 %collective-permute-start.2 = (f32[2,16,128]{2,1,0:T(8,128)S(1)}, f32[2,16,128]{2,1,0:T(8,128)S(1)}, u32[]{:S(2)}, u32[]{:S(2)}) collective-permute-start(f32[2,16,128]{2,1,0:T(8,128)S(1)} %get-tuple-element.37), channel_id=1, source_target_pairs={{0,32},{32,64},{64,96},{96,128},{128,160},{160,192},{192,224},{224... | collective-permute-start | bytes 49160 | tf_op jit(solution)/shard_map/ppermute | solution.py:477
  34.3 0.0 collective-permute-start.3
  34.3 4.7 %all-to-all-done = f32[256,1,256]{2,1,0:T(1,128)S(1)} async-done(((f32[256,1,256]{2,1,0:T(1,128)}), f32[256,1,256]{2,1,0:T(1,128)S(1)}, u32[]{:S(2)}, u32[]{:S(2)}) %all-to-all-start) | async-done | bytes 262176 | tf_op jit(solution)/shard_map/all_to_all | solution.py:496
  39.1 0.0 collective-permute-done.2.from_up
  39.1 0.0 collective-permute-done.3.from_down
  39.1 0.0 collective-permute-done.5.right_edge
  39.1 0.5 collective-permute-done.4.left_edge
  39.6 0.0 copy-done.1
  39.7 0.0 copy-done.3
  39.7 4.5 %shard_map.97 = (f32[6,24,128]{2,1,0:T(8,128)S(1)}, f32[2,6,24,128]{3,2,1,0:T(8,128)S(1)}, f32[2,24,128]{2,1,0:T(8,128)S(1)}, f32[2,24,128]{2,1,0:T(8,128)S(1)},...) custom-call(s32[2]{0:T(128)S(1)} %copy-done.3, ...), custom_call_target="tpu_custom_call" | custom-call | tf_op jit(solution)/shard_map/pallas_call | solution.py:506
  44.2 3.3 %collective-permute-start.6 = (f32[2,24,128]{2,1,0:T(8,128)S(1)}, f32[2,24,128]{2,1,0:T(8,128)S(1)}, u32[]{:S(2)}, u32[]{:S(2)}) collective-permute-start(f32[2,24,128]{2,1,0:T(8,128)S(1)} %get-tuple-element.42), channel_id=1, source_target_pairs={{0,32},{32,64},{64,96},{96,128},{128,160},{160,192},{192,224},{224... | collective-permute-start | bytes 73736 | tf_op jit(solution)/shard_map/ppermute | solution.py:477
  47.4 0.0 collective-permute-start.7
  47.4 1.6 %shard_map.99.sums0 = f32[256,128]{1,0:T(8,128)S(1)} custom-call(s32[2]{0:T(128)S(1)} %copy-done.3, f32[7,32,128]{2,1,0:T(8,128)S(1)} %copy-done.2, f32[2,32,128]{2,1,0:T(8,128)S(1)} %get-tuple-element.44.tcell, f32[2,32,128]{2,1,0:T(8,128)S(1)} %get-tuple-element.53.dcell, f32[6,32,128]{2,1,0:T(8,128)S(1)} %get-tuple-element.51.main_f, ...), custom_call_target="tpu_custom_call" | custom-call | flops 300000000 | bytes 1048576 | tf_op jit(solution)/shard_map/pallas_call | solution.py:519
  49.1 0.0 collective-permute-done.6.from_up
  49.1 1.6 %collective-permute-done.7.from_down = f32[2,24,128]{2,1,0:T(8,128)S(1)} collective-permute-done((f32[2,24,128]{2,1,0:T(8,128)S(1)}, f32[2,24,128]{2,1,0:T(8,128)S(1)}, u32[]{:S(2)}, u32[]{:S(2)}) %collective-permute-start.7) | collective-permute-done | bytes 24608 | tf_op jit(solution)/shard_map/ppermute | solution.py:477
  50.7 3.1 %shard_map.98 = (f32[6,32,128]{2,1,0:T(8,128)S(1)}, f32[6,32,128]{2,1,0:T(8,128)S(1)}, f32[6,24,128]{2,1,0:T(8,128)S(1)}, f32[2,6,24,128]{3,2,1,0:T(8,128)S(1)},...) custom-call(s32[2]{0:T(128)S(1)} %copy-done.3, f32[2,6,24,128]{3,2,1,0:T(8,128)S(1)} %get-tuple-element.41.local, ...), custom_call_target="tpu_custom_call" | custom-call | tf_op jit(solution)/shard_map/pallas_call | solution.py:523
  53.8 0.8 collective-permute-start.8
  54.6 0.1 collective-permute-start.9
  54.7 1.8 %shard_map.100.sums1 = f32[256,256]{1,0:T(8,128)S(1)} custom-call(s32[2]{0:T(128)S(1)} %copy-done.3, f32[7,32,128]{2,1,0:T(8,128)S(1)} %copy-done.2, f32[2,32,128]{2,1,0:T(8,128)S(1)} %get-tuple-element.44.tcell, f32[6,32,128]{2,1,0:T(8,128)S(1)} %get-tuple-element.51.main_f, f32[6,32,128]{2,1,0:T(8,128)S(1)} %get-tuple-element.52.side_f, ...), custom_call_target="tpu_custom_call" | custom-call | flops 500000000 | bytes 1048576 | tf_op jit(solution)/shard_map/pallas_call | solution.py:529
  56.5 0.0 collective-permute-done.8.from_up
  56.5 1.3 %collective-permute-done.9.from_down = f32[2,24,128]{2,1,0:T(8,128)S(1)} collective-permute-done((f32[2,24,128]{2,1,0:T(8,128)S(1)}, f32[2,24,128]{2,1,0:T(8,128)S(1)}, u32[]{:S(2)}, u32[]{:S(2)}) %collective-permute-start.9) | collective-permute-done | bytes 24608 | tf_op jit(solution)/shard_map/ppermute | solution.py:477
  57.9 2.0 %shard_map.101 = (f32[6,32,128]{2,1,0:T(8,128)S(1)}, f32[128,768]{1,0:T(8,128)S(1)}, f32[128,768]{1,0:T(8,128)S(1)}) custom-call(s32[2]{0:T(128)S(1)} %copy-done.3, f32[7,32,128]{2,1,0:T(8,128)S(1)} %copy-done.2, f32[6,24,128]{2,1,0:T(8,128)S(1)} %get-tuple-element.40.resid, f32[6,24,128]{2,1,0:T(8,128)S(1)} %get-tuple-element.46.image, ...), custom_call_target="tpu_custom_call" | custom-call | tf_op jit(solution)/shard_map/pallas_call | solution.py:533
  59.8 1.9 %collective-permute-start.10 = (f32[128,768]{1,0:T(8,128)S(1)}, f32[128,768]{1,0:T(8,128)S(1)}, u32[]{:S(2)}, u32[]{:S(2)}) collective-permute-start(f32[128,768]{1,0:T(8,128)S(1)} %get-tuple-element.56), channel_id=1, source_target_pairs={{0,32},{32,0},{1,33},{33,1},{2,34},{34,2},{3,35},{35,3},{4,36},{36... | collective-permute-start | bytes 1179656 | tf_op jit(solution)/shard_map/ppermute | solution.py:538
  61.7 1.3 %collective-permute-done.10 = f32[128,768]{1,0:T(8,128)S(1)} collective-permute-done((f32[128,768]{1,0:T(8,128)S(1)}, f32[128,768]{1,0:T(8,128)S(1)}, u32[]{:S(2)}, u32[]{:S(2)}) %collective-permute-start.10) | collective-permute-done | bytes 393248 | tf_op jit(solution)/shard_map/ppermute | solution.py:538
  63.1 0.4 copy.11
  63.5 24.0 %all_to_all.16 = f32[128,1,768]{2,1,0:T(1,128)S(1)} all-to-all(f32[128,1,768]{2,1,0:T(1,128)S(1)} %copy.11), channel_id=1, replica_groups=mesh['y'=4,'core'=2,'pcol'=32] {'y','pcol'}, dimensions={0} | all-to-all | bytes 786432 | tf_op jit(solution)/shard_map/all_to_all | solution.py:539
  87.6 0.8 shard_map.102
  (3 shorter events, 0.1 us)
Async XLA Ops:
  4.3 28.1 %copy-start.2 = (f32[7,32,128]{2,1,0:T(8,128)S(1)}, f32[7,32,128]{2,1,0:T(8,128)}, u32[]{:S(2)}) copy-start(f32[7,32,128]{2,1,0:T(8,128)} %get-tuple-element.32.frame) | copy-start | bytes 344068
  4.3 19.0 %collective-permute-start = (f32[8,128]{1,0:T(8,128)}, f32[8,128]{1,0:T(8,128)S(1)}, u32[]{:S(2)}, u32[]{:S(2)}) collective-permute-start(f32[8,128]{1,0:T(8,128)} %get-tuple-element.34), channel_id=1, source_target_pairs={{0,1},{1,2},{2,3},{3,4},{4,5},{5,6},{6,7},{7,8},{8,9},{9,10},{10,1... | collective-permute-start | bytes 12296 | tf_op jit(solution)/shard_map/ppermute | solution.py:477
  6.9 25.5 %collective-permute-start.1 = (f32[8,128]{1,0:T(8,128)}, f32[8,128]{1,0:T(8,128)S(1)}, u32[]{:S(2)}, u32[]{:S(2)}) collective-permute-start(f32[8,128]{1,0:T(8,128)} %get-tuple-element.35), channel_id=1, source_target_pairs={{1,0},{2,1},{3,2},{4,3},{5,4},{6,5},{7,6},{8,7},{9,8},{10,9},{11,1... | collective-permute-start | bytes 12296 | tf_op jit(solution)/shard_map/ppermute | solution.py:477
  13.1 26.0 %all-to-all-start = ((f32[256,1,256]{2,1,0:T(1,128)}), f32[256,1,256]{2,1,0:T(1,128)S(1)}, u32[]{:S(2)}, u32[]{:S(2)}) async-start(f32[256,1,256]{2,1,0:T(1,128)} %get-tuple-element.33), calls=%async_computation | async-start | bytes 524288 | tf_op jit(solution)/shard_map/all_to_all | solution.py:496
  23.3 1.8 %copy-start = (f32[72,72,128]{2,1,0:T(8,128)S(1)}, f32[72,72,128]{2,1,0:T(8,128)}, u32[]{:S(2)}) copy-start(f32[72,72,128]{2,1,0:T(8,128)} %mats.5) | copy-start | bytes 7962628
  25.8 13.3 %collective-permute-start.5 = (f32[3,72,128]{2,1,0:T(8,128)S(1)}, f32[3,72,128]{2,1,0:T(8,128)S(1)}, u32[]{:S(2)}, u32[]{:S(2)}) collective-permute-start(f32[3,72,128]{2,1,0:T(8,128)S(1)} %shard_map.96), channel_id=1, source_target_pairs={{1,0},{2,1},{3,2},{4,3},{5,4},{6,5},{7,6},{8,7},{9,8},{10,9},{11,1... | collective-permute-start | bytes 331784 | tf_op jit(solution)/shard_map/ppermute | solution.py:477
  32.4 7.3 %collective-permute-start.4 = (f32[3,72,128]{2,1,0:T(8,128)S(1)}, f32[3,72,128]{2,1,0:T(8,128)S(1)}, u32[]{:S(2)}, u32[]{:S(2)}) collective-permute-start(f32[3,72,128]{2,1,0:T(8,128)S(1)} %shard_map.96), channel_id=1, source_target_pairs={{0,1},{1,2},{2,3},{3,4},{4,5},{5,6},{6,7},{7,8},{8,9},{9,10},{10,1... | collective-permute-start | bytes 331784 | tf_op jit(solution)/shard_map/ppermute | solution.py:477
  32.4 7.3 %copy-start.1 = (f32[72,72,128]{2,1,0:T(8,128)S(1)}, f32[72,72,128]{2,1,0:T(8,128)}, u32[]{:S(2)}) copy-start(f32[72,72,128]{2,1,0:T(8,128)} %mats.5) | copy-start | bytes 7962628
  32.4 7.3 %copy-start.3 = (s32[2]{0:T(128)S(1)}, s32[2]{0:T(128)}, u32[]{:S(2)}) copy-start(s32[2]{0:T(128)} %pad_add_fusion.info) | copy-start | bytes 28
  32.5 6.5 %collective-permute-start.2 = (f32[2,16,128]{2,1,0:T(8,128)S(1)}, f32[2,16,128]{2,1,0:T(8,128)S(1)}, u32[]{:S(2)}, u32[]{:S(2)}) collective-permute-start(f32[2,16,128]{2,1,0:T(8,128)S(1)} %get-tuple-element.37), channel_id=1, source_target_pairs={{0,32},{32,64},{64,96},{96,128},{128,160},{160,192},{192,224},{224... | collective-permute-start | bytes 49160 | tf_op jit(solution)/shard_map/ppermute | solution.py:477
  34.3 4.8 %collective-permute-start.3 = (f32[2,16,128]{2,1,0:T(8,128)S(1)}, f32[2,16,128]{2,1,0:T(8,128)S(1)}, u32[]{:S(2)}, u32[]{:S(2)}) collective-permute-start(f32[2,16,128]{2,1,0:T(8,128)S(1)} %get-tuple-element.38), channel_id=1, source_target_pairs={{32,0},{64,32},{96,64},{128,96},{160,128},{192,160},{224,192},{0,2... | collective-permute-start | bytes 49160 | tf_op jit(solution)/shard_map/ppermute | solution.py:477
  44.2 4.9 %collective-permute-start.6 = (f32[2,24,128]{2,1,0:T(8,128)S(1)}, f32[2,24,128]{2,1,0:T(8,128)S(1)}, u32[]{:S(2)}, u32[]{:S(2)}) collective-permute-start(f32[2,24,128]{2,1,0:T(8,128)S(1)} %get-tuple-element.42), channel_id=1, source_target_pairs={{0,32},{32,64},{64,96},{96,128},{128,160},{160,192},{192,224},{224... | collective-permute-start | bytes 73736 | tf_op jit(solution)/shard_map/ppermute | solution.py:477
  47.4 3.3 %collective-permute-start.7 = (f32[2,24,128]{2,1,0:T(8,128)S(1)}, f32[2,24,128]{2,1,0:T(8,128)S(1)}, u32[]{:S(2)}, u32[]{:S(2)}) collective-permute-start(f32[2,24,128]{2,1,0:T(8,128)S(1)} %get-tuple-element.43), channel_id=1, source_target_pairs={{32,0},{64,32},{96,64},{128,96},{160,128},{192,160},{224,192},{0,2... | collective-permute-start | bytes 73736 | tf_op jit(solution)/shard_map/ppermute | solution.py:477
  53.8 2.7 %collective-permute-start.8 = (f32[2,24,128]{2,1,0:T(8,128)S(1)}, f32[2,24,128]{2,1,0:T(8,128)S(1)}, u32[]{:S(2)}, u32[]{:S(2)}) collective-permute-start(f32[2,24,128]{2,1,0:T(8,128)S(1)} %get-tuple-element.49), channel_id=1, source_target_pairs={{0,32},{32,64},{64,96},{96,128},{128,160},{160,192},{192,224},{224... | collective-permute-start | bytes 73736 | tf_op jit(solution)/shard_map/ppermute | solution.py:477
  54.6 3.3 %collective-permute-start.9 = (f32[2,24,128]{2,1,0:T(8,128)S(1)}, f32[2,24,128]{2,1,0:T(8,128)S(1)}, u32[]{:S(2)}, u32[]{:S(2)}) collective-permute-start(f32[2,24,128]{2,1,0:T(8,128)S(1)} %get-tuple-element.50), channel_id=1, source_target_pairs={{32,0},{64,32},{96,64},{128,96},{160,128},{192,160},{224,192},{0,2... | collective-permute-start | bytes 73736 | tf_op jit(solution)/shard_map/ppermute | solution.py:477
  59.8 3.2 %collective-permute-start.10 = (f32[128,768]{1,0:T(8,128)S(1)}, f32[128,768]{1,0:T(8,128)S(1)}, u32[]{:S(2)}, u32[]{:S(2)}) collective-permute-start(f32[128,768]{1,0:T(8,128)S(1)} %get-tuple-element.56), channel_id=1, source_target_pairs={{0,32},{32,0},{1,33},{33,1},{2,34},{34,2},{3,35},{35,3},{4,36},{36... | collective-permute-start | bytes 1179656 | tf_op jit(solution)/shard_map/ppermute | solution.py:538

commit v7 on v6

--- a/solution.py
+++ b/solution.py
@@ -91,9 +91,14 @@
     return jnp.where(outside, 0.0, 1.0).astype(F32)
 
 
+PIECE = 24
+EDGE = 3 * BLK
+
+
 def start_kernel(
-    info, thickness, direction, state, adjoint, dmap, own_out, frame_out, first_out, last_out,
-    known, cells, own, sems,
+    levels, thickness, direction, state, adjoint, dmap, blocks,
+    own_out, frame_out, first_out, last_out,
+    level, known, cells, own, mats, sems, block_sems,
 ):
     copies = [
         pltpu.make_async_copy(thickness, own.at[0], sems.at[0]),
@@ -101,12 +106,16 @@
         pltpu.make_async_copy(state, known.at[0:3], sems.at[2]),
         pltpu.make_async_copy(adjoint, known.at[3:6], sems.at[3]),
         pltpu.make_async_copy(dmap, cells, sems.at[4]),
+        pltpu.make_async_copy(levels, level, sems.at[5]),
     ]
-    for copy in copies:
+    pieces = []
+    for k in range(BLK // PIECE):
+        cut = pl.ds(k * PIECE, PIECE)
+        pieces.append(pltpu.make_async_copy(blocks.at[cut], mats.at[cut], block_sems.at[k]))
+    for copy in copies + pieces:
         copy.start()
     frame_out[...] = jnp.zeros_like(frame_out)
     upper = iota((8, CC), 1) >= 64
-    level = info[0].astype(F32)
     for copy in copies:
         copy.wait()
     for k in range(2):
@@ -115,26 +124,28 @@
     frame_out[6, 8:8 + CR, :] = cells[...].astype(F32)
     tiles = [frame_out[f, 8 + 8 * g:16 + 8 * g, :] for f in range(7) for g in range(3)]
     first, last = pack_edges(tiles, WIDE)
-    first_out[...] = jnp.where(upper, level, first)
-    last_out[...] = jnp.where(upper, level, last)
-
-
-def edge_kernel(mats, after, edge_out):
+    depth = jnp.broadcast_to(level[...].astype(F32), (8, CC))
+    first_out[EDGE:, :] = jnp.where(upper, depth, first)
+    last_out[EDGE:, :] = jnp.where(upper, depth, last)
     lane = iota((BLK, CC), 1)
     for c in range(3):
         packed = jnp.zeros((BLK, CC), F32)
         for i in range(min(32, BLK - 32 * c)):
             at = 32 * c + i
+            if at % PIECE == 0:
+                pieces[at // PIECE].wait()
             mat = mats[at]
             here = ((lane - 4 * i + 2) & (CC - 1)) < 4
             packed = jnp.where(here, pltpu.roll(mat, 4 * i, 1) if i else mat, packed)
-        edge_out[c] = packed
+        first_out[c * BLK:(c + 1) * BLK, :] = packed
+        last_out[c * BLK:(c + 1) * BLK, :] = packed
 
 
 def rows_kernel(
-    frame, from_left, from_right, side_out, up_out, down_out, levels_out,
+    frame, from_left, from_right, side_out, up_out, down_out, levels_out, edge_out,
 ):
-    tiles = unpack_edges(from_left[...], from_right[...], 21, WIDE)
+    left_end, right_end = from_left[EDGE:, :], from_right[EDGE:, :]
+    tiles = unpack_edges(left_end, right_end, 21, WIDE)
     side_out[...] = jnp.zeros_like(side_out)
     for f in range(7):
         for g in range(3):
@@ -146,7 +157,11 @@
             up_out[tile, 2 * f:2 * f + 2, :] = ref[f, 8:10, :]
             down_out[tile, 2 * f:2 * f + 2, :] = ref[f, 6 + CR:8 + CR, :]
     upper = iota((8, CC), 1) >= 64
-    levels_out[...] = jnp.where(upper, from_left[...], pltpu.roll(from_right[...], 64, 1))
+    levels_out[...] = jnp.where(upper, left_end, pltpu.roll(right_end, 64, 1))
+    lane = iota((BLK, CC), 1)
+    for c in range(3):
+        cut = slice(c * BLK, (c + 1) * BLK)
+        edge_out[c] = jnp.where(lane % 4 < 2, from_right[cut, :], pltpu.roll(from_left[cut, :], 4, 1))
 
 
 def apply_blocks(mats, vec):
@@ -289,13 +304,10 @@
 
 
 def first_kernel(
-    last, info, table, frame, side, from_up, from_down, mats, left_edge, right_edge, levels,
-    resid_out, local_out, up_out, down_out, main_f, side_f, tcell, dcell, edge,
+    last, info, table, frame, side, from_up, from_down, mats, edge, levels,
+    resid_out, local_out, up_out, down_out, main_f, side_f, tcell, dcell,
     vec, total, side_vec, side_total, index_scr,
 ):
-    lane = iota((BLK, CC), 1)
-    for c in range(3):
-        edge[c] = jnp.where(lane % 4 < 2, right_edge[c], pltpu.roll(left_edge[c], 4, 1))
     level, prow = info[0], info[1]
     inside = grid_mask(prow, last, 0, FR)
     for tile, ref, source in ((0, main_f, frame), (1, side_f, side)):
@@ -486,32 +498,34 @@
     cols = functools.partial(ring, "pcol", n_col)
 
     own, frame, first, end = call(
-        start_kernel, [(n_dev, 1, 2 * DV), (7, FR, CC), (8, CC), (8, CC)], [SMEM] + [HBM] * 5,
+        start_kernel, [(n_dev, 1, 2 * DV), (7, FR, CC), (EDGE + 8, CC), (EDGE + 8, CC)], [HBM] * 7,
         [
-            pltpu.VMEM((6, CR, CC), F32), pltpu.VMEM((CR, CC), jnp.int32),
-            pltpu.VMEM((2, 1, DV), F32), pltpu.SemaphoreType.DMA((5,)),
+            pltpu.VMEM((1, 1), jnp.int32), pltpu.VMEM((6, CR, CC), F32),
+            pltpu.VMEM((CR, CC), jnp.int32), pltpu.VMEM((2, 1, DV), F32),
+            pltpu.VMEM((BLK, BLK, CC), F32), pltpu.SemaphoreType.DMA((6,)),
+            pltpu.SemaphoreType.DMA((BLK // PIECE,)),
         ],
         work=10**9, limit=LARGE,
-    )(info, thickness.reshape(1, DV), direction.reshape(1, DV), state, adjoint, design_map)
+    )(levels, thickness.reshape(1, DV), direction.reshape(1, DV), state, adjoint, design_map, blocks)
     table = lax.all_to_all(own, ROW + ("pcol",), 0, 0, tiled=True).reshape(n_dev, 2 * DV)
     if n_dev < 256:
         table = jnp.concatenate([table, jnp.zeros((256 - n_dev, 2 * DV), F32)], axis=0)
     from_left, from_right = cols(end, first)
-    (edge,) = call(edge_kernel, [(3, BLK, CC)], [VMEM] * 2)(blocks, from_left)
-    side, up, down, around = call(
-        rows_kernel, [(7, FR, CC), (2, 16, CC), (2, 16, CC), (8, CC)], [VMEM] * 3, work=10**11
+    side, up, down, around, edge = call(
+        rows_kernel, [(7, FR, CC), (2, 16, CC), (2, 16, CC), (8, CC), (3, BLK, CC)], [VMEM] * 3,
+        work=10**11,
     )(frame, from_left, from_right)
 
     solve_scratch = [pltpu.VMEM((2, BLK, CC), F32)] * 4
-    resid, local, up, down, main_f, side_f, tcell, dcell, edge = call(
+    resid, local, up, down, main_f, side_f, tcell, dcell = call(
         functools.partial(first_kernel, last),
         [
             (6, EXT, CC), (2, 6, EXT, CC), (2, 24, CC), (2, 24, CC), (6, FR, CC), (6, FR, CC),
-            (2, FR, CC), (2, FR, CC), (3, BLK, CC),
+            (2, FR, CC), (2, FR, CC),
         ],
-        [SMEM] + [VMEM] * 9,
+        [SMEM] + [VMEM] * 8,
         solve_scratch + [pltpu.VMEM((2, FR, CC), F32)],
-    )(info, table, frame, side, *rows(down, up), blocks, *cols(edge, edge), around)
+    )(info, table, frame, side, *rows(down, up), blocks, edge, around)
 
     def operands(count):
         return [pltpu.VMEM((256, CR * CC), BF16), pltpu.VMEM((2 * count * DV, CR * CC), BF16)]

time: 88.6 us -> 86.8 us (0.980)
  starting transfers between devices: 33.4 us -> 24.1 us
  waiting for transfers between devices: 9.55 us -> 16.5 us
  blocking collectives: 24 us -> 25.1 us
  Pallas kernels: 17 us -> 18 us
    all_to_all x1, waiting for transfers between devices: 4.73 us -> 12.4 us  [per_device(): lax.all_to_all(own, ROW + ('pcol',), 0, 0, tiled=True)]
    ppermute x5 -> x4, starting transfers between devices: 12.9 us -> 7.1 us  [ring(): lax.ppermute(to_previous, axis, backward)]
    ppermute x5 -> x4, starting transfers between devices: 8.42 us -> 5.01 us  [ring(): lax.ppermute(to_next, axis, forward)]
    all_to_all x1, blocking collectives: 24 us -> 25.1 us  [per_device(): got = lax.all_to_all(sums, ('y', 'pcol'), 0, 0, tiled=True)]
    unnamed x10 -> x8, local copies, waits for them, and re-layouts: 1.8 us -> 0.94 us
    ppermute x5 -> x4, waiting for transfers between devices: 2.91 us -> 2.69 us  [ring(): lax.ppermute(to_previous, axis, backward)]
    pallas_call x3 -> x2, Pallas kernels: 3.21 us -> 3.04 us  [the longest x1 2.89 us: per_device(): call(start_kernel, [(n_dev, 1, 2 * DV), (7, FR, CC), (EDGE + 8, CC), (EDG...]
  transfers between devices with their start and end apart: 12 -> 10, of which waited for: 5 -> 4; matrix products, arithmetic and copies ran while one was open for 0% -> 0% of each run, Pallas kernels for 5% -> 4%
where the time goes in v7:
time: 86.8 us; the launch traced here: 86.6 us
  blocking collectives  25.1 us (29%)
  starting transfers between devices  24.1 us (28%)
  Pallas kernels  18 us (21%)
  waiting for transfers between devices  16.5 us (19%)
  between operations  1.44 us (2%)
  local copies, waits for them, and re-layouts  1.35 us (2%)
    all_to_all x1, blocking collectives, per_device(): got = lax.all_to_all(sums, ('y', 'pcol'), 0, 0, tiled=True)  25.1 us
    all_to_all x1, waiting for transfers between devices, per_device(): lax.all_to_all(own, ROW + ('pcol',), 0, 0, tiled=True)  12.4 us
    all_to_all x1, starting transfers between devices, per_device(): lax.all_to_all(own, ROW + ('pcol',), 0, 0, tiled=True)  10.2 us
    ppermute x4, starting transfers between devices, ring(): lax.ppermute(to_previous, axis, backward)  7.1 us
    pallas_call x1, Pallas kernels, per_device(): call(functools.partial(first_kernel, last), [(6, EXT, CC), (2, 6, EXT, CC...  5.08 us
    ppermute x4, starting transfers between devices, ring(): lax.ppermute(to_next, axis, forward)  5.01 us
    pallas_call x1, Pallas kernels, per_device(): call(functools.partial(second_kernel, last), [(6, FR, CC), (6, FR, CC), (...  3.72 us
    pallas_call x1, Pallas kernels, per_device(): call(start_kernel, [(n_dev, 1, 2 * DV), (7, FR, CC), (EDGE + 8, CC), (EDG...  2.89 us
  transfers between devices with their start and end apart: 10, of which 4 were waited for; matrix products, arithmetic and copies ran while one was open for 0% of the time, Pallas kernels for 4%

profile of v7, /device:TPU:1, one launch (start us, length us, event | category | flops | bytes accessed | tf_op | source)
XLA Modules:
  0.0 86.6 jit_solution(7799555971725418743)
XLA Ops:
  1.3 2.9 %shard_map.94 = (f32[256,1,256]{2,1,0:T(1,128)}, f32[7,32,128]{2,1,0:T(8,128)}, f32[224,128]{1,0:T(8,128)}, f32[224,128]{1,0:T(8,128)}) custom-call(s32[1,1]{1,0:T(1,128)} %copy.18.levels, f32[1,128]{1,0:T(1,128)} %bitcast.16, f32[1,128]{1,0:T(1,128)} %bitcast.17, f32[3,22,128]{2,1,0:T(8,128)} %state.1, f32[3,22,128]{2,1,0:T(8,128)} %adjoint.1, ...), custom_call_target="tpu_custom_call" | custom-call | flops 1000000000 | bytes 1048576 | tf_op jit(solution)/shard_map/pallas_call | solution.py:500
  4.2 2.5 %collective-permute-start = (f32[224,128]{1,0:T(8,128)}, f32[224,128]{1,0:T(8,128)S(1)}, u32[]{:S(2)}, u32[]{:S(2)}) collective-permute-start(f32[224,128]{1,0:T(8,128)} %get-tuple-element.34), channel_id=1, source_target_pairs={{0,1},{1,2},{2,3},{3,4},{4,5},{5,6},{6,7},{7,8},{8,9},{9,10},{10,1... | collective-permute-start | bytes 344072 | tf_op jit(solution)/shard_map/ppermute | solution.py:489
  6.7 6.2 %collective-permute-start.1 = (f32[224,128]{1,0:T(8,128)}, f32[224,128]{1,0:T(8,128)S(1)}, u32[]{:S(2)}, u32[]{:S(2)}) collective-permute-start(f32[224,128]{1,0:T(8,128)} %get-tuple-element.35), channel_id=1, source_target_pairs={{1,0},{2,1},{3,2},{4,3},{5,4},{6,5},{7,6},{8,7},{9,8},{10,9},{11,1... | collective-permute-start | bytes 344072 | tf_op jit(solution)/shard_map/ppermute | solution.py:489
  12.9 10.2 %all-to-all-start = ((f32[256,1,256]{2,1,0:T(1,128)}), f32[256,1,256]{2,1,0:T(1,128)S(1)}, u32[]{:S(2)}, u32[]{:S(2)}) async-start(f32[256,1,256]{2,1,0:T(1,128)} %get-tuple-element.33), calls=%async_computation | async-start | bytes 524288 | tf_op jit(solution)/shard_map/all_to_all | solution.py:510
  23.2 0.0 collective-permute-done.from_left
  23.2 0.0 collective-permute-done.1.from_right
  23.2 0.0 copy-start.1
  23.2 0.9 %copy-done.1 = f32[7,32,128]{2,1,0:T(8,128)S(1)} copy-done((f32[7,32,128]{2,1,0:T(8,128)S(1)}, f32[7,32,128]{2,1,0:T(8,128)}, u32[]{:S(2)}) %copy-start.1) | copy-done | bytes 114712
  24.1 0.0 copy-start
  24.1 0.0 copy-start.2
  24.1 0.1 shard_map.95
  24.2 1.6 %collective-permute-start.2 = (f32[2,16,128]{2,1,0:T(8,128)S(1)}, f32[2,16,128]{2,1,0:T(8,128)S(1)}, u32[]{:S(2)}, u32[]{:S(2)}) collective-permute-start(f32[2,16,128]{2,1,0:T(8,128)S(1)} %get-tuple-element.37), channel_id=1, source_target_pairs={{0,32},{32,64},{64,96},{96,128},{128,160},{160,192},{192,224},{224... | collective-permute-start | bytes 49160 | tf_op jit(solution)/shard_map/ppermute | solution.py:489
  25.9 0.5 collective-permute-start.3
  26.4 0.1 pad_add_fusion.info
  26.5 12.4 %all-to-all-done = f32[256,1,256]{2,1,0:T(1,128)S(1)} async-done(((f32[256,1,256]{2,1,0:T(1,128)}), f32[256,1,256]{2,1,0:T(1,128)S(1)}, u32[]{:S(2)}, u32[]{:S(2)}) %all-to-all-start) | async-done | bytes 262176 | tf_op jit(solution)/shard_map/all_to_all | solution.py:510
  38.9 0.0 collective-permute-done.2.from_up
  38.9 0.0 collective-permute-done.3.from_down
  39.0 0.0 copy-done
  39.0 0.0 copy-done.2
  39.0 5.1 %shard_map.96 = (f32[6,24,128]{2,1,0:T(8,128)S(1)}, f32[2,6,24,128]{3,2,1,0:T(8,128)S(1)}, f32[2,24,128]{2,1,0:T(8,128)S(1)}, f32[2,24,128]{2,1,0:T(8,128)S(1)},...) custom-call(s32[2]{0:T(128)S(1)} %pad_add_fusion.info, ...), custom_call_target="tpu_custom_call" | custom-call | tf_op jit(solution)/shard_map/pallas_call | solution.py:520
  44.1 0.6 collective-permute-start.4
  44.7 0.0 collective-permute-start.5
  44.7 1.6 %shard_map.98.sums0 = f32[256,128]{1,0:T(8,128)S(1)} custom-call(s32[2]{0:T(128)S(1)} %pad_add_fusion.info, f32[7,32,128]{2,1,0:T(8,128)S(1)} %copy-done.2, f32[2,32,128]{2,1,0:T(8,128)S(1)} %get-tuple-element.45.tcell, f32[2,32,128]{2,1,0:T(8,128)S(1)} %get-tuple-element.53.dcell, f32[6,32,128]{2,1,0:T(8,128)S(1)} %get-tuple-element.51.main_f, ...), custom_call_target="tpu_custom_call" | custom-call | flops 300000000 | bytes 1048576 | tf_op jit(solution)/shard_map/pallas_call | solution.py:533
  46.4 0.0 collective-permute-done.4.from_up
  46.4 1.6 %collective-permute-done.5.from_down = f32[2,24,128]{2,1,0:T(8,128)S(1)} collective-permute-done((f32[2,24,128]{2,1,0:T(8,128)S(1)}, f32[2,24,128]{2,1,0:T(8,128)S(1)}, u32[]{:S(2)}, u32[]{:S(2)}) %collective-permute-start.5) | collective-permute-done | bytes 24608 | tf_op jit(solution)/shard_map/ppermute | solution.py:489
  47.9 3.7 %shard_map.97 = (f32[6,32,128]{2,1,0:T(8,128)S(1)}, f32[6,32,128]{2,1,0:T(8,128)S(1)}, f32[6,24,128]{2,1,0:T(8,128)S(1)}, f32[2,6,24,128]{3,2,1,0:T(8,128)S(1)},...) custom-call(s32[2]{0:T(128)S(1)} %pad_add_fusion.info, f32[2,6,24,128]{3,2,1,0:T(8,128)S(1)} %get-tuple-element.42.local, ...), custom_call_target="tpu_custom_call" | custom-call | tf_op jit(solution)/shard_map/pallas_call | solution.py:537
  51.7 0.2 collective-permute-start.6
  51.9 0.3 collective-permute-start.7
  52.2 1.8 %shard_map.99.sums1 = f32[256,256]{1,0:T(8,128)S(1)} custom-call(s32[2]{0:T(128)S(1)} %pad_add_fusion.info, f32[7,32,128]{2,1,0:T(8,128)S(1)} %copy-done.2, f32[2,32,128]{2,1,0:T(8,128)S(1)} %get-tuple-element.45.tcell, f32[6,32,128]{2,1,0:T(8,128)S(1)} %get-tuple-element.51.main_f, f32[6,32,128]{2,1,0:T(8,128)S(1)} %get-tuple-element.52.side_f, ...), custom_call_target="tpu_custom_call" | custom-call | flops 500000000 | bytes 1048576 | tf_op jit(solution)/shard_map/pallas_call | solution.py:543
  54.0 0.0 collective-permute-done.6.from_up
  54.0 1.1 %collective-permute-done.7.from_down = f32[2,24,128]{2,1,0:T(8,128)S(1)} collective-permute-done((f32[2,24,128]{2,1,0:T(8,128)S(1)}, f32[2,24,128]{2,1,0:T(8,128)S(1)}, u32[]{:S(2)}, u32[]{:S(2)}) %collective-permute-start.7) | collective-permute-done | bytes 24608 | tf_op jit(solution)/shard_map/ppermute | solution.py:489
  55.1 2.0 %shard_map.100 = (f32[6,32,128]{2,1,0:T(8,128)S(1)}, f32[128,768]{1,0:T(8,128)S(1)}, f32[128,768]{1,0:T(8,128)S(1)}) custom-call(s32[2]{0:T(128)S(1)} %pad_add_fusion.info, f32[7,32,128]{2,1,0:T(8,128)S(1)} %copy-done.2, f32[6,24,128]{2,1,0:T(8,128)S(1)} %get-tuple-element.41.resid, f32[6,24,128]{2,1,0:T(8,128)S(1)} %get-tuple-element.46.image, ...), custom_call_target="tpu_custom_call" | custom-call | tf_op jit(solution)/shard_map/pallas_call | solution.py:547
  57.1 1.8 %collective-permute-start.8 = (f32[128,768]{1,0:T(8,128)S(1)}, f32[128,768]{1,0:T(8,128)S(1)}, u32[]{:S(2)}, u32[]{:S(2)}) collective-permute-start(f32[128,768]{1,0:T(8,128)S(1)} %get-tuple-element.56), channel_id=1, source_target_pairs={{0,32},{32,0},{1,33},{33,1},{2,34},{34,2},{3,35},{35,3},{4,36},{36... | collective-permute-start | bytes 1179656 | tf_op jit(solution)/shard_map/ppermute | solution.py:552
  58.9 1.3 %collective-permute-done.8 = f32[128,768]{1,0:T(8,128)S(1)} collective-permute-done((f32[128,768]{1,0:T(8,128)S(1)}, f32[128,768]{1,0:T(8,128)S(1)}, u32[]{:S(2)}, u32[]{:S(2)}) %collective-permute-start.8) | collective-permute-done | bytes 393248 | tf_op jit(solution)/shard_map/ppermute | solution.py:552
  60.3 0.4 copy.11
  60.7 25.1 %all_to_all.16 = f32[128,1,768]{2,1,0:T(1,128)S(1)} all-to-all(f32[128,1,768]{2,1,0:T(1,128)S(1)} %copy.11), channel_id=1, replica_groups=mesh['y'=4,'core'=2,'pcol'=32] {'y','pcol'}, dimensions={0} | all-to-all | bytes 786432 | tf_op jit(solution)/shard_map/all_to_all | solution.py:553
  85.8 0.8 shard_map.101
  (3 shorter events, 0.1 us)
Async XLA Ops:
  4.2 19.0 %collective-permute-start = (f32[224,128]{1,0:T(8,128)}, f32[224,128]{1,0:T(8,128)S(1)}, u32[]{:S(2)}, u32[]{:S(2)}) collective-permute-start(f32[224,128]{1,0:T(8,128)} %get-tuple-element.34), channel_id=1, source_target_pairs={{0,1},{1,2},{2,3},{3,4},{4,5},{5,6},{6,7},{7,8},{8,9},{9,10},{10,1... | collective-permute-start | bytes 344072 | tf_op jit(solution)/shard_map/ppermute | solution.py:489
  6.7 16.5 %collective-permute-start.1 = (f32[224,128]{1,0:T(8,128)}, f32[224,128]{1,0:T(8,128)S(1)}, u32[]{:S(2)}, u32[]{:S(2)}) collective-permute-start(f32[224,128]{1,0:T(8,128)} %get-tuple-element.35), channel_id=1, source_target_pairs={{1,0},{2,1},{3,2},{4,3},{5,4},{6,5},{7,6},{8,7},{9,8},{10,9},{11,1... | collective-permute-start | bytes 344072 | tf_op jit(solution)/shard_map/ppermute | solution.py:489
  12.9 26.0 %all-to-all-start = ((f32[256,1,256]{2,1,0:T(1,128)}), f32[256,1,256]{2,1,0:T(1,128)S(1)}, u32[]{:S(2)}, u32[]{:S(2)}) async-start(f32[256,1,256]{2,1,0:T(1,128)} %get-tuple-element.33), calls=%async_computation | async-start | bytes 524288 | tf_op jit(solution)/shard_map/all_to_all | solution.py:510
  23.2 0.9 %copy-start.1 = (f32[7,32,128]{2,1,0:T(8,128)S(1)}, f32[7,32,128]{2,1,0:T(8,128)}, u32[]{:S(2)}) copy-start(f32[7,32,128]{2,1,0:T(8,128)} %get-tuple-element.32.frame) | copy-start | bytes 344068
  24.1 14.9 %copy-start = (f32[72,72,128]{2,1,0:T(8,128)S(1)}, f32[72,72,128]{2,1,0:T(8,128)}, u32[]{:S(2)}) copy-start(f32[72,72,128]{2,1,0:T(8,128)} %mats.3) | copy-start | bytes 7962628
  24.1 14.9 %copy-start.2 = (f32[7,32,128]{2,1,0:T(8,128)S(1)}, f32[7,32,128]{2,1,0:T(8,128)}, u32[]{:S(2)}) copy-start(f32[7,32,128]{2,1,0:T(8,128)} %get-tuple-element.32.frame) | copy-start | bytes 344068
  24.2 14.7 %collective-permute-start.2 = (f32[2,16,128]{2,1,0:T(8,128)S(1)}, f32[2,16,128]{2,1,0:T(8,128)S(1)}, u32[]{:S(2)}, u32[]{:S(2)}) collective-permute-start(f32[2,16,128]{2,1,0:T(8,128)S(1)} %get-tuple-element.37), channel_id=1, source_target_pairs={{0,32},{32,64},{64,96},{96,128},{128,160},{160,192},{192,224},{224... | collective-permute-start | bytes 49160 | tf_op jit(solution)/shard_map/ppermute | solution.py:489
  25.9 13.1 %collective-permute-start.3 = (f32[2,16,128]{2,1,0:T(8,128)S(1)}, f32[2,16,128]{2,1,0:T(8,128)S(1)}, u32[]{:S(2)}, u32[]{:S(2)}) collective-permute-start(f32[2,16,128]{2,1,0:T(8,128)S(1)} %get-tuple-element.38), channel_id=1, source_target_pairs={{32,0},{64,32},{96,64},{128,96},{160,128},{192,160},{224,192},{0,2... | collective-permute-start | bytes 49160 | tf_op jit(solution)/shard_map/ppermute | solution.py:489
  44.1 2.3 %collective-permute-start.4 = (f32[2,24,128]{2,1,0:T(8,128)S(1)}, f32[2,24,128]{2,1,0:T(8,128)S(1)}, u32[]{:S(2)}, u32[]{:S(2)}) collective-permute-start(f32[2,24,128]{2,1,0:T(8,128)S(1)} %get-tuple-element.43), channel_id=1, source_target_pairs={{0,32},{32,64},{64,96},{96,128},{128,160},{160,192},{192,224},{224... | collective-permute-start | bytes 73736 | tf_op jit(solution)/shard_map/ppermute | solution.py:489
  44.7 3.3 %collective-permute-start.5 = (f32[2,24,128]{2,1,0:T(8,128)S(1)}, f32[2,24,128]{2,1,0:T(8,128)S(1)}, u32[]{:S(2)}, u32[]{:S(2)}) collective-permute-start(f32[2,24,128]{2,1,0:T(8,128)S(1)} %get-tuple-element.44), channel_id=1, source_target_pairs={{32,0},{64,32},{96,64},{128,96},{160,128},{192,160},{224,192},{0,2... | collective-permute-start | bytes 73736 | tf_op jit(solution)/shard_map/ppermute | solution.py:489
  51.7 2.3 %collective-permute-start.6 = (f32[2,24,128]{2,1,0:T(8,128)S(1)}, f32[2,24,128]{2,1,0:T(8,128)S(1)}, u32[]{:S(2)}, u32[]{:S(2)}) collective-permute-start(f32[2,24,128]{2,1,0:T(8,128)S(1)} %get-tuple-element.49), channel_id=1, source_target_pairs={{0,32},{32,64},{64,96},{96,128},{128,160},{160,192},{192,224},{224... | collective-permute-start | bytes 73736 | tf_op jit(solution)/shard_map/ppermute | solution.py:489
  51.9 3.3 %collective-permute-start.7 = (f32[2,24,128]{2,1,0:T(8,128)S(1)}, f32[2,24,128]{2,1,0:T(8,128)S(1)}, u32[]{:S(2)}, u32[]{:S(2)}) collective-permute-start(f32[2,24,128]{2,1,0:T(8,128)S(1)} %get-tuple-element.50), channel_id=1, source_target_pairs={{32,0},{64,32},{96,64},{128,96},{160,128},{192,160},{224,192},{0,2... | collective-permute-start | bytes 73736 | tf_op jit(solution)/shard_map/ppermute | solution.py:489
  57.1 3.2 %collective-permute-start.8 = (f32[128,768]{1,0:T(8,128)S(1)}, f32[128,768]{1,0:T(8,128)S(1)}, u32[]{:S(2)}, u32[]{:S(2)}) collective-permute-start(f32[128,768]{1,0:T(8,128)S(1)} %get-tuple-element.56), channel_id=1, source_target_pairs={{0,32},{32,0},{1,33},{33,1},{2,34},{34,2},{3,35},{35,3},{4,36},{36... | collective-permute-start | bytes 1179656 | tf_op jit(solution)/shard_map/ppermute | solution.py:552

commit v8 on v7

--- a/solution.py
+++ b/solution.py
@@ -26,15 +26,18 @@
 LARGE = 62 * 1024 * 1024
 
 
-def call(kernel, out_shapes, in_specs, scratch=(), work=None, limit=SMALL):
+def call(kernel, out_shapes, in_specs, scratch=(), work=None, limit=SMALL, outs=None):
     cost = None
     if work is not None:
         cost = pl.CostEstimate(flops=work, bytes_accessed=1 << 20, transcendentals=0)
     return pl.pallas_call(
         kernel,
-        out_shape=[jax.ShapeDtypeStruct(s, F32) for s in out_shapes],
+        out_shape=[
+            s if isinstance(s, jax.ShapeDtypeStruct) else jax.ShapeDtypeStruct(s, F32)
+            for s in out_shapes
+        ],
         in_specs=list(in_specs),
-        out_specs=[VMEM] * len(out_shapes),
+        out_specs=[VMEM] * len(out_shapes) if outs is None else outs,
         cost_estimate=cost,
         scratch_shapes=list(scratch),
         compiler_params=pltpu.CompilerParams(vmem_limit_bytes=limit),
@@ -98,7 +101,7 @@
 def start_kernel(
     levels, thickness, direction, state, adjoint, dmap, blocks,
     own_out, frame_out, first_out, last_out,
-    level, known, cells, own, mats, sems, block_sems,
+    level, known, cells, own, many, mats, sems, block_sems,
 ):
     copies = [
         pltpu.make_async_copy(thickness, own.at[0], sems.at[0]),
@@ -119,7 +122,9 @@
     for copy in copies:
         copy.wait()
     for k in range(2):
-        own_out[:, :, k * DV:(k + 1) * DV] = jnp.broadcast_to(own[k][None], (own_out.shape[0], 1, DV))
+        many[:, :, k * DV:(k + 1) * DV] = jnp.broadcast_to(own[k][None], (many.shape[0], 1, DV))
+    written = pltpu.make_async_copy(many, own_out, sems.at[6])
+    written.start()
     frame_out[0:6, 8:8 + CR, :] = known[...]
     frame_out[6, 8:8 + CR, :] = cells[...].astype(F32)
     tiles = [frame_out[f, 8 + 8 * g:16 + 8 * g, :] for f in range(7) for g in range(3)]
@@ -139,6 +144,7 @@
             packed = jnp.where(here, pltpu.roll(mat, 4 * i, 1) if i else mat, packed)
         first_out[c * BLK:(c + 1) * BLK, :] = packed
         last_out[c * BLK:(c + 1) * BLK, :] = packed
+    written.wait()
 
 
 def rows_kernel(
@@ -239,30 +245,12 @@
         frame[...] = frame[...] * inside[None]
 
 
-def look_up(table, index, tcell, dcell):
-    flipped = table[...].T
-    part0 = flipped.astype(BF16)
-    part1 = (flipped - part0.astype(F32)).astype(BF16)
-    lhs = jnp.concatenate([part0, part1], axis=0)
-    high = [ix // DV for ix in index]
-    low = [ix % DV for ix in index]
+PAIRS = range(6, FR, 2)
+
+
+def place_cells(index, cells):
     lane1 = iota((1, CC), 1)
-
-    def both(vh, vl):
-        hot = jnp.where(iota((256, 2 * CC), 0) == vh, 1.0, 0.0).astype(BF16)
-        got = jnp.dot(lhs, hot, preferred_element_type=F32)
-        mine = iota((DV, 2 * CC), 0) == vl
-        tv = jnp.sum(jnp.where(mine, got[0:DV] + got[2 * DV:3 * DV], 0.0), axis=0, keepdims=True)
-        dv = jnp.sum(jnp.where(mine, got[DV:2 * DV] + got[3 * DV:4 * DV], 0.0), axis=0, keepdims=True)
-        return tv, dv
-
-    for r in range(6, FR, 2):
-        vh = jnp.concatenate([high[0][r:r + 1], high[0][r + 1:r + 2]], axis=1)
-        vl = jnp.concatenate([low[0][r:r + 1], low[0][r + 1:r + 2]], axis=1)
-        tv, dv = both(vh, vl)
-        for h in range(2):
-            tcell[0, r + h:r + h + 1, :] = tv[:, h * CC:(h + 1) * CC]
-            dcell[0, r + h:r + h + 1, :] = dv[:, h * CC:(h + 1) * CC]
+    vecs = [jnp.concatenate([index[0][r:r + 1], index[0][r + 1:r + 2]], axis=1) for r in PAIRS]
     packs = []
     for half in range(2):
         vec = jnp.zeros((1, CC), jnp.int32)
@@ -270,8 +258,33 @@
             r = 16 * half + i
             vec = jnp.where(lane1 // 8 == i, pltpu.roll(index[1][r:r + 1], (8 * i + 4) % CC, 1), vec)
         packs.append(vec)
-    vec = jnp.concatenate(packs, axis=1)
-    tv, dv = both(vec // DV, vec % DV)
+    vecs.append(jnp.concatenate(packs, axis=1))
+    for k, vec in enumerate(vecs):
+        cells[k:k + 1, :] = vec
+
+
+def look_up(table, cells, tcell, dcell):
+    flipped = table[...].T
+    part0 = flipped.astype(BF16)
+    part1 = (flipped - part0.astype(F32)).astype(BF16)
+    lhs = jnp.concatenate([part0, part1], axis=0)
+    lane1 = iota((1, CC), 1)
+
+    def both(k):
+        vec = cells[k:k + 1, :]
+        hot = jnp.where(iota((256, 2 * CC), 0) == vec // DV, 1.0, 0.0).astype(BF16)
+        got = jnp.dot(lhs, hot, preferred_element_type=F32)
+        mine = iota((DV, 2 * CC), 0) == vec % DV
+        tv = jnp.sum(jnp.where(mine, got[0:DV] + got[2 * DV:3 * DV], 0.0), axis=0, keepdims=True)
+        dv = jnp.sum(jnp.where(mine, got[DV:2 * DV] + got[3 * DV:4 * DV], 0.0), axis=0, keepdims=True)
+        return tv, dv
+
+    for k, r in enumerate(PAIRS):
+        tv, dv = both(k)
+        for h in range(2):
+            tcell[0, r + h:r + h + 1, :] = tv[:, h * CC:(h + 1) * CC]
+            dcell[0, r + h:r + h + 1, :] = dv[:, h * CC:(h + 1) * CC]
+    tv, dv = both(len(PAIRS))
     for half in range(2):
         for i in range(16):
             r = 16 * half + i
@@ -303,23 +316,27 @@
     ]
 
 
-def first_kernel(
-    last, info, table, frame, side, from_up, from_down, mats, edge, levels,
-    resid_out, local_out, up_out, down_out, main_f, side_f, tcell, dcell,
-    vec, total, side_vec, side_total, index_scr,
-):
-    level, prow = info[0], info[1]
-    inside = grid_mask(prow, last, 0, FR)
+def place_kernel(last, info, frame, side, from_up, from_down, main_f, side_f, cells, index_scr):
+    inside = grid_mask(info[1], last, 0, FR)
     for tile, ref, source in ((0, main_f, frame), (1, side_f, side)):
         for f in range(7):
             out = ref.at[f] if f < 6 else index_scr.at[tile]
             out[...] = source[f]
             out[6:8, :] = from_up[tile, 2 * f:2 * f + 2, :] * inside[6:8]
             out[8 + CR:10 + CR, :] = from_down[tile, 2 * f:2 * f + 2, :] * inside[8 + CR:10 + CR]
-    index = [index_scr[tile].astype(jnp.int32) for tile in range(2)]
+    place_cells([index_scr[tile].astype(jnp.int32) for tile in range(2)], cells)
+
+
+def first_kernel(
+    last, info, table, main_f, side_f, cells, mats, edge, levels,
+    resid_out, local_out, up_out, down_out, tcell, dcell,
+    vec, total, side_vec, side_total,
+):
+    level, prow = info[0], info[1]
+    inside = grid_mask(prow, last, 0, FR)
     tcell[...] = jnp.zeros_like(tcell)
     dcell[...] = jnp.zeros_like(dcell)
-    look_up(table, index, tcell, dcell)
+    look_up(table, cells, tcell, dcell)
     for tile in range(2):
         tcell[tile] = tcell[tile] * inside
     slope = [3.0 * tcell[tile] * tcell[tile] * dcell[tile] for tile in range(2)]
@@ -502,10 +519,11 @@
         [
             pltpu.VMEM((1, 1), jnp.int32), pltpu.VMEM((6, CR, CC), F32),
             pltpu.VMEM((CR, CC), jnp.int32), pltpu.VMEM((2, 1, DV), F32),
-            pltpu.VMEM((BLK, BLK, CC), F32), pltpu.SemaphoreType.DMA((6,)),
+            pltpu.VMEM((n_dev, 1, 2 * DV), F32), pltpu.VMEM((BLK, BLK, CC), F32),
+            pltpu.SemaphoreType.DMA((7,)),
             pltpu.SemaphoreType.DMA((BLK // PIECE,)),
         ],
-        work=10**9, limit=LARGE,
+        work=10**9, limit=LARGE, outs=[HBM] + [VMEM] * 3,
     )(levels, thickness.reshape(1, DV), direction.reshape(1, DV), state, adjoint, design_map, blocks)
     table = lax.all_to_all(own, ROW + ("pcol",), 0, 0, tiled=True).reshape(n_dev, 2 * DV)
     if n_dev < 256:
@@ -517,15 +535,21 @@
     )(frame, from_left, from_right)
 
     solve_scratch = [pltpu.VMEM((2, BLK, CC), F32)] * 4
-    resid, local, up, down, main_f, side_f, tcell, dcell = call(
+    pairs = len(PAIRS) + 1
+    main_f, side_f, cells = call(
+        functools.partial(place_kernel, last),
+        [
+            (6, FR, CC), (6, FR, CC), jax.ShapeDtypeStruct((pairs, 2 * CC), jnp.int32),
+        ],
+        [SMEM] + [VMEM] * 4, [pltpu.VMEM((2, FR, CC), F32)], work=3 * 10**9,
+    )(info, frame, side, *rows(down, up))
+    resid, local, up, down, tcell, dcell = call(
         functools.partial(first_kernel, last),
         [
-            (6, EXT, CC), (2, 6, EXT, CC), (2, 24, CC), (2, 24, CC), (6, FR, CC), (6, FR, CC),
-            (2, FR, CC), (2, FR, CC),
+            (6, EXT, CC), (2, 6, EXT, CC), (2, 24, CC), (2, 24, CC), (2, FR, CC), (2, FR, CC),
         ],
-        [SMEM] + [VMEM] * 8,
-        solve_scratch + [pltpu.VMEM((2, FR, CC), F32)],
-    )(info, table, frame, side, *rows(down, up), blocks, edge, around)
+        [SMEM] + [VMEM] * 7, solve_scratch,
+    )(info, table, main_f, side_f, cells, blocks, edge, around)
 
     def operands(count):
         return [pltpu.VMEM((256, CR * CC), BF16), pltpu.VMEM((2 * count * DV, CR * CC), BF16)]

time: 86.8 us -> 86.9 us (level)
  starting transfers between devices: 24.1 us -> 26.5 us
  waiting for transfers between devices: 16.5 us -> 15.5 us
    all_to_all x1, waiting for transfers between devices: 12.4 us -> 8.88 us  [per_device(): lax.all_to_all(own, ROW + ('pcol',), 0, 0, tiled=True)]
    ppermute x4, waiting for transfers between devices: 2.69 us -> 4.65 us  [ring(): lax.ppermute(to_previous, axis, backward)]
    ppermute x4, starting transfers between devices: 5.01 us -> 6.03 us  [ring(): lax.ppermute(to_next, axis, forward)]
  transfers between devices with their start and end apart: 10 -> 10, of which waited for: 4 -> 6; matrix products, arithmetic and copies ran while one was open for 0% -> 0% of each run, Pallas kernels for 4% -> 5%
where the time goes in v8:
time: 86.9 us; the launch traced here: 86.7 us
  starting transfers between devices  26.5 us (30%)
  blocking collectives  24.3 us (28%)
  Pallas kernels  17.5 us (20%)
  waiting for transfers between devices  15.5 us (18%)
  between operations  1.43 us (2%)
  local copies, waits for them, and re-layouts  1.35 us (2%)
    all_to_all x1, blocking collectives, per_device(): got = lax.all_to_all(sums, ('y', 'pcol'), 0, 0, tiled=True)  24.3 us
    all_to_all x1, starting transfers between devices, per_device(): lax.all_to_all(own, ROW + ('pcol',), 0, 0, tiled=True)  10.2 us
    all_to_all x1, waiting for transfers between devices, per_device(): lax.all_to_all(own, ROW + ('pcol',), 0, 0, tiled=True)  8.88 us
    ppermute x4, starting transfers between devices, ring(): lax.ppermute(to_previous, axis, backward)  7.71 us
    ppermute x4, starting transfers between devices, ring(): lax.ppermute(to_next, axis, forward)  6.03 us
    ppermute x4, waiting for transfers between devices, ring(): lax.ppermute(to_previous, axis, backward)  4.65 us
    pallas_call x1, Pallas kernels, per_device(): call(functools.partial(first_kernel, last), [(6, EXT, CC), (2, 6, EXT, CC...  4.47 us
    pallas_call x1, Pallas kernels, per_device(): call(functools.partial(second_kernel, last), [(6, FR, CC), (6, FR, CC), (...  3.09 us
  transfers between devices with their start and end apart: 10, of which 6 were waited for; matrix products, arithmetic and copies ran while one was open for 0% of the time, Pallas kernels for 5%

profile of v8, /device:TPU:1, one launch (start us, length us, event | category | flops | bytes accessed | tf_op | source)
XLA Modules:
  0.0 86.7 jit_solution(11739242430147903818)
XLA Ops:
  1.3 2.9 %shard_map.94 = (f32[256,1,256]{2,1,0:T(1,128)}, f32[7,32,128]{2,1,0:T(8,128)}, f32[224,128]{1,0:T(8,128)}, f32[224,128]{1,0:T(8,128)}) custom-call(s32[1,1]{1,0:T(1,128)} %copy.18.levels, f32[1,128]{1,0:T(1,128)} %bitcast.16, f32[1,128]{1,0:T(1,128)} %bitcast.17, f32[3,22,128]{2,1,0:T(8,128)} %state.1, f32[3,22,128]{2,1,0:T(8,128)} %adjoint.1, ...), custom_call_target="tpu_custom_call" | custom-call | flops 1000000000 | bytes 1048576 | tf_op jit(solution)/shard_map/pallas_call | solution.py:517
  4.2 2.5 %collective-permute-start = (f32[224,128]{1,0:T(8,128)}, f32[224,128]{1,0:T(8,128)S(1)}, u32[]{:S(2)}, u32[]{:S(2)}) collective-permute-start(f32[224,128]{1,0:T(8,128)} %get-tuple-element.35), channel_id=1, source_target_pairs={{0,1},{1,2},{2,3},{3,4},{4,5},{5,6},{6,7},{7,8},{8,9},{9,10},{10,1... | collective-permute-start | bytes 344072 | tf_op jit(solution)/shard_map/ppermute | solution.py:506
  6.8 6.2 %collective-permute-start.1 = (f32[224,128]{1,0:T(8,128)}, f32[224,128]{1,0:T(8,128)S(1)}, u32[]{:S(2)}, u32[]{:S(2)}) collective-permute-start(f32[224,128]{1,0:T(8,128)} %get-tuple-element.36), channel_id=1, source_target_pairs={{1,0},{2,1},{3,2},{4,3},{5,4},{6,5},{7,6},{8,7},{9,8},{10,9},{11,1... | collective-permute-start | bytes 344072 | tf_op jit(solution)/shard_map/ppermute | solution.py:506
  13.0 10.2 %all-to-all-start = ((f32[256,1,256]{2,1,0:T(1,128)}), f32[256,1,256]{2,1,0:T(1,128)S(1)}, u32[]{:S(2)}, u32[]{:S(2)}) async-start(f32[256,1,256]{2,1,0:T(1,128)} %get-tuple-element.34), calls=%async_computation | async-start | bytes 524288 | tf_op jit(solution)/shard_map/all_to_all | solution.py:528
  23.2 0.0 collective-permute-done.from_left
  23.2 0.0 collective-permute-done.1.from_right
  23.2 0.0 copy-start.1
  23.2 0.9 %copy-done.1 = f32[7,32,128]{2,1,0:T(8,128)S(1)} copy-done((f32[7,32,128]{2,1,0:T(8,128)S(1)}, f32[7,32,128]{2,1,0:T(8,128)}, u32[]{:S(2)}) %copy-start.1) | copy-done | bytes 114712
  24.1 0.1 shard_map.95
  24.3 1.6 %collective-permute-start.2 = (f32[2,16,128]{2,1,0:T(8,128)S(1)}, f32[2,16,128]{2,1,0:T(8,128)S(1)}, u32[]{:S(2)}, u32[]{:S(2)}) collective-permute-start(f32[2,16,128]{2,1,0:T(8,128)S(1)} %get-tuple-element.38), channel_id=1, source_target_pairs={{0,32},{32,64},{64,96},{96,128},{128,160},{160,192},{192,224},{224... | collective-permute-start | bytes 49160 | tf_op jit(solution)/shard_map/ppermute | solution.py:506
  25.9 0.5 collective-permute-start.3
  26.5 0.1 pad_add_fusion.info
  26.5 0.6 collective-permute-done.2.from_up
  27.1 2.3 %collective-permute-done.3.from_down = f32[2,16,128]{2,1,0:T(8,128)S(1)} collective-permute-done((f32[2,16,128]{2,1,0:T(8,128)S(1)}, f32[2,16,128]{2,1,0:T(8,128)S(1)}, u32[]{:S(2)}, u32[]{:S(2)}) %collective-permute-start.3) | collective-permute-done | bytes 16416 | tf_op jit(solution)/shard_map/ppermute | solution.py:506
  29.4 0.0 copy-start
  29.4 0.7 shard_map.96
  30.1 0.0 copy-start.2
  30.1 8.9 %all-to-all-done = f32[256,1,256]{2,1,0:T(1,128)S(1)} async-done(((f32[256,1,256]{2,1,0:T(1,128)}), f32[256,1,256]{2,1,0:T(1,128)S(1)}, u32[]{:S(2)}, u32[]{:S(2)}) %all-to-all-start) | async-done | bytes 262176 | tf_op jit(solution)/shard_map/all_to_all | solution.py:528
  39.0 0.0 copy-done
  39.0 4.5 %shard_map.97 = (f32[6,24,128]{2,1,0:T(8,128)S(1)}, f32[2,6,24,128]{3,2,1,0:T(8,128)S(1)}, f32[2,24,128]{2,1,0:T(8,128)S(1)}, f32[2,24,128]{2,1,0:T(8,128)S(1)},...) custom-call(s32[2]{0:T(128)S(1)} %pad_add_fusion.info, f32[256,256]{1,0:T(8,128)S(1)} %bitcast.15, ...), custom_call_target="tpu_custom_call" | custom-call | tf_op jit(solution)/shard_map/pallas_call | solution.py:546
  43.5 1.3 %collective-permute-start.4 = (f32[2,24,128]{2,1,0:T(8,128)S(1)}, f32[2,24,128]{2,1,0:T(8,128)S(1)}, u32[]{:S(2)}, u32[]{:S(2)}) collective-permute-start(f32[2,24,128]{2,1,0:T(8,128)S(1)} %get-tuple-element.47), channel_id=1, source_target_pairs={{0,32},{32,64},{64,96},{96,128},{128,160},{160,192},{192,224},{224... | collective-permute-start | bytes 73736 | tf_op jit(solution)/shard_map/ppermute | solution.py:506
  44.8 0.0 collective-permute-start.5
  44.8 0.0 copy-done.2
  44.8 1.7 %shard_map.99.sums0 = f32[256,128]{1,0:T(8,128)S(1)} custom-call(s32[2]{0:T(128)S(1)} %pad_add_fusion.info, f32[7,32,128]{2,1,0:T(8,128)S(1)} %copy-done.2, f32[2,32,128]{2,1,0:T(8,128)S(1)} %get-tuple-element.49.tcell, f32[2,32,128]{2,1,0:T(8,128)S(1)} %get-tuple-element.55.dcell, f32[6,32,128]{2,1,0:T(8,128)S(1)} %get-tuple-element.40.main_f, ...), custom_call_target="tpu_custom_call" | custom-call | flops 300000000 | bytes 1048576 | tf_op jit(solution)/shard_map/pallas_call | solution.py:557
  46.4 0.0 collective-permute-done.4.from_up
  46.5 1.9 %collective-permute-done.5.from_down = f32[2,24,128]{2,1,0:T(8,128)S(1)} collective-permute-done((f32[2,24,128]{2,1,0:T(8,128)S(1)}, f32[2,24,128]{2,1,0:T(8,128)S(1)}, u32[]{:S(2)}, u32[]{:S(2)}) %collective-permute-start.5) | collective-permute-done | bytes 24608 | tf_op jit(solution)/shard_map/ppermute | solution.py:506
  48.3 3.1 %shard_map.98 = (f32[6,32,128]{2,1,0:T(8,128)S(1)}, f32[6,32,128]{2,1,0:T(8,128)S(1)}, f32[6,24,128]{2,1,0:T(8,128)S(1)}, f32[2,6,24,128]{3,2,1,0:T(8,128)S(1)},...) custom-call(s32[2]{0:T(128)S(1)} %pad_add_fusion.info, f32[2,6,24,128]{3,2,1,0:T(8,128)S(1)} %get-tuple-element.46.local, ...), custom_call_target="tpu_custom_call" | custom-call | tf_op jit(solution)/shard_map/pallas_call | solution.py:561
  51.4 0.5 collective-permute-start.6
  51.9 0.9 %collective-permute-start.7 = (f32[2,24,128]{2,1,0:T(8,128)S(1)}, f32[2,24,128]{2,1,0:T(8,128)S(1)}, u32[]{:S(2)}, u32[]{:S(2)}) collective-permute-start(f32[2,24,128]{2,1,0:T(8,128)S(1)} %get-tuple-element.54), channel_id=1, source_target_pairs={{32,0},{64,32},{96,64},{128,96},{160,128},{192,160},{224,192},{0,2... | collective-permute-start | bytes 73736 | tf_op jit(solution)/shard_map/ppermute | solution.py:506
  52.9 1.8 %shard_map.100.sums1 = f32[256,256]{1,0:T(8,128)S(1)} custom-call(s32[2]{0:T(128)S(1)} %pad_add_fusion.info, f32[7,32,128]{2,1,0:T(8,128)S(1)} %copy-done.2, f32[2,32,128]{2,1,0:T(8,128)S(1)} %get-tuple-element.49.tcell, f32[6,32,128]{2,1,0:T(8,128)S(1)} %get-tuple-element.40.main_f, f32[6,32,128]{2,1,0:T(8,128)S(1)} %get-tuple-element.41.side_f, ...), custom_call_target="tpu_custom_call" | custom-call | flops 500000000 | bytes 1048576 | tf_op jit(solution)/shard_map/pallas_call | solution.py:567
  54.7 0.0 collective-permute-done.6.from_up
  54.7 0.5 collective-permute-done.7.from_down
  55.2 2.0 %shard_map.101 = (f32[6,32,128]{2,1,0:T(8,128)S(1)}, f32[128,768]{1,0:T(8,128)S(1)}, f32[128,768]{1,0:T(8,128)S(1)}) custom-call(s32[2]{0:T(128)S(1)} %pad_add_fusion.info, f32[7,32,128]{2,1,0:T(8,128)S(1)} %copy-done.2, f32[6,24,128]{2,1,0:T(8,128)S(1)} %get-tuple-element.45.resid, f32[6,24,128]{2,1,0:T(8,128)S(1)} %get-tuple-element.50.image, ...), custom_call_target="tpu_custom_call" | custom-call | tf_op jit(solution)/shard_map/pallas_call | solution.py:571
  57.2 2.5 %collective-permute-start.8 = (f32[128,768]{1,0:T(8,128)S(1)}, f32[128,768]{1,0:T(8,128)S(1)}, u32[]{:S(2)}, u32[]{:S(2)}) collective-permute-start(f32[128,768]{1,0:T(8,128)S(1)} %get-tuple-element.58), channel_id=1, source_target_pairs={{0,32},{32,0},{1,33},{33,1},{2,34},{34,2},{3,35},{35,3},{4,36},{36... | collective-permute-start | bytes 1179656 | tf_op jit(solution)/shard_map/ppermute | solution.py:576
  59.7 1.3 %collective-permute-done.8 = f32[128,768]{1,0:T(8,128)S(1)} collective-permute-done((f32[128,768]{1,0:T(8,128)S(1)}, f32[128,768]{1,0:T(8,128)S(1)}, u32[]{:S(2)}, u32[]{:S(2)}) %collective-permute-start.8) | collective-permute-done | bytes 393248 | tf_op jit(solution)/shard_map/ppermute | solution.py:576
  61.1 0.4 copy.11
  61.5 24.3 %all_to_all.16 = f32[128,1,768]{2,1,0:T(1,128)S(1)} all-to-all(f32[128,1,768]{2,1,0:T(1,128)S(1)} %copy.11), channel_id=1, replica_groups=mesh['y'=4,'core'=2,'pcol'=32] {'y','pcol'}, dimensions={0} | all-to-all | bytes 786432 | tf_op jit(solution)/shard_map/all_to_all | solution.py:577
  85.9 0.8 shard_map.102
  (3 shorter events, 0.1 us)
Async XLA Ops:
  4.2 19.0 %collective-permute-start = (f32[224,128]{1,0:T(8,128)}, f32[224,128]{1,0:T(8,128)S(1)}, u32[]{:S(2)}, u32[]{:S(2)}) collective-permute-start(f32[224,128]{1,0:T(8,128)} %get-tuple-element.35), channel_id=1, source_target_pairs={{0,1},{1,2},{2,3},{3,4},{4,5},{5,6},{6,7},{7,8},{8,9},{9,10},{10,1... | collective-permute-start | bytes 344072 | tf_op jit(solution)/shard_map/ppermute | solution.py:506
  6.8 16.5 %collective-permute-start.1 = (f32[224,128]{1,0:T(8,128)}, f32[224,128]{1,0:T(8,128)S(1)}, u32[]{:S(2)}, u32[]{:S(2)}) collective-permute-start(f32[224,128]{1,0:T(8,128)} %get-tuple-element.36), channel_id=1, source_target_pairs={{1,0},{2,1},{3,2},{4,3},{5,4},{6,5},{7,6},{8,7},{9,8},{10,9},{11,1... | collective-permute-start | bytes 344072 | tf_op jit(solution)/shard_map/ppermute | solution.py:506
  13.0 26.0 %all-to-all-start = ((f32[256,1,256]{2,1,0:T(1,128)}), f32[256,1,256]{2,1,0:T(1,128)S(1)}, u32[]{:S(2)}, u32[]{:S(2)}) async-start(f32[256,1,256]{2,1,0:T(1,128)} %get-tuple-element.34), calls=%async_computation | async-start | bytes 524288 | tf_op jit(solution)/shard_map/all_to_all | solution.py:528
  23.2 0.9 %copy-start.1 = (f32[7,32,128]{2,1,0:T(8,128)S(1)}, f32[7,32,128]{2,1,0:T(8,128)}, u32[]{:S(2)}) copy-start(f32[7,32,128]{2,1,0:T(8,128)} %get-tuple-element.33.frame) | copy-start | bytes 344068
  24.3 2.8 %collective-permute-start.2 = (f32[2,16,128]{2,1,0:T(8,128)S(1)}, f32[2,16,128]{2,1,0:T(8,128)S(1)}, u32[]{:S(2)}, u32[]{:S(2)}) collective-permute-start(f32[2,16,128]{2,1,0:T(8,128)S(1)} %get-tuple-element.38), channel_id=1, source_target_pairs={{0,32},{32,64},{64,96},{96,128},{128,160},{160,192},{192,224},{224... | collective-permute-start | bytes 49160 | tf_op jit(solution)/shard_map/ppermute | solution.py:506
  25.9 3.5 %collective-permute-start.3 = (f32[2,16,128]{2,1,0:T(8,128)S(1)}, f32[2,16,128]{2,1,0:T(8,128)S(1)}, u32[]{:S(2)}, u32[]{:S(2)}) collective-permute-start(f32[2,16,128]{2,1,0:T(8,128)S(1)} %get-tuple-element.39), channel_id=1, source_target_pairs={{32,0},{64,32},{96,64},{128,96},{160,128},{192,160},{224,192},{0,2... | collective-permute-start | bytes 49160 | tf_op jit(solution)/shard_map/ppermute | solution.py:506
  29.4 9.6 %copy-start = (f32[72,72,128]{2,1,0:T(8,128)S(1)}, f32[72,72,128]{2,1,0:T(8,128)}, u32[]{:S(2)}) copy-start(f32[72,72,128]{2,1,0:T(8,128)} %mats.3) | copy-start | bytes 7962628
  30.1 14.7 %copy-start.2 = (f32[7,32,128]{2,1,0:T(8,128)S(1)}, f32[7,32,128]{2,1,0:T(8,128)}, u32[]{:S(2)}) copy-start(f32[7,32,128]{2,1,0:T(8,128)} %get-tuple-element.33.frame) | copy-start | bytes 344068
  43.5 3.0 %collective-permute-start.4 = (f32[2,24,128]{2,1,0:T(8,128)S(1)}, f32[2,24,128]{2,1,0:T(8,128)S(1)}, u32[]{:S(2)}, u32[]{:S(2)}) collective-permute-start(f32[2,24,128]{2,1,0:T(8,128)S(1)} %get-tuple-element.47), channel_id=1, source_target_pairs={{0,32},{32,64},{64,96},{96,128},{128,160},{160,192},{192,224},{224... | collective-permute-start | bytes 73736 | tf_op jit(solution)/shard_map/ppermute | solution.py:506
  44.8 3.5 %collective-permute-start.5 = (f32[2,24,128]{2,1,0:T(8,128)S(1)}, f32[2,24,128]{2,1,0:T(8,128)S(1)}, u32[]{:S(2)}, u32[]{:S(2)}) collective-permute-start(f32[2,24,128]{2,1,0:T(8,128)S(1)} %get-tuple-element.48), channel_id=1, source_target_pairs={{32,0},{64,32},{96,64},{128,96},{160,128},{192,160},{224,192},{0,2... | collective-permute-start | bytes 73736 | tf_op jit(solution)/shard_map/ppermute | solution.py:506
  51.4 3.3 %collective-permute-start.6 = (f32[2,24,128]{2,1,0:T(8,128)S(1)}, f32[2,24,128]{2,1,0:T(8,128)S(1)}, u32[]{:S(2)}, u32[]{:S(2)}) collective-permute-start(f32[2,24,128]{2,1,0:T(8,128)S(1)} %get-tuple-element.53), channel_id=1, source_target_pairs={{0,32},{32,64},{64,96},{96,128},{128,160},{160,192},{192,224},{224... | collective-permute-start | bytes 73736 | tf_op jit(solution)/shard_map/ppermute | solution.py:506
  51.9 3.3 %collective-permute-start.7 = (f32[2,24,128]{2,1,0:T(8,128)S(1)}, f32[2,24,128]{2,1,0:T(8,128)S(1)}, u32[]{:S(2)}, u32[]{:S(2)}) collective-permute-start(f32[2,24,128]{2,1,0:T(8,128)S(1)} %get-tuple-element.54), channel_id=1, source_target_pairs={{32,0},{64,32},{96,64},{128,96},{160,128},{192,160},{224,192},{0,2... | collective-permute-start | bytes 73736 | tf_op jit(solution)/shard_map/ppermute | solution.py:506
  57.2 3.9 %collective-permute-start.8 = (f32[128,768]{1,0:T(8,128)S(1)}, f32[128,768]{1,0:T(8,128)S(1)}, u32[]{:S(2)}, u32[]{:S(2)}) collective-permute-start(f32[128,768]{1,0:T(8,128)S(1)} %get-tuple-element.58), channel_id=1, source_target_pairs={{0,32},{32,0},{1,33},{33,1},{2,34},{34,2},{3,35},{35,3},{4,36},{36... | collective-permute-start | bytes 1179656 | tf_op jit(solution)/shard_map/ppermute | solution.py:576

commit v9 on v8

--- a/solution.py
+++ b/solution.py
@@ -15,7 +15,6 @@
 FR = 32
 ROW = ("y", "core")
 WIDE = 3
-HALVES = (4, 8, 16, 32, 64)
 F32 = jnp.float32
 BF16 = jnp.bfloat16
 
@@ -129,7 +128,7 @@
     frame_out[6, 8:8 + CR, :] = cells[...].astype(F32)
     tiles = [frame_out[f, 8 + 8 * g:16 + 8 * g, :] for f in range(7) for g in range(3)]
     first, last = pack_edges(tiles, WIDE)
-    depth = jnp.broadcast_to(level[...].astype(F32), (8, CC))
+    depth = level[0].astype(F32)
     first_out[EDGE:, :] = jnp.where(upper, depth, first)
     last_out[EDGE:, :] = jnp.where(upper, depth, last)
     lane = iota((BLK, CC), 1)
@@ -181,9 +180,13 @@
 
 
 def over_columns(x):
-    for shift in HALVES:
-        x = x + pltpu.roll(x, shift, 1)
-    return x
+    same = (iota((2 * CC, CC), 0) - iota((2 * CC, CC), 1)) % 4 == 0
+    top = x.astype(BF16)
+    rest = (x - top.astype(F32)).astype(BF16)
+    return jnp.dot(
+        jnp.concatenate([top, rest], axis=1), jnp.where(same, 1.0, 0.0).astype(BF16),
+        preferred_element_type=F32,
+    )
 
 
 def apply_edge(edge, vec):
@@ -195,14 +198,16 @@
         mine = row[low:high] == place[low:high] + 32 * c
         flat = jnp.sum(jnp.where(mine, vec[low:high], 0.0), axis=0, keepdims=True)
         out = out + edge[c] * flat
-    return over_columns(out)
+    return out
 
 
 def local_solve(mats, edge, vec, total, side_vec, side_total, level, levels):
     lane = iota((BLK, CC), 1)
     ours = (lane < 2) | (lane >= CC - 2)
-    for n in range(2):
-        side_vec[n] = over_columns(jnp.where(ours, side_vec[n], 0.0))
+    kept = [jnp.where(ours, side_vec[n], 0.0) for n in range(2)]
+    spread = over_columns(jnp.concatenate(kept, axis=0))
+    side_vec[0] = spread[:BLK]
+    side_vec[1] = spread[BLK:]
     total[...] = jnp.zeros_like(total)
     side_total[...] = jnp.zeros_like(side_total)
     top = jnp.maximum(level, jnp.max(levels[...]).astype(jnp.int32))
@@ -211,8 +216,10 @@
         scale = jnp.where(order == 0, 1.0, 0.5).astype(F32)
         keep = jnp.where(order < level, 1.0, 0.0).astype(F32)
         side_keep = levels[0:1, :] > order.astype(F32)
+        parts = [apply_edge(edge, side_vec[n]) for n in range(2)]
+        outs = scale * over_columns(jnp.concatenate(parts, axis=0))
         for n in range(2):
-            out = scale * apply_edge(edge, side_vec[n])
+            out = outs[n * BLK:(n + 1) * BLK]
             side_vec[n] = out
             side_total[n] += jnp.where(side_keep, out, 0.0)
         for n, out in enumerate(apply_blocks(mats, vec)):
@@ -517,14 +524,14 @@
     own, frame, first, end = call(
         start_kernel, [(n_dev, 1, 2 * DV), (7, FR, CC), (EDGE + 8, CC), (EDGE + 8, CC)], [HBM] * 7,
         [
-            pltpu.VMEM((1, 1), jnp.int32), pltpu.VMEM((6, CR, CC), F32),
+            pltpu.SMEM((1,), jnp.int32), pltpu.VMEM((6, CR, CC), F32),
             pltpu.VMEM((CR, CC), jnp.int32), pltpu.VMEM((2, 1, DV), F32),
             pltpu.VMEM((n_dev, 1, 2 * DV), F32), pltpu.VMEM((BLK, BLK, CC), F32),
             pltpu.SemaphoreType.DMA((7,)),
             pltpu.SemaphoreType.DMA((BLK // PIECE,)),
         ],
         work=10**9, limit=LARGE, outs=[HBM] + [VMEM] * 3,
-    )(levels, thickness.reshape(1, DV), direction.reshape(1, DV), state, adjoint, design_map, blocks)
+    )(levels.reshape(1), thickness.reshape(1, DV), direction.reshape(1, DV), state, adjoint, design_map, blocks)
     table = lax.all_to_all(own, ROW + ("pcol",), 0, 0, tiled=True).reshape(n_dev, 2 * DV)
     if n_dev < 256:
         table = jnp.concatenate([table, jnp.zeros((256 - n_dev, 2 * DV), F32)], axis=0)

time: 86.9 us -> 84.7 us (0.975)
  Pallas kernels: 17.5 us -> 15.8 us
  waiting for transfers between devices: 15.5 us -> 14.5 us
    ppermute x4, starting transfers between devices: 7.71 us -> 8.76 us  [ring(): lax.ppermute(to_previous, axis, backward)]
    ppermute x4, starting transfers between devices: 6.03 us -> 5.06 us  [ring(): lax.ppermute(to_next, axis, forward)]
    ppermute x4, waiting for transfers between devices: 4.65 us -> 3.69 us  [ring(): lax.ppermute(to_previous, axis, backward)]
    pallas_call x1, Pallas kernels: 3.09 us -> 2.22 us  [per_device(): call(functools.partial(second_kernel, last), [(6, FR, CC), (6, FR, CC), (...]
  transfers between devices with their start and end apart: 10 -> 10, of which waited for: 6 -> 5; matrix products, arithmetic and copies ran while one was open for 0% -> 0% of each run, Pallas kernels for 5% -> 5%
where the time goes in v9:
time: 84.7 us; the launch traced here: 84.5 us
  starting transfers between devices  27 us (32%)
  blocking collectives  24.3 us (29%)
  Pallas kernels  15.8 us (19%)
  waiting for transfers between devices  14.5 us (17%)
  between operations  1.44 us (2%)
  local copies, waits for them, and re-layouts  1.35 us (2%)
    all_to_all x1, blocking collectives, per_device(): got = lax.all_to_all(sums, ('y', 'pcol'), 0, 0, tiled=True)  24.3 us
    all_to_all x1, starting transfers between devices, per_device(): lax.all_to_all(own, ROW + ('pcol',), 0, 0, tiled=True)  10.2 us
    all_to_all x1, waiting for transfers between devices, per_device(): lax.all_to_all(own, ROW + ('pcol',), 0, 0, tiled=True)  8.88 us
    ppermute x4, starting transfers between devices, ring(): lax.ppermute(to_previous, axis, backward)  8.76 us
    ppermute x4, starting transfers between devices, ring(): lax.ppermute(to_next, axis, forward)  5.06 us
    ppermute x4, waiting for transfers between devices, ring(): lax.ppermute(to_previous, axis, backward)  3.69 us
    pallas_call x1, Pallas kernels, per_device(): call(functools.partial(first_kernel, last), [(6, EXT, CC), (2, 6, EXT, CC...  3.65 us
    ppermute x1, starting transfers between devices, per_device(): sums = keep + lax.ppermute(send, 'core', [(0, 1), (1, 0)])  3.02 us
  transfers between devices with their start and end apart: 10, of which 5 were waited for; matrix products, arithmetic and copies ran while one was open for 0% of the time, Pallas kernels for 5%

profile of v9, /device:TPU:1, one launch (start us, length us, event | category | flops | bytes accessed | tf_op | source)
XLA Modules:
  0.0 84.5 jit_solution(9011468348383706927)
XLA Ops:
  1.3 2.9 %shard_map.94 = (f32[256,1,256]{2,1,0:T(1,128)}, f32[7,32,128]{2,1,0:T(8,128)}, f32[224,128]{1,0:T(8,128)}, f32[224,128]{1,0:T(8,128)}) custom-call(s32[1]{0:T(128)} %bitcast.14.levels, f32[1,128]{1,0:T(1,128)} %bitcast.17, f32[1,128]{1,0:T(1,128)} %bitcast.18, f32[3,22,128]{2,1,0:T(8,128)} %state.1, f32[3,22,128]{2,1,0:T(8,128)} %adjoint.1, ...), custom_call_target="tpu_custom_call" | custom-call | flops 1000000000 | bytes 1048576 | tf_op jit(solution)/shard_map/pallas_call | solution.py:524
  4.2 2.5 %collective-permute-start = (f32[224,128]{1,0:T(8,128)}, f32[224,128]{1,0:T(8,128)S(1)}, u32[]{:S(2)}, u32[]{:S(2)}) collective-permute-start(f32[224,128]{1,0:T(8,128)} %get-tuple-element.35), channel_id=1, source_target_pairs={{0,1},{1,2},{2,3},{3,4},{4,5},{5,6},{6,7},{7,8},{8,9},{9,10},{10,1... | collective-permute-start | bytes 344072 | tf_op jit(solution)/shard_map/ppermute | solution.py:513
  6.8 6.2 %collective-permute-start.1 = (f32[224,128]{1,0:T(8,128)}, f32[224,128]{1,0:T(8,128)S(1)}, u32[]{:S(2)}, u32[]{:S(2)}) collective-permute-start(f32[224,128]{1,0:T(8,128)} %get-tuple-element.36), channel_id=1, source_target_pairs={{1,0},{2,1},{3,2},{4,3},{5,4},{6,5},{7,6},{8,7},{9,8},{10,9},{11,1... | collective-permute-start | bytes 344072 | tf_op jit(solution)/shard_map/ppermute | solution.py:513
  13.0 10.2 %all-to-all-start = ((f32[256,1,256]{2,1,0:T(1,128)}), f32[256,1,256]{2,1,0:T(1,128)S(1)}, u32[]{:S(2)}, u32[]{:S(2)}) async-start(f32[256,1,256]{2,1,0:T(1,128)} %get-tuple-element.34), calls=%async_computation | async-start | bytes 524288 | tf_op jit(solution)/shard_map/all_to_all | solution.py:535
  23.2 0.0 collective-permute-done.from_left
  23.2 0.0 collective-permute-done.1.from_right
  23.2 0.0 copy-start.1
  23.2 0.9 %copy-done.1 = f32[7,32,128]{2,1,0:T(8,128)S(1)} copy-done((f32[7,32,128]{2,1,0:T(8,128)S(1)}, f32[7,32,128]{2,1,0:T(8,128)}, u32[]{:S(2)}) %copy-start.1) | copy-done | bytes 114712
  24.1 0.1 shard_map.95
  24.3 1.6 %collective-permute-start.2 = (f32[2,16,128]{2,1,0:T(8,128)S(1)}, f32[2,16,128]{2,1,0:T(8,128)S(1)}, u32[]{:S(2)}, u32[]{:S(2)}) collective-permute-start(f32[2,16,128]{2,1,0:T(8,128)S(1)} %get-tuple-element.38), channel_id=1, source_target_pairs={{0,32},{32,64},{64,96},{96,128},{128,160},{160,192},{192,224},{224... | collective-permute-start | bytes 49160 | tf_op jit(solution)/shard_map/ppermute | solution.py:513
  25.9 0.5 collective-permute-start.3
  26.5 0.1 pad_add_fusion.info
  26.5 0.6 collective-permute-done.2.from_up
  27.1 2.3 %collective-permute-done.3.from_down = f32[2,16,128]{2,1,0:T(8,128)S(1)} collective-permute-done((f32[2,16,128]{2,1,0:T(8,128)S(1)}, f32[2,16,128]{2,1,0:T(8,128)S(1)}, u32[]{:S(2)}, u32[]{:S(2)}) %collective-permute-start.3) | collective-permute-done | bytes 16416 | tf_op jit(solution)/shard_map/ppermute | solution.py:513
  29.4 0.0 copy-start
  29.4 0.7 shard_map.96
  30.1 0.0 copy-start.2
  30.1 8.9 %all-to-all-done = f32[256,1,256]{2,1,0:T(1,128)S(1)} async-done(((f32[256,1,256]{2,1,0:T(1,128)}), f32[256,1,256]{2,1,0:T(1,128)S(1)}, u32[]{:S(2)}, u32[]{:S(2)}) %all-to-all-start) | async-done | bytes 262176 | tf_op jit(solution)/shard_map/all_to_all | solution.py:535
  39.0 0.0 copy-done
  39.0 3.6 %shard_map.97 = (f32[6,24,128]{2,1,0:T(8,128)S(1)}, f32[2,6,24,128]{3,2,1,0:T(8,128)S(1)}, f32[2,24,128]{2,1,0:T(8,128)S(1)}, f32[2,24,128]{2,1,0:T(8,128)S(1)},...) custom-call(s32[2]{0:T(128)S(1)} %pad_add_fusion.info, f32[256,256]{1,0:T(8,128)S(1)} %bitcast.16, ...), custom_call_target="tpu_custom_call" | custom-call | tf_op jit(solution)/shard_map/pallas_call | solution.py:553
  42.6 0.7 collective-permute-start.4
  43.3 0.2 collective-permute-start.5
  43.5 0.0 copy-done.2
  43.5 1.7 %shard_map.99.sums0 = f32[256,128]{1,0:T(8,128)S(1)} custom-call(s32[2]{0:T(128)S(1)} %pad_add_fusion.info, f32[7,32,128]{2,1,0:T(8,128)S(1)} %copy-done.2, f32[2,32,128]{2,1,0:T(8,128)S(1)} %get-tuple-element.49.tcell, f32[2,32,128]{2,1,0:T(8,128)S(1)} %get-tuple-element.55.dcell, f32[6,32,128]{2,1,0:T(8,128)S(1)} %get-tuple-element.40.main_f, ...), custom_call_target="tpu_custom_call" | custom-call | flops 300000000 | bytes 1048576 | tf_op jit(solution)/shard_map/pallas_call | solution.py:564
  45.1 0.0 collective-permute-done.4.from_up
  45.2 1.4 %collective-permute-done.5.from_down = f32[2,24,128]{2,1,0:T(8,128)S(1)} collective-permute-done((f32[2,24,128]{2,1,0:T(8,128)S(1)}, f32[2,24,128]{2,1,0:T(8,128)S(1)}, u32[]{:S(2)}, u32[]{:S(2)}) %collective-permute-start.5) | collective-permute-done | bytes 24608 | tf_op jit(solution)/shard_map/ppermute | solution.py:513
  46.6 2.2 %shard_map.98 = (f32[6,32,128]{2,1,0:T(8,128)S(1)}, f32[6,32,128]{2,1,0:T(8,128)S(1)}, f32[6,24,128]{2,1,0:T(8,128)S(1)}, f32[2,6,24,128]{3,2,1,0:T(8,128)S(1)},...) custom-call(s32[2]{0:T(128)S(1)} %pad_add_fusion.info, f32[2,6,24,128]{3,2,1,0:T(8,128)S(1)} %get-tuple-element.46.local, ...), custom_call_target="tpu_custom_call" | custom-call | tf_op jit(solution)/shard_map/pallas_call | solution.py:568
  48.8 0.2 collective-permute-start.6
  49.0 1.8 %collective-permute-start.7 = (f32[2,24,128]{2,1,0:T(8,128)S(1)}, f32[2,24,128]{2,1,0:T(8,128)S(1)}, u32[]{:S(2)}, u32[]{:S(2)}) collective-permute-start(f32[2,24,128]{2,1,0:T(8,128)S(1)} %get-tuple-element.54), channel_id=1, source_target_pairs={{32,0},{64,32},{96,64},{128,96},{160,128},{192,160},{224,192},{0,2... | collective-permute-start | bytes 73736 | tf_op jit(solution)/shard_map/ppermute | solution.py:513
  50.8 1.8 %shard_map.100.sums1 = f32[256,256]{1,0:T(8,128)S(1)} custom-call(s32[2]{0:T(128)S(1)} %pad_add_fusion.info, f32[7,32,128]{2,1,0:T(8,128)S(1)} %copy-done.2, f32[2,32,128]{2,1,0:T(8,128)S(1)} %get-tuple-element.49.tcell, f32[6,32,128]{2,1,0:T(8,128)S(1)} %get-tuple-element.40.main_f, f32[6,32,128]{2,1,0:T(8,128)S(1)} %get-tuple-element.41.side_f, ...), custom_call_target="tpu_custom_call" | custom-call | flops 500000000 | bytes 1048576 | tf_op jit(solution)/shard_map/pallas_call | solution.py:574
  52.6 0.0 collective-permute-done.6.from_up
  52.6 0.0 collective-permute-done.7.from_down
  52.6 2.0 %shard_map.101 = (f32[6,32,128]{2,1,0:T(8,128)S(1)}, f32[128,768]{1,0:T(8,128)S(1)}, f32[128,768]{1,0:T(8,128)S(1)}) custom-call(s32[2]{0:T(128)S(1)} %pad_add_fusion.info, f32[7,32,128]{2,1,0:T(8,128)S(1)} %copy-done.2, f32[6,24,128]{2,1,0:T(8,128)S(1)} %get-tuple-element.45.resid, f32[6,24,128]{2,1,0:T(8,128)S(1)} %get-tuple-element.50.image, ...), custom_call_target="tpu_custom_call" | custom-call | tf_op jit(solution)/shard_map/pallas_call | solution.py:578
  54.6 3.0 %collective-permute-start.8 = (f32[128,768]{1,0:T(8,128)S(1)}, f32[128,768]{1,0:T(8,128)S(1)}, u32[]{:S(2)}, u32[]{:S(2)}) collective-permute-start(f32[128,768]{1,0:T(8,128)S(1)} %get-tuple-element.58), channel_id=1, source_target_pairs={{0,32},{32,0},{1,33},{33,1},{2,34},{34,2},{3,35},{35,3},{4,36},{36... | collective-permute-start | bytes 1179656 | tf_op jit(solution)/shard_map/ppermute | solution.py:583
  57.6 1.3 %collective-permute-done.8 = f32[128,768]{1,0:T(8,128)S(1)} collective-permute-done((f32[128,768]{1,0:T(8,128)S(1)}, f32[128,768]{1,0:T(8,128)S(1)}, u32[]{:S(2)}, u32[]{:S(2)}) %collective-permute-start.8) | collective-permute-done | bytes 393248 | tf_op jit(solution)/shard_map/ppermute | solution.py:583
  59.0 0.4 copy.11
  59.4 24.3 %all_to_all.16 = f32[128,1,768]{2,1,0:T(1,128)S(1)} all-to-all(f32[128,1,768]{2,1,0:T(1,128)S(1)} %copy.11), channel_id=1, replica_groups=mesh['y'=4,'core'=2,'pcol'=32] {'y','pcol'}, dimensions={0} | all-to-all | bytes 786432 | tf_op jit(solution)/shard_map/all_to_all | solution.py:584
  83.8 0.8 shard_map.102
  (3 shorter events, 0.1 us)
Async XLA Ops:
  4.2 19.0 %collective-permute-start = (f32[224,128]{1,0:T(8,128)}, f32[224,128]{1,0:T(8,128)S(1)}, u32[]{:S(2)}, u32[]{:S(2)}) collective-permute-start(f32[224,128]{1,0:T(8,128)} %get-tuple-element.35), channel_id=1, source_target_pairs={{0,1},{1,2},{2,3},{3,4},{4,5},{5,6},{6,7},{7,8},{8,9},{9,10},{10,1... | collective-permute-start | bytes 344072 | tf_op jit(solution)/shard_map/ppermute | solution.py:513
  6.8 16.5 %collective-permute-start.1 = (f32[224,128]{1,0:T(8,128)}, f32[224,128]{1,0:T(8,128)S(1)}, u32[]{:S(2)}, u32[]{:S(2)}) collective-permute-start(f32[224,128]{1,0:T(8,128)} %get-tuple-element.36), channel_id=1, source_target_pairs={{1,0},{2,1},{3,2},{4,3},{5,4},{6,5},{7,6},{8,7},{9,8},{10,9},{11,1... | collective-permute-start | bytes 344072 | tf_op jit(solution)/shard_map/ppermute | solution.py:513
  13.0 26.0 %all-to-all-start = ((f32[256,1,256]{2,1,0:T(1,128)}), f32[256,1,256]{2,1,0:T(1,128)S(1)}, u32[]{:S(2)}, u32[]{:S(2)}) async-start(f32[256,1,256]{2,1,0:T(1,128)} %get-tuple-element.34), calls=%async_computation | async-start | bytes 524288 | tf_op jit(solution)/shard_map/all_to_all | solution.py:535
  23.2 0.9 %copy-start.1 = (f32[7,32,128]{2,1,0:T(8,128)S(1)}, f32[7,32,128]{2,1,0:T(8,128)}, u32[]{:S(2)}) copy-start(f32[7,32,128]{2,1,0:T(8,128)} %get-tuple-element.33.frame) | copy-start | bytes 344068
  24.3 2.8 %collective-permute-start.2 = (f32[2,16,128]{2,1,0:T(8,128)S(1)}, f32[2,16,128]{2,1,0:T(8,128)S(1)}, u32[]{:S(2)}, u32[]{:S(2)}) collective-permute-start(f32[2,16,128]{2,1,0:T(8,128)S(1)} %get-tuple-element.38), channel_id=1, source_target_pairs={{0,32},{32,64},{64,96},{96,128},{128,160},{160,192},{192,224},{224... | collective-permute-start | bytes 49160 | tf_op jit(solution)/shard_map/ppermute | solution.py:513
  25.9 3.5 %collective-permute-start.3 = (f32[2,16,128]{2,1,0:T(8,128)S(1)}, f32[2,16,128]{2,1,0:T(8,128)S(1)}, u32[]{:S(2)}, u32[]{:S(2)}) collective-permute-start(f32[2,16,128]{2,1,0:T(8,128)S(1)} %get-tuple-element.39), channel_id=1, source_target_pairs={{32,0},{64,32},{96,64},{128,96},{160,128},{192,160},{224,192},{0,2... | collective-permute-start | bytes 49160 | tf_op jit(solution)/shard_map/ppermute | solution.py:513
  29.4 9.6 %copy-start = (f32[72,72,128]{2,1,0:T(8,128)S(1)}, f32[72,72,128]{2,1,0:T(8,128)}, u32[]{:S(2)}) copy-start(f32[72,72,128]{2,1,0:T(8,128)} %mats.3) | copy-start | bytes 7962628
  30.1 13.4 %copy-start.2 = (f32[7,32,128]{2,1,0:T(8,128)S(1)}, f32[7,32,128]{2,1,0:T(8,128)}, u32[]{:S(2)}) copy-start(f32[7,32,128]{2,1,0:T(8,128)} %get-tuple-element.33.frame) | copy-start | bytes 344068
  42.6 2.5 %collective-permute-start.4 = (f32[2,24,128]{2,1,0:T(8,128)S(1)}, f32[2,24,128]{2,1,0:T(8,128)S(1)}, u32[]{:S(2)}, u32[]{:S(2)}) collective-permute-start(f32[2,24,128]{2,1,0:T(8,128)S(1)} %get-tuple-element.47), channel_id=1, source_target_pairs={{0,32},{32,64},{64,96},{96,128},{128,160},{160,192},{192,224},{224... | collective-permute-start | bytes 73736 | tf_op jit(solution)/shard_map/ppermute | solution.py:513
  43.3 3.3 %collective-permute-start.5 = (f32[2,24,128]{2,1,0:T(8,128)S(1)}, f32[2,24,128]{2,1,0:T(8,128)S(1)}, u32[]{:S(2)}, u32[]{:S(2)}) collective-permute-start(f32[2,24,128]{2,1,0:T(8,128)S(1)} %get-tuple-element.48), channel_id=1, source_target_pairs={{32,0},{64,32},{96,64},{128,96},{160,128},{192,160},{224,192},{0,2... | collective-permute-start | bytes 73736 | tf_op jit(solution)/shard_map/ppermute | solution.py:513
  48.8 3.8 %collective-permute-start.6 = (f32[2,24,128]{2,1,0:T(8,128)S(1)}, f32[2,24,128]{2,1,0:T(8,128)S(1)}, u32[]{:S(2)}, u32[]{:S(2)}) collective-permute-start(f32[2,24,128]{2,1,0:T(8,128)S(1)} %get-tuple-element.53), channel_id=1, source_target_pairs={{0,32},{32,64},{64,96},{96,128},{128,160},{160,192},{192,224},{224... | collective-permute-start | bytes 73736 | tf_op jit(solution)/shard_map/ppermute | solution.py:513
  49.0 3.6 %collective-permute-start.7 = (f32[2,24,128]{2,1,0:T(8,128)S(1)}, f32[2,24,128]{2,1,0:T(8,128)S(1)}, u32[]{:S(2)}, u32[]{:S(2)}) collective-permute-start(f32[2,24,128]{2,1,0:T(8,128)S(1)} %get-tuple-element.54), channel_id=1, source_target_pairs={{32,0},{64,32},{96,64},{128,96},{160,128},{192,160},{224,192},{0,2... | collective-permute-start | bytes 73736 | tf_op jit(solution)/shard_map/ppermute | solution.py:513
  54.6 4.4 %collective-permute-start.8 = (f32[128,768]{1,0:T(8,128)S(1)}, f32[128,768]{1,0:T(8,128)S(1)}, u32[]{:S(2)}, u32[]{:S(2)}) collective-permute-start(f32[128,768]{1,0:T(8,128)S(1)} %get-tuple-element.58), channel_id=1, source_target_pairs={{0,32},{32,0},{1,33},{33,1},{2,34},{34,2},{3,35},{35,3},{4,36},{36... | collective-permute-start | bytes 1179656 | tf_op jit(solution)/shard_map/ppermute | solution.py:583

commit v10 on v9

--- a/solution.py
+++ b/solution.py
@@ -146,8 +146,13 @@
     written.wait()
 
 
+def by_turn(prow, up, down):
+    even = prow % 2 == 0
+    return jnp.where(even, down, up), jnp.where(even, up, down)
+
+
 def rows_kernel(
-    frame, from_left, from_right, side_out, up_out, down_out, levels_out, edge_out,
+    info, frame, from_left, from_right, side_out, one_out, two_out, levels_out, edge_out,
 ):
     left_end, right_end = from_left[EDGE:, :], from_right[EDGE:, :]
     tiles = unpack_edges(left_end, right_end, 21, WIDE)
@@ -155,12 +160,13 @@
     for f in range(7):
         for g in range(3):
             side_out[f, 8 + 8 * g:16 + 8 * g, :] = tiles[3 * f + g]
-    up_out[...] = jnp.zeros_like(up_out)
-    down_out[...] = jnp.zeros_like(down_out)
+    one_out[...] = jnp.zeros_like(one_out)
+    two_out[...] = jnp.zeros_like(two_out)
     for tile, ref in ((0, frame), (1, side_out)):
         for f in range(7):
-            up_out[tile, 2 * f:2 * f + 2, :] = ref[f, 8:10, :]
-            down_out[tile, 2 * f:2 * f + 2, :] = ref[f, 6 + CR:8 + CR, :]
+            one, two = by_turn(info[1], ref[f, 8:10, :], ref[f, 6 + CR:8 + CR, :])
+            one_out[tile, 2 * f:2 * f + 2, :] = one
+            two_out[tile, 2 * f:2 * f + 2, :] = two
     upper = iota((8, CC), 1) >= 64
     levels_out[...] = jnp.where(upper, left_end, pltpu.roll(right_end, 64, 1))
     lane = iota((BLK, CC), 1)
@@ -231,24 +237,27 @@
     lax.fori_loop(0, top, term, 0)
 
 
-def put_results(total, side_total, local_out, up_out, down_out):
-    up_out[...] = jnp.zeros_like(up_out)
-    down_out[...] = jnp.zeros_like(down_out)
+def put_results(prow, total, side_total, local_out, one_out, two_out):
+    one_out[...] = jnp.zeros_like(one_out)
+    two_out[...] = jnp.zeros_like(two_out)
     for tile, ref in ((0, total), (1, side_total)):
         local_out[tile] = ref[...].reshape(6, EXT, CC)
         for f in range(6):
-            up_out[tile, 3 * f:3 * f + 3, :] = local_out[tile, f, 0:3, :]
-            down_out[tile, 3 * f:3 * f + 3, :] = local_out[tile, f, EXT - 3:EXT, :]
-
-
-def join(prow, last, local, from_up, from_down, frames):
+            one, two = by_turn(prow, local_out[tile, f, 0:3, :], local_out[tile, f, EXT - 3:EXT, :])
+            one_out[tile, 3 * f:3 * f + 3, :] = one
+            two_out[tile, 3 * f:3 * f + 3, :] = two
+
+
+def join(prow, last, local, got_one, got_two, frames):
     inside = grid_mask(prow, last, 0, FR)
     for tile, frame in enumerate(frames):
         frame[...] = jnp.zeros_like(frame)
         frame[:, 7:7 + EXT, :] = local[tile]
         for f in range(6):
-            frame[f, 6:9, :] += jnp.where(prow == 0, 0.0, from_up[tile, 3 * f:3 * f + 3, :])
-            frame[f, 7 + CR:10 + CR, :] += jnp.where(prow == last, 0.0, from_down[tile, 3 * f:3 * f + 3, :])
+            cut = slice(3 * f, 3 * f + 3)
+            above, below = by_turn(prow, got_one[tile, cut, :], got_two[tile, cut, :])
+            frame[f, 6:9, :] += jnp.where(prow == 0, 0.0, above)
+            frame[f, 7 + CR:10 + CR, :] += jnp.where(prow == last, 0.0, below)
         frame[...] = frame[...] * inside[None]
 
 
@@ -323,20 +332,22 @@
     ]
 
 
-def place_kernel(last, info, frame, side, from_up, from_down, main_f, side_f, cells, index_scr):
+def place_kernel(last, info, frame, side, got_one, got_two, main_f, side_f, cells, index_scr):
     inside = grid_mask(info[1], last, 0, FR)
     for tile, ref, source in ((0, main_f, frame), (1, side_f, side)):
         for f in range(7):
             out = ref.at[f] if f < 6 else index_scr.at[tile]
             out[...] = source[f]
-            out[6:8, :] = from_up[tile, 2 * f:2 * f + 2, :] * inside[6:8]
-            out[8 + CR:10 + CR, :] = from_down[tile, 2 * f:2 * f + 2, :] * inside[8 + CR:10 + CR]
+            cut = slice(2 * f, 2 * f + 2)
+            above, below = by_turn(info[1], got_one[tile, cut, :], got_two[tile, cut, :])
+            out[6:8, :] = above * inside[6:8]
+            out[8 + CR:10 + CR, :] = below * inside[8 + CR:10 + CR]
     place_cells([index_scr[tile].astype(jnp.int32) for tile in range(2)], cells)
 
 
 def first_kernel(
     last, info, table, main_f, side_f, cells, mats, edge, levels,
-    resid_out, local_out, up_out, down_out, tcell, dcell,
+    resid_out, local_out, one_out, two_out, tcell, dcell,
     vec, total, side_vec, side_total,
 ):
     level, prow = info[0], info[1]
@@ -361,7 +372,7 @@
             resid_out[...] = rhs
         out[...] = rhs.reshape(2, BLK, CC)
     local_solve(mats, edge, vec, total, side_vec, side_total, level, levels)
-    put_results(total, side_total, local_out, up_out, down_out)
+    put_results(prow, total, side_total, local_out, one_out, two_out)
 
 
 def stiffness(main_f, side_f, main_t, side_t, lo, hi):
@@ -374,13 +385,13 @@
 
 
 def second_kernel(
-    last, info, local, from_up, from_down, tcell, mats, edge, levels,
-    main_f, side_f, image_out, local_out, up_out, down_out,
+    last, info, local, got_one, got_two, tcell, mats, edge, levels,
+    main_f, side_f, image_out, local_out, one_out, two_out,
     vec, total, side_vec, side_total,
 ):
     level, prow = info[0], info[1]
     frames = (main_f, side_f)
-    join(prow, last, local, from_up, from_down, frames)
+    join(prow, last, local, got_one, got_two, frames)
     lo, hi = 7, 7 + EXT
     inside = grid_mask(prow, last, lo, EXT)
     for tile, out in ((0, vec), (1, side_vec)):
@@ -391,7 +402,7 @@
             image_out[...] = image
         out[...] = image.reshape(2, BLK, CC)
     local_solve(mats, edge, vec, total, side_vec, side_total, level, levels)
-    put_results(total, side_total, local_out, up_out, down_out)
+    put_results(prow, total, side_total, local_out, one_out, two_out)
 
 
 def dot3(a, b, i, j):
@@ -448,11 +459,11 @@
 
 
 def third_kernel(
-    last, n_col, info, frame, resid, image, zframe, local, from_up, from_down,
+    last, n_col, info, frame, resid, image, zframe, local, got_one, got_two,
     tcell, main_f, side_f, sums0, sums1,
     wframe, keep_out, send_out, wside, left_op, right_op,
 ):
-    join(info[1], last, local, from_up, from_down, (wframe, wside))
+    join(info[1], last, local, got_one, got_two, (wframe, wside))
     v = stiffness(wframe, wside, tcell.at[0], tcell.at[1], LO, HI)
     r = resid[:, 1:1 + CR, :]
     q = image[:, 1:1 + CR, :]
@@ -474,10 +485,10 @@
     for half, out in ((0, keep_out), (1, send_out)):
         count = out.shape[0]
         rows = slice(128 * half, 128 * half + count)
-        out[:, 0:CC] = jnp.broadcast_to(dots, (count, CC))
-        out[:, CC:2 * CC] = sums0[rows, :]
-        out[:, 2 * CC:4 * CC] = sums1[rows, :]
-        out[:, 4 * CC:] = sums[rows]
+        out[:, 0, 0:CC] = jnp.broadcast_to(dots, (count, CC))
+        out[:, 0, CC:2 * CC] = sums0[rows, :]
+        out[:, 0, 2 * CC:4 * CC] = sums1[rows, :]
+        out[:, 0, 4 * CC:] = sums[rows]
 
 
 def last_kernel(got, zframe, wframe, tangent, second, owned):
@@ -507,6 +518,12 @@
     )
 
 
+def pairwise(count, one, two):
+    first = [(i, i ^ 1) for i in range(count)]
+    second = [(i, min(max(i + (1 if i % 2 else -1), 0), count - 1)) for i in range(count)]
+    return lax.ppermute(one, ROW, first), lax.ppermute(two, ROW, second)
+
+
 def ring(axis, count, to_next, to_previous):
     forward = [(i, (i + 1) % count) for i in range(count)]
     backward = [(b, a) for a, b in forward]
@@ -518,7 +535,7 @@
     n_dev = n_row * n_col
     last = n_row - 1
     info = jnp.stack([levels[0, 0], lax.axis_index(ROW).astype(jnp.int32)])
-    rows = functools.partial(ring, ROW, n_row)
+    rows = functools.partial(pairwise, n_row)
     cols = functools.partial(ring, "pcol", n_col)
 
     own, frame, first, end = call(
@@ -536,10 +553,10 @@
     if n_dev < 256:
         table = jnp.concatenate([table, jnp.zeros((256 - n_dev, 2 * DV), F32)], axis=0)
     from_left, from_right = cols(end, first)
-    side, up, down, around, edge = call(
-        rows_kernel, [(7, FR, CC), (2, 16, CC), (2, 16, CC), (8, CC), (3, BLK, CC)], [VMEM] * 3,
+    side, one, two, around, edge = call(
+        rows_kernel, [(7, FR, CC), (2, 16, CC), (2, 16, CC), (8, CC), (3, BLK, CC)], [SMEM] + [VMEM] * 3,
         work=10**11,
-    )(frame, from_left, from_right)
+    )(info, frame, from_left, from_right)
 
     solve_scratch = [pltpu.VMEM((2, BLK, CC), F32)] * 4
     pairs = len(PAIRS) + 1
@@ -549,8 +566,8 @@
             (6, FR, CC), (6, FR, CC), jax.ShapeDtypeStruct((pairs, 2 * CC), jnp.int32),
         ],
         [SMEM] + [VMEM] * 4, [pltpu.VMEM((2, FR, CC), F32)], work=3 * 10**9,
-    )(info, frame, side, *rows(down, up))
-    resid, local, up, down, tcell, dcell = call(
+    )(info, frame, side, *rows(one, two))
+    resid, local, one, two, tcell, dcell = call(
         functools.partial(first_kernel, last),
         [
             (6, EXT, CC), (2, 6, EXT, CC), (2, 24, CC), (2, 24, CC), (2, FR, CC), (2, FR, CC),
@@ -565,23 +582,23 @@
         functools.partial(known_sums_kernel, n_col), [(256, DV)], [SMEM] + [VMEM] * 5, operands(1),
         work=3 * 10**8,
     )(info, frame, tcell, dcell, main_f, side_f)
-    zframe, zside, image, local, up, down = call(
+    zframe, zside, image, local, one, two = call(
         functools.partial(second_kernel, last),
         [(6, FR, CC), (6, FR, CC), (6, EXT, CC), (2, 6, EXT, CC), (2, 24, CC), (2, 24, CC)],
         [SMEM] + [VMEM] * 7,
         solve_scratch,
-    )(info, local, *rows(down, up), tcell, blocks, edge, around)
+    )(info, local, *rows(one, two), tcell, blocks, edge, around)
     (sums1,) = call(
         functools.partial(solved_sums_kernel, n_col), [(256, 2 * DV)], [SMEM] + [VMEM] * 6,
         operands(2), work=5 * 10**8,
     )(info, frame, tcell, main_f, side_f, zframe, zside)
     wframe, keep, send = call(
         functools.partial(third_kernel, last, n_col),
-        [(6, FR, CC)] + [(n_dev // 2, 6 * CC)] * 2, [SMEM] + [VMEM] * 12,
+        [(6, FR, CC)] + [(n_dev // 2, 1, 6 * CC)] * 2, [SMEM] + [VMEM] * 12,
         [pltpu.VMEM((6, FR, CC), F32)] + operands(2),
-    )(info, frame, resid, image, zframe, local, *rows(down, up), tcell, main_f, side_f, sums0, sums1)
+    )(info, frame, resid, image, zframe, local, *rows(one, two), tcell, main_f, side_f, sums0, sums1)
     sums = keep + lax.ppermute(send, "core", [(0, 1), (1, 0)])
-    got = lax.all_to_all(sums, ("y", "pcol"), 0, 0, tiled=True)
+    got = lax.all_to_all(sums, ("y", "pcol"), 0, 0, tiled=True).reshape(n_dev // 2, 6 * CC)
     tangent, second, owned = call(
         last_kernel, [(3, CR, CC), (3, CR, CC), (1, CC)], [VMEM] * 3
     )(got, zframe, wframe)

time: 84.7 us -> 86.5 us (1.021)
  waiting for transfers between devices: 14.5 us -> 12.6 us
  starting transfers between devices: 27 us -> 28.9 us
  Pallas kernels: 15.8 us -> 17.4 us
    ppermute x0 -> x6, starting transfers between devices: none -> 9.85 us  [pairwise(): return (lax.ppermute(one, ROW, first), lax.ppermute(two, ROW, second))]
    ppermute x0 -> x6, waiting for transfers between devices: none -> 5.18 us  [pairwise(): return (lax.ppermute(one, ROW, first), lax.ppermute(two, ROW, second))]
    ppermute x4 -> x1, waiting for transfers between devices: 3.69 us -> 0.01 us  [ring(): lax.ppermute(to_previous, axis, backward)]
    all_to_all x1, waiting for transfers between devices: 8.88 us -> 5.69 us  [per_device(): lax.all_to_all(own, ROW + ('pcol',), 0, 0, tiled=True)]
    ppermute x1, starting transfers between devices: 3.02 us -> 0.09 us  [per_device(): sums = keep + lax.ppermute(send, 'core', [(0, 1), (1, 0)])]
    ppermute x4 -> x1, starting transfers between devices: 8.76 us -> 6.22 us  [ring(): lax.ppermute(to_previous, axis, backward)]
    ppermute x4 -> x1, starting transfers between devices: 5.06 us -> 2.54 us  [ring(): lax.ppermute(to_next, axis, forward)]
  transfers between devices with their start and end apart: 10 -> 10, of which waited for: 5 -> 5; matrix products, arithmetic and copies ran while one was open for 0% -> 0% of each run, Pallas kernels for 5% -> 6%
where the time goes in v10:
time: 86.5 us; the launch traced here: 85.8 us
  starting transfers between devices  28.9 us (33%)
  blocking collectives  24 us (28%)
  Pallas kernels  17.4 us (20%)
  waiting for transfers between devices  12.6 us (15%)
  between operations  1.46 us (2%)
  local copies, waits for them, and re-layouts  0.95 us (1%)
    all_to_all x1, blocking collectives, per_device(): lax.all_to_all(sums, ('y', 'pcol'), 0, 0, tiled=True)  24 us
    all_to_all x1, starting transfers between devices, per_device(): lax.all_to_all(own, ROW + ('pcol',), 0, 0, tiled=True)  10.2 us
    ppermute x6, starting transfers between devices, pairwise(): return (lax.ppermute(one, ROW, first), lax.ppermute(two, ROW, second))  9.85 us
    ppermute x1, starting transfers between devices, ring(): lax.ppermute(to_previous, axis, backward)  6.22 us
    all_to_all x1, waiting for transfers between devices, per_device(): lax.all_to_all(own, ROW + ('pcol',), 0, 0, tiled=True)  5.69 us
    ppermute x6, waiting for transfers between devices, pairwise(): return (lax.ppermute(one, ROW, first), lax.ppermute(two, ROW, second))  5.18 us
    pallas_call x1, Pallas kernels, per_device(): call(functools.partial(first_kernel, last), [(6, EXT, CC), (2, 6, EXT, CC...  4.09 us
    pallas_call x1, Pallas kernels, per_device(): call(start_kernel, [(n_dev, 1, 2 * DV), (7, FR, CC), (EDGE + 8, CC), (EDG...  2.92 us
  transfers between devices with their start and end apart: 10, of which 5 were waited for; matrix products, arithmetic and copies ran while one was open for 0% of the time, Pallas kernels for 6%

profile of v10, /device:TPU:1, one launch (start us, length us, event | category | flops | bytes accessed | tf_op | source)
XLA Modules:
  0.0 85.8 jit_solution(6351504976572633678)
XLA Ops:
  1.3 2.9 %shard_map.94 = (f32[256,1,256]{2,1,0:T(1,128)}, f32[7,32,128]{2,1,0:T(8,128)}, f32[224,128]{1,0:T(8,128)}, f32[224,128]{1,0:T(8,128)}) custom-call(s32[1]{0:T(128)} %bitcast.12.levels, f32[1,128]{1,0:T(1,128)} %bitcast.15, f32[1,128]{1,0:T(1,128)} %bitcast.16, f32[3,22,128]{2,1,0:T(8,128)} %state.1, f32[3,22,128]{2,1,0:T(8,128)} %adjoint.1, ...), custom_call_target="tpu_custom_call" | custom-call | flops 1000000000 | bytes 1048576 | tf_op jit(solution)/shard_map/pallas_call | solution.py:541
  4.2 2.5 %collective-permute-start = (f32[224,128]{1,0:T(8,128)}, f32[224,128]{1,0:T(8,128)S(1)}, u32[]{:S(2)}, u32[]{:S(2)}) collective-permute-start(f32[224,128]{1,0:T(8,128)} %get-tuple-element.35), channel_id=1, source_target_pairs={{0,1},{1,2},{2,3},{3,4},{4,5},{5,6},{6,7},{7,8},{8,9},{9,10},{10,1... | collective-permute-start | bytes 344072 | tf_op jit(solution)/shard_map/ppermute | solution.py:530
  6.8 6.2 %collective-permute-start.1 = (f32[224,128]{1,0:T(8,128)}, f32[224,128]{1,0:T(8,128)S(1)}, u32[]{:S(2)}, u32[]{:S(2)}) collective-permute-start(f32[224,128]{1,0:T(8,128)} %get-tuple-element.36), channel_id=1, source_target_pairs={{1,0},{2,1},{3,2},{4,3},{5,4},{6,5},{7,6},{8,7},{9,8},{10,9},{11,1... | collective-permute-start | bytes 344072 | tf_op jit(solution)/shard_map/ppermute | solution.py:530
  13.0 10.2 %all-to-all-start = ((f32[256,1,256]{2,1,0:T(1,128)}), f32[256,1,256]{2,1,0:T(1,128)S(1)}, u32[]{:S(2)}, u32[]{:S(2)}) async-start(f32[256,1,256]{2,1,0:T(1,128)} %get-tuple-element.34), calls=%async_computation | async-start | bytes 524288 | tf_op jit(solution)/shard_map/all_to_all | solution.py:552
  23.2 0.1 pad_add_fusion.info
  23.3 0.0 collective-permute-done.from_left
  23.3 0.0 collective-permute-done.1.from_right
  23.3 0.0 copy-start.1
  23.3 0.9 %copy-done.1 = f32[7,32,128]{2,1,0:T(8,128)S(1)} copy-done((f32[7,32,128]{2,1,0:T(8,128)S(1)}, f32[7,32,128]{2,1,0:T(8,128)}, u32[]{:S(2)}) %copy-start.1) | copy-done | bytes 114712
  24.2 0.7 shard_map.95
  24.9 2.2 %collective-permute-start.2 = (f32[2,16,128]{2,1,0:T(8,128)S(1)}, f32[2,16,128]{2,1,0:T(8,128)S(1)}, u32[]{:S(2)}, u32[]{:S(2)}) collective-permute-start(f32[2,16,128]{2,1,0:T(8,128)S(1)} %get-tuple-element.38), channel_id=1, source_target_pairs={{0,32},{32,0},{64,96},{96,64},{128,160},{160,128},{192,224},{224,1... | collective-permute-start | bytes 49160 | tf_op jit(solution)/shard_map/ppermute | solution.py:524
  27.1 1.9 %collective-permute-start.3 = (f32[2,16,128]{2,1,0:T(8,128)S(1)}, f32[2,16,128]{2,1,0:T(8,128)S(1)}, u32[]{:S(2)}, u32[]{:S(2)}) collective-permute-start(f32[2,16,128]{2,1,0:T(8,128)S(1)} %get-tuple-element.39), channel_id=1, source_target_pairs={{0,0},{32,64},{64,32},{96,128},{128,96},{160,192},{192,160},{224,2... | collective-permute-start | bytes 49160 | tf_op jit(solution)/shard_map/ppermute | solution.py:524
  29.0 0.0 collective-permute-done.2.got_one
  29.0 3.5 %collective-permute-done.3.got_two = f32[2,16,128]{2,1,0:T(8,128)S(1)} collective-permute-done((f32[2,16,128]{2,1,0:T(8,128)S(1)}, f32[2,16,128]{2,1,0:T(8,128)S(1)}, u32[]{:S(2)}, u32[]{:S(2)}) %collective-permute-start.3) | collective-permute-done | bytes 16416 | tf_op jit(solution)/shard_map/ppermute | solution.py:524
  32.6 0.0 copy-start
  32.6 0.7 shard_map.96
  33.2 0.0 copy-start.2
  33.3 5.7 %all-to-all-done = f32[256,1,256]{2,1,0:T(1,128)S(1)} async-done(((f32[256,1,256]{2,1,0:T(1,128)}), f32[256,1,256]{2,1,0:T(1,128)S(1)}, u32[]{:S(2)}, u32[]{:S(2)}) %all-to-all-start) | async-done | bytes 262176 | tf_op jit(solution)/shard_map/all_to_all | solution.py:552
  39.0 0.0 copy-done
  39.0 4.1 %shard_map.97 = (f32[6,24,128]{2,1,0:T(8,128)S(1)}, f32[2,6,24,128]{3,2,1,0:T(8,128)S(1)}, f32[2,24,128]{2,1,0:T(8,128)S(1)}, f32[2,24,128]{2,1,0:T(8,128)S(1)},...) custom-call(s32[2]{0:T(128)S(1)} %pad_add_fusion.info, f32[256,256]{1,0:T(8,128)S(1)} %bitcast.14, ...), custom_call_target="tpu_custom_call" | custom-call | tf_op jit(solution)/shard_map/pallas_call | solution.py:570
  43.1 0.5 collective-permute-start.4
  43.5 2.3 %collective-permute-start.5 = (f32[2,24,128]{2,1,0:T(8,128)S(1)}, f32[2,24,128]{2,1,0:T(8,128)S(1)}, u32[]{:S(2)}, u32[]{:S(2)}) collective-permute-start(f32[2,24,128]{2,1,0:T(8,128)S(1)} %get-tuple-element.48), channel_id=1, source_target_pairs={{0,0},{32,64},{64,32},{96,128},{128,96},{160,192},{192,160},{224,2... | collective-permute-start | bytes 73736 | tf_op jit(solution)/shard_map/ppermute | solution.py:524
  45.8 0.0 copy-done.2
  45.9 1.7 %shard_map.99.sums0 = f32[256,128]{1,0:T(8,128)S(1)} custom-call(s32[2]{0:T(128)S(1)} %pad_add_fusion.info, f32[7,32,128]{2,1,0:T(8,128)S(1)} %copy-done.2, f32[2,32,128]{2,1,0:T(8,128)S(1)} %get-tuple-element.49.tcell, f32[2,32,128]{2,1,0:T(8,128)S(1)} %get-tuple-element.55.dcell, f32[6,32,128]{2,1,0:T(8,128)S(1)} %get-tuple-element.40.main_f, ...), custom_call_target="tpu_custom_call" | custom-call | flops 300000000 | bytes 1048576 | tf_op jit(solution)/shard_map/pallas_call | solution.py:581
  47.5 0.0 collective-permute-done.4.got_one
  47.5 1.2 %collective-permute-done.5.got_two = f32[2,24,128]{2,1,0:T(8,128)S(1)} collective-permute-done((f32[2,24,128]{2,1,0:T(8,128)S(1)}, f32[2,24,128]{2,1,0:T(8,128)S(1)}, u32[]{:S(2)}, u32[]{:S(2)}) %collective-permute-start.5) | collective-permute-done | bytes 24608 | tf_op jit(solution)/shard_map/ppermute | solution.py:524
  48.7 2.6 %shard_map.98 = (f32[6,32,128]{2,1,0:T(8,128)S(1)}, f32[6,32,128]{2,1,0:T(8,128)S(1)}, f32[6,24,128]{2,1,0:T(8,128)S(1)}, f32[2,6,24,128]{3,2,1,0:T(8,128)S(1)},...) custom-call(s32[2]{0:T(128)S(1)} %pad_add_fusion.info, f32[2,6,24,128]{3,2,1,0:T(8,128)S(1)} %get-tuple-element.46.local, ...), custom_call_target="tpu_custom_call" | custom-call | tf_op jit(solution)/shard_map/pallas_call | solution.py:585
  51.3 0.1 collective-permute-start.6
  51.4 2.9 %collective-permute-start.7 = (f32[2,24,128]{2,1,0:T(8,128)S(1)}, f32[2,24,128]{2,1,0:T(8,128)S(1)}, u32[]{:S(2)}, u32[]{:S(2)}) collective-permute-start(f32[2,24,128]{2,1,0:T(8,128)S(1)} %get-tuple-element.54), channel_id=1, source_target_pairs={{0,0},{32,64},{64,32},{96,128},{128,96},{160,192},{192,160},{224,2... | collective-permute-start | bytes 73736 | tf_op jit(solution)/shard_map/ppermute | solution.py:524
  54.3 1.8 %shard_map.100.sums1 = f32[256,256]{1,0:T(8,128)S(1)} custom-call(s32[2]{0:T(128)S(1)} %pad_add_fusion.info, f32[7,32,128]{2,1,0:T(8,128)S(1)} %copy-done.2, f32[2,32,128]{2,1,0:T(8,128)S(1)} %get-tuple-element.49.tcell, f32[6,32,128]{2,1,0:T(8,128)S(1)} %get-tuple-element.40.main_f, f32[6,32,128]{2,1,0:T(8,128)S(1)} %get-tuple-element.41.side_f, ...), custom_call_target="tpu_custom_call" | custom-call | flops 500000000 | bytes 1048576 | tf_op jit(solution)/shard_map/pallas_call | solution.py:591
  56.1 0.0 collective-permute-done.6.got_one
  56.1 0.5 collective-permute-done.7.got_two
  56.6 2.2 %shard_map.101 = (f32[6,32,128]{2,1,0:T(8,128)S(1)}, f32[128,1,768]{2,1,0:T(1,128)S(1)}, f32[128,1,768]{2,1,0:T(1,128)S(1)}) custom-call(s32[2]{0:T(128)S(1)} %pad_add_fusion.info, f32[7,32,128]{2,1,0:T(8,128)S(1)} %copy-done.2, f32[6,24,128]{2,1,0:T(8,128)S(1)} %get-tuple-element.45.resid, f32[6,24,128]{2,1,0:T(8,128)S(1)} %get-tuple-element.50.image, ...), custom_call_target="tpu_custom_call" | custom-call | tf_op jit(solution)/shard_map/pallas_call | solution.py:595
  58.8 0.1 collective-permute-start.8
  58.9 1.7 %collective-permute-done.8 = f32[128,1,768]{2,1,0:T(1,128)S(1)} collective-permute-done((f32[128,1,768]{2,1,0:T(1,128)S(1)}, f32[128,1,768]{2,1,0:T(1,128)S(1)}, u32[]{:S(2)}, u32[]{:S(2)}) %collective-permute-start.8) | collective-permute-done | bytes 393248 | tf_op jit(solution)/shard_map/ppermute | solution.py:600
  60.6 0.4 add.7
  61.0 24.0 %all_to_all.10 = f32[128,1,768]{2,1,0:T(1,128)S(1)} all-to-all(f32[128,1,768]{2,1,0:T(1,128)S(1)} %add.7), channel_id=1, replica_groups=mesh['y'=4,'core'=2,'pcol'=32] {'y','pcol'}, dimensions={0} | all-to-all | bytes 786432 | tf_op jit(solution)/shard_map/all_to_all | solution.py:601
  85.1 0.8 shard_map.102
  (2 shorter events, 0.0 us)
Async XLA Ops:
  4.2 19.1 %collective-permute-start = (f32[224,128]{1,0:T(8,128)}, f32[224,128]{1,0:T(8,128)S(1)}, u32[]{:S(2)}, u32[]{:S(2)}) collective-permute-start(f32[224,128]{1,0:T(8,128)} %get-tuple-element.35), channel_id=1, source_target_pairs={{0,1},{1,2},{2,3},{3,4},{4,5},{5,6},{6,7},{7,8},{8,9},{9,10},{10,1... | collective-permute-start | bytes 344072 | tf_op jit(solution)/shard_map/ppermute | solution.py:530
  6.8 16.5 %collective-permute-start.1 = (f32[224,128]{1,0:T(8,128)}, f32[224,128]{1,0:T(8,128)S(1)}, u32[]{:S(2)}, u32[]{:S(2)}) collective-permute-start(f32[224,128]{1,0:T(8,128)} %get-tuple-element.36), channel_id=1, source_target_pairs={{1,0},{2,1},{3,2},{4,3},{5,4},{6,5},{7,6},{8,7},{9,8},{10,9},{11,1... | collective-permute-start | bytes 344072 | tf_op jit(solution)/shard_map/ppermute | solution.py:530
  13.0 26.0 %all-to-all-start = ((f32[256,1,256]{2,1,0:T(1,128)}), f32[256,1,256]{2,1,0:T(1,128)S(1)}, u32[]{:S(2)}, u32[]{:S(2)}) async-start(f32[256,1,256]{2,1,0:T(1,128)} %get-tuple-element.34), calls=%async_computation | async-start | bytes 524288 | tf_op jit(solution)/shard_map/all_to_all | solution.py:552
  23.3 0.9 %copy-start.1 = (f32[7,32,128]{2,1,0:T(8,128)S(1)}, f32[7,32,128]{2,1,0:T(8,128)}, u32[]{:S(2)}) copy-start(f32[7,32,128]{2,1,0:T(8,128)} %get-tuple-element.33.frame) | copy-start | bytes 344068
  24.9 4.2 %collective-permute-start.2 = (f32[2,16,128]{2,1,0:T(8,128)S(1)}, f32[2,16,128]{2,1,0:T(8,128)S(1)}, u32[]{:S(2)}, u32[]{:S(2)}) collective-permute-start(f32[2,16,128]{2,1,0:T(8,128)S(1)} %get-tuple-element.38), channel_id=1, source_target_pairs={{0,32},{32,0},{64,96},{96,64},{128,160},{160,128},{192,224},{224,1... | collective-permute-start | bytes 49160 | tf_op jit(solution)/shard_map/ppermute | solution.py:524
  27.1 5.5 %collective-permute-start.3 = (f32[2,16,128]{2,1,0:T(8,128)S(1)}, f32[2,16,128]{2,1,0:T(8,128)S(1)}, u32[]{:S(2)}, u32[]{:S(2)}) collective-permute-start(f32[2,16,128]{2,1,0:T(8,128)S(1)} %get-tuple-element.39), channel_id=1, source_target_pairs={{0,0},{32,64},{64,32},{96,128},{128,96},{160,192},{192,160},{224,2... | collective-permute-start | bytes 49160 | tf_op jit(solution)/shard_map/ppermute | solution.py:524
  32.6 6.4 %copy-start = (f32[72,72,128]{2,1,0:T(8,128)S(1)}, f32[72,72,128]{2,1,0:T(8,128)}, u32[]{:S(2)}) copy-start(f32[72,72,128]{2,1,0:T(8,128)} %mats.3) | copy-start | bytes 7962628
  33.2 12.6 %copy-start.2 = (f32[7,32,128]{2,1,0:T(8,128)S(1)}, f32[7,32,128]{2,1,0:T(8,128)}, u32[]{:S(2)}) copy-start(f32[7,32,128]{2,1,0:T(8,128)} %get-tuple-element.33.frame) | copy-start | bytes 344068
  43.1 4.5 %collective-permute-start.4 = (f32[2,24,128]{2,1,0:T(8,128)S(1)}, f32[2,24,128]{2,1,0:T(8,128)S(1)}, u32[]{:S(2)}, u32[]{:S(2)}) collective-permute-start(f32[2,24,128]{2,1,0:T(8,128)S(1)} %get-tuple-element.47), channel_id=1, source_target_pairs={{0,32},{32,0},{64,96},{96,64},{128,160},{160,128},{192,224},{224,1... | collective-permute-start | bytes 73736 | tf_op jit(solution)/shard_map/ppermute | solution.py:524
  43.5 5.1 %collective-permute-start.5 = (f32[2,24,128]{2,1,0:T(8,128)S(1)}, f32[2,24,128]{2,1,0:T(8,128)S(1)}, u32[]{:S(2)}, u32[]{:S(2)}) collective-permute-start(f32[2,24,128]{2,1,0:T(8,128)S(1)} %get-tuple-element.48), channel_id=1, source_target_pairs={{0,0},{32,64},{64,32},{96,128},{128,96},{160,192},{192,160},{224,2... | collective-permute-start | bytes 73736 | tf_op jit(solution)/shard_map/ppermute | solution.py:524
  51.3 4.8 %collective-permute-start.6 = (f32[2,24,128]{2,1,0:T(8,128)S(1)}, f32[2,24,128]{2,1,0:T(8,128)S(1)}, u32[]{:S(2)}, u32[]{:S(2)}) collective-permute-start(f32[2,24,128]{2,1,0:T(8,128)S(1)} %get-tuple-element.53), channel_id=1, source_target_pairs={{0,32},{32,0},{64,96},{96,64},{128,160},{160,128},{192,224},{224,1... | collective-permute-start | bytes 73736 | tf_op jit(solution)/shard_map/ppermute | solution.py:524
  51.4 5.1 %collective-permute-start.7 = (f32[2,24,128]{2,1,0:T(8,128)S(1)}, f32[2,24,128]{2,1,0:T(8,128)S(1)}, u32[]{:S(2)}, u32[]{:S(2)}) collective-permute-start(f32[2,24,128]{2,1,0:T(8,128)S(1)} %get-tuple-element.54), channel_id=1, source_target_pairs={{0,0},{32,64},{64,32},{96,128},{128,96},{160,192},{192,160},{224,2... | collective-permute-start | bytes 73736 | tf_op jit(solution)/shard_map/ppermute | solution.py:524
  58.8 1.8 %collective-permute-start.8 = (f32[128,1,768]{2,1,0:T(1,128)S(1)}, f32[128,1,768]{2,1,0:T(1,128)S(1)}, u32[]{:S(2)}, u32[]{:S(2)}) collective-permute-start(f32[128,1,768]{2,1,0:T(1,128)S(1)} %get-tuple-element.58), channel_id=1, source_target_pairs={{0,32},{32,0},{1,33},{33,1},{2,34},{34,2},{3,35},{35,3},{4,36},{36... | collective-permute-start | bytes 1179656 | tf_op jit(solution)/shard_map/ppermute | solution.py:600

commit v11 on v10

--- a/solution.py
+++ b/solution.py
@@ -485,10 +485,10 @@
     for half, out in ((0, keep_out), (1, send_out)):
         count = out.shape[0]
         rows = slice(128 * half, 128 * half + count)
-        out[:, 0, 0:CC] = jnp.broadcast_to(dots, (count, CC))
-        out[:, 0, CC:2 * CC] = sums0[rows, :]
-        out[:, 0, 2 * CC:4 * CC] = sums1[rows, :]
-        out[:, 0, 4 * CC:] = sums[rows]
+        out[:, 0:CC] = jnp.broadcast_to(dots, (count, CC))
+        out[:, CC:2 * CC] = sums0[rows, :]
+        out[:, 2 * CC:4 * CC] = sums1[rows, :]
+        out[:, 4 * CC:] = sums[rows]
 
 
 def last_kernel(got, zframe, wframe, tangent, second, owned):
@@ -520,7 +520,7 @@
 
 def pairwise(count, one, two):
     first = [(i, i ^ 1) for i in range(count)]
-    second = [(i, min(max(i + (1 if i % 2 else -1), 0), count - 1)) for i in range(count)]
+    second = [(i, (i + (1 if i % 2 else -1)) % count) for i in range(count)]
     return lax.ppermute(one, ROW, first), lax.ppermute(two, ROW, second)
 
 
@@ -594,11 +594,11 @@
     )(info, frame, tcell, main_f, side_f, zframe, zside)
     wframe, keep, send = call(
         functools.partial(third_kernel, last, n_col),
-        [(6, FR, CC)] + [(n_dev // 2, 1, 6 * CC)] * 2, [SMEM] + [VMEM] * 12,
+        [(6, FR, CC)] + [(n_dev // 2, 6 * CC)] * 2, [SMEM] + [VMEM] * 12,
         [pltpu.VMEM((6, FR, CC), F32)] + operands(2),
     )(info, frame, resid, image, zframe, local, *rows(one, two), tcell, main_f, side_f, sums0, sums1)
     sums = keep + lax.ppermute(send, "core", [(0, 1), (1, 0)])
-    got = lax.all_to_all(sums, ("y", "pcol"), 0, 0, tiled=True).reshape(n_dev // 2, 6 * CC)
+    got = lax.all_to_all(sums, ("y", "pcol"), 0, 0, tiled=True)
     tangent, second, owned = call(
         last_kernel, [(3, CR, CC), (3, CR, CC), (1, CC)], [VMEM] * 3
     )(got, zframe, wframe)

time: 86.5 us -> 84.4 us (0.976)
  waiting for transfers between devices: 12.6 us -> 15.1 us
  starting transfers between devices: 28.9 us -> 26.8 us
  Pallas kernels: 17.4 us -> 15.5 us
    ppermute x6, starting transfers between devices: 9.85 us -> 6.23 us  [pairwise(): return (lax.ppermute(one, ROW, first), lax.ppermute(two, ROW, second))]
    all_to_all x1, waiting for transfers between devices: 5.69 us -> 7.66 us  [per_device(): lax.all_to_all(own, ROW + ('pcol',), 0, 0, tiled=True)]
    ppermute x1, starting transfers between devices: 0.09 us -> 1.58 us  [per_device(): sums = keep + lax.ppermute(send, 'core', [(0, 1), (1, 0)])]
    ppermute x6, waiting for transfers between devices: 5.18 us -> 6.12 us  [pairwise(): return (lax.ppermute(one, ROW, first), lax.ppermute(two, ROW, second))]
  transfers between devices with their start and end apart: 10 -> 10, of which waited for: 5 -> 6; matrix products, arithmetic and copies ran while one was open for 0% -> 0% of each run, Pallas kernels for 6% -> 6%
where the time goes in v11:
time: 84.4 us; the launch traced here: 84.2 us
  starting transfers between devices  26.8 us (32%)
  blocking collectives  23.9 us (28%)
  Pallas kernels  15.5 us (18%)
  waiting for transfers between devices  15.1 us (18%)
  between operations  1.41 us (2%)
  local copies, waits for them, and re-layouts  1.36 us (2%)
    all_to_all x1, blocking collectives, per_device(): got = lax.all_to_all(sums, ('y', 'pcol'), 0, 0, tiled=True)  23.9 us
    all_to_all x1, starting transfers between devices, per_device(): lax.all_to_all(own, ROW + ('pcol',), 0, 0, tiled=True)  10.2 us
    all_to_all x1, waiting for transfers between devices, per_device(): lax.all_to_all(own, ROW + ('pcol',), 0, 0, tiled=True)  7.66 us
    ppermute x6, starting transfers between devices, pairwise(): return (lax.ppermute(one, ROW, first), lax.ppermute(two, ROW, second))  6.23 us
    ppermute x1, starting transfers between devices, ring(): lax.ppermute(to_previous, axis, backward)  6.22 us
    ppermute x6, waiting for transfers between devices, pairwise(): return (lax.ppermute(one, ROW, first), lax.ppermute(two, ROW, second))  6.12 us
    pallas_call x1, Pallas kernels, per_device(): call(functools.partial(first_kernel, last), [(6, EXT, CC), (2, 6, EXT, CC...  3.22 us
    pallas_call x1, Pallas kernels, per_device(): call(start_kernel, [(n_dev, 1, 2 * DV), (7, FR, CC), (EDGE + 8, CC), (EDG...  2.92 us
  transfers between devices with their start and end apart: 10, of which 6 were waited for; matrix products, arithmetic and copies ran while one was open for 0% of the time, Pallas kernels for 6%

profile of v11, /device:TPU:1, one launch (start us, length us, event | category | flops | bytes accessed | tf_op | source)
XLA Modules:
  0.0 84.2 jit_solution(15599336001747661648)
XLA Ops:
  1.3 2.9 %shard_map.94 = (f32[256,1,256]{2,1,0:T(1,128)}, f32[7,32,128]{2,1,0:T(8,128)}, f32[224,128]{1,0:T(8,128)}, f32[224,128]{1,0:T(8,128)}) custom-call(s32[1]{0:T(128)} %bitcast.14.levels, f32[1,128]{1,0:T(1,128)} %bitcast.17, f32[1,128]{1,0:T(1,128)} %bitcast.18, f32[3,22,128]{2,1,0:T(8,128)} %state.1, f32[3,22,128]{2,1,0:T(8,128)} %adjoint.1, ...), custom_call_target="tpu_custom_call" | custom-call | flops 1000000000 | bytes 1048576 | tf_op jit(solution)/shard_map/pallas_call | solution.py:541
  4.2 2.5 %collective-permute-start = (f32[224,128]{1,0:T(8,128)}, f32[224,128]{1,0:T(8,128)S(1)}, u32[]{:S(2)}, u32[]{:S(2)}) collective-permute-start(f32[224,128]{1,0:T(8,128)} %get-tuple-element.35), channel_id=1, source_target_pairs={{0,1},{1,2},{2,3},{3,4},{4,5},{5,6},{6,7},{7,8},{8,9},{9,10},{10,1... | collective-permute-start | bytes 344072 | tf_op jit(solution)/shard_map/ppermute | solution.py:530
  6.8 6.2 %collective-permute-start.1 = (f32[224,128]{1,0:T(8,128)}, f32[224,128]{1,0:T(8,128)S(1)}, u32[]{:S(2)}, u32[]{:S(2)}) collective-permute-start(f32[224,128]{1,0:T(8,128)} %get-tuple-element.36), channel_id=1, source_target_pairs={{1,0},{2,1},{3,2},{4,3},{5,4},{6,5},{7,6},{8,7},{9,8},{10,9},{11,1... | collective-permute-start | bytes 344072 | tf_op jit(solution)/shard_map/ppermute | solution.py:530
  13.0 10.2 %all-to-all-start = ((f32[256,1,256]{2,1,0:T(1,128)}), f32[256,1,256]{2,1,0:T(1,128)S(1)}, u32[]{:S(2)}, u32[]{:S(2)}) async-start(f32[256,1,256]{2,1,0:T(1,128)} %get-tuple-element.34), calls=%async_computation | async-start | bytes 524288 | tf_op jit(solution)/shard_map/all_to_all | solution.py:552
  23.2 0.1 pad_add_fusion.info
  23.3 0.0 collective-permute-done.from_left
  23.3 0.0 collective-permute-done.1.from_right
  23.3 0.0 copy-start.1
  23.3 0.9 %copy-done.1 = f32[7,32,128]{2,1,0:T(8,128)S(1)} copy-done((f32[7,32,128]{2,1,0:T(8,128)S(1)}, f32[7,32,128]{2,1,0:T(8,128)}, u32[]{:S(2)}) %copy-start.1) | copy-done | bytes 114712
  24.2 0.7 shard_map.95
  24.9 2.2 %collective-permute-start.2 = (f32[2,16,128]{2,1,0:T(8,128)S(1)}, f32[2,16,128]{2,1,0:T(8,128)S(1)}, u32[]{:S(2)}, u32[]{:S(2)}) collective-permute-start(f32[2,16,128]{2,1,0:T(8,128)S(1)} %get-tuple-element.38), channel_id=1, source_target_pairs={{0,32},{32,0},{64,96},{96,64},{128,160},{160,128},{192,224},{224,1... | collective-permute-start | bytes 49160 | tf_op jit(solution)/shard_map/ppermute | solution.py:524
  27.1 0.0 collective-permute-start.3
  27.1 0.8 collective-permute-done.2.got_one
  27.9 2.7 %collective-permute-done.3.got_two = f32[2,16,128]{2,1,0:T(8,128)S(1)} collective-permute-done((f32[2,16,128]{2,1,0:T(8,128)S(1)}, f32[2,16,128]{2,1,0:T(8,128)S(1)}, u32[]{:S(2)}, u32[]{:S(2)}) %collective-permute-start.3) | collective-permute-done | bytes 16416 | tf_op jit(solution)/shard_map/ppermute | solution.py:524
  30.6 0.0 copy-start
  30.6 0.7 shard_map.96
  31.3 0.0 copy-start.2
  31.3 7.7 %all-to-all-done = f32[256,1,256]{2,1,0:T(1,128)S(1)} async-done(((f32[256,1,256]{2,1,0:T(1,128)}), f32[256,1,256]{2,1,0:T(1,128)S(1)}, u32[]{:S(2)}, u32[]{:S(2)}) %all-to-all-start) | async-done | bytes 262176 | tf_op jit(solution)/shard_map/all_to_all | solution.py:552
  39.0 0.0 copy-done
  39.0 3.2 %shard_map.97 = (f32[6,24,128]{2,1,0:T(8,128)S(1)}, f32[2,6,24,128]{3,2,1,0:T(8,128)S(1)}, f32[2,24,128]{2,1,0:T(8,128)S(1)}, f32[2,24,128]{2,1,0:T(8,128)S(1)},...) custom-call(s32[2]{0:T(128)S(1)} %pad_add_fusion.info, f32[256,256]{1,0:T(8,128)S(1)} %bitcast.16, ...), custom_call_target="tpu_custom_call" | custom-call | tf_op jit(solution)/shard_map/pallas_call | solution.py:570
  42.2 1.3 %collective-permute-start.4 = (f32[2,24,128]{2,1,0:T(8,128)S(1)}, f32[2,24,128]{2,1,0:T(8,128)S(1)}, u32[]{:S(2)}, u32[]{:S(2)}) collective-permute-start(f32[2,24,128]{2,1,0:T(8,128)S(1)} %get-tuple-element.47), channel_id=1, source_target_pairs={{0,32},{32,0},{64,96},{96,64},{128,160},{160,128},{192,224},{224,1... | collective-permute-start | bytes 73736 | tf_op jit(solution)/shard_map/ppermute | solution.py:524
  43.5 0.4 collective-permute-start.5
  43.9 0.0 copy-done.2
  43.9 1.6 %shard_map.99.sums0 = f32[256,128]{1,0:T(8,128)S(1)} custom-call(s32[2]{0:T(128)S(1)} %pad_add_fusion.info, f32[7,32,128]{2,1,0:T(8,128)S(1)} %copy-done.2, f32[2,32,128]{2,1,0:T(8,128)S(1)} %get-tuple-element.49.tcell, f32[2,32,128]{2,1,0:T(8,128)S(1)} %get-tuple-element.55.dcell, f32[6,32,128]{2,1,0:T(8,128)S(1)} %get-tuple-element.40.main_f, ...), custom_call_target="tpu_custom_call" | custom-call | flops 300000000 | bytes 1048576 | tf_op jit(solution)/shard_map/pallas_call | solution.py:581
  45.6 0.0 collective-permute-done.4.got_one
  45.6 1.2 %collective-permute-done.5.got_two = f32[2,24,128]{2,1,0:T(8,128)S(1)} collective-permute-done((f32[2,24,128]{2,1,0:T(8,128)S(1)}, f32[2,24,128]{2,1,0:T(8,128)S(1)}, u32[]{:S(2)}, u32[]{:S(2)}) %collective-permute-start.5) | collective-permute-done | bytes 24608 | tf_op jit(solution)/shard_map/ppermute | solution.py:524
  46.8 1.8 %shard_map.98 = (f32[6,32,128]{2,1,0:T(8,128)S(1)}, f32[6,32,128]{2,1,0:T(8,128)S(1)}, f32[6,24,128]{2,1,0:T(8,128)S(1)}, f32[2,6,24,128]{3,2,1,0:T(8,128)S(1)},...) custom-call(s32[2]{0:T(128)S(1)} %pad_add_fusion.info, f32[2,6,24,128]{3,2,1,0:T(8,128)S(1)} %get-tuple-element.46.local, ...), custom_call_target="tpu_custom_call" | custom-call | tf_op jit(solution)/shard_map/pallas_call | solution.py:585
  48.6 2.2 %collective-permute-start.6 = (f32[2,24,128]{2,1,0:T(8,128)S(1)}, f32[2,24,128]{2,1,0:T(8,128)S(1)}, u32[]{:S(2)}, u32[]{:S(2)}) collective-permute-start(f32[2,24,128]{2,1,0:T(8,128)S(1)} %get-tuple-element.53), channel_id=1, source_target_pairs={{0,32},{32,0},{64,96},{96,64},{128,160},{160,128},{192,224},{224,1... | collective-permute-start | bytes 73736 | tf_op jit(solution)/shard_map/ppermute | solution.py:524
  50.8 0.0 collective-permute-start.7
  50.8 1.8 %shard_map.100.sums1 = f32[256,256]{1,0:T(8,128)S(1)} custom-call(s32[2]{0:T(128)S(1)} %pad_add_fusion.info, f32[7,32,128]{2,1,0:T(8,128)S(1)} %copy-done.2, f32[2,32,128]{2,1,0:T(8,128)S(1)} %get-tuple-element.49.tcell, f32[6,32,128]{2,1,0:T(8,128)S(1)} %get-tuple-element.40.main_f, f32[6,32,128]{2,1,0:T(8,128)S(1)} %get-tuple-element.41.side_f, ...), custom_call_target="tpu_custom_call" | custom-call | flops 500000000 | bytes 1048576 | tf_op jit(solution)/shard_map/pallas_call | solution.py:591
  52.6 0.0 collective-permute-done.6.got_one
  52.6 1.4 %collective-permute-done.7.got_two = f32[2,24,128]{2,1,0:T(8,128)S(1)} collective-permute-done((f32[2,24,128]{2,1,0:T(8,128)S(1)}, f32[2,24,128]{2,1,0:T(8,128)S(1)}, u32[]{:S(2)}, u32[]{:S(2)}) %collective-permute-start.7) | collective-permute-done | bytes 24608 | tf_op jit(solution)/shard_map/ppermute | solution.py:524
  54.1 2.0 %shard_map.101 = (f32[6,32,128]{2,1,0:T(8,128)S(1)}, f32[128,768]{1,0:T(8,128)S(1)}, f32[128,768]{1,0:T(8,128)S(1)}) custom-call(s32[2]{0:T(128)S(1)} %pad_add_fusion.info, f32[7,32,128]{2,1,0:T(8,128)S(1)} %copy-done.2, f32[6,24,128]{2,1,0:T(8,128)S(1)} %get-tuple-element.45.resid, f32[6,24,128]{2,1,0:T(8,128)S(1)} %get-tuple-element.50.image, ...), custom_call_target="tpu_custom_call" | custom-call | tf_op jit(solution)/shard_map/pallas_call | solution.py:595
  56.1 1.6 %collective-permute-start.8 = (f32[128,768]{1,0:T(8,128)S(1)}, f32[128,768]{1,0:T(8,128)S(1)}, u32[]{:S(2)}, u32[]{:S(2)}) collective-permute-start(f32[128,768]{1,0:T(8,128)S(1)} %get-tuple-element.58), channel_id=1, source_target_pairs={{0,32},{32,0},{1,33},{33,1},{2,34},{34,2},{3,35},{35,3},{4,36},{36... | collective-permute-start | bytes 1179656 | tf_op jit(solution)/shard_map/ppermute | solution.py:600
  57.7 1.3 %collective-permute-done.8 = f32[128,768]{1,0:T(8,128)S(1)} collective-permute-done((f32[128,768]{1,0:T(8,128)S(1)}, f32[128,768]{1,0:T(8,128)S(1)}, u32[]{:S(2)}, u32[]{:S(2)}) %collective-permute-start.8) | collective-permute-done | bytes 393248 | tf_op jit(solution)/shard_map/ppermute | solution.py:600
  59.1 0.4 copy.11
  59.5 23.9 %all_to_all.16 = f32[128,1,768]{2,1,0:T(1,128)S(1)} all-to-all(f32[128,1,768]{2,1,0:T(1,128)S(1)} %copy.11), channel_id=1, replica_groups=mesh['y'=4,'core'=2,'pcol'=32] {'y','pcol'}, dimensions={0} | all-to-all | bytes 786432 | tf_op jit(solution)/shard_map/all_to_all | solution.py:601
  83.4 0.8 shard_map.102
  (3 shorter events, 0.1 us)
Async XLA Ops:
  4.2 19.1 %collective-permute-start = (f32[224,128]{1,0:T(8,128)}, f32[224,128]{1,0:T(8,128)S(1)}, u32[]{:S(2)}, u32[]{:S(2)}) collective-permute-start(f32[224,128]{1,0:T(8,128)} %get-tuple-element.35), channel_id=1, source_target_pairs={{0,1},{1,2},{2,3},{3,4},{4,5},{5,6},{6,7},{7,8},{8,9},{9,10},{10,1... | collective-permute-start | bytes 344072 | tf_op jit(solution)/shard_map/ppermute | solution.py:530
  6.8 16.5 %collective-permute-start.1 = (f32[224,128]{1,0:T(8,128)}, f32[224,128]{1,0:T(8,128)S(1)}, u32[]{:S(2)}, u32[]{:S(2)}) collective-permute-start(f32[224,128]{1,0:T(8,128)} %get-tuple-element.36), channel_id=1, source_target_pairs={{1,0},{2,1},{3,2},{4,3},{5,4},{6,5},{7,6},{8,7},{9,8},{10,9},{11,1... | collective-permute-start | bytes 344072 | tf_op jit(solution)/shard_map/ppermute | solution.py:530
  13.0 26.0 %all-to-all-start = ((f32[256,1,256]{2,1,0:T(1,128)}), f32[256,1,256]{2,1,0:T(1,128)S(1)}, u32[]{:S(2)}, u32[]{:S(2)}) async-start(f32[256,1,256]{2,1,0:T(1,128)} %get-tuple-element.34), calls=%async_computation | async-start | bytes 524288 | tf_op jit(solution)/shard_map/all_to_all | solution.py:552
  23.3 0.9 %copy-start.1 = (f32[7,32,128]{2,1,0:T(8,128)S(1)}, f32[7,32,128]{2,1,0:T(8,128)}, u32[]{:S(2)}) copy-start(f32[7,32,128]{2,1,0:T(8,128)} %get-tuple-element.33.frame) | copy-start | bytes 344068
  24.9 3.1 %collective-permute-start.2 = (f32[2,16,128]{2,1,0:T(8,128)S(1)}, f32[2,16,128]{2,1,0:T(8,128)S(1)}, u32[]{:S(2)}, u32[]{:S(2)}) collective-permute-start(f32[2,16,128]{2,1,0:T(8,128)S(1)} %get-tuple-element.38), channel_id=1, source_target_pairs={{0,32},{32,0},{64,96},{96,64},{128,160},{160,128},{192,224},{224,1... | collective-permute-start | bytes 49160 | tf_op jit(solution)/shard_map/ppermute | solution.py:524
  27.1 3.5 %collective-permute-start.3 = (f32[2,16,128]{2,1,0:T(8,128)S(1)}, f32[2,16,128]{2,1,0:T(8,128)S(1)}, u32[]{:S(2)}, u32[]{:S(2)}) collective-permute-start(f32[2,16,128]{2,1,0:T(8,128)S(1)} %get-tuple-element.39), channel_id=1, source_target_pairs={{0,224},{32,64},{64,32},{96,128},{128,96},{160,192},{192,160},{224... | collective-permute-start | bytes 49160 | tf_op jit(solution)/shard_map/ppermute | solution.py:524
  30.6 8.4 %copy-start = (f32[72,72,128]{2,1,0:T(8,128)S(1)}, f32[72,72,128]{2,1,0:T(8,128)}, u32[]{:S(2)}) copy-start(f32[72,72,128]{2,1,0:T(8,128)} %mats.3) | copy-start | bytes 7962628
  31.3 12.7 %copy-start.2 = (f32[7,32,128]{2,1,0:T(8,128)S(1)}, f32[7,32,128]{2,1,0:T(8,128)}, u32[]{:S(2)}) copy-start(f32[7,32,128]{2,1,0:T(8,128)} %get-tuple-element.33.frame) | copy-start | bytes 344068
  42.2 3.4 %collective-permute-start.4 = (f32[2,24,128]{2,1,0:T(8,128)S(1)}, f32[2,24,128]{2,1,0:T(8,128)S(1)}, u32[]{:S(2)}, u32[]{:S(2)}) collective-permute-start(f32[2,24,128]{2,1,0:T(8,128)S(1)} %get-tuple-element.47), channel_id=1, source_target_pairs={{0,32},{32,0},{64,96},{96,64},{128,160},{160,128},{192,224},{224,1... | collective-permute-start | bytes 73736 | tf_op jit(solution)/shard_map/ppermute | solution.py:524
  43.5 3.3 %collective-permute-start.5 = (f32[2,24,128]{2,1,0:T(8,128)S(1)}, f32[2,24,128]{2,1,0:T(8,128)S(1)}, u32[]{:S(2)}, u32[]{:S(2)}) collective-permute-start(f32[2,24,128]{2,1,0:T(8,128)S(1)} %get-tuple-element.48), channel_id=1, source_target_pairs={{0,224},{32,64},{64,32},{96,128},{128,96},{160,192},{192,160},{224... | collective-permute-start | bytes 73736 | tf_op jit(solution)/shard_map/ppermute | solution.py:524
  48.6 4.1 %collective-permute-start.6 = (f32[2,24,128]{2,1,0:T(8,128)S(1)}, f32[2,24,128]{2,1,0:T(8,128)S(1)}, u32[]{:S(2)}, u32[]{:S(2)}) collective-permute-start(f32[2,24,128]{2,1,0:T(8,128)S(1)} %get-tuple-element.53), channel_id=1, source_target_pairs={{0,32},{32,0},{64,96},{96,64},{128,160},{160,128},{192,224},{224,1... | collective-permute-start | bytes 73736 | tf_op jit(solution)/shard_map/ppermute | solution.py:524
  50.8 3.3 %collective-permute-start.7 = (f32[2,24,128]{2,1,0:T(8,128)S(1)}, f32[2,24,128]{2,1,0:T(8,128)S(1)}, u32[]{:S(2)}, u32[]{:S(2)}) collective-permute-start(f32[2,24,128]{2,1,0:T(8,128)S(1)} %get-tuple-element.54), channel_id=1, source_target_pairs={{0,224},{32,64},{64,32},{96,128},{128,96},{160,192},{192,160},{224... | collective-permute-start | bytes 73736 | tf_op jit(solution)/shard_map/ppermute | solution.py:524
  56.1 2.9 %collective-permute-start.8 = (f32[128,768]{1,0:T(8,128)S(1)}, f32[128,768]{1,0:T(8,128)S(1)}, u32[]{:S(2)}, u32[]{:S(2)}) collective-permute-start(f32[128,768]{1,0:T(8,128)S(1)} %get-tuple-element.58), channel_id=1, source_target_pairs={{0,32},{32,0},{1,33},{33,1},{2,34},{34,2},{3,35},{35,3},{4,36},{36... | collective-permute-start | bytes 1179656 | tf_op jit(solution)/shard_map/ppermute | solution.py:600

commit v12 on v11

--- a/solution.py
+++ b/solution.py
@@ -11,6 +11,7 @@
 CC = 128
 DV = 128
 BLK = 72
+MAXLEVEL = 4
 EXT = CR + 2
 FR = 32
 ROW = ("y", "core")
@@ -216,7 +217,6 @@
     side_vec[1] = spread[BLK:]
     total[...] = jnp.zeros_like(total)
     side_total[...] = jnp.zeros_like(side_total)
-    top = jnp.maximum(level, jnp.max(levels[...]).astype(jnp.int32))
 
     def term(order, carry):
         scale = jnp.where(order == 0, 1.0, 0.5).astype(F32)
@@ -234,7 +234,7 @@
             total[n] += keep * out
         return carry
 
-    lax.fori_loop(0, top, term, 0)
+    lax.fori_loop(0, MAXLEVEL, term, 0)
 
 
 def put_results(prow, total, side_total, local_out, one_out, two_out):

time: 84.4 us -> 84.5 us (level)
  Pallas kernels: 15.5 us -> 17.2 us
  starting transfers between devices: 26.8 us -> 25.1 us
    ppermute x6, starting transfers between devices: 6.23 us -> 4.53 us  [pairwise(): return (lax.ppermute(one, ROW, first), lax.ppermute(two, ROW, second))]
    pallas_call x1, Pallas kernels: 1.78 us -> 2.65 us  [per_device(): call(functools.partial(second_kernel, last), [(6, FR, CC), (6, FR, CC), (...]
    pallas_call x1, Pallas kernels: 3.22 us -> 4.09 us  [per_device(): call(functools.partial(first_kernel, last), [(6, EXT, CC), (2, 6, EXT, CC...]
where the time goes in v12:
time: 84.5 us; the launch traced here: 84.2 us
  starting transfers between devices  25.1 us (30%)
  blocking collectives  23.9 us (28%)
  Pallas kernels  17.2 us (20%)
  waiting for transfers between devices  15.1 us (18%)
  between operations  1.41 us (2%)
  local copies, waits for them, and re-layouts  1.36 us (2%)
    all_to_all x1, blocking collectives, per_device(): got = lax.all_to_all(sums, ('y', 'pcol'), 0, 0, tiled=True)  23.9 us
    all_to_all x1, starting transfers between devices, per_device(): lax.all_to_all(own, ROW + ('pcol',), 0, 0, tiled=True)  10.2 us
    all_to_all x1, waiting for transfers between devices, per_device(): lax.all_to_all(own, ROW + ('pcol',), 0, 0, tiled=True)  7.66 us
    ppermute x1, starting transfers between devices, ring(): lax.ppermute(to_previous, axis, backward)  6.22 us
    ppermute x6, waiting for transfers between devices, pairwise(): return (lax.ppermute(one, ROW, first), lax.ppermute(two, ROW, second))  6.12 us
    ppermute x6, starting transfers between devices, pairwise(): return (lax.ppermute(one, ROW, first), lax.ppermute(two, ROW, second))  4.53 us
    pallas_call x1, Pallas kernels, per_device(): call(functools.partial(first_kernel, last), [(6, EXT, CC), (2, 6, EXT, CC...  4.09 us
    pallas_call x1, Pallas kernels, per_device(): call(start_kernel, [(n_dev, 1, 2 * DV), (7, FR, CC), (EDGE + 8, CC), (EDG...  2.92 us
  transfers between devices with their start and end apart: 10, of which 6 were waited for; matrix products, arithmetic and copies ran while one was open for 0% of the time, Pallas kernels for 6%

profile of v12, /device:TPU:1, one launch (start us, length us, event | category | flops | bytes accessed | tf_op | source)
XLA Modules:
  0.0 84.2 jit_solution(12007384841657561209)
XLA Ops:
  1.3 2.9 %shard_map.94 = (f32[256,1,256]{2,1,0:T(1,128)}, f32[7,32,128]{2,1,0:T(8,128)}, f32[224,128]{1,0:T(8,128)}, f32[224,128]{1,0:T(8,128)}) custom-call(s32[1]{0:T(128)} %bitcast.14.levels, f32[1,128]{1,0:T(1,128)} %bitcast.17, f32[1,128]{1,0:T(1,128)} %bitcast.18, f32[3,22,128]{2,1,0:T(8,128)} %state.1, f32[3,22,128]{2,1,0:T(8,128)} %adjoint.1, ...), custom_call_target="tpu_custom_call" | custom-call | flops 1000000000 | bytes 1048576 | tf_op jit(solution)/shard_map/pallas_call | solution.py:541
  4.2 2.5 %collective-permute-start = (f32[224,128]{1,0:T(8,128)}, f32[224,128]{1,0:T(8,128)S(1)}, u32[]{:S(2)}, u32[]{:S(2)}) collective-permute-start(f32[224,128]{1,0:T(8,128)} %get-tuple-element.35), channel_id=1, source_target_pairs={{0,1},{1,2},{2,3},{3,4},{4,5},{5,6},{6,7},{7,8},{8,9},{9,10},{10,1... | collective-permute-start | bytes 344072 | tf_op jit(solution)/shard_map/ppermute | solution.py:530
  6.8 6.2 %collective-permute-start.1 = (f32[224,128]{1,0:T(8,128)}, f32[224,128]{1,0:T(8,128)S(1)}, u32[]{:S(2)}, u32[]{:S(2)}) collective-permute-start(f32[224,128]{1,0:T(8,128)} %get-tuple-element.36), channel_id=1, source_target_pairs={{1,0},{2,1},{3,2},{4,3},{5,4},{6,5},{7,6},{8,7},{9,8},{10,9},{11,1... | collective-permute-start | bytes 344072 | tf_op jit(solution)/shard_map/ppermute | solution.py:530
  13.0 10.2 %all-to-all-start = ((f32[256,1,256]{2,1,0:T(1,128)}), f32[256,1,256]{2,1,0:T(1,128)S(1)}, u32[]{:S(2)}, u32[]{:S(2)}) async-start(f32[256,1,256]{2,1,0:T(1,128)} %get-tuple-element.34), calls=%async_computation | async-start | bytes 524288 | tf_op jit(solution)/shard_map/all_to_all | solution.py:552
  23.2 0.1 pad_add_fusion.info
  23.3 0.0 collective-permute-done.from_left
  23.3 0.0 collective-permute-done.1.from_right
  23.3 0.0 copy-start.1
  23.3 0.9 %copy-done.1 = f32[7,32,128]{2,1,0:T(8,128)S(1)} copy-done((f32[7,32,128]{2,1,0:T(8,128)S(1)}, f32[7,32,128]{2,1,0:T(8,128)}, u32[]{:S(2)}) %copy-start.1) | copy-done | bytes 114712
  24.2 0.7 shard_map.95
  24.9 2.2 %collective-permute-start.2 = (f32[2,16,128]{2,1,0:T(8,128)S(1)}, f32[2,16,128]{2,1,0:T(8,128)S(1)}, u32[]{:S(2)}, u32[]{:S(2)}) collective-permute-start(f32[2,16,128]{2,1,0:T(8,128)S(1)} %get-tuple-element.38), channel_id=1, source_target_pairs={{0,32},{32,0},{64,96},{96,64},{128,160},{160,128},{192,224},{224,1... | collective-permute-start | bytes 49160 | tf_op jit(solution)/shard_map/ppermute | solution.py:524
  27.1 0.0 collective-permute-start.3
  27.1 0.8 collective-permute-done.2.got_one
  27.9 2.7 %collective-permute-done.3.got_two = f32[2,16,128]{2,1,0:T(8,128)S(1)} collective-permute-done((f32[2,16,128]{2,1,0:T(8,128)S(1)}, f32[2,16,128]{2,1,0:T(8,128)S(1)}, u32[]{:S(2)}, u32[]{:S(2)}) %collective-permute-start.3) | collective-permute-done | bytes 16416 | tf_op jit(solution)/shard_map/ppermute | solution.py:524
  30.6 0.0 copy-start
  30.6 0.7 shard_map.96
  31.3 0.0 copy-start.2
  31.3 7.7 %all-to-all-done = f32[256,1,256]{2,1,0:T(1,128)S(1)} async-done(((f32[256,1,256]{2,1,0:T(1,128)}), f32[256,1,256]{2,1,0:T(1,128)S(1)}, u32[]{:S(2)}, u32[]{:S(2)}) %all-to-all-start) | async-done | bytes 262176 | tf_op jit(solution)/shard_map/all_to_all | solution.py:552
  39.0 0.0 copy-done
  39.0 4.1 %shard_map.97 = (f32[6,24,128]{2,1,0:T(8,128)S(1)}, f32[2,6,24,128]{3,2,1,0:T(8,128)S(1)}, f32[2,24,128]{2,1,0:T(8,128)S(1)}, f32[2,24,128]{2,1,0:T(8,128)S(1)},...) custom-call(s32[2]{0:T(128)S(1)} %pad_add_fusion.info, f32[256,256]{1,0:T(8,128)S(1)} %bitcast.16, ...), custom_call_target="tpu_custom_call" | custom-call | tf_op jit(solution)/shard_map/pallas_call | solution.py:570
  43.1 0.5 collective-permute-start.4
  43.5 0.4 collective-permute-start.5
  43.9 0.0 copy-done.2
  43.9 1.6 %shard_map.99.sums0 = f32[256,128]{1,0:T(8,128)S(1)} custom-call(s32[2]{0:T(128)S(1)} %pad_add_fusion.info, f32[7,32,128]{2,1,0:T(8,128)S(1)} %copy-done.2, f32[2,32,128]{2,1,0:T(8,128)S(1)} %get-tuple-element.49.tcell, f32[2,32,128]{2,1,0:T(8,128)S(1)} %get-tuple-element.55.dcell, f32[6,32,128]{2,1,0:T(8,128)S(1)} %get-tuple-element.40.main_f, ...), custom_call_target="tpu_custom_call" | custom-call | flops 300000000 | bytes 1048576 | tf_op jit(solution)/shard_map/pallas_call | solution.py:581
  45.6 0.0 collective-permute-done.4.got_one
  45.6 1.2 %collective-permute-done.5.got_two = f32[2,24,128]{2,1,0:T(8,128)S(1)} collective-permute-done((f32[2,24,128]{2,1,0:T(8,128)S(1)}, f32[2,24,128]{2,1,0:T(8,128)S(1)}, u32[]{:S(2)}, u32[]{:S(2)}) %collective-permute-start.5) | collective-permute-done | bytes 24608 | tf_op jit(solution)/shard_map/ppermute | solution.py:524
  46.8 2.6 %shard_map.98 = (f32[6,32,128]{2,1,0:T(8,128)S(1)}, f32[6,32,128]{2,1,0:T(8,128)S(1)}, f32[6,24,128]{2,1,0:T(8,128)S(1)}, f32[2,6,24,128]{3,2,1,0:T(8,128)S(1)},...) custom-call(s32[2]{0:T(128)S(1)} %pad_add_fusion.info, f32[2,6,24,128]{3,2,1,0:T(8,128)S(1)} %get-tuple-element.46.local, ...), custom_call_target="tpu_custom_call" | custom-call | tf_op jit(solution)/shard_map/pallas_call | solution.py:585
  49.4 1.4 %collective-permute-start.6 = (f32[2,24,128]{2,1,0:T(8,128)S(1)}, f32[2,24,128]{2,1,0:T(8,128)S(1)}, u32[]{:S(2)}, u32[]{:S(2)}) collective-permute-start(f32[2,24,128]{2,1,0:T(8,128)S(1)} %get-tuple-element.53), channel_id=1, source_target_pairs={{0,32},{32,0},{64,96},{96,64},{128,160},{160,128},{192,224},{224,1... | collective-permute-start | bytes 73736 | tf_op jit(solution)/shard_map/ppermute | solution.py:524
  50.9 0.0 collective-permute-start.7
  50.9 1.8 %shard_map.100.sums1 = f32[256,256]{1,0:T(8,128)S(1)} custom-call(s32[2]{0:T(128)S(1)} %pad_add_fusion.info, f32[7,32,128]{2,1,0:T(8,128)S(1)} %copy-done.2, f32[2,32,128]{2,1,0:T(8,128)S(1)} %get-tuple-element.49.tcell, f32[6,32,128]{2,1,0:T(8,128)S(1)} %get-tuple-element.40.main_f, f32[6,32,128]{2,1,0:T(8,128)S(1)} %get-tuple-element.41.side_f, ...), custom_call_target="tpu_custom_call" | custom-call | flops 500000000 | bytes 1048576 | tf_op jit(solution)/shard_map/pallas_call | solution.py:591
  52.7 0.0 collective-permute-done.6.got_one
  52.7 1.4 %collective-permute-done.7.got_two = f32[2,24,128]{2,1,0:T(8,128)S(1)} collective-permute-done((f32[2,24,128]{2,1,0:T(8,128)S(1)}, f32[2,24,128]{2,1,0:T(8,128)S(1)}, u32[]{:S(2)}, u32[]{:S(2)}) %collective-permute-start.7) | collective-permute-done | bytes 24608 | tf_op jit(solution)/shard_map/ppermute | solution.py:524
  54.1 2.0 %shard_map.101 = (f32[6,32,128]{2,1,0:T(8,128)S(1)}, f32[128,768]{1,0:T(8,128)S(1)}, f32[128,768]{1,0:T(8,128)S(1)}) custom-call(s32[2]{0:T(128)S(1)} %pad_add_fusion.info, f32[7,32,128]{2,1,0:T(8,128)S(1)} %copy-done.2, f32[6,24,128]{2,1,0:T(8,128)S(1)} %get-tuple-element.45.resid, f32[6,24,128]{2,1,0:T(8,128)S(1)} %get-tuple-element.50.image, ...), custom_call_target="tpu_custom_call" | custom-call | tf_op jit(solution)/shard_map/pallas_call | solution.py:595
  56.1 1.6 %collective-permute-start.8 = (f32[128,768]{1,0:T(8,128)S(1)}, f32[128,768]{1,0:T(8,128)S(1)}, u32[]{:S(2)}, u32[]{:S(2)}) collective-permute-start(f32[128,768]{1,0:T(8,128)S(1)} %get-tuple-element.58), channel_id=1, source_target_pairs={{0,32},{32,0},{1,33},{33,1},{2,34},{34,2},{3,35},{35,3},{4,36},{36... | collective-permute-start | bytes 1179656 | tf_op jit(solution)/shard_map/ppermute | solution.py:600
  57.7 1.3 %collective-permute-done.8 = f32[128,768]{1,0:T(8,128)S(1)} collective-permute-done((f32[128,768]{1,0:T(8,128)S(1)}, f32[128,768]{1,0:T(8,128)S(1)}, u32[]{:S(2)}, u32[]{:S(2)}) %collective-permute-start.8) | collective-permute-done | bytes 393248 | tf_op jit(solution)/shard_map/ppermute | solution.py:600
  59.1 0.4 copy.11
  59.5 23.9 %all_to_all.16 = f32[128,1,768]{2,1,0:T(1,128)S(1)} all-to-all(f32[128,1,768]{2,1,0:T(1,128)S(1)} %copy.11), channel_id=1, replica_groups=mesh['y'=4,'core'=2,'pcol'=32] {'y','pcol'}, dimensions={0} | all-to-all | bytes 786432 | tf_op jit(solution)/shard_map/all_to_all | solution.py:601
  83.5 0.8 shard_map.102
  (3 shorter events, 0.1 us)
Async XLA Ops:
  4.2 19.1 %collective-permute-start = (f32[224,128]{1,0:T(8,128)}, f32[224,128]{1,0:T(8,128)S(1)}, u32[]{:S(2)}, u32[]{:S(2)}) collective-permute-start(f32[224,128]{1,0:T(8,128)} %get-tuple-element.35), channel_id=1, source_target_pairs={{0,1},{1,2},{2,3},{3,4},{4,5},{5,6},{6,7},{7,8},{8,9},{9,10},{10,1... | collective-permute-start | bytes 344072 | tf_op jit(solution)/shard_map/ppermute | solution.py:530
  6.8 16.5 %collective-permute-start.1 = (f32[224,128]{1,0:T(8,128)}, f32[224,128]{1,0:T(8,128)S(1)}, u32[]{:S(2)}, u32[]{:S(2)}) collective-permute-start(f32[224,128]{1,0:T(8,128)} %get-tuple-element.36), channel_id=1, source_target_pairs={{1,0},{2,1},{3,2},{4,3},{5,4},{6,5},{7,6},{8,7},{9,8},{10,9},{11,1... | collective-permute-start | bytes 344072 | tf_op jit(solution)/shard_map/ppermute | solution.py:530
  13.0 26.0 %all-to-all-start = ((f32[256,1,256]{2,1,0:T(1,128)}), f32[256,1,256]{2,1,0:T(1,128)S(1)}, u32[]{:S(2)}, u32[]{:S(2)}) async-start(f32[256,1,256]{2,1,0:T(1,128)} %get-tuple-element.34), calls=%async_computation | async-start | bytes 524288 | tf_op jit(solution)/shard_map/all_to_all | solution.py:552
  23.3 0.9 %copy-start.1 = (f32[7,32,128]{2,1,0:T(8,128)S(1)}, f32[7,32,128]{2,1,0:T(8,128)}, u32[]{:S(2)}) copy-start(f32[7,32,128]{2,1,0:T(8,128)} %get-tuple-element.33.frame) | copy-start | bytes 344068
  24.9 3.1 %collective-permute-start.2 = (f32[2,16,128]{2,1,0:T(8,128)S(1)}, f32[2,16,128]{2,1,0:T(8,128)S(1)}, u32[]{:S(2)}, u32[]{:S(2)}) collective-permute-start(f32[2,16,128]{2,1,0:T(8,128)S(1)} %get-tuple-element.38), channel_id=1, source_target_pairs={{0,32},{32,0},{64,96},{96,64},{128,160},{160,128},{192,224},{224,1... | collective-permute-start | bytes 49160 | tf_op jit(solution)/shard_map/ppermute | solution.py:524
  27.1 3.5 %collective-permute-start.3 = (f32[2,16,128]{2,1,0:T(8,128)S(1)}, f32[2,16,128]{2,1,0:T(8,128)S(1)}, u32[]{:S(2)}, u32[]{:S(2)}) collective-permute-start(f32[2,16,128]{2,1,0:T(8,128)S(1)} %get-tuple-element.39), channel_id=1, source_target_pairs={{0,224},{32,64},{64,32},{96,128},{128,96},{160,192},{192,160},{224... | collective-permute-start | bytes 49160 | tf_op jit(solution)/shard_map/ppermute | solution.py:524
  30.6 8.4 %copy-start = (f32[72,72,128]{2,1,0:T(8,128)S(1)}, f32[72,72,128]{2,1,0:T(8,128)}, u32[]{:S(2)}) copy-start(f32[72,72,128]{2,1,0:T(8,128)} %mats.3) | copy-start | bytes 7962628
  31.3 12.7 %copy-start.2 = (f32[7,32,128]{2,1,0:T(8,128)S(1)}, f32[7,32,128]{2,1,0:T(8,128)}, u32[]{:S(2)}) copy-start(f32[7,32,128]{2,1,0:T(8,128)} %get-tuple-element.33.frame) | copy-start | bytes 344068
  43.1 2.5 %collective-permute-start.4 = (f32[2,24,128]{2,1,0:T(8,128)S(1)}, f32[2,24,128]{2,1,0:T(8,128)S(1)}, u32[]{:S(2)}, u32[]{:S(2)}) collective-permute-start(f32[2,24,128]{2,1,0:T(8,128)S(1)} %get-tuple-element.47), channel_id=1, source_target_pairs={{0,32},{32,0},{64,96},{96,64},{128,160},{160,128},{192,224},{224,1... | collective-permute-start | bytes 73736 | tf_op jit(solution)/shard_map/ppermute | solution.py:524
  43.5 3.3 %collective-permute-start.5 = (f32[2,24,128]{2,1,0:T(8,128)S(1)}, f32[2,24,128]{2,1,0:T(8,128)S(1)}, u32[]{:S(2)}, u32[]{:S(2)}) collective-permute-start(f32[2,24,128]{2,1,0:T(8,128)S(1)} %get-tuple-element.48), channel_id=1, source_target_pairs={{0,224},{32,64},{64,32},{96,128},{128,96},{160,192},{192,160},{224... | collective-permute-start | bytes 73736 | tf_op jit(solution)/shard_map/ppermute | solution.py:524
  49.4 3.2 %collective-permute-start.6 = (f32[2,24,128]{2,1,0:T(8,128)S(1)}, f32[2,24,128]{2,1,0:T(8,128)S(1)}, u32[]{:S(2)}, u32[]{:S(2)}) collective-permute-start(f32[2,24,128]{2,1,0:T(8,128)S(1)} %get-tuple-element.53), channel_id=1, source_target_pairs={{0,32},{32,0},{64,96},{96,64},{128,160},{160,128},{192,224},{224,1... | collective-permute-start | bytes 73736 | tf_op jit(solution)/shard_map/ppermute | solution.py:524
  50.9 3.3 %collective-permute-start.7 = (f32[2,24,128]{2,1,0:T(8,128)S(1)}, f32[2,24,128]{2,1,0:T(8,128)S(1)}, u32[]{:S(2)}, u32[]{:S(2)}) collective-permute-start(f32[2,24,128]{2,1,0:T(8,128)S(1)} %get-tuple-element.54), channel_id=1, source_target_pairs={{0,224},{32,64},{64,32},{96,128},{128,96},{160,192},{192,160},{224... | collective-permute-start | bytes 73736 | tf_op jit(solution)/shard_map/ppermute | solution.py:524
  56.1 2.9 %collective-permute-start.8 = (f32[128,768]{1,0:T(8,128)S(1)}, f32[128,768]{1,0:T(8,128)S(1)}, u32[]{:S(2)}, u32[]{:S(2)}) collective-permute-start(f32[128,768]{1,0:T(8,128)S(1)} %get-tuple-element.58), channel_id=1, source_target_pairs={{0,32},{32,0},{1,33},{33,1},{2,34},{34,2},{3,35},{35,3},{4,36},{36... | collective-permute-start | bytes 1179656 | tf_op jit(solution)/shard_map/ppermute | solution.py:600
